TPU v7x, 32 devices: a whole 2x2x4 slice. The times are simulated.
32 devices in a mesh: dp: 4 (over y, x), expert: 8 (over z, core).
Axes of the slice: x: 2, y: 2, z: 4, core: 2. Of those that a mesh axis runs over, the one named last changes fastest.
Arguments:
- tokens: bfloat16 [5120, 2048], P(('dp', 'expert')), may hold values from -6 to 6
- teacher: bfloat16 [5120, 2048], P(('dp', 'expert')), may hold values from -6 to 6
- routes: int32 [5120, 8], P(('dp', 'expert')), may hold values from 0 to 31, all different within a row; in each aligned block of 160 rows (0 to 159, 160 to 319, ...) at most 50 rows name the same one
- cont_lengths: int32 [32], replicated, may hold values from 1 to 128, as said below
- query_weight: bfloat16 [2048, 4096], P('dp'), may hold values from -0.125 to 0.125
- key_projection: bfloat16 [2048, 512], P('dp'), may hold values from -0.125 to 0.125
- value_projection: bfloat16 [2048, 512], P('dp'), may hold values from -0.125 to 0.125
- output_weight: bfloat16 [4096, 2048], P('dp'), may hold values from -0.75 to 0.75
- router_weight: bfloat16 [2048, 32], replicated, may hold values from -0.0625 to 0.0625
- gate_weight: bfloat16 [32, 2048, 768], P(('dp', 'expert')), may hold values from -0.125 to 0.125
- up_weight: bfloat16 [32, 2048, 768], P(('dp', 'expert')), may hold values from -0.125 to 0.125
- down_weight: bfloat16 [32, 768, 2048], P(('dp', 'expert')), may hold values from -0.625 to 0.625
- input_gain: float32 [2048], replicated, may hold values from 0.5 to 1.5
- post_gain: float32 [2048], replicated, may hold values from 0.5 to 1.5
- query_gain: float32 [128], replicated, may hold values from 0.5 to 1.5
- key_gain: float32 [128], replicated, may hold values from 0.5 to 1.5
Outputs:
- layer_out: float32 [5120, 2048], P(('dp', 'expert'))
- loss: float32 [], replicated
- tokens_grad: float32 [5120, 2048], P(('dp', 'expert'))
- query_grad: float32 [2048, 4096], P(('dp', 'expert'))
- key_grad: float32 [2048, 512], P(('dp', 'expert'))
- value_grad: float32 [2048, 512], P(('dp', 'expert'))
- output_grad: float32 [4096, 2048], P(('dp', 'expert'))
- router_grad: float32 [2048, 32], replicated
- gate_grad: float32 [32, 2048, 768], P(('dp', 'expert'))
- up_grad: float32 [32, 2048, 768], P(('dp', 'expert'))
- down_grad: float32 [32, 768, 2048], P(('dp', 'expert'))
- input_gain_grad: float32 [2048], replicated
- post_gain_grad: float32 [2048], replicated
- query_gain_grad: float32 [128], replicated
- key_gain_grad: float32 [128], replicated
Inputs may be any that keep to these rules, and one draw needn't show every extreme that they name: `routes`: each row names 8 different experts; within the rows of one device (aligned blocks of 160 rows) no expert is named by more than 50 rows, a bound that some block reaches. `cont_lengths`: at least one continuation fills all 128 slots.
All inputs are finite; a program needn't handle non-finite values.
Results may differ from a plain program's by a relative error of at most 0.015.
Values may be sent and summed in bfloat16 or wider, within the bound.
A program may use at most 384 MiB of HBM per device.

v0:
```python
import jax
import jax.numpy as jnp
from jax import lax
from jax.sharding import PartitionSpec as P

CMAX = 128


norm_eps = 1e-06
rope_base = 1000000.0


def partner(shard, axis, bit):
    return lax.ppermute(shard, axis, [(i, i ^ 1 << bit) for i in range(lax.axis_size(axis))])


def root_mean_scale(value_rows, gain_vec):
    return (
        value_rows
        * lax.rsqrt(jnp.mean(value_rows * value_rows, axis=-1, keepdims=True) + norm_eps)
        * gain_vec
    )


def rotary_apply(value_rows, token_positions):
    head_width = value_rows.shape[-1]
    half_width = head_width // 2
    frequency = rope_base ** (-(jnp.arange(half_width, dtype=jnp.float32) * 2.0) / head_width)
    angles = token_positions.astype(jnp.float32)[:, None] * frequency[None, :]
    cosine = jnp.concatenate([jnp.cos(angles), jnp.cos(angles)], axis=-1)[:, None, :]
    sine_table = jnp.concatenate([jnp.sin(angles), jnp.sin(angles)], axis=-1)[:, None, :]
    turned = jnp.concatenate([-value_rows[..., half_width:], value_rows[..., :half_width]], axis=-1)
    return value_rows * cosine + turned * sine_table


def contract(left_side, right_side, left_dim, right_dim):
    return lax.dot_general(
        left_side,
        right_side,
        (((left_dim,), (right_dim,)), ((), ())),
        preferred_element_type=jnp.float32,
    )


def body(
    tokens,
    teacher,
    routes,
    cont_lengths,
    query_weight,
    key_projection,
    value_projection,
    output_weight,
    router_weight,
    gate_weight,
    up_weight,
    down_weight,
    input_gain,
    post_gain,
    query_gain,
    key_gain,
):
    n_dp = lax.axis_size("dp")
    n_owner = lax.axis_size("expert")
    devices = n_dp * n_owner
    rank_dp = lax.axis_index("dp")
    rank_owner = lax.axis_index("expert")
    flat_rank = rank_dp * n_owner + rank_owner
    first_column = rank_owner % 2 == 0
    tok_dev, model_width = tokens.shape
    top_count = routes.shape[1]
    head_dim = query_gain.shape[0]
    kv_width = key_projection.shape[1]
    kv_heads = kv_width // head_dim
    query_width = query_weight.shape[1]
    query_heads = query_width // head_dim
    key_value_group = query_heads // kv_heads
    ffn_width = gate_weight.shape[2]
    prompt_block = tok_dev - CMAX
    half_prompt = n_dp * prompt_block
    prompt_len = 2 * half_prompt
    key_total = prompt_len + CMAX
    capacity = max(2, tok_dev * top_count * 5 // (4 * devices))
    slots_all = devices * tok_dev
    score_scale = head_dim ** (-0.5)
    slot_ids = jnp.arange(tok_dev, dtype=jnp.int32)
    own_length = cont_lengths[flat_rank]
    piece_index = rank_owner % 2 * n_dp + rank_dp
    token_positions = jnp.where(
        slot_ids < prompt_block,
        piece_index * prompt_block + slot_ids,
        prompt_len + slot_ids - prompt_block,
    )
    valid_slot = (slot_ids < prompt_block) | (slot_ids - prompt_block < own_length)
    valid_count = (devices * prompt_block + jnp.sum(cont_lengths)).astype(jnp.float32)
    tokens_float = tokens.astype(jnp.float32)
    normed_float, first_norm_back = jax.vjp(root_mean_scale, tokens_float, input_gain)
    normed = normed_float.astype(jnp.bfloat16)
    whole_query, whole_key, whole_value = (
        lax.all_gather(query_weight, "dp", axis=0, tiled=True),
        lax.all_gather(key_projection, "dp", axis=0, tiled=True),
        lax.all_gather(value_projection, "dp", axis=0, tiled=True),
    )
    query_lin = jnp.dot(normed, whole_query, preferred_element_type=jnp.float32)
    key_linear = jnp.dot(normed, whole_key, preferred_element_type=jnp.float32)
    value_linear = jnp.dot(normed, whole_value, preferred_element_type=jnp.float32)
    query_rot, query_back = jax.vjp(
        lambda linear, gain_vec: rotary_apply(
            root_mean_scale(linear.reshape(tok_dev, query_heads, head_dim), gain_vec),
            token_positions,
        ),
        query_lin,
        query_gain,
    )
    key_rot, key_back = jax.vjp(
        lambda linear, gain_vec: rotary_apply(
            root_mean_scale(linear.reshape(tok_dev, kv_heads, head_dim), gain_vec), token_positions
        ),
        key_linear,
        key_gain,
    )
    queries = query_rot.astype(jnp.bfloat16)
    keys_own = key_rot.astype(jnp.bfloat16).reshape(tok_dev, kv_width)
    values_own = value_linear.astype(jnp.bfloat16)
    column_kv = lax.all_gather(
        jnp.stack([keys_own[:prompt_block], values_own[:prompt_block]]), "dp", axis=1, tiled=True
    )
    other_kv = partner(column_kv, "expert", 0)
    full_kv = jnp.where(
        first_column,
        jnp.concatenate([column_kv, other_kv], axis=1),
        jnp.concatenate([other_kv, column_kv], axis=1),
    )
    all_keys = jnp.concatenate([full_kv[0], keys_own[prompt_block:]], axis=0).reshape(
        key_total, kv_heads, head_dim
    )
    all_values = jnp.concatenate([full_kv[1], values_own[prompt_block:]], axis=0).reshape(
        key_total, kv_heads, head_dim
    )
    key_ids = jnp.arange(key_total, dtype=jnp.int32)[None, :]
    prompt_query = (slot_ids < prompt_block)[:, None]
    sees_prompt = (key_ids < prompt_len) & (~prompt_query | (key_ids <= token_positions[:, None]))
    cont_key = key_ids - prompt_len
    sees_cont = (
        (key_ids >= prompt_len)
        & ~prompt_query
        & (cont_key <= (slot_ids - prompt_block)[:, None])
        & (cont_key < own_length)
    )
    allowed = (sees_prompt | sees_cont)[None]
    grouped_q = queries.reshape(tok_dev, kv_heads, key_value_group, head_dim).transpose(1, 0, 2, 3)
    head_keys = all_keys.transpose(1, 0, 2)
    head_values = all_values.transpose(1, 0, 2)

    def forward_head(operands):
        query_block, key_block, value_block = operands
        scores = (
            jnp.einsum("trd,kd->rtk", query_block, key_block, preferred_element_type=jnp.float32)
            * score_scale
        )
        masked = jnp.where(allowed, scores, -jnp.inf)
        peak_score = jnp.max(masked, axis=-1, keepdims=True)
        exponent = jnp.exp(masked - peak_score)
        row_total = jnp.sum(exponent, axis=-1, keepdims=True)
        probs_low = (exponent / row_total).astype(jnp.bfloat16)
        out_block = jnp.einsum(
            "rtk,kd->trd", probs_low, value_block, preferred_element_type=jnp.float32
        ).astype(jnp.bfloat16)
        return (out_block, peak_score + jnp.log(row_total))

    head_out, log_total = lax.map(forward_head, (grouped_q, head_keys, head_values))
    attended = head_out.transpose(1, 0, 2, 3).reshape(tok_dev, query_width)
    whole_output = lax.all_gather(output_weight, "dp", axis=0, tiled=True)
    state = tokens_float + jnp.dot(attended, whole_output, preferred_element_type=jnp.float32)
    mixed_float, second_norm_back = jax.vjp(root_mean_scale, state, post_gain)
    mixed = mixed_float.astype(jnp.bfloat16)
    logits = jnp.dot(mixed, router_weight, preferred_element_type=jnp.float32)
    gates = jax.nn.softmax(jnp.take_along_axis(logits, routes, axis=1), axis=-1)
    rows_total = tok_dev * top_count
    expert_ids = routes.reshape(rows_total)
    live_rows = jnp.repeat(valid_slot, top_count)
    expert_range = jnp.arange(devices, dtype=jnp.int32)
    hit_table = ((expert_ids[:, None] == expert_range[None, :]) & live_rows[:, None]).astype(
        jnp.int32
    )
    earlier = jnp.cumsum(hit_table, axis=0) - hit_table
    position_in = jnp.sum(earlier * hit_table, axis=1)
    slot_index = jnp.where(live_rows, expert_ids * capacity + position_in, devices * capacity)
    row_of_slot = (
        jnp.full((devices * capacity + 1,), rows_total, jnp.int32)
        .at[slot_index]
        .set(jnp.arange(rows_total, dtype=jnp.int32))[: devices * capacity]
    )
    token_of_slot = jnp.where(row_of_slot < rows_total, row_of_slot // top_count, tok_dev)
    mixed_pad = jnp.concatenate([mixed, jnp.zeros((1, model_width), jnp.bfloat16)], axis=0)
    send_rows = mixed_pad[token_of_slot].reshape(devices, capacity, model_width)
    arrived = lax.all_to_all(send_rows, ("dp", "expert"), split_axis=0, concat_axis=0, tiled=True)
    sources = arrived.shape[0]
    items = arrived.shape[1]
    flat_in = arrived.reshape(sources * items, model_width)
    gate_pre = jnp.dot(flat_in, gate_weight[0], preferred_element_type=jnp.float32)
    up_pre = jnp.dot(flat_in, up_weight[0], preferred_element_type=jnp.float32)
    hidden_units = (jax.nn.silu(gate_pre) * up_pre).astype(jnp.bfloat16)
    produced = jnp.dot(hidden_units, down_weight[0], preferred_element_type=jnp.float32).astype(
        jnp.bfloat16
    )
    produced, gate_pre, up_pre, hidden_units, arrived = (
        produced.reshape(sources, items, model_width),
        gate_pre.reshape(sources, items, ffn_width),
        up_pre.reshape(sources, items, ffn_width),
        hidden_units.reshape(sources, items, ffn_width),
        arrived,
    )
    returned = lax.all_to_all(produced, ("dp", "expert"), split_axis=0, concat_axis=0, tiled=True)
    returned_pad = jnp.concatenate(
        [
            returned.reshape(devices * capacity, model_width),
            jnp.zeros((1, model_width), jnp.bfloat16),
        ],
        axis=0,
    )
    copies = returned_pad[slot_index].reshape(tok_dev, top_count, model_width)
    layer_out = state + jnp.sum(gates[:, :, None] * copies, axis=1)
    live_tokens = valid_slot.astype(jnp.float32)[:, None]
    diff = (layer_out - teacher.astype(jnp.float32)) * live_tokens
    local_square = jnp.sum(diff * diff)
    d_out = 2.0 * slots_all * diff / valid_count
    d_gates = jnp.sum(d_out[:, None, :] * copies, axis=-1)
    d_chosen = gates * (d_gates - jnp.sum(gates * d_gates, axis=-1, keepdims=True))
    d_logits = jnp.sum(
        jnp.where(routes[:, :, None] == expert_range[None, None, :], d_chosen[:, :, None], 0.0),
        axis=1,
    ).astype(jnp.bfloat16)
    d_copies = (
        (gates[:, :, None] * d_out[:, None, :])
        .astype(jnp.bfloat16)
        .reshape(rows_total, model_width)
    )
    d_copies_pad = jnp.concatenate([d_copies, jnp.zeros((1, model_width), jnp.bfloat16)], axis=0)
    d_send = d_copies_pad[row_of_slot].reshape(devices, capacity, model_width)
    d_arrived = lax.all_to_all(d_send, ("dp", "expert"), split_axis=0, concat_axis=0, tiled=True)
    flat_d = d_arrived.reshape(-1, model_width)
    flat_in = arrived.reshape(-1, model_width)
    flat_gate = gate_pre.reshape(-1, ffn_width)
    flat_up = up_pre.reshape(-1, ffn_width)
    flat_hidden = hidden_units.reshape(-1, ffn_width)
    d_hidden = contract(flat_d, down_weight[0], 1, 1)
    sigmoid_gate = jax.nn.sigmoid(flat_gate)
    d_gate = (d_hidden * flat_up * sigmoid_gate * (1.0 + flat_gate * (1.0 - sigmoid_gate))).astype(
        jnp.bfloat16
    )
    d_up = (d_hidden * flat_gate * sigmoid_gate).astype(jnp.bfloat16)
    down_grad = contract(flat_hidden, flat_d, 0, 0)[None]
    gate_grad = contract(flat_in, d_gate, 0, 0)[None]
    up_grad = contract(flat_in, d_up, 0, 0)[None]
    d_in = (contract(d_gate, gate_weight[0], 1, 1) + contract(d_up, up_weight[0], 1, 1)).astype(
        jnp.bfloat16
    )
    d_returned = lax.all_to_all(
        d_in.reshape(devices, capacity, model_width),
        ("dp", "expert"),
        split_axis=0,
        concat_axis=0,
        tiled=True,
    )
    d_returned_pad = jnp.concatenate(
        [
            d_returned.reshape(devices * capacity, model_width),
            jnp.zeros((1, model_width), jnp.bfloat16),
        ],
        axis=0,
    )
    d_mixed = jnp.sum(
        d_returned_pad[slot_index].reshape(tok_dev, top_count, model_width),
        axis=1,
        dtype=jnp.float32,
    )
    d_mixed = d_mixed + contract(d_logits, router_weight, 1, 1)
    router_local = contract(mixed, d_logits, 0, 0)
    d_state_norm, d_post_gain = second_norm_back(d_mixed)
    d_state = d_out + d_state_norm
    d_branch = d_state.astype(jnp.bfloat16)
    d_attended = contract(
        d_branch, lax.all_gather(output_weight, "dp", axis=0, tiled=True), 1, 1
    ).astype(jnp.bfloat16)
    d_grouped = d_attended.reshape(tok_dev, kv_heads, key_value_group, head_dim).transpose(
        1, 0, 2, 3
    )

    def backward_head(operands):
        query_block, key_block, value_block, d_block, log_block = operands
        scores_again = (
            jnp.einsum("trd,kd->rtk", query_block, key_block, preferred_element_type=jnp.float32)
            * score_scale
        )
        probs = jnp.exp(jnp.where(allowed, scores_again, -jnp.inf) - log_block)
        probs_again = probs.astype(jnp.bfloat16)
        d_probs = jnp.einsum(
            "trd,kd->rtk", d_block, value_block, preferred_element_type=jnp.float32
        )
        inner_sum = jnp.sum(probs * d_probs, axis=-1, keepdims=True)
        d_scores = (probs * (d_probs - inner_sum)).astype(jnp.bfloat16)
        d_query_block = (
            jnp.einsum("rtk,kd->trd", d_scores, key_block, preferred_element_type=jnp.float32)
            * score_scale
        )
        d_key_block = (
            jnp.einsum("rtk,trd->kd", d_scores, query_block, preferred_element_type=jnp.float32)
            * score_scale
        )
        d_value_block = jnp.einsum(
            "rtk,trd->kd", probs_again, d_block, preferred_element_type=jnp.float32
        )
        return (d_query_block, d_key_block, d_value_block)

    d_query_heads, d_key_heads, d_value_heads = lax.map(
        backward_head, (grouped_q, head_keys, head_values, d_grouped, log_total)
    )
    d_queries = d_query_heads.transpose(1, 0, 2, 3).reshape(tok_dev, query_heads, head_dim)
    d_keys = d_key_heads.transpose(1, 0, 2).reshape(key_total, kv_width)
    d_values = d_value_heads.transpose(1, 0, 2).reshape(key_total, kv_width)
    prompt_grads = jnp.stack([d_keys[:prompt_len], d_values[:prompt_len]])
    mine_part = jnp.where(
        first_column, prompt_grads[:, :half_prompt], prompt_grads[:, half_prompt:]
    )
    their_part = jnp.where(
        first_column, prompt_grads[:, half_prompt:], prompt_grads[:, :half_prompt]
    )
    partner_part = partner(their_part.astype(jnp.bfloat16), "expert", 0).astype(their_part.dtype)
    own_prompt = lax.psum_scatter(
        (mine_part + partner_part).astype(jnp.bfloat16), "dp", scatter_dimension=1, tiled=True
    ).astype(jnp.float32)
    d_key_post = jnp.concatenate([own_prompt[0], d_keys[prompt_len:]], axis=0).reshape(
        tok_dev, kv_heads, head_dim
    )
    d_value_lin = jnp.concatenate([own_prompt[1], d_values[prompt_len:]], axis=0).astype(
        jnp.bfloat16
    )
    d_query_float, d_query_gain = query_back(d_queries)
    d_key_float, d_key_gain = key_back(d_key_post)
    d_query_lin = d_query_float.astype(jnp.bfloat16)
    d_key_lin = d_key_float.astype(jnp.bfloat16)
    blocks = lax.all_gather(
        (query_weight, key_projection, value_projection), "dp", axis=0, tiled=True
    )
    d_normed = (
        contract(d_query_lin, blocks[0], 1, 1)
        + contract(d_key_lin, blocks[1], 1, 1)
        + contract(d_value_lin, blocks[2], 1, 1)
    )
    d_tokens_norm, d_input_gain = first_norm_back(d_normed)
    tokens_grad = d_state + d_tokens_norm
    pieces = [
        contract(normed, d_query_lin, 0, 0),
        contract(normed, d_key_lin, 0, 0),
        contract(normed, d_value_lin, 0, 0),
        contract(attended, d_branch, 0, 0).reshape(
            model_width // devices * lax.axis_size(("dp", "expert")), 2 * model_width
        ),
    ]
    weight_rows = lax.psum_scatter(
        jnp.concatenate(pieces, axis=1), ("dp", "expert"), scatter_dimension=0, tiled=True
    )
    rows_here = weight_rows.shape[0]
    query_grad = weight_rows[:, :query_width]
    key_grad = weight_rows[:, query_width : query_width + kv_width]
    value_grad = weight_rows[:, query_width + kv_width : query_width + 2 * kv_width]
    output_grad = weight_rows[:, query_width + 2 * kv_width :].reshape(2 * rows_here, model_width)
    total_square, input_gain_grad, post_gain_grad, query_gain_grad, key_gain_grad, router_grad = (
        lax.psum(
            (local_square, d_input_gain, d_post_gain, d_query_gain, d_key_gain, router_local),
            ("dp", "expert"),
        )
    )
    loss = total_square / (valid_count * model_width)
    return (
        layer_out,
        loss,
        tokens_grad,
        query_grad,
        key_grad,
        value_grad,
        output_grad,
        router_grad,
        gate_grad,
        up_grad,
        down_grad,
        input_gain_grad,
        post_gain_grad,
        query_gain_grad,
        key_gain_grad,
    )


def solution(mesh):
    in_specs = (
        P(("dp", "expert"), None),
        P(("dp", "expert"), None),
        P(("dp", "expert"), None),
        P(),
        P("dp", None),
        P("dp", None),
        P("dp", None),
        P("dp", None),
        P(),
        P(("dp", "expert"), None, None),
        P(("dp", "expert"), None, None),
        P(("dp", "expert"), None, None),
        P(),
        P(),
        P(),
        P(),
    )
    out_specs = (
        P(("dp", "expert"), None),
        P(),
        P(("dp", "expert"), None),
        P(("dp", "expert"), None),
        P(("dp", "expert"), None),
        P(("dp", "expert"), None),
        P(("dp", "expert"), None),
        P(),
        P(("dp", "expert"), None, None),
        P(("dp", "expert"), None, None),
        P(("dp", "expert"), None, None),
        P(),
        P(),
        P(),
        P(),
    )
    return jax.shard_map(body, mesh=mesh, in_specs=in_specs, out_specs=out_specs, check_vma=False)
```

profile of v0, /device:TPU:8, one launch (start us, length us, event | category | flops | bytes accessed | tf_op | source)
XLA Modules:
  0.0 2294.9 jit_solution(15996888919398194085)
XLA Ops:
  13.8 15.9 reduce-window.6
  57.5 26.0 %all-gather.7.cloned.1.call-done = bf16[2048,512]{1,0:T(8,128)(2,1)} async-done(((bf16[512,512]{1,0:T(8,128)(2,1)}), bf16[2048,512]{1,0:T(8,128)(2,1)}) %all-gather.7.cloned.1.call-update) | async-done | bytes 2097168 | tf_op jit(solution)/shard_map/all_gather | solution.py:102
  109.1 133.8 %all-gather.9.cloned.1.call-done = bf16[2048,4096]{1,0:T(8,128)(2,1)} async-done(((bf16[512,4096]{1,0:T(8,128)(2,1)}), bf16[2048,4096]{1,0:T(8,128)(2,1)}) %all-gather.9.cloned.1.call-update) | async-done | bytes 16777232 | tf_op jit(solution)/shard_map/all_gather | solution.py:100
  279.5 24.6 %while.28 = (s32[]{:T(128)}, bf16[4,160,8,128]{3,1,2,0:T(8,128)(2,1)}, f32[4,8,160,1]{2,1,3,0:T(8,128)}, bf16[4,384,128]{2,1,0:T(8,128)(2,1)}, bf16[4,384,128]{2...) while((s32[]{:T(128)}, ...), condition=%wide.region_6.7_spmd.clone, body=%wide.region_3.6_spmd.clone.sunk | while | flops 256244480 | bytes 6923441 | solution.py:171
  307.1 94.9 %all-gather.11.cloned.1.call-done = bf16[4096,2048]{1,0:T(8,128)(2,1)} async-done(((bf16[1024,2048]{1,0:T(8,128)(2,1)}), bf16[4096,2048]{1,0:T(8,128)(2,1)}) %all-gather.11.cloned.1.call-update) | async-done | bytes 16777232 | tf_op jit(solution)/shard_map/all_gather | solution.py:173
  414.5 15.9 gather_fusion
  439.1 164.6 %all_to_all.20 = bf16[32,50,2048]{2,1,0:T(8,128)(2,1)} all-to-all(bf16[32,50,2048]{2,1,0:T(8,128)(2,1)} %reshape.623), channel_id=1, replica_groups=mesh['dp'=4,'expert'=8] {'dp','expert'}, dimensions={0} | all-to-all | bytes 13107200 | tf_op jit(solution)/shard_map/all_to_all | solution.py:197
  666.4 143.4 %all-to-all-done.1 = bf16[32,50,2048]{2,1,0:T(8,128)(2,1)} async-done(((bf16[32,50,2048]{2,1,0:T(8,128)(2,1)}), bf16[32,50,2048]{2,1,0:T(8,128)(2,1)}, u32[]{:S(2)}, u32[]{:S(2)}) %all-to-all-start.1) | async-done | bytes 6553632 | tf_op jit(solution)/shard_map/all_to_all | solution.py:214
  825.3 14.7 gather_fusion.1
  853.4 17.5 gather_fusion.2
  879.5 168.2 %all_to_all.21 = bf16[32,50,2048]{2,1,0:T(8,128)(2,1)} all-to-all(bf16[32,50,2048]{2,1,0:T(8,128)(2,1)} %reshape.627), channel_id=1, replica_groups=mesh['dp'=4,'expert'=8] {'dp','expert'}, dimensions={0} | all-to-all | bytes 13107200 | tf_op jit(solution)/shard_map/all_to_all | solution.py:241
  1056.5 12.3 multiply_convert_fusion
  1104.7 152.7 %all-to-all-done.3 = bf16[32,50,2048]{2,1,0:T(8,128)(2,1)} async-done(((bf16[32,50,2048]{2,1,0:T(8,128)(2,1)}), bf16[32,50,2048]{2,1,0:T(8,128)(2,1)}, u32[]{:S(2)}, u32[]{:S(2)}) %all-to-all-start.3) | async-done | bytes 6553632 | tf_op jit(solution)/shard_map/all_to_all | solution.py:259
  1273.3 14.5 gather_fusion.3
  1297.0 13.6 fusion.83
  1310.6 11.9 fusion.76
  1323.5 35.9 %while.29 = (s32[]{:T(128)}, f32[4,160,8,128]{3,1,2,0:T(8,128)}, f32[4,384,128]{1,2,0:T(8,128)}, f32[4,384,128]{1,2,0:T(8,128)}, bf16[4,384,128]{2,1,0:T(8,128)(...) while((s32[]{:T(128)}, f32[4,160,8,128]{3,1,2,0:T(8,128)}, ...), condition=%wide.region_25.26_spmd.clone, body=%wide.region_23.25_spmd.clone.sunk | while | flops 634272512 | bytes 34074916 | solution.py:316
  1379.9 13.6 fusion.130
  1396.2 37.9 %reshape.633 = f32[2048,4096]{1,0:T(8,128)} reshape(f32[4096,2048]{1,0:T(8,128)} %fusion.83) | data formatting | bytes 67108864 | tf_op jit(solution)/shard_map/reshape | solution.py:357
  1447.1 48.8 %pad_maximum_fusion = f32[2048,9216]{1,0:T(8,128)} fusion(f32[2048,4096]{1,0:T(8,128)} %reshape.633, f32[2048,512]{1,0:T(8,128)} %fusion.98, f32[2048,512]{1,0:T(8,128)} %fusion.128, f32[2048,4096]{1,0:T(8,128)} %fusion.130), kind=kLoop, calls=%fused_computation.73 | loop fusion | flops 56623104 | bytes 150994944 | tf_op jit(solution)/shard_map/concatenate | solution.py:362
  1530.9 15.2 fusion.145
  1552.5 44.4 %all-reduce.9 = (f32[]{:T(128)}, f32[2048]{0:T(1024)}, f32[2048]{0:T(1024)}, f32[128]{0:T(128)}, f32[128]{0:T(128)}) all-reduce(f32[]{:T(128)} %multiply_reduce_fusion.5, f32[2048]{0:T(1024)S(1)} %get-tuple-element.192, f32[2048]{0:T(1024)S(1)} %copy-done.60, ...), channel_id=1, replica_groups=mesh['dp'=4,'expert'=8] {'dp','expert'}, use_global_device_ids=true, to_apply=%region_16.17 | all-reduce | flops 4353 | bytes 34824 | tf_op jit(solution)/shard_map/psum | solution.py:370
  1597.6 556.2 %reduce-scatter.2.cloned.1.call-done = f32[64,9216]{1,0:T(8,128)} async-done(((f32[2048,9216]{1,0:T(8,128)}), f32[64,9216]{1,0:T(8,128)}) %reduce-scatter.2.cloned.1.call-update) | async-done | bytes 2359312 | tf_op jit(solution)/shard_map/reduce_scatter | solution.py:361
  2161.1 123.7 %all-reduce.13.cloned.1.call-done = f32[2048,32]{0,1:T(8,128)} async-done(((f32[2048,32]{0,1:T(8,128)}), f32[2048,32]{0,1:T(8,128)}) %all-reduce.13.cloned.1.call-update) | async-done | bytes 262160 | tf_op jit(solution)/shard_map/psum | solution.py:370
  (451 shorter events, 435.7 us)
Async XLA Ops:
  7.2 622.3 %copy-start = (bf16[1,768,2048]{2,1,0:T(8,128)(2,1)S(1)}, bf16[1,768,2048]{2,1,0:T(8,128)(2,1)}, u32[]{:S(2)}) copy-start(bf16[1,768,2048]{2,1,0:T(8,128)(2,1)} %param.31) | copy-start | bytes 9437188
  7.2 39.2 %all-gather.5.cloned.1.call-start = ((), (), s32[]{:S(2)}) async-start(), calls=%async_computation.5 | async-start | bytes 2621440 | tf_op jit(solution)/shard_map/all_gather | solution.py:101
  7.9 75.6 %all-gather.7.cloned.1.call-start = ((), (), s32[]{:S(2)}) async-start(), calls=%async_computation.6 | async-start | bytes 2621440 | tf_op jit(solution)/shard_map/all_gather | solution.py:102
  8.7 234.2 %all-gather.9.cloned.1.call-start = ((), (), s32[]{:S(2)}) async-start(), calls=%async_computation.7 | async-start | bytes 20971520 | tf_op jit(solution)/shard_map/all_gather | solution.py:100
  9.4 392.6 %all-gather.11.cloned.1.call-start = ((), (), s32[]{:S(2)}) async-start(), calls=%async_computation.8 | async-start | bytes 20971520 | tf_op jit(solution)/shard_map/all_gather | solution.py:173
  10.0 36.4 %copy-start.33 = (f32[2048]{0:T(1024)S(1)}, f32[2048]{0:T(1024)}, u32[]{:S(2)}) copy-start(f32[2048]{0:T(1024)} %param.32) | copy-start | bytes 24580
  41.8 54.4 %copy-start.26 = (f32[160,128]{0,1:T(8,128)}, f32[160,128]{0,1:T(8,128)S(1)}, u32[]{:S(2)}) copy-start(f32[160,128]{0,1:T(8,128)S(1)} %pad_maximum_fusion.6) | copy-start | bytes 245764
  41.8 55.1 %copy-start.28 = (f32[160,128]{0,1:T(8,128)}, f32[160,128]{0,1:T(8,128)S(1)}, u32[]{:S(2)}) copy-start(f32[160,128]{0,1:T(8,128)S(1)} %pad_maximum_fusion.7) | copy-start | bytes 245764
  43.3 11.4 copy-start.69
  57.5 28.4 %copy-start.47 = (bf16[1,32,512]{2,1,0:T(8,128)(2,1)S(1)}, bf16[1,32,512]{2,1,0:T(8,128)(2,1)}, u32[]{:S(2)}) copy-start(bf16[1,32,512]{2,1,0:T(8,128)(2,1)} %copy.287) | copy-start | bytes 98308
  95.6 5.6 collective-permute-start
  304.1 107.4 %copy-start.18 = (bf16[4,384,128]{2,1,0:T(8,128)(2,1)}, bf16[4,384,128]{2,1,0:T(8,128)(2,1)S(1)}, u32[]{:S(2)}) copy-start(bf16[4,384,128]{2,1,0:T(8,128)(2,1)S(1)} %get-tuple-element.609) | copy-start | bytes 1179652
  411.6 18.8 copy-start.65
  645.5 164.3 %all-to-all-start.1 = ((bf16[32,50,2048]{2,1,0:T(8,128)(2,1)}), bf16[32,50,2048]{2,1,0:T(8,128)(2,1)}, u32[]{:S(2)}, u32[]{:S(2)}) async-start(bf16[32,50,2048]{2,1,0:T(8,128)(2,1)} %reshape.625), calls=%async_computation.1 | async-start | bytes 14680064 | tf_op jit(solution)/shard_map/all_to_all | solution.py:214
  654.2 193.8 %copy-start.72 = (f32[160]{0:T(256)}, f32[160]{0:T(256)S(1)}, u32[]{:S(2)}) copy-start(f32[160]{0:T(256)S(1)} %fusion.125) | copy-start | bytes 1924
  1056.5 12.3 copy-start.78
  1093.2 164.3 %all-to-all-start.3 = ((bf16[32,50,2048]{2,1,0:T(8,128)(2,1)}), bf16[32,50,2048]{2,1,0:T(8,128)(2,1)}, u32[]{:S(2)}, u32[]{:S(2)}) async-start(bf16[32,50,2048]{2,1,0:T(8,128)(2,1)} %reshape.629), calls=%async_computation.3 | async-start | bytes 14680064 | tf_op jit(solution)/shard_map/all_to_all | solution.py:259
  1099.6 334.5 %all-reduce.15.cloned.1.call-start = ((), (), s32[]{:S(2)}) async-start(), calls=%async_computation.11 | async-start | bytes 524288
  1104.7 189.5 %copy-start.45 = (bf16[160,32]{0,1:T(8,128)(2,1)}, bf16[160,32]{0,1:T(8,128)(2,1)S(1)}, u32[]{:S(2)}) copy-start(bf16[160,32]{0,1:T(8,128)(2,1)S(1)} %select_reduce_fusion) | copy-start | bytes 30724
  1361.8 16.0 collective-permute-start.1
  1379.9 774.0 %reduce-scatter.2.cloned.1.call-start = ((), (), s32[]{:S(2)}) async-start(), calls=%async_computation.9 | async-start | bytes 77856768 | tf_op jit(solution)/shard_map/reduce_scatter | solution.py:361
  1495.9 788.8 %all-reduce.13.cloned.1.call-start = ((), (), s32[]{:S(2)}) async-start(), calls=%async_computation.10 | async-start | bytes 524288 | tf_op jit(solution)/shard_map/psum | solution.py:370
  1501.1 21.6 slice-start
  2153.8 132.6 %copy-start.1 = (bf16[1,768,2048]{2,1,0:T(8,128)(2,1)S(1)}, bf16[1,768,2048]{2,1,0:T(8,128)(2,1)}, u32[]{:S(2)}) copy-start(bf16[1,768,2048]{2,1,0:T(8,128)(2,1)} %param.31) | copy-start | bytes 9437188
  (87 other events, 344.2 us)
Sparse Core Ops, SparseCore 0:
  9.9 36.4 all-gather.4
  48.2 35.2 all-gather.6
  85.4 157.4 all-gather.8
  244.6 157.4 all-gather.10
  1380.0 45.0 all-reduce.14
  1496.0 657.7 reduce-scatter.1
  2159.9 124.7 all-reduce.12
where the time goes:
time: 2310 us; the launch traced here: 2290 us
  waiting for transfers between devices  1240 us (54%)
  blocking collectives  387 us (17%)
  local copies, waits for them, and re-layouts  279 us (12%)
  matrix products  215 us (9%)
  other arithmetic  145 us (6%)
    reduce_scatter x1, waiting for transfers between devices, body(): lax.psum_scatter(jnp.concatenate(pieces, axis=1), ('dp', 'expert'), scatt...  556 us
    all_to_all x1, blocking collectives, body(): lax.all_to_all(d_send, ('dp', 'expert'), split_axis=0, concat_axis=0, til...  168 us
    all_to_all x1, blocking collectives, body(): lax.all_to_all(send_rows, ('dp', 'expert'), split_axis=0, concat_axis=0,...  165 us
    all_to_all x1, waiting for transfers between devices, body(): lax.all_to_all(d_in.reshape(devices, capacity, model_width), ('dp', 'expe...  153 us
    all_to_all x1, waiting for transfers between devices, body(): lax.all_to_all(produced, ('dp', 'expert'), split_axis=0, concat_axis=0, t...  143 us
    all_gather x1, waiting for transfers between devices, body(): lax.all_gather(query_weight, 'dp', axis=0, tiled=True)  134 us
    dot_general x16, matrix products, contract(): lax.dot_general(left_side, right_side, (((left_dim,), (right_dim,)), ((),...  126 us
    psum x1, waiting for transfers between devices, body(): lax.psum((local_square, d_input_gain, d_post_gain, d_query_gain, d_key_ga...  124 us
  transfers between devices with their start and end apart: 11, of which 8 were waited for; matrix products, arithmetic and copies ran while one was open for 12% of the time, Pallas kernels for 0%

commit v1 on v0

v1 whole, which is shorter than its diff:
```python
import functools

import jax
import jax.numpy as jnp
from jax import lax
from jax.experimental import pallas as pl
from jax.experimental.pallas import tpu as pltpu
from jax.sharding import PartitionSpec as P

CMAX = 128
norm_eps = 1e-06
rope_base = 1000000.0
MESH = pl.DeviceIdType.MESH
F32 = jnp.float32
BF16 = jnp.bfloat16
VMEM_SPEC = pl.BlockSpec(memory_space=pltpu.VMEM)
ANY_SPEC = pl.BlockSpec(memory_space=pl.ANY)
VMEM_LIMIT = 56 * 1024 * 1024


def params(collective_id=None):
    return pltpu.CompilerParams(
        collective_id=collective_id,
        has_side_effects=collective_id is not None,
        vmem_limit_bytes=VMEM_LIMIT,
    )


def greet(devices):
    barrier = pltpu.get_barrier_semaphore()
    for device in devices:
        pl.semaphore_signal(barrier, inc=1, device_id=device, device_id_type=MESH)
    pl.semaphore_wait(barrier, len(devices))


def remote(src, dst, send_sem, recv_sem, device):
    return pltpu.make_async_remote_copy(
        src_ref=src,
        dst_ref=dst,
        send_sem=send_sem,
        recv_sem=recv_sem,
        device_id=device,
        device_id_type=MESH,
    )


def aligned(index, size):
    return pl.ds(pl.multiple_of(index * size, size), size)


def dot_nn(a, b):
    return lax.dot_general(a, b, (((1,), (0,)), ((), ())), preferred_element_type=F32)


def dot_nt(a, b):
    return lax.dot_general(a, b, (((1,), (1,)), ((), ())), preferred_element_type=F32)


def dot_tn(a, b):
    return lax.dot_general(a, b, (((0,), (0,)), ((), ())), preferred_element_type=F32)


PEER_MASKS = (3, 1, 2)


def qkv_kernel(tok, normed, wq, wk, wv, lin, cols, send, recv, asend, arecv, ssem, rsem):
    r, e = lax.axis_index("dp"), lax.axis_index("expert")
    peers = [r ^ m for m in PEER_MASKS]
    width = wq.shape[0]
    qg = wq.shape[1] // 4
    kg = wk.shape[1] // 4
    rows = cols.shape[0]
    greet([(p, e) for p in peers])
    first = []
    for i, p in enumerate(peers):
        copy = remote(
            normed.at[:, aligned(p, width)], cols.at[aligned(r, tok), :],
            asend.at[i], arecv.at[i], (p, e),
        )
        copy.start()
        first.append(copy)
    cols[aligned(r, tok), :] = normed[:, aligned(r, width)]
    for copy in first:
        copy.wait()

    def products(p, dst):
        def chunk(c, carry):
            t = aligned(c, tok)
            x = cols[t, :]
            dst[t, :qg] = dot_nn(x, wq[:, aligned(p, qg)]).astype(dst.dtype)
            dst[t, qg : qg + kg] = dot_nn(x, wk[:, aligned(p, kg)]).astype(dst.dtype)
            dst[t, qg + kg :] = dot_nn(x, wv[:, aligned(p, kg)]).astype(dst.dtype)
            return carry

        lax.fori_loop(0, rows // tok, chunk, 0)

    second = []
    for i, p in enumerate(peers):
        products(p, send.at[i])
        copy = remote(send.at[i], recv.at[i], ssem.at[i], rsem.at[i], (p, e))
        copy.start()
        second.append(copy)
    products(r, lin)
    for i in (1, 2, 0):
        second[i].wait()

    def total(c, carry):
        t = aligned(c, 32)
        lin[t, :] = lin[t, :] + (
            recv[0, t, :].astype(F32) + recv[1, t, :].astype(F32) + recv[2, t, :].astype(F32)
        )
        return carry

    lax.fori_loop(0, rows // 32, total, 0)


def project_qkv(normed, wq, wk, wv):
    tok = normed.shape[0]
    rows = 4 * tok
    group = (wq.shape[1] + wk.shape[1] + wv.shape[1]) // 4
    return pl.pallas_call(
        functools.partial(qkv_kernel, tok),
        out_shape=(
            jax.ShapeDtypeStruct((rows, group), F32),
            jax.ShapeDtypeStruct((rows, wq.shape[0]), BF16),
        ),
        in_specs=[VMEM_SPEC] * 4,
        out_specs=(VMEM_SPEC, VMEM_SPEC),
        scratch_shapes=[
            pltpu.VMEM((3, rows, group), BF16),
            pltpu.VMEM((3, rows, group), BF16),
        ]
        + [pltpu.SemaphoreType.DMA((3,))] * 4,
        compiler_params=params(1),
        name="qkv_exchange",
    )(normed, wq, wk, wv)


def out_kernel(attn, wo, total, send, recv, ssem, rsem):
    r, e = lax.axis_index("dp"), lax.axis_index("expert")
    peers = [r ^ m for m in PEER_MASKS]
    tok = total.shape[0]
    width = total.shape[1]
    step = width // 4
    greet([(p, e) for p in peers])

    def products(p, dst):
        def chunk(c, carry):
            n = aligned(c, step)
            dst[:, n] = dot_nn(attn[aligned(p, tok), :], wo[:, n]).astype(dst.dtype)
            return carry

        lax.fori_loop(0, width // step, chunk, 0)

    copies = []
    for i, p in enumerate(peers):
        products(p, send.at[i])
        copy = remote(send.at[i], recv.at[i], ssem.at[i], rsem.at[i], (p, e))
        copy.start()
        copies.append(copy)
    products(r, total)
    for i in (1, 2, 0):
        copies[i].wait()

    def add(c, carry):
        t = aligned(c, 32)
        total[t, :] = total[t, :] + (
            recv[0, t, :].astype(F32) + recv[1, t, :].astype(F32) + recv[2, t, :].astype(F32)
        )
        return carry

    lax.fori_loop(0, tok // 32, add, 0)


def project_out(attn, wo):
    tok = attn.shape[0] // 4
    return pl.pallas_call(
        out_kernel,
        out_shape=jax.ShapeDtypeStruct((tok, wo.shape[1]), F32),
        in_specs=[VMEM_SPEC] * 2,
        out_specs=VMEM_SPEC,
        scratch_shapes=[
            pltpu.VMEM((3, tok, wo.shape[1]), BF16),
            pltpu.VMEM((3, tok, wo.shape[1]), BF16),
        ]
        + [pltpu.SemaphoreType.DMA((3,))] * 2,
        compiler_params=params(2),
        name="out_exchange",
    )(attn, wo)


def dgrad_kernel(mine, wq, wk, wv, cols_t, normal, grads, blocks, dsum, dsend, drecv, ssem, rsem, bsend, brecv):
    r, e = lax.axis_index("dp"), lax.axis_index("expert")
    rows = mine.shape[0]
    tok = rows // 4
    half = rows // 2
    qg = wq.shape[1] // 4
    kg = wk.shape[1] // 4
    width = wq.shape[0]
    peers = [r ^ m for m in PEER_MASKS]
    near, far, diag = r ^ 1, r ^ 2, r ^ 3
    greet([(p, e) for p in peers])
    low, high = pl.ds(0, half), pl.ds(half, half)
    first_near = remote(mine.at[low], blocks.at[0, low], ssem.at[0], rsem.at[0], (near, e))
    first_far = remote(mine.at[high], blocks.at[1, high], ssem.at[1], rsem.at[1], (far, e))
    second_near = remote(mine.at[high], blocks.at[0, high], ssem.at[2], rsem.at[2], (near, e))
    second_far = remote(mine.at[low], blocks.at[1, low], ssem.at[3], rsem.at[3], (far, e))
    pass_far = remote(blocks.at[0, low], blocks.at[2, low], ssem.at[4], rsem.at[4], (far, e))
    pass_near = remote(blocks.at[1, high], blocks.at[2, high], ssem.at[5], rsem.at[5], (near, e))
    for copy in (first_near, first_far, second_near, second_far):
        copy.start()

    def products(p, src, start):
        def chunk(c, carry):
            t = aligned(c, tok)
            x = src[t, :]
            value = (
                dot_nt(x[:, :qg], wq[:, aligned(p, qg)])
                + dot_nt(x[:, qg : qg + kg], wk[:, aligned(p, kg)])
                + dot_nt(x[:, qg + kg :], wv[:, aligned(p, kg)])
            )
            if start:
                dsum[t, :] = value
            else:
                dsum[t, :] = dsum[t, :] + value
            return carry

        lax.fori_loop(0, 4, chunk, 0)

        def outer(c, carry):
            n = aligned(c, 128)
            grads[aligned(p, width), n] = dot_nn(cols_t[...], src[:, n]).astype(BF16)
            return carry

        lax.fori_loop(0, (qg + 2 * kg) // 128, outer, 0)

    products(r, mine, True)
    first_near.wait()
    pass_far.start()
    first_far.wait()
    pass_near.start()
    second_near.wait()
    products(near, blocks.at[0], False)
    second_far.wait()
    products(far, blocks.at[1], False)
    pass_far.wait()
    pass_near.wait()
    products(diag, blocks.at[2], False)
    back = []
    for i, p in enumerate(peers):
        dsend[i] = dsum[aligned(p, tok), :].astype(BF16)
        copy = remote(dsend.at[i], drecv.at[i], bsend.at[i], brecv.at[i], (p, e))
        copy.start()
        back.append(copy)
    normal[:, aligned(r, width)] = dsum[aligned(r, tok), :]
    for i, p in enumerate(peers):
        back[i].wait()
        normal[:, aligned(p, width)] = drecv[i].astype(F32)


def grad_qkv(mine, wq, wk, wv, cols_t):
    rows, group = mine.shape
    tok = rows // 4
    width = wq.shape[0]
    return pl.pallas_call(
        dgrad_kernel,
        out_shape=(
            jax.ShapeDtypeStruct((tok, 4 * width), F32),
            jax.ShapeDtypeStruct((4 * width, group), BF16),
        ),
        in_specs=[VMEM_SPEC] * 5,
        out_specs=(VMEM_SPEC, VMEM_SPEC),
        scratch_shapes=[
            pltpu.VMEM((3, rows, group), BF16),
            pltpu.VMEM((rows, width), F32),
            pltpu.VMEM((3, tok, width), BF16),
            pltpu.VMEM((3, tok, width), BF16),
            pltpu.SemaphoreType.DMA((6,)),
            pltpu.SemaphoreType.DMA((6,)),
            pltpu.SemaphoreType.DMA((3,)),
            pltpu.SemaphoreType.DMA((3,)),
        ],
        compiler_params=params(4),
        name="dqkv_exchange",
    )(mine, wq, wk, wv, cols_t)


def branch_kernel(mine, wo, attn_t, d_attn, grads, full, ssem, rsem):
    r, e = lax.axis_index("dp"), lax.axis_index("expert")
    tok = mine.shape[0]
    half = tok // 2
    peers = [r ^ m for m in PEER_MASKS]
    near, far, diag = r ^ 1, r ^ 2, r ^ 3
    greet([(p, e) for p in peers])

    def part(q, which):
        return pl.ds(pl.multiple_of(q * tok + which * half, half), half)

    low, high = pl.ds(0, half), pl.ds(half, half)
    first_near = remote(mine.at[low], full.at[part(r, 0)], ssem.at[0], rsem.at[0], (near, e))
    first_far = remote(mine.at[high], full.at[part(r, 1)], ssem.at[1], rsem.at[1], (far, e))
    second_near = remote(mine.at[high], full.at[part(r, 1)], ssem.at[2], rsem.at[2], (near, e))
    second_far = remote(mine.at[low], full.at[part(r, 0)], ssem.at[3], rsem.at[3], (far, e))
    pass_far = remote(full.at[part(near, 0)], full.at[part(near, 0)], ssem.at[4], rsem.at[4], (far, e))
    pass_near = remote(full.at[part(far, 1)], full.at[part(far, 1)], ssem.at[5], rsem.at[5], (near, e))
    for copy in (first_near, first_far, second_near, second_far):
        copy.start()
    full[aligned(r, tok), :] = mine[...]
    heads = wo.shape[0]
    step = heads // 4

    def products(q):
        def chunk(c, carry):
            n = aligned(c, step)
            d_attn[aligned(q, tok), n] = dot_nt(full[aligned(q, tok), :], wo[n, :]).astype(BF16)
            return carry

        lax.fori_loop(0, 4, chunk, 0)

    products(r)
    first_near.wait()
    pass_far.start()
    first_far.wait()
    pass_near.start()
    second_near.wait()
    products(near)
    second_far.wait()
    products(far)
    pass_far.wait()
    pass_near.wait()
    products(diag)

    def outer(c, carry):
        n = aligned(c, 256)
        grads[:, n] = dot_nn(attn_t[...], full[:, n]).astype(BF16)
        return carry

    lax.fori_loop(0, mine.shape[1] // 256, outer, 0)


def grad_branch(mine, wo, attn_t):
    tok, width = mine.shape
    return pl.pallas_call(
        branch_kernel,
        out_shape=(
            jax.ShapeDtypeStruct((4 * tok, wo.shape[0]), BF16),
            jax.ShapeDtypeStruct((wo.shape[0], width), BF16),
        ),
        in_specs=[VMEM_SPEC] * 3,
        out_specs=(VMEM_SPEC, VMEM_SPEC),
        scratch_shapes=[
            pltpu.VMEM((4 * tok, width), BF16),
            pltpu.SemaphoreType.DMA((6,)),
            pltpu.SemaphoreType.DMA((6,)),
        ],
        compiler_params=params(3),
        name="branch_exchange",
    )(mine, wo, attn_t)


def owner_sum_kernel(n_owner, n_arrays, *refs):
    arrays = refs[:n_arrays]
    outs = refs[n_arrays : 2 * n_arrays]
    scratch = refs[2 * n_arrays :]
    pair_in = scratch[:n_arrays]
    send = scratch[n_arrays : 2 * n_arrays]
    recv = scratch[2 * n_arrays : 3 * n_arrays]
    psend, precv, zsend, zrecv = scratch[3 * n_arrays :]
    r, e = lax.axis_index("dp"), lax.axis_index("expert")
    n_z = n_owner // 2
    z, core = e // 2, e % 2
    targets = [lax.rem(z + j, n_z) for j in range(n_z)]
    order = list(range(1, n_z)) + [0]
    order = order[1:2] + order[:1] + order[2:] if n_z > 2 else order
    greet([(r, e ^ 1)] + [(r, targets[j] * 2 + core) for j in range(1, n_z)])
    pair = {}
    for j in order:
        for a in range(n_arrays):
            copy = remote(
                arrays[a].at[targets[j] * 2 + (1 - core)], pair_in[a].at[j],
                psend.at[a, j], precv.at[a, j], (r, e ^ 1),
            )
            copy.start()
            pair[a, j] = copy
    moves = []
    for j in order:
        for a in range(n_arrays):
            pair[a, j].wait()
            own = arrays[a][targets[j] * 2 + core].astype(F32) + pair_in[a][j].astype(F32)
            if j == 0:
                outs[a][...] = own
            else:
                send[a][j - 1] = own.astype(BF16)
                copy = remote(
                    send[a].at[j - 1], recv[a].at[j - 1],
                    zsend.at[a, j - 1], zrecv.at[a, j - 1], (r, targets[j] * 2 + core),
                )
                copy.start()
                moves.append(copy)
    for copy in moves:
        copy.wait()
    for a in range(n_arrays):
        value = outs[a][...]
        for j in range(n_z - 1):
            value = value + recv[a][j].astype(F32)
        outs[a][...] = value


def owner_sums(arrays, n_owner, collective_id):
    n = len(arrays)
    n_z = n_owner // 2
    shapes = [a.shape[1:] for a in arrays]
    return pl.pallas_call(
        functools.partial(owner_sum_kernel, n_owner, n),
        out_shape=tuple(jax.ShapeDtypeStruct(s, F32) for s in shapes),
        in_specs=[VMEM_SPEC] * n,
        out_specs=(VMEM_SPEC,) * n,
        scratch_shapes=[pltpu.VMEM((n_z, *s), BF16) for s in shapes]
        + [pltpu.VMEM((n_z - 1, *s), BF16) for s in shapes]
        + [pltpu.VMEM((n_z - 1, *s), BF16) for s in shapes]
        + [pltpu.SemaphoreType.DMA((n, n_z))] * 2
        + [pltpu.SemaphoreType.DMA((n, n_z - 1))] * 2,
        compiler_params=params(collective_id),
        name="owner_sums",
    )(*arrays)


def masks_of(block, own_length, slots, prompt_block, prompt_len, column, keys):
    slot = lax.broadcasted_iota(jnp.int32, (slots, keys), 0)
    key = lax.broadcasted_iota(jnp.int32, (slots, keys), 1)
    is_prompt = slot < prompt_block
    position = (column * 4 + block) * prompt_block + slot
    sees_prompt = (key < prompt_len) & (jnp.logical_not(is_prompt) | (key <= position))
    cont = key - prompt_len
    sees_cont = (
        (key >= prompt_len)
        & jnp.logical_not(is_prompt)
        & (cont <= slot - prompt_block)
        & (cont < own_length)
    )
    return sees_prompt | sees_cont


def attention_fwd_kernel(prompt_len, lengths, lin, gain, cos, sin, keys, values, queries, attn):
    block = pl.program_id(0)
    slots = lin.shape[0]
    head = gain.shape[1]
    allowed = masks_of(
        block, lengths[block], slots, slots - CMAX, prompt_len, lengths[4], keys.shape[1]
    )
    scale = head ** (-0.5)
    k, v = keys[0], values[0]
    c, s, g = cos[0], sin[0], gain[...]
    for h in range(lin.shape[1] // head):
        part = slice(h * head, (h + 1) * head)
        x = lin[:, part]
        x = x * lax.rsqrt(jnp.mean(x * x, axis=-1, keepdims=True) + norm_eps) * g
        q = (x * c + pltpu.roll(x, head // 2, 1) * s).astype(BF16)
        queries[:, part] = q
        score = jnp.where(allowed, dot_nt(q, k) * scale, -jnp.inf)
        peak = jnp.max(score, axis=-1, keepdims=True)
        exponent = jnp.exp(score - peak)
        low = (exponent * (1.0 / jnp.sum(exponent, axis=-1, keepdims=True))).astype(BF16)
        attn[:, part] = dot_nn(low, v).astype(BF16)


def attention_fwd(lengths, lin, gain, cos, sin, keys, values, prompt_len):
    blocks, total_keys, head = keys.shape
    slots = lin.shape[0] // blocks
    width = lin.shape[1] - 2 * head
    row = pl.BlockSpec((slots, width), lambda i, *_: (i, 0))
    table = pl.BlockSpec((1, slots, head), lambda i, *_: (i, 0, 0))
    kv = pl.BlockSpec((1, total_keys, head), lambda i, *_: (i, 0, 0))
    one = pl.BlockSpec((1, head), lambda i, *_: (0, 0))
    return pl.pallas_call(
        functools.partial(attention_fwd_kernel, prompt_len),
        grid_spec=pltpu.PrefetchScalarGridSpec(
            num_scalar_prefetch=1,
            grid=(blocks,),
            in_specs=[row, one, table, table, kv, kv],
            out_specs=[row, row],
        ),
        out_shape=(
            jax.ShapeDtypeStruct((lin.shape[0], width), BF16),
            jax.ShapeDtypeStruct((lin.shape[0], width), BF16),
        ),
        compiler_params=params(),
        name="attention_fwd",
    )(lengths, lin, gain, cos, sin, keys, values)


def attention_bwd_kernel(
    prompt_len, lengths, lin, queries, d_attn, gain, cos, sin, keys, values, d_lin, d_keys, d_values, d_gain
):
    block = pl.program_id(0)
    slots = lin.shape[0]
    head = gain.shape[1]
    allowed = masks_of(
        block, lengths[block], slots, slots - CMAX, prompt_len, lengths[4], keys.shape[1]
    )
    scale = head ** (-0.5)
    k, v = keys[0], values[0]
    c, s, g = cos[0], sin[0], gain[...]
    key_total = jnp.zeros(k.shape, F32)
    value_total = jnp.zeros(v.shape, F32)
    gain_total = jnp.zeros((8, head), F32)
    for h in range(lin.shape[1] // head):
        part = slice(h * head, (h + 1) * head)
        q = queries[:, part]
        score = jnp.where(allowed, dot_nt(q, k) * scale, -jnp.inf)
        peak = jnp.max(score, axis=-1, keepdims=True)
        exponent = jnp.exp(score - peak)
        probs = exponent * (1.0 / jnp.sum(exponent, axis=-1, keepdims=True))
        d_out = d_attn[:, part]
        d_probs = dot_nt(d_out, v)
        inner = jnp.sum(probs * d_probs, axis=-1, keepdims=True)
        d_score = (probs * (d_probs - inner)).astype(BF16)
        key_total = key_total + dot_tn(d_score, q)
        value_total = value_total + dot_tn(probs.astype(BF16), d_out)
        d_q = dot_nn(d_score, k) * scale
        turned = d_q * c + pltpu.roll(d_q * s, head // 2, 1)
        x = lin[:, part]
        inverse = lax.rsqrt(jnp.mean(x * x, axis=-1, keepdims=True) + norm_eps)
        unit = x * inverse
        pairs = turned * unit
        for j in range(slots // 8):
            gain_total = gain_total + pairs[j * 8 : (j + 1) * 8]
        weighted = turned * g
        d_lin[:, part] = (
            inverse * (weighted - unit * jnp.mean(weighted * unit, axis=-1, keepdims=True))
        ).astype(BF16)
    d_keys[0] = key_total * scale
    d_values[0] = value_total
    d_gain[0] = gain_total


def attention_bwd(lengths, lin, queries, d_attn, gain, cos, sin, keys, values, prompt_len):
    blocks, total_keys, head = keys.shape
    slots = lin.shape[0] // blocks
    width = lin.shape[1] - 2 * head
    row = pl.BlockSpec((slots, width), lambda i, *_: (i, 0))
    table = pl.BlockSpec((1, slots, head), lambda i, *_: (i, 0, 0))
    kv = pl.BlockSpec((1, total_keys, head), lambda i, *_: (i, 0, 0))
    one = pl.BlockSpec((1, head), lambda i, *_: (0, 0))
    return pl.pallas_call(
        functools.partial(attention_bwd_kernel, prompt_len),
        grid_spec=pltpu.PrefetchScalarGridSpec(
            num_scalar_prefetch=1,
            grid=(blocks,),
            in_specs=[row, row, row, one, table, table, kv, kv],
            out_specs=[row, kv, kv, pl.BlockSpec((1, 8, head), lambda i, *_: (i, 0, 0))],
        ),
        out_shape=(
            jax.ShapeDtypeStruct((lin.shape[0], width), BF16),
            jax.ShapeDtypeStruct(keys.shape, F32),
            jax.ShapeDtypeStruct(values.shape, F32),
            jax.ShapeDtypeStruct((blocks, 8, head), F32),
        ),
        compiler_params=params(),
        name="attention_bwd",
    )(lengths, lin, queries, d_attn, gain, cos, sin, keys, values)


def partner(shard, axis, bit):
    return lax.ppermute(shard, axis, [(i, i ^ 1 << bit) for i in range(lax.axis_size(axis))])


def root_mean_scale(value_rows, gain_vec):
    return (
        value_rows
        * lax.rsqrt(jnp.mean(value_rows * value_rows, axis=-1, keepdims=True) + norm_eps)
        * gain_vec
    )


def contract(left_side, right_side, left_dim, right_dim):
    return lax.dot_general(
        left_side,
        right_side,
        (((left_dim,), (right_dim,)), ((), ())),
        preferred_element_type=F32,
    )


def head_rope(linear, gain_vec, cos, sin):
    value = root_mean_scale(linear, gain_vec)
    half = value.shape[-1] // 2
    return value * cos + jnp.roll(value, half, axis=-1) * sin


def body(
    tokens,
    teacher,
    routes,
    cont_lengths,
    query_weight,
    key_projection,
    value_projection,
    output_weight,
    router_weight,
    gate_weight,
    up_weight,
    down_weight,
    input_gain,
    post_gain,
    query_gain,
    key_gain,
):
    n_dp = lax.axis_size("dp")
    n_owner = lax.axis_size("expert")
    devices = n_dp * n_owner
    rank_dp = lax.axis_index("dp")
    rank_owner = lax.axis_index("expert")
    flat_rank = rank_dp * n_owner + rank_owner
    column = rank_owner % 2
    first_column = column == 0
    tok_dev, model_width = tokens.shape
    top_count = routes.shape[1]
    head_dim = query_gain.shape[0]
    kv_width = key_projection.shape[1]
    query_width = query_weight.shape[1]
    query_group = query_width // n_dp
    assert n_dp == 4 and kv_width == n_dp * head_dim
    ffn_width = gate_weight.shape[2]
    prompt_block = tok_dev - CMAX
    half_prompt = n_dp * prompt_block
    prompt_len = 2 * half_prompt
    capacity = max(2, tok_dev * top_count * 5 // (4 * devices))
    slots_all = devices * tok_dev
    slot_ids = jnp.arange(tok_dev, dtype=jnp.int32)
    own_length = cont_lengths[flat_rank]
    valid_slot = (slot_ids < prompt_block) | (slot_ids - prompt_block < own_length)
    valid_count = (devices * prompt_block + jnp.sum(cont_lengths)).astype(F32)
    tokens_float = tokens.astype(F32)
    normed_float, first_norm_back = jax.vjp(root_mean_scale, tokens_float, input_gain)
    normed = normed_float.astype(BF16)

    block_ids = jnp.arange(n_dp, dtype=jnp.int32)[:, None]
    positions = jnp.where(
        slot_ids[None] < prompt_block,
        (column * n_dp + block_ids) * prompt_block + slot_ids[None],
        prompt_len + slot_ids[None] - prompt_block,
    )
    half_head = head_dim // 2
    frequency = rope_base ** (-(jnp.arange(half_head, dtype=F32) * 2.0) / head_dim)
    angles = positions.astype(F32)[:, :, None] * frequency
    cos_half, sin_half = jnp.cos(angles), jnp.sin(angles)
    cos = jnp.concatenate([cos_half, cos_half], axis=-1)
    sin = jnp.concatenate([-sin_half, sin_half], axis=-1)
    lengths = jnp.concatenate(
        [lax.dynamic_index_in_dim(cont_lengths.reshape(n_dp, n_owner), rank_owner, 1, False), column[None]]
    ).astype(jnp.int32)

    lin, normed_cols = project_qkv(normed, query_weight, key_projection, value_projection)
    key_lin = lin[:, query_group : query_group + head_dim].reshape(n_dp, tok_dev, head_dim)
    keys_float, key_back = jax.vjp(lambda a, b: head_rope(a, b, cos, sin), key_lin, key_gain)
    keys_own = keys_float.astype(BF16)
    values_own = lin[:, query_group + head_dim :].reshape(n_dp, tok_dev, head_dim).astype(BF16)
    column_kv = jnp.stack([keys_own[:, :prompt_block], values_own[:, :prompt_block]]).reshape(
        2, half_prompt, head_dim
    )
    other_kv = partner(column_kv, "expert", 0)
    full_kv = jnp.where(
        first_column,
        jnp.concatenate([column_kv, other_kv], axis=1),
        jnp.concatenate([other_kv, column_kv], axis=1),
    )
    spread = jnp.broadcast_to(full_kv[:, None], (2, n_dp, prompt_len, head_dim))
    all_keys = jnp.concatenate([spread[0], keys_own[:, prompt_block:]], axis=1)
    all_values = jnp.concatenate([spread[1], values_own[:, prompt_block:]], axis=1)
    query_gain_row = query_gain[None]
    queries, attended = attention_fwd(
        lengths, lin, query_gain_row, cos, sin, all_keys, all_values, prompt_len
    )
    state = tokens_float + project_out(attended, output_weight)
    mixed_float, second_norm_back = jax.vjp(root_mean_scale, state, post_gain)
    mixed = mixed_float.astype(BF16)
    logits = jnp.dot(mixed, router_weight, preferred_element_type=jnp.float32)
    gates = jax.nn.softmax(jnp.take_along_axis(logits, routes, axis=1), axis=-1)
    rows_total = tok_dev * top_count
    expert_ids = routes.reshape(rows_total)
    live_rows = jnp.repeat(valid_slot, top_count)
    expert_range = jnp.arange(devices, dtype=jnp.int32)
    hit_table = ((expert_ids[:, None] == expert_range[None, :]) & live_rows[:, None]).astype(
        jnp.int32
    )
    earlier = jnp.cumsum(hit_table, axis=0) - hit_table
    position_in = jnp.sum(earlier * hit_table, axis=1)
    slot_index = jnp.where(live_rows, expert_ids * capacity + position_in, devices * capacity)
    row_of_slot = (
        jnp.full((devices * capacity + 1,), rows_total, jnp.int32)
        .at[slot_index]
        .set(jnp.arange(rows_total, dtype=jnp.int32))[: devices * capacity]
    )
    token_of_slot = jnp.where(row_of_slot < rows_total, row_of_slot // top_count, tok_dev)
    mixed_pad = jnp.concatenate([mixed, jnp.zeros((1, model_width), jnp.bfloat16)], axis=0)
    send_rows = mixed_pad[token_of_slot].reshape(devices, capacity, model_width)
    arrived = lax.all_to_all(send_rows, ("dp", "expert"), split_axis=0, concat_axis=0, tiled=True)
    sources = arrived.shape[0]
    items = arrived.shape[1]
    flat_in = arrived.reshape(sources * items, model_width)
    gate_pre = jnp.dot(flat_in, gate_weight[0], preferred_element_type=jnp.float32)
    up_pre = jnp.dot(flat_in, up_weight[0], preferred_element_type=jnp.float32)
    hidden_units = (jax.nn.silu(gate_pre) * up_pre).astype(jnp.bfloat16)
    produced = jnp.dot(hidden_units, down_weight[0], preferred_element_type=jnp.float32).astype(
        jnp.bfloat16
    )
    produced, gate_pre, up_pre, hidden_units, arrived = (
        produced.reshape(sources, items, model_width),
        gate_pre.reshape(sources, items, ffn_width),
        up_pre.reshape(sources, items, ffn_width),
        hidden_units.reshape(sources, items, ffn_width),
        arrived,
    )
    returned = lax.all_to_all(produced, ("dp", "expert"), split_axis=0, concat_axis=0, tiled=True)
    returned_pad = jnp.concatenate(
        [
            returned.reshape(devices * capacity, model_width),
            jnp.zeros((1, model_width), jnp.bfloat16),
        ],
        axis=0,
    )
    copies = returned_pad[slot_index].reshape(tok_dev, top_count, model_width)
    layer_out = state + jnp.sum(gates[:, :, None] * copies, axis=1)
    live_tokens = valid_slot.astype(jnp.float32)[:, None]
    diff = (layer_out - teacher.astype(jnp.float32)) * live_tokens
    local_square = jnp.sum(diff * diff)
    d_out = 2.0 * slots_all * diff / valid_count
    d_gates = jnp.sum(d_out[:, None, :] * copies, axis=-1)
    d_chosen = gates * (d_gates - jnp.sum(gates * d_gates, axis=-1, keepdims=True))
    d_logits = jnp.sum(
        jnp.where(routes[:, :, None] == expert_range[None, None, :], d_chosen[:, :, None], 0.0),
        axis=1,
    ).astype(jnp.bfloat16)
    d_copies = (
        (gates[:, :, None] * d_out[:, None, :])
        .astype(jnp.bfloat16)
        .reshape(rows_total, model_width)
    )
    d_copies_pad = jnp.concatenate([d_copies, jnp.zeros((1, model_width), jnp.bfloat16)], axis=0)
    d_send = d_copies_pad[row_of_slot].reshape(devices, capacity, model_width)
    d_arrived = lax.all_to_all(d_send, ("dp", "expert"), split_axis=0, concat_axis=0, tiled=True)
    flat_d = d_arrived.reshape(-1, model_width)
    flat_in = arrived.reshape(-1, model_width)
    flat_gate = gate_pre.reshape(-1, ffn_width)
    flat_up = up_pre.reshape(-1, ffn_width)
    flat_hidden = hidden_units.reshape(-1, ffn_width)
    d_hidden = contract(flat_d, down_weight[0], 1, 1)
    sigmoid_gate = jax.nn.sigmoid(flat_gate)
    d_gate = (d_hidden * flat_up * sigmoid_gate * (1.0 + flat_gate * (1.0 - sigmoid_gate))).astype(
        jnp.bfloat16
    )
    d_up = (d_hidden * flat_gate * sigmoid_gate).astype(jnp.bfloat16)
    down_grad = contract(flat_hidden, flat_d, 0, 0)[None]
    gate_grad = contract(flat_in, d_gate, 0, 0)[None]
    up_grad = contract(flat_in, d_up, 0, 0)[None]
    d_in = (contract(d_gate, gate_weight[0], 1, 1) + contract(d_up, up_weight[0], 1, 1)).astype(
        jnp.bfloat16
    )
    d_returned = lax.all_to_all(
        d_in.reshape(devices, capacity, model_width),
        ("dp", "expert"),
        split_axis=0,
        concat_axis=0,
        tiled=True,
    )
    d_returned_pad = jnp.concatenate(
        [
            d_returned.reshape(devices * capacity, model_width),
            jnp.zeros((1, model_width), jnp.bfloat16),
        ],
        axis=0,
    )
    d_mixed = jnp.sum(
        d_returned_pad[slot_index].reshape(tok_dev, top_count, model_width),
        axis=1,
        dtype=jnp.float32,
    )
    d_mixed = d_mixed + contract(d_logits, router_weight, 1, 1)
    router_local = contract(mixed, d_logits, 0, 0)
    d_state_norm, d_post_gain = second_norm_back(d_mixed)
    d_state = d_out + d_state_norm
    d_branch = d_state.astype(BF16)
    d_attended, out_part = grad_branch(d_branch, output_weight, attended.T)
    d_query_lin, d_keys, d_values, gain_parts = attention_bwd(
        lengths, lin, queries, d_attended, query_gain_row, cos, sin, all_keys, all_values, prompt_len
    )
    d_query_gain = jnp.sum(gain_parts, axis=(0, 1))
    prompt_grads = jnp.stack(
        [jnp.sum(d_keys[:, :prompt_len], axis=0), jnp.sum(d_values[:, :prompt_len], axis=0)]
    )
    mine_part = jnp.where(first_column, prompt_grads[:, :half_prompt], prompt_grads[:, half_prompt:])
    their_part = jnp.where(first_column, prompt_grads[:, half_prompt:], prompt_grads[:, :half_prompt])
    own_prompt = (mine_part + partner(their_part, "expert", 0)).reshape(
        2, n_dp, prompt_block, head_dim
    )
    d_key_post = jnp.concatenate([own_prompt[0], d_keys[:, prompt_len:]], axis=1)
    d_value_lin = jnp.concatenate([own_prompt[1], d_values[:, prompt_len:]], axis=1)
    d_key_float, d_key_gain = key_back(d_key_post)
    rows = n_dp * tok_dev
    d_lin = jnp.concatenate(
        [
            d_query_lin,
            d_key_float.astype(BF16).reshape(rows, head_dim),
            d_value_lin.astype(BF16).reshape(rows, head_dim),
        ],
        axis=1,
    )
    d_normed, qkv_part = grad_qkv(
        d_lin, query_weight, key_projection, value_projection, normed_cols.T
    )
    d_tokens_norm, d_input_gain = first_norm_back(d_normed)
    tokens_grad = d_state + d_tokens_norm
    width = query_weight.shape[0]
    group = d_lin.shape[1]
    rows_here = width // n_owner
    by_owner = (
        qkv_part.reshape(n_dp, n_owner, rows_here, group)
        .transpose(1, 0, 2, 3)
        .reshape(n_owner, n_dp * rows_here, group)
    )
    qkv_rows, output_grad = owner_sums(
        [by_owner, out_part.reshape(n_owner, -1, model_width)], n_owner, 5
    )
    qkv_rows = qkv_rows.reshape(n_dp, rows_here, group)

    def columns(start, size):
        return qkv_rows[:, :, start : start + size].transpose(1, 0, 2).reshape(rows_here, n_dp * size)

    query_grad = columns(0, query_group)
    key_grad = columns(query_group, head_dim)
    value_grad = columns(query_group + head_dim, head_dim)
    total_square, input_gain_grad, post_gain_grad, query_gain_grad, key_gain_grad, router_grad = (
        lax.psum(
            (local_square, d_input_gain, d_post_gain, d_query_gain, d_key_gain, router_local),
            ("dp", "expert"),
        )
    )
    loss = total_square / (valid_count * model_width)
    return (
        layer_out,
        loss,
        tokens_grad,
        query_grad,
        key_grad,
        value_grad,
        output_grad,
        router_grad,
        gate_grad,
        up_grad,
        down_grad,
        input_gain_grad,
        post_gain_grad,
        query_gain_grad,
        key_gain_grad,
    )


def solution(mesh):
    in_specs = (
        P(("dp", "expert"), None),
        P(("dp", "expert"), None),
        P(("dp", "expert"), None),
        P(),
        P("dp", None),
        P("dp", None),
        P("dp", None),
        P("dp", None),
        P(),
        P(("dp", "expert"), None, None),
        P(("dp", "expert"), None, None),
        P(("dp", "expert"), None, None),
        P(),
        P(),
        P(),
        P(),
    )
    out_specs = (
        P(("dp", "expert"), None),
        P(),
        P(("dp", "expert"), None),
        P(("dp", "expert"), None),
        P(("dp", "expert"), None),
        P(("dp", "expert"), None),
        P(("dp", "expert"), None),
        P(),
        P(("dp", "expert"), None, None),
        P(("dp", "expert"), None, None),
        P(("dp", "expert"), None, None),
        P(),
        P(),
        P(),
        P(),
    )
    return jax.shard_map(body, mesh=mesh, in_specs=in_specs, out_specs=out_specs, check_vma=False)
```

time: 2310 us -> 1440 us (0.62)
  waiting for transfers between devices: 1240 us -> 274 us
  Pallas kernels: 0 us -> 398 us
  matrix products: 215 us -> 84.3 us
  other arithmetic: 145 us -> 67.7 us
  local copies, waits for them, and re-layouts: 279 us -> 206 us
    reduce_scatter x1 -> x0, waiting for transfers between devices: 556 us -> none  [body(): lax.psum_scatter(jnp.concatenate(pieces, axis=1), ('dp', 'expert'), scatt...]
    pallas_call x0 -> x7, Pallas kernels: none -> 398 us  [the longest x1 116 us: owner_sums(): pl.pallas_call(functools.partial(owner_sum_kernel, n_owner, n), out_shape...]
    all_gather x4 -> x0, waiting for transfers between devices: 258 us -> none  [the longest x1 134 us: body(): lax.all_gather(query_weight, 'dp', axis=0, tiled=True)]
    psum x1, waiting for transfers between devices: 124 us -> 0.02 us  [body(): lax.psum((local_square, d_input_gain, d_post_gain, d_query_gain, d_key_ga...]
    dot_general x16 -> x8, matrix products: 126 us -> 59.9 us  [contract(): lax.dot_general(left_side, right_side, (((left_dim,), (right_dim,)), ((),...]
    dot_general x32 -> x0, matrix products: 65 us -> none  [the longest x1 10.6 us: body(): query_lin = jnp.dot(normed, whole_query, preferred_element_type=jnp.float32)]
    concatenate x3 -> x5, other arithmetic: 48.8 us -> 4.5 us  [the longest x1 1.88 us: body(): all_keys = jnp.concatenate([spread[0], keys_own[:, prompt_block:]], axis=1)]
    reshape x5, local copies, waits for them, and re-layouts: 44.5 us -> 8.48 us  [the longest x1 5.4 us: body(): qkv_part.reshape(n_dp, n_owner, rows_here, group).transpose(1, 0, 2, 3)]
  transfers between devices with their start and end apart: 11 -> 5, of which waited for: 8 -> 2; matrix products, arithmetic and copies ran while one was open for 12% -> 11% of each run, Pallas kernels for 0% -> 18%
where the time goes in v1:
time: 1440 us; the launch traced here: 1430 us
  Pallas kernels  398 us (28%)
  blocking collectives  371 us (26%)
  waiting for transfers between devices  274 us (19%)
  local copies, waits for them, and re-layouts  206 us (14%)
  matrix products  84.3 us (6%)
  other arithmetic  67.7 us (5%)
  between operations  18 us (1%)
    all_to_all x1, blocking collectives, body(): lax.all_to_all(d_send, ('dp', 'expert'), split_axis=0, concat_axis=0, til...  168 us
    all_to_all x1, blocking collectives, body(): lax.all_to_all(send_rows, ('dp', 'expert'), split_axis=0, concat_axis=0,...  165 us
    all_to_all x1, waiting for transfers between devices, body(): lax.all_to_all(produced, ('dp', 'expert'), split_axis=0, concat_axis=0, t...  144 us
    all_to_all x1, waiting for transfers between devices, body(): lax.all_to_all(d_in.reshape(devices, capacity, model_width), ('dp', 'expe...  130 us
    pallas_call x1, Pallas kernels, owner_sums(): pl.pallas_call(functools.partial(owner_sum_kernel, n_owner, n), out_shape...  116 us
    pallas_call x1, Pallas kernels, project_qkv(): pl.pallas_call(functools.partial(qkv_kernel, tok), out_shape=(jax.ShapeDt...  89.2 us
    pallas_call x1, Pallas kernels, grad_qkv(): pl.pallas_call(dgrad_kernel, out_shape=(jax.ShapeDtypeStruct((tok, 4 * wi...  76.6 us
    dot_general x8, matrix products, contract(): lax.dot_general(left_side, right_side, (((left_dim,), (right_dim,)), ((),...  59.9 us
  transfers between devices with their start and end apart: 5, of which 2 were waited for; matrix products, arithmetic and copies ran while one was open for 11% of the time, Pallas kernels for 18%

profile of v1, /device:TPU:8, one launch (start us, length us, event | category | flops | bytes accessed | tf_op | source)
XLA Modules:
  0.0 1432.6 jit_solution(16049099817504402892)
XLA Ops:
  12.0 89.2 %qkv_exchange.1 = (f32[640,1280]{1,0:T(8,128)}, bf16[640,512]{1,0:T(8,128)(2,1)}) custom-call(bf16[160,2048]{1,0:T(8,128)(2,1)} %fusion.15.normed, bf16[512,4096]{1,0:T(8,128)(2,1)} %wq.3, bf16[512,512]{1,0:T(8,128)(2,1)} %wk.3, bf16[512,512]{1,0:T(8,128)(2,1)} %wv.3), custom_call_target="tpu_custom_call" | custom-call | tf_op jit(solution)/shard_map/qkv_exchange/pallas_call | solution.py:121
  118.3 15.9 %reduce-window.6 = s32[32,10,128]{2,1,0:T(8,128)S(1)} reduce-window(s32[32,10,128]{2,1,0:T(8,128)} %fusion.26, s32[]{:T(128)} %constant.47.clone.1), window={size=1x1x128 pad=0_0x0_0x127_0}, to_apply=%region_5.6 | reduce-window | flops 5201920 | bytes 327684 | tf_op jit(solution)/shard_map/reduce-window
  152.7 15.6 %attention_fwd.1 = (bf16[640,1024]{1,0:T(8,128)(2,1)}, bf16[640,1024]{1,0:T(8,128)(2,1)}) custom-call(s32[5]{0:T(128)} %pad_add_fusion.lengths, f32[640,1280]{1,0:T(8,128)} %get-tuple-element.29.lin, f32[1,128]{1,0:T(1,128)} %bitcast.151, f32[4,160,128]{2,1,0:T(8,128)} %get-tuple-element.71.cos, f32[4,160,128]{2,1,0:T(8,128)} %get-tuple-element.62.sin, ...), custom_call_target="tpu_custom_call" | custom-call | tf_op jit(solution)/shard_map/attention_fwd/pallas_call | solution.py:475
  168.2 38.4 %out_exchange.1 = f32[160,2048]{1,0:T(8,128)} custom-call(bf16[640,1024]{1,0:T(8,128)(2,1)} %get-tuple-element.30.attn, bf16[1024,2048]{1,0:T(8,128)(2,1)} %wo.3), custom_call_target="tpu_custom_call" | custom-call | tf_op jit(solution)/shard_map/out_exchange/pallas_call | solution.py:177
  211.2 15.5 %gather_fusion = bf16[1600,2048]{1,0:T(8,128)(2,1)} fusion(bf16[161,2048]{1,0:T(8,128)(2,1)} %concatenate.76, s32[2048]{0:T(1024)S(1)} %pad_clamp_fusion.2), kind=kCustom, calls=%fused_computation | custom fusion | bytes 13113600 | tf_op jit(solution)/shard_map/gather | solution.py:697
  235.4 165.0 %all_to_all.20 = bf16[32,50,2048]{2,1,0:T(8,128)(2,1)} all-to-all(bf16[32,50,2048]{2,1,0:T(8,128)(2,1)} %reshape.460), channel_id=1, replica_groups=mesh['dp'=4,'expert'=8] {'dp','expert'}, dimensions={0} | all-to-all | bytes 13107200 | tf_op jit(solution)/shard_map/all_to_all | solution.py:698
  451.7 10.2 gather_fusion.4
  462.4 144.1 %all-to-all-done.1 = bf16[32,50,2048]{2,1,0:T(8,128)(2,1)} async-done(((bf16[32,50,2048]{2,1,0:T(8,128)(2,1)}), bf16[32,50,2048]{2,1,0:T(8,128)(2,1)}, u32[]{:S(2)}, u32[]{:S(2)}) %all-to-all-start.1) | async-done | bytes 6553632 | tf_op jit(solution)/shard_map/all_to_all | solution.py:715
  622.1 14.7 %gather_fusion.1 = bf16[1280,2048]{1,0:T(8,128)(2,1)} fusion(bf16[1601,2048]{1,0:T(8,128)(2,1)} %concatenate.77, s32[2048]{0:T(1024)S(1)} %pad_clamp_fusion.1), kind=kCustom, calls=%fused_computation.1 | custom fusion | bytes 10490880 | tf_op jit(solution)/shard_map/gather | solution.py:723
  650.2 17.5 %gather_fusion.2 = bf16[1600,2048]{1,0:T(8,128)(2,1)} fusion(bf16[1281,2048]{1,0:T(8,128)(2,1)} %concatenate.78, s32[2048]{0:T(1024)S(1)} %pad_clamp_fusion), kind=kCustom, calls=%fused_computation.2 | custom fusion | bytes 13113600 | tf_op jit(solution)/shard_map/gather | solution.py:741
  676.3 168.4 %all_to_all.21 = bf16[32,50,2048]{2,1,0:T(8,128)(2,1)} all-to-all(bf16[32,50,2048]{2,1,0:T(8,128)(2,1)} %reshape.464), channel_id=1, replica_groups=mesh['dp'=4,'expert'=8] {'dp','expert'}, dimensions={0} | all-to-all | bytes 13107200 | tf_op jit(solution)/shard_map/all_to_all | solution.py:742
  844.8 8.8 reshape.465
  853.6 12.2 multiply_convert_fusion
  907.6 10.7 convolution_bitcast_fusion.1
  918.4 9.8 convolution_bitcast_fusion.2
  928.2 129.5 %all-to-all-done.3 = bf16[32,50,2048]{2,1,0:T(8,128)(2,1)} async-done(((bf16[32,50,2048]{2,1,0:T(8,128)(2,1)}), bf16[32,50,2048]{2,1,0:T(8,128)(2,1)}, u32[]{:S(2)}, u32[]{:S(2)}) %all-to-all-start.3) | async-done | bytes 6553632 | tf_op jit(solution)/shard_map/all_to_all | solution.py:760
  1057.7 8.8 reshape.467
  1073.3 14.7 %gather_fusion.3 = bf16[1280,2048]{1,0:T(8,128)(2,1)} fusion(bf16[1601,2048]{1,0:T(8,128)(2,1)} %concatenate.79, s32[2048]{0:T(1024)S(1)} %pad_clamp_fusion.1), kind=kCustom, calls=%fused_computation.3 | custom fusion | bytes 10490880 | tf_op jit(solution)/shard_map/gather | solution.py:775
  1096.8 36.5 %branch_exchange.1 = (bf16[640,1024]{1,0:T(8,128)(2,1)}, bf16[1024,2048]{1,0:T(8,128)(2,1)}) custom-call(bf16[160,2048]{1,0:T(8,128)(2,1)} %get-tuple-element.55.mine, bf16[1024,2048]{1,0:T(8,128)(2,1)} %wo.3, bf16[1024,640]{1,0:T(8,128)(2,1)} %bitcast.127), custom_call_target="tpu_custom_call" | custom-call | tf_op jit(solution)/shard_map/branch_exchange/pallas_call | solution.py:343
  1133.4 26.6 %attention_bwd.1 = (bf16[640,1024]{1,0:T(8,128)(2,1)}, f32[4,384,128]{2,1,0:T(8,128)}, f32[4,384,128]{2,1,0:T(8,128)}, f32[4,8,128]{2,1,0:T(8,128)}) custom-call(s32[5]{0:T(128)} %pad_add_fusion.lengths, f32[640,1280]{1,0:T(8,128)} %get-tuple-element.29.lin, bf16[640,1024]{1,0:T(8,128)(2,1)} %get-tuple-element.31.queries, ...), custom_call_target="tpu_custom_call" | custom-call | tf_op jit(solution)/shard_map/attention_bwd/pallas_call | solution.py:545
  1162.3 10.0 convolution_bitcast_fusion
  1177.0 76.6 %dqkv_exchange.1 = (f32[160,2048]{1,0:T(8,128)}, bf16[2048,1280]{1,0:T(8,128)(2,1)}) custom-call(bf16[640,1280]{1,0:T(8,128)(2,1)} %pad_maximum_fusion.mine, bf16[512,4096]{1,0:T(8,128)(2,1)} %wq.3, bf16[512,512]{1,0:T(8,128)(2,1)} %wk.3, bf16[512,512]{1,0:T(8,128)(2,1)} %wv.3, bf16[512,640]{1,0:T(8,128)(2,1)} %bitcast.129), custom_call_target="tpu_custom_call" | custom-call | tf_op jit(solution)/shard_map/dqkv_exchange/pallas_call | solution.py:265
  1258.9 115.6 %owner_sums.1 = (f32[256,1280]{1,0:T(8,128)}, f32[128,2048]{1,0:T(8,128)}) custom-call(bf16[8,256,1280]{2,1,0:T(8,128)(2,1)} %bitcast.121, bf16[8,128,2048]{2,1,0:T(8,128)(2,1)} %bitcast.128), custom_call_target="tpu_custom_call" | custom-call | tf_op jit(solution)/shard_map/owner_sums/pallas_call | solution.py:413
  1379.2 38.1 %all-reduce.6 = (f32[]{:T(128)}, f32[2048]{0:T(1024)}, f32[2048]{0:T(1024)}, f32[128]{0:T(128)}, f32[128]{0:T(128)}) all-reduce(f32[]{:T(128)} %multiply_reduce_fusion.2, f32[2048]{0:T(1024)S(1)} %get-tuple-element.45, f32[2048]{0:T(1024)S(1)} %get-tuple-element.43, ...), channel_id=1, replica_groups=mesh['dp'=4,'expert'=8] {'dp','expert'}, use_global_device_ids=true, to_apply=%region_11.12 | all-reduce | flops 4353 | bytes 34824 | tf_op jit(solution)/shard_map/psum | solution.py:834
  (252 shorter events, 222.4 us)
Async XLA Ops:
  7.2 419.1 %copy-start = (bf16[1,768,2048]{2,1,0:T(8,128)(2,1)S(1)}, bf16[1,768,2048]{2,1,0:T(8,128)(2,1)}, u32[]{:S(2)}) copy-start(bf16[1,768,2048]{2,1,0:T(8,128)(2,1)} %param.27) | copy-start | bytes 9437188
  12.0 92.2 %copy-start.44 = (f32[128]{0:T(128)S(1)}, f32[128]{0:T(128)}, u32[]{:S(2)}) copy-start(f32[128]{0:T(128)} %param.31) | copy-start | bytes 1540
  104.4 9.9 copy-start.26
  108.6 41.1 %collective-permute-start = (bf16[2,128,128]{2,1,0:T(8,128)(2,1)}, bf16[2,128,128]{2,1,0:T(8,128)(2,1)}, u32[]{:S(2)}, u32[]{:S(2)}) collective-permute-start(bf16[2,128,128]{2,1,0:T(8,128)(2,1)} %get-tuple-element.77), channel_id=1, source_target_pairs={{0,1},{1,0},{2,3},{3,2},{4,5},{5,4},{6,7},{7,6},{8,9},{9,8},{10,11... | collective-permute-start | bytes 196616 | tf_op jit(solution)/shard_map/ppermute | solution.py:565
  168.2 38.4 %copy-start.7 = (bf16[160,2048]{1,0:T(8,128)(2,1)S(1)}, bf16[160,2048]{1,0:T(8,128)(2,1)}, u32[]{:S(2)}) copy-start(bf16[160,2048]{1,0:T(8,128)(2,1)} %param.16) | copy-start | bytes 1966084
  208.2 18.5 %copy-start.42 = (f32[160]{0:T(256)}, f32[160]{0:T(256)S(1)}, u32[]{:S(2)}) copy-start(f32[160]{0:T(256)S(1)} %get-tuple-element.59) | copy-start | bytes 1924
  208.3 18.5 %copy-start.35 = (f32[160]{0:T(256)}, f32[160]{0:T(256)S(1)}, u32[]{:S(2)}) copy-start(f32[160]{0:T(256)S(1)} %fusion.47) | copy-start | bytes 1924
  409.1 8.5 copy-start.13
  409.1 8.5 copy-start.49
  442.3 8.0 copy-start.24
  442.3 164.2 %all-to-all-start.1 = ((bf16[32,50,2048]{2,1,0:T(8,128)(2,1)}), bf16[32,50,2048]{2,1,0:T(8,128)(2,1)}, u32[]{:S(2)}, u32[]{:S(2)}) async-start(bf16[32,50,2048]{2,1,0:T(8,128)(2,1)} %reshape.462), calls=%async_computation.1 | async-start | bytes 14680064 | tf_op jit(solution)/shard_map/all_to_all | solution.py:715
  636.8 8.0 copy-start.3
  853.6 12.2 copy-start.48
  865.7 8.0 copy-start.53
  865.7 8.1 copy-start.50
  890.1 8.8 copy-start.14
  890.1 167.6 %all-to-all-start.3 = ((bf16[32,50,2048]{2,1,0:T(8,128)(2,1)}), bf16[32,50,2048]{2,1,0:T(8,128)(2,1)}, u32[]{:S(2)}, u32[]{:S(2)}) async-start(bf16[32,50,2048]{2,1,0:T(8,128)(2,1)} %reshape.466), calls=%async_computation.3 | async-start | bytes 14680064 | tf_op jit(solution)/shard_map/all_to_all | solution.py:760
  896.5 523.7 %all-reduce.9.cloned.1.call-start = ((), (), s32[]{:S(2)}) async-start(), calls=%async_computation.4 | async-start | bytes 524288 | tf_op jit(solution)/shard_map/psum | solution.py:834
  907.6 10.7 copy-start.54
  1133.3 28.9 %copy-start.52 = (bf16[1600,768]{1,0:T(8,128)(2,1)S(1)}, bf16[1600,768]{1,0:T(8,128)(2,1)}, u32[]{:S(2)}) copy-start(bf16[1600,768]{1,0:T(8,128)(2,1)} %copy-done.51) | copy-start | bytes 7372804
  1162.1 12.2 copy-start.34
  1162.2 12.2 copy-start.17
  1162.2 12.2 collective-permute-start.1
  1377.7 46.5 %copy-start.1 = (bf16[1,768,2048]{2,1,0:T(8,128)(2,1)S(1)}, bf16[1,768,2048]{2,1,0:T(8,128)(2,1)}, u32[]{:S(2)}) copy-start(bf16[1,768,2048]{2,1,0:T(8,128)(2,1)} %param.27) | copy-start | bytes 9437188
  (37 other events, 130.6 us)
Sparse Core Ops, SparseCore 0:
  905.4 168.0 all-reduce.8

commit v2 on v1

--- a/solution.py
+++ b/solution.py
@@ -582,6 +582,731 @@
     )
 
 
+def plane_order(z):
+    upper, odd = z // 2, z % 2
+    return [z, z + 1 - 2 * upper, 2 + upper - 2 * odd, 3 - 3 * upper]
+
+
+def world(with_diag):
+    r, e = lax.axis_index("dp"), lax.axis_index("expert")
+    z, core = e // 2, e % 2
+    near, far = r ^ 1, r ^ 2
+    devices = [(near, e), (far, e), (r, e ^ 1)]
+    devices += [(r, lax.rem(z + j, 4) * 2 + core) for j in (1, 2, 3)]
+    return r, e, z, core, near, far, devices
+
+
+def gather_world(mine, buf, zs, zr, ps, pr, ds, dr, before, group):
+    r, e, z, core, near, far, greeted = world(True)
+    half = mine.shape[0] // 2
+    low, high = pl.ds(0, half), pl.ds(half, half)
+    order = plane_order(z)
+    greet(greeted)
+
+    def slot(q, b, c):
+        return q * 8 + b * 2 + c
+
+    buf[slot(r, z, core)] = mine[...]
+    diag = r ^ 3
+    plane, pairs, lines = {}, {}, []
+
+    def hand(k, i, q):
+        at = slot(q, order[k], core)
+        copy = remote(buf.at[at], buf.at[at], ds.at[k, i], dr.at[k, i], (r, e ^ 1))
+        copy.start()
+        pairs[k, i] = copy
+
+    def issue(k):
+        b = order[k]
+        at = slot(r, b, core)
+        for side, cond, to in (
+            (0, (b <= z) & (z < 3), jnp.minimum(z + 1, 3)),
+            (1, (b >= z) & (z > 0), jnp.maximum(z - 1, 0)),
+        ):
+            copy = remote(buf.at[at], buf.at[at], zs.at[k, side], zr.at[b], (r, to * 2 + core))
+            lines.append((cond, copy))
+
+            @pl.when(cond)
+            def _():
+                copy.start()
+
+        mine_at, near_at, far_at = at, slot(near, b, core), slot(far, b, core)
+        for i, (src, part, p) in enumerate(
+            (
+                (mine_at, low, near),
+                (mine_at, high, far),
+                (mine_at, high, near),
+                (mine_at, low, far),
+                (near_at, low, far),
+                (far_at, high, near),
+            )
+        ):
+            plane[k, i] = remote(
+                buf.at[src, part], buf.at[src, part], ps.at[k, i], pr.at[k, i], (p, e)
+            )
+        for i in range(4):
+            plane[k, i].start()
+        hand(k, 0, r)
+
+    def line_wait(k):
+        b = order[k]
+        at = slot(r, b, core)
+        remote(buf.at[at], buf.at[at], zs.at[k, 0], zr.at[b], (r, e ^ 1)).wait_recv()
+        issue(k)
+
+    def passes(k):
+        plane[k, 0].wait_recv()
+        plane[k, 4].start()
+        plane[k, 1].wait_recv()
+        plane[k, 5].start()
+
+    def finish(k):
+        plane[k, 2].wait_recv()
+        hand(k, 1, near)
+        plane[k, 3].wait_recv()
+        hand(k, 2, far)
+
+    def corner(k):
+        plane[k, 4].wait_recv()
+        plane[k, 5].wait_recv()
+        hand(k, 3, diag)
+
+    def ready(k):
+        for i in range(4):
+            pairs[k, i].wait_recv()
+        group(k, order[k])
+
+    issue(0)
+    passes(0)
+    line_wait(1)
+    finish(0)
+    passes(1)
+    line_wait(2)
+    corner(0)
+    finish(1)
+    before(0, order[0])
+    ready(0)
+    passes(2)
+    line_wait(3)
+    corner(1)
+    finish(2)
+    before(1, order[1])
+    ready(1)
+    passes(3)
+    corner(2)
+    finish(3)
+    before(2, order[2])
+    ready(2)
+    before(3, order[3])
+    corner(3)
+    ready(3)
+    for copy in plane.values():
+        copy.wait_send()
+    for copy in pairs.values():
+        copy.wait_send()
+    for cond, copy in lines:
+
+        @pl.when(cond)
+        def _():
+            copy.wait_send()
+
+
+GATHER_SEMS = [
+    pltpu.SemaphoreType.DMA((4, 2)),
+    pltpu.SemaphoreType.DMA((4,)),
+    pltpu.SemaphoreType.DMA((4, 6)),
+    pltpu.SemaphoreType.DMA((4, 6)),
+    pltpu.SemaphoreType.DMA((4, 4)),
+    pltpu.SemaphoreType.DMA((4, 4)),
+]
+
+
+def selector(pos, source, room):
+    row = pos[source]
+    ids = lax.broadcasted_iota(jnp.int32, (room, row.shape[1]), 0)
+    return jnp.where(ids == row, 1.0, 0.0).astype(BF16)
+
+
+def experts_fwd_kernel(
+    mine, pos, wg, wu, wd, x_out, y_out, gate_out,
+    buf, wg_v, wu_v, wd_v, x_v, y_v, hid_v, gate_v, local, zs, zr, ps, pr, ds, dr,
+):
+    model = wg.shape[0]
+    room = x_v.shape[0] // 8
+    me = lax.axis_index("dp") * 8 + lax.axis_index("expert")
+    loads = [
+        pltpu.make_async_copy(a, b, local.at[i])
+        for i, (a, b) in enumerate(((wg, wg_v), (wu, wu_v), (wd, wd_v)))
+    ]
+    for copy in loads:
+        copy.start()
+
+    def before(k, b):
+        if k == 0:
+            for copy in loads:
+                copy.wait()
+
+    def group(k, b):
+        def pick(j, carry):
+            s = j // 2 * 8 + b * 2 + j % 2
+            rows = aligned(j, room)
+            sel = selector(pos, s, room)
+            for c in range(4):
+                n = slice(c * model // 4, (c + 1) * model // 4)
+                x_v[rows, n] = dot_nn(sel, buf[s, :, n]).astype(BF16)
+            extra = dot_nn(sel, buf[s, :, model:])
+            lane = lax.broadcasted_iota(jnp.int32, extra.shape, 1)
+            hit = (lane == me) | (lane == me + 64)
+            gate = jnp.sum(jnp.where(hit, extra, 0.0), axis=-1, keepdims=True)
+            gate_v[rows, :] = jnp.broadcast_to(gate, extra.shape)
+            return carry
+
+        lax.fori_loop(0, 8, pick, 0)
+
+        def first(c, carry):
+            n = aligned(c, 256)
+            g = dot_nn(x_v[...], wg_v[:, n])
+            u = dot_nn(x_v[...], wu_v[:, n])
+            hid_v[:, n] = (g / (1.0 + jnp.exp(-g)) * u).astype(BF16)
+            return carry
+
+        lax.fori_loop(0, wg.shape[1] // 256, first, 0)
+
+        def second(c, carry):
+            n = aligned(c, 256)
+            o = dot_nn(hid_v[...], wd_v[:, n]).astype(BF16).astype(F32)
+            y_v[:, n] = (o * gate_v[:, :1]).astype(BF16)
+            return carry
+
+        lax.fori_loop(0, model // 256, second, 0)
+        outs = [
+            pltpu.make_async_copy(a, o.at[b], local.at[i])
+            for i, (a, o) in enumerate(((x_v, x_out), (y_v, y_out), (gate_v, gate_out)))
+        ]
+        for copy in outs:
+            copy.start()
+        for copy in outs:
+            copy.wait()
+
+    gather_world(mine, buf, zs, zr, ps, pr, ds, dr, before, group)
+
+
+def experts_fwd(mine, pos, wg, wu, wd, room):
+    rows, width = mine.shape
+    model, ff = wg.shape
+    group = 8 * room
+    return pl.pallas_call(
+        experts_fwd_kernel,
+        out_shape=(
+            jax.ShapeDtypeStruct((4, group, model), BF16),
+            jax.ShapeDtypeStruct((4, group, model), BF16),
+            jax.ShapeDtypeStruct((4, group, 128), F32),
+        ),
+        in_specs=[VMEM_SPEC, VMEM_SPEC, ANY_SPEC, ANY_SPEC, ANY_SPEC],
+        out_specs=(ANY_SPEC,) * 3,
+        scratch_shapes=[
+            pltpu.VMEM((32, rows, width), BF16),
+            pltpu.VMEM((model, ff), BF16),
+            pltpu.VMEM((model, ff), BF16),
+            pltpu.VMEM((ff, model), BF16),
+            pltpu.VMEM((group, model), BF16),
+            pltpu.VMEM((group, model), BF16),
+            pltpu.VMEM((group, ff), BF16),
+            pltpu.VMEM((group, 128), F32),
+            pltpu.SemaphoreType.DMA((3,)),
+        ]
+        + GATHER_SEMS,
+        compiler_params=params(6),
+        name="experts_fwd",
+    )(mine, pos, wg, wu, wd)
+
+
+def experts_bwd_kernel(
+    mine, pos, x_in, gate_in, wg, wu, wd, y_out, d_copy_out, hid_out, dg_out, du_out,
+    buf, wg_v, wu_v, wd_v, x_v, gate_v, g_v, u_v, o_v, y_v, d_copy_v, hid_v, dg_v, du_v,
+    local, zs, zr, ps, pr, ds, dr,
+):
+    model, ff = wg.shape
+    room = x_v.shape[0] // 8
+    me = lax.axis_index("dp") * 8 + lax.axis_index("expert")
+    loads = [
+        pltpu.make_async_copy(a, b, local.at[i])
+        for i, (a, b) in enumerate(((wg, wg_v), (wu, wu_v), (wd, wd_v)))
+    ]
+    for copy in loads:
+        copy.start()
+
+    def before(k, b):
+        if k == 0:
+            for copy in loads:
+                copy.wait()
+        ins = [
+            pltpu.make_async_copy(x_in.at[b], x_v, local.at[3]),
+            pltpu.make_async_copy(gate_in.at[b], gate_v, local.at[4]),
+        ]
+        for copy in ins:
+            copy.start()
+        for copy in ins:
+            copy.wait()
+
+        def first(c, carry):
+            n = aligned(c, 256)
+            g = dot_nn(x_v[...], wg_v[:, n])
+            u = dot_nn(x_v[...], wu_v[:, n])
+            g_v[:, n] = g
+            u_v[:, n] = u
+            hid_v[:, n] = (g / (1.0 + jnp.exp(-g)) * u).astype(BF16)
+            return carry
+
+        lax.fori_loop(0, ff // 256, first, 0)
+
+        def second(c, carry):
+            n = aligned(c, 256)
+            o_v[:, n] = dot_nn(hid_v[...], wd_v[:, n]).astype(BF16)
+            return carry
+
+        lax.fori_loop(0, model // 256, second, 0)
+
+    def group(k, b):
+        def pick(j, carry):
+            s = j // 2 * 8 + b * 2 + j % 2
+            rows = aligned(j, room)
+            sel = selector(pos, s, room)
+            gate = gate_v[rows, :1]
+            inner = jnp.zeros((room, 1), F32)
+            for c in range(4):
+                n = slice(c * model // 4, (c + 1) * model // 4)
+                picked = dot_nn(sel, buf[s, :, n])
+                d_copy_v[rows, n] = (gate * picked).astype(BF16)
+                inner = inner + jnp.sum(picked * o_v[rows, n].astype(F32), axis=-1, keepdims=True)
+            top = inner.astype(BF16).astype(F32)
+            rest = inner - top
+            lane = lax.broadcasted_iota(jnp.int32, (room, 128), 1)
+            extra = jnp.where(lane == me, top, 0.0) + jnp.where(lane == me + 64, rest, 0.0)
+            y_v[rows, model:] = extra.astype(BF16)
+            return carry
+
+        lax.fori_loop(0, 8, pick, 0)
+
+        def third(c, carry):
+            n = aligned(c, 256)
+            d_hidden = dot_nt(d_copy_v[...], wd_v[n, :])
+            g, u = g_v[:, n], u_v[:, n]
+            s = 1.0 / (1.0 + jnp.exp(-g))
+            dg_v[:, n] = (d_hidden * u * s * (1.0 + g * (1.0 - s))).astype(BF16)
+            du_v[:, n] = (d_hidden * g * s).astype(BF16)
+            return carry
+
+        lax.fori_loop(0, ff // 256, third, 0)
+
+        def fourth(c, carry):
+            n = aligned(c, 256)
+            y_v[:, n] = (dot_nt(dg_v[...], wg_v[n, :]) + dot_nt(du_v[...], wu_v[n, :])).astype(BF16)
+            return carry
+
+        lax.fori_loop(0, model // 256, fourth, 0)
+        outs = [
+            pltpu.make_async_copy(a, o.at[b], local.at[i])
+            for i, (a, o) in enumerate(
+                (
+                    (y_v, y_out),
+                    (d_copy_v, d_copy_out),
+                    (hid_v, hid_out),
+                    (dg_v, dg_out),
+                    (du_v, du_out),
+                )
+            )
+        ]
+        for copy in outs:
+            copy.start()
+        for copy in outs:
+            copy.wait()
+
+    gather_world(mine, buf, zs, zr, ps, pr, ds, dr, before, group)
+
+
+def experts_bwd(mine, pos, x_in, gate_in, wg, wu, wd, room):
+    rows, width = mine.shape
+    model, ff = wg.shape
+    group = 8 * room
+    return pl.pallas_call(
+        experts_bwd_kernel,
+        out_shape=(
+            jax.ShapeDtypeStruct((4, group, model + 128), BF16),
+            jax.ShapeDtypeStruct((4, group, model), BF16),
+            jax.ShapeDtypeStruct((4, group, ff), BF16),
+            jax.ShapeDtypeStruct((4, group, ff), BF16),
+            jax.ShapeDtypeStruct((4, group, ff), BF16),
+        ),
+        in_specs=[VMEM_SPEC, VMEM_SPEC] + [ANY_SPEC] * 5,
+        out_specs=(ANY_SPEC,) * 5,
+        scratch_shapes=[
+            pltpu.VMEM((32, rows, width), BF16),
+            pltpu.VMEM((model, ff), BF16),
+            pltpu.VMEM((model, ff), BF16),
+            pltpu.VMEM((ff, model), BF16),
+            pltpu.VMEM((group, model), BF16),
+            pltpu.VMEM((group, 128), F32),
+            pltpu.VMEM((group, ff), F32),
+            pltpu.VMEM((group, ff), F32),
+            pltpu.VMEM((group, model), BF16),
+            pltpu.VMEM((group, model + 128), BF16),
+            pltpu.VMEM((group, model), BF16),
+            pltpu.VMEM((group, ff), BF16),
+            pltpu.VMEM((group, ff), BF16),
+            pltpu.VMEM((group, ff), BF16),
+            pltpu.SemaphoreType.DMA((5,)),
+        ]
+        + GATHER_SEMS,
+        compiler_params=params(7),
+        name="experts_bwd",
+    )(mine, pos, x_in, gate_in, wg, wu, wd)
+
+
+def sum_world_kernel(
+    y, pos, out, psend, pair, half_near, half_far, full_near, full_far, lines,
+    ds, dr, hs, hr, fs, fr, zs, zr,
+):
+    r, e, z, core, near, far, greeted = world(True)
+    rows, width = out.shape
+    room = y.shape[2]
+    half = rows // 2
+    low, high = pl.ds(0, half), pl.ds(half, half)
+    order = plane_order(z)[::-1]
+    diag = r ^ 3
+    who = [r, near, far, diag]
+    body_width = width // 512 * 512
+    greet(greeted)
+
+    def for_columns(fn):
+        def step(c, carry):
+            fn(aligned(c, 512))
+            return carry
+
+        lax.fori_loop(0, body_width // 512, step, 0)
+        if width > body_width:
+            fn(pl.ds(body_width, width - body_width))
+
+    def scattered(sel, q, b, c, n):
+        return dot_tn(sel, y[b, q * 2 + c, :, n])
+
+    pairs, halves, fulls, moves = {}, {}, {}, []
+
+    def stage_a(k):
+        b = order[k]
+        for i in (3, 1, 2, 0):
+            at = k * 4 + i
+            sel = selector(pos, who[i] * 8 + b * 2 + (1 - core), room)
+
+            def fill(n):
+                psend[at, :, n] = scattered(sel, who[i], b, 1 - core, n).astype(BF16)
+
+            for_columns(fill)
+            copy = remote(psend.at[at], pair.at[at], ds.at[at], dr.at[at], (r, e ^ 1))
+            copy.start()
+            pairs[at] = copy
+        for i in (3, 1, 2, 0):
+            at = k * 4 + i
+            sel = selector(pos, who[i] * 8 + b * 2 + core, room)
+            pairs[at].wait_recv()
+
+            def add(n):
+                value = scattered(sel, who[i], b, core, n) + pair[at, :, n].astype(F32)
+                pair[at, :, n] = value.astype(BF16)
+
+            for_columns(add)
+            if i == 3:
+                for side, (part, dst, p) in enumerate(
+                    ((low, half_near, near), (high, half_far, far))
+                ):
+                    copy = remote(
+                        pair.at[at, part], dst.at[k], hs.at[k, side], hr.at[k, side], (p, e)
+                    )
+                    copy.start()
+                    halves[k, side] = copy
+
+    def stage_b(k):
+        for side, (i, part, src, dst, p) in enumerate(
+            (
+                (2, low, half_near, full_far, far),
+                (1, high, half_far, full_near, near),
+            )
+        ):
+            at = k * 4 + i
+            halves[k, side].wait_recv()
+
+            def add(n):
+                value = pair[at, part, n].astype(F32) + src[k, :, n].astype(F32)
+                pair[at, part, n] = value.astype(BF16)
+
+            for_columns(add)
+            copy = remote(pair.at[at], dst.at[k], fs.at[k, side], fr.at[k, side], (p, e))
+            copy.start()
+            fulls[k, side] = copy
+
+    def stage_c(k):
+        b = order[k]
+        at = k * 4
+        fulls[k, 0].wait_recv()
+        fulls[k, 1].wait_recv()
+
+        def add(n):
+            out[:, n] = (
+                pair[at, :, n].astype(F32)
+                + full_near[k, :, n].astype(F32)
+                + full_far[k, :, n].astype(F32)
+            )
+
+        for_columns(add)
+        for side, cond in ((0, (b >= z) & (z > 0)), (1, (b <= z) & (z < 3))):
+
+            @pl.when(cond)
+            def _():
+                remote(
+                    lines.at[side, b], lines.at[side, b], zs.at[side, k], zr.at[side, b], (r, e ^ 1)
+                ).wait_recv()
+
+                def more(n):
+                    out[:, n] = out[:, n] + lines[side, b, :, n].astype(F32)
+
+                for_columns(more)
+
+        if k < 3:
+
+            def keep(n):
+                pair[at, :, n] = out[:, n].astype(BF16)
+
+            for_columns(keep)
+            for side, cond, to in (
+                (0, b > z, jnp.minimum(z + 1, 3)),
+                (1, b < z, jnp.maximum(z - 1, 0)),
+            ):
+                copy = remote(
+                    pair.at[at], lines.at[side, b], zs.at[side, k], zr.at[side, b], (r, to * 2 + core)
+                )
+                moves.append((cond, copy))
+
+                @pl.when(cond)
+                def _():
+                    copy.start()
+
+    stage_a(0)
+    stage_a(1)
+    stage_b(0)
+    stage_a(2)
+    stage_b(1)
+    stage_c(0)
+    stage_a(3)
+    stage_b(2)
+    stage_c(1)
+    stage_b(3)
+    stage_c(2)
+    stage_c(3)
+    for copies in (pairs, halves, fulls):
+        for copy in copies.values():
+            copy.wait_send()
+    for cond, copy in moves:
+
+        @pl.when(cond)
+        def _():
+            copy.wait_send()
+
+
+def sum_world(y, pos, rows, collective_id):
+    groups, per, room, width = y.shape
+
+    def blocks(n, size):
+        return pltpu.VMEM((n, size, width), BF16)
+
+    return pl.pallas_call(
+        sum_world_kernel,
+        out_shape=jax.ShapeDtypeStruct((rows, width), F32),
+        in_specs=[VMEM_SPEC, VMEM_SPEC],
+        out_specs=VMEM_SPEC,
+        scratch_shapes=[
+            blocks(16, rows),
+            blocks(16, rows),
+            blocks(4, rows // 2),
+            blocks(4, rows // 2),
+            blocks(4, rows),
+            blocks(4, rows),
+            pltpu.VMEM((2, 4, rows, width), BF16),
+            pltpu.SemaphoreType.DMA((16,)),
+            pltpu.SemaphoreType.DMA((16,)),
+            pltpu.SemaphoreType.DMA((4, 2)),
+            pltpu.SemaphoreType.DMA((4, 2)),
+            pltpu.SemaphoreType.DMA((4, 2)),
+            pltpu.SemaphoreType.DMA((4, 2)),
+            pltpu.SemaphoreType.DMA((2, 4)),
+            pltpu.SemaphoreType.DMA((2, 4)),
+        ],
+        compiler_params=params(collective_id),
+        name="sum_world",
+    )(y, pos)
+
+
+def experts_by_all_to_all(
+    mixed, state, teacher, routes, valid_slot, valid_count, router_weight, gate_weight, up_weight, down_weight,
+    devices, capacity, slots_all,
+):
+    tok_dev, model_width = mixed.shape
+    top_count = routes.shape[1]
+    ffn_width = gate_weight.shape[2]
+    logits = jnp.dot(mixed, router_weight, preferred_element_type=jnp.float32)
+    gates = jax.nn.softmax(jnp.take_along_axis(logits, routes, axis=1), axis=-1)
+    rows_total = tok_dev * top_count
+    expert_ids = routes.reshape(rows_total)
+    live_rows = jnp.repeat(valid_slot, top_count)
+    expert_range = jnp.arange(devices, dtype=jnp.int32)
+    hit_table = ((expert_ids[:, None] == expert_range[None, :]) & live_rows[:, None]).astype(
+        jnp.int32
+    )
+    earlier = jnp.cumsum(hit_table, axis=0) - hit_table
+    position_in = jnp.sum(earlier * hit_table, axis=1)
+    slot_index = jnp.where(live_rows, expert_ids * capacity + position_in, devices * capacity)
+    row_of_slot = (
+        jnp.full((devices * capacity + 1,), rows_total, jnp.int32)
+        .at[slot_index]
+        .set(jnp.arange(rows_total, dtype=jnp.int32))[: devices * capacity]
+    )
+    token_of_slot = jnp.where(row_of_slot < rows_total, row_of_slot // top_count, tok_dev)
+    mixed_pad = jnp.concatenate([mixed, jnp.zeros((1, model_width), jnp.bfloat16)], axis=0)
+    send_rows = mixed_pad[token_of_slot].reshape(devices, capacity, model_width)
+    arrived = lax.all_to_all(send_rows, ("dp", "expert"), split_axis=0, concat_axis=0, tiled=True)
+    sources = arrived.shape[0]
+    items = arrived.shape[1]
+    flat_in = arrived.reshape(sources * items, model_width)
+    gate_pre = jnp.dot(flat_in, gate_weight[0], preferred_element_type=jnp.float32)
+    up_pre = jnp.dot(flat_in, up_weight[0], preferred_element_type=jnp.float32)
+    hidden_units = (jax.nn.silu(gate_pre) * up_pre).astype(jnp.bfloat16)
+    produced = jnp.dot(hidden_units, down_weight[0], preferred_element_type=jnp.float32).astype(
+        jnp.bfloat16
+    )
+    produced, gate_pre, up_pre, hidden_units, arrived = (
+        produced.reshape(sources, items, model_width),
+        gate_pre.reshape(sources, items, ffn_width),
+        up_pre.reshape(sources, items, ffn_width),
+        hidden_units.reshape(sources, items, ffn_width),
+        arrived,
+    )
+    returned = lax.all_to_all(produced, ("dp", "expert"), split_axis=0, concat_axis=0, tiled=True)
+    returned_pad = jnp.concatenate(
+        [
+            returned.reshape(devices * capacity, model_width),
+            jnp.zeros((1, model_width), jnp.bfloat16),
+        ],
+        axis=0,
+    )
+    copies = returned_pad[slot_index].reshape(tok_dev, top_count, model_width)
+    layer_out = state + jnp.sum(gates[:, :, None] * copies, axis=1)
+    live_tokens = valid_slot.astype(jnp.float32)[:, None]
+    diff = (layer_out - teacher.astype(jnp.float32)) * live_tokens
+    local_square = jnp.sum(diff * diff)
+    d_out = 2.0 * slots_all * diff / valid_count
+    d_gates = jnp.sum(d_out[:, None, :] * copies, axis=-1)
+    d_chosen = gates * (d_gates - jnp.sum(gates * d_gates, axis=-1, keepdims=True))
+    d_logits = jnp.sum(
+        jnp.where(routes[:, :, None] == expert_range[None, None, :], d_chosen[:, :, None], 0.0),
+        axis=1,
+    ).astype(jnp.bfloat16)
+    d_copies = (
+        (gates[:, :, None] * d_out[:, None, :])
+        .astype(jnp.bfloat16)
+        .reshape(rows_total, model_width)
+    )
+    d_copies_pad = jnp.concatenate([d_copies, jnp.zeros((1, model_width), jnp.bfloat16)], axis=0)
+    d_send = d_copies_pad[row_of_slot].reshape(devices, capacity, model_width)
+    d_arrived = lax.all_to_all(d_send, ("dp", "expert"), split_axis=0, concat_axis=0, tiled=True)
+    flat_d = d_arrived.reshape(-1, model_width)
+    flat_in = arrived.reshape(-1, model_width)
+    flat_gate = gate_pre.reshape(-1, ffn_width)
+    flat_up = up_pre.reshape(-1, ffn_width)
+    flat_hidden = hidden_units.reshape(-1, ffn_width)
+    d_hidden = contract(flat_d, down_weight[0], 1, 1)
+    sigmoid_gate = jax.nn.sigmoid(flat_gate)
+    d_gate = (d_hidden * flat_up * sigmoid_gate * (1.0 + flat_gate * (1.0 - sigmoid_gate))).astype(
+        jnp.bfloat16
+    )
+    d_up = (d_hidden * flat_gate * sigmoid_gate).astype(jnp.bfloat16)
+    down_grad = contract(flat_hidden, flat_d, 0, 0)[None]
+    gate_grad = contract(flat_in, d_gate, 0, 0)[None]
+    up_grad = contract(flat_in, d_up, 0, 0)[None]
+    d_in = (contract(d_gate, gate_weight[0], 1, 1) + contract(d_up, up_weight[0], 1, 1)).astype(
+        jnp.bfloat16
+    )
+    d_returned = lax.all_to_all(
+        d_in.reshape(devices, capacity, model_width),
+        ("dp", "expert"),
+        split_axis=0,
+        concat_axis=0,
+        tiled=True,
+    )
+    d_returned_pad = jnp.concatenate(
+        [
+            d_returned.reshape(devices * capacity, model_width),
+            jnp.zeros((1, model_width), jnp.bfloat16),
+        ],
+        axis=0,
+    )
+    d_mixed = jnp.sum(
+        d_returned_pad[slot_index].reshape(tok_dev, top_count, model_width),
+        axis=1,
+        dtype=jnp.float32,
+    )
+    d_mixed = d_mixed + contract(d_logits, router_weight, 1, 1)
+    router_local = contract(mixed, d_logits, 0, 0)
+    return layer_out, d_out, d_mixed, local_square, router_local, gate_grad, up_grad, down_grad
+
+
+def experts_by_gather(
+    mixed, state, teacher, routes, cont_lengths, valid_slot, valid_count, router_weight,
+    gate_weight, up_weight, down_weight, devices, capacity, slots_all, flat_rank,
+):
+    tok_dev, model_width = mixed.shape
+    room = -(-capacity // 16) * 16
+    expert_range = jnp.arange(devices, dtype=jnp.int32)
+    slot_ids = jnp.arange(tok_dev, dtype=jnp.int32)
+    prompt_block = tok_dev - CMAX
+    routes_all = lax.all_gather(routes, ("dp", "expert"), axis=0, tiled=False)
+    valid_all = (slot_ids[None] < prompt_block) | (slot_ids[None] - prompt_block < cont_lengths[:, None])
+    named = jnp.any(routes_all == flat_rank, axis=-1) & valid_all
+    upto = (slot_ids[:, None] <= slot_ids[None]).astype(F32)
+    place = jnp.dot(named.astype(F32), upto, preferred_element_type=F32).astype(jnp.int32) - 1
+    pos = jnp.where(named, place, -1)[:, None, :]
+
+    logits = jnp.dot(mixed, router_weight, preferred_element_type=F32)
+    chosen = jnp.any(routes[:, :, None] == expert_range[None, None], axis=1)
+    gates = jax.nn.softmax(jnp.where(chosen, logits, -jnp.inf), axis=-1)
+    gates_high = gates.astype(BF16)
+    gates_low = (gates - gates_high.astype(F32)).astype(BF16)
+    gap = jnp.zeros((tok_dev, 64 - devices), BF16)
+    payload = jnp.concatenate([mixed, gates_high, gap, gates_low, gap], axis=1)
+    x_rows, y_rows, slot_gates = experts_fwd(
+        payload, pos, gate_weight[0], up_weight[0], down_weight[0], room
+    )
+    layer_out = state + sum_world(y_rows.reshape(4, 8, room, model_width), pos, tok_dev, 8)
+    live_tokens = valid_slot.astype(F32)[:, None]
+    diff = (layer_out - teacher.astype(F32)) * live_tokens
+    local_square = jnp.sum(diff * diff)
+    d_out = 2.0 * slots_all * diff / valid_count
+    d_rows, d_copy, hidden, d_gate, d_up = experts_bwd(
+        d_out.astype(BF16), pos, x_rows, slot_gates, gate_weight[0], up_weight[0], down_weight[0], room
+    )
+    back = sum_world(d_rows.reshape(4, 8, room, model_width + 128), pos, tok_dev, 9)
+
+    def flat(a):
+        return a.reshape(4 * 8 * room, a.shape[-1])
+
+    down_grad = contract(flat(hidden), flat(d_copy), 0, 0)[None]
+    gate_grad = contract(flat(x_rows), flat(d_gate), 0, 0)[None]
+    up_grad = contract(flat(x_rows), flat(d_up), 0, 0)[None]
+    d_gates = back[:, model_width : model_width + devices] + back[:, model_width + 64 : model_width + 64 + devices]
+    d_logits = (gates * (d_gates - jnp.sum(gates * d_gates, axis=-1, keepdims=True))).astype(BF16)
+    d_mixed = back[:, :model_width] + contract(d_logits, router_weight, 1, 1)
+    router_local = contract(mixed, d_logits, 0, 0)
+    return layer_out, d_out, d_mixed, local_square, router_local, gate_grad, up_grad, down_grad
+
+
 def head_rope(linear, gain_vec, cos, sin):
     value = root_mean_scale(linear, gain_vec)
     half = value.shape[-1] // 2
@@ -621,7 +1346,6 @@
     query_width = query_weight.shape[1]
     query_group = query_width // n_dp
     assert n_dp == 4 and kv_width == n_dp * head_dim
-    ffn_width = gate_weight.shape[2]
     prompt_block = tok_dev - CMAX
     half_prompt = n_dp * prompt_block
     prompt_len = 2 * half_prompt
@@ -675,109 +1399,17 @@
     state = tokens_float + project_out(attended, output_weight)
     mixed_float, second_norm_back = jax.vjp(root_mean_scale, state, post_gain)
     mixed = mixed_float.astype(BF16)
-    logits = jnp.dot(mixed, router_weight, preferred_element_type=jnp.float32)
-    gates = jax.nn.softmax(jnp.take_along_axis(logits, routes, axis=1), axis=-1)
-    rows_total = tok_dev * top_count
-    expert_ids = routes.reshape(rows_total)
-    live_rows = jnp.repeat(valid_slot, top_count)
-    expert_range = jnp.arange(devices, dtype=jnp.int32)
-    hit_table = ((expert_ids[:, None] == expert_range[None, :]) & live_rows[:, None]).astype(
-        jnp.int32
-    )
-    earlier = jnp.cumsum(hit_table, axis=0) - hit_table
-    position_in = jnp.sum(earlier * hit_table, axis=1)
-    slot_index = jnp.where(live_rows, expert_ids * capacity + position_in, devices * capacity)
-    row_of_slot = (
-        jnp.full((devices * capacity + 1,), rows_total, jnp.int32)
-        .at[slot_index]
-        .set(jnp.arange(rows_total, dtype=jnp.int32))[: devices * capacity]
-    )
-    token_of_slot = jnp.where(row_of_slot < rows_total, row_of_slot // top_count, tok_dev)
-    mixed_pad = jnp.concatenate([mixed, jnp.zeros((1, model_width), jnp.bfloat16)], axis=0)
-    send_rows = mixed_pad[token_of_slot].reshape(devices, capacity, model_width)
-    arrived = lax.all_to_all(send_rows, ("dp", "expert"), split_axis=0, concat_axis=0, tiled=True)
-    sources = arrived.shape[0]
-    items = arrived.shape[1]
-    flat_in = arrived.reshape(sources * items, model_width)
-    gate_pre = jnp.dot(flat_in, gate_weight[0], preferred_element_type=jnp.float32)
-    up_pre = jnp.dot(flat_in, up_weight[0], preferred_element_type=jnp.float32)
-    hidden_units = (jax.nn.silu(gate_pre) * up_pre).astype(jnp.bfloat16)
-    produced = jnp.dot(hidden_units, down_weight[0], preferred_element_type=jnp.float32).astype(
-        jnp.bfloat16
-    )
-    produced, gate_pre, up_pre, hidden_units, arrived = (
-        produced.reshape(sources, items, model_width),
-        gate_pre.reshape(sources, items, ffn_width),
-        up_pre.reshape(sources, items, ffn_width),
-        hidden_units.reshape(sources, items, ffn_width),
-        arrived,
-    )
-    returned = lax.all_to_all(produced, ("dp", "expert"), split_axis=0, concat_axis=0, tiled=True)
-    returned_pad = jnp.concatenate(
-        [
-            returned.reshape(devices * capacity, model_width),
-            jnp.zeros((1, model_width), jnp.bfloat16),
-        ],
-        axis=0,
-    )
-    copies = returned_pad[slot_index].reshape(tok_dev, top_count, model_width)
-    layer_out = state + jnp.sum(gates[:, :, None] * copies, axis=1)
-    live_tokens = valid_slot.astype(jnp.float32)[:, None]
-    diff = (layer_out - teacher.astype(jnp.float32)) * live_tokens
-    local_square = jnp.sum(diff * diff)
-    d_out = 2.0 * slots_all * diff / valid_count
-    d_gates = jnp.sum(d_out[:, None, :] * copies, axis=-1)
-    d_chosen = gates * (d_gates - jnp.sum(gates * d_gates, axis=-1, keepdims=True))
-    d_logits = jnp.sum(
-        jnp.where(routes[:, :, None] == expert_range[None, None, :], d_chosen[:, :, None], 0.0),
-        axis=1,
-    ).astype(jnp.bfloat16)
-    d_copies = (
-        (gates[:, :, None] * d_out[:, None, :])
-        .astype(jnp.bfloat16)
-        .reshape(rows_total, model_width)
-    )
-    d_copies_pad = jnp.concatenate([d_copies, jnp.zeros((1, model_width), jnp.bfloat16)], axis=0)
-    d_send = d_copies_pad[row_of_slot].reshape(devices, capacity, model_width)
-    d_arrived = lax.all_to_all(d_send, ("dp", "expert"), split_axis=0, concat_axis=0, tiled=True)
-    flat_d = d_arrived.reshape(-1, model_width)
-    flat_in = arrived.reshape(-1, model_width)
-    flat_gate = gate_pre.reshape(-1, ffn_width)
-    flat_up = up_pre.reshape(-1, ffn_width)
-    flat_hidden = hidden_units.reshape(-1, ffn_width)
-    d_hidden = contract(flat_d, down_weight[0], 1, 1)
-    sigmoid_gate = jax.nn.sigmoid(flat_gate)
-    d_gate = (d_hidden * flat_up * sigmoid_gate * (1.0 + flat_gate * (1.0 - sigmoid_gate))).astype(
-        jnp.bfloat16
-    )
-    d_up = (d_hidden * flat_gate * sigmoid_gate).astype(jnp.bfloat16)
-    down_grad = contract(flat_hidden, flat_d, 0, 0)[None]
-    gate_grad = contract(flat_in, d_gate, 0, 0)[None]
-    up_grad = contract(flat_in, d_up, 0, 0)[None]
-    d_in = (contract(d_gate, gate_weight[0], 1, 1) + contract(d_up, up_weight[0], 1, 1)).astype(
-        jnp.bfloat16
-    )
-    d_returned = lax.all_to_all(
-        d_in.reshape(devices, capacity, model_width),
-        ("dp", "expert"),
-        split_axis=0,
-        concat_axis=0,
-        tiled=True,
-    )
-    d_returned_pad = jnp.concatenate(
-        [
-            d_returned.reshape(devices * capacity, model_width),
-            jnp.zeros((1, model_width), jnp.bfloat16),
-        ],
-        axis=0,
-    )
-    d_mixed = jnp.sum(
-        d_returned_pad[slot_index].reshape(tok_dev, top_count, model_width),
-        axis=1,
-        dtype=jnp.float32,
-    )
-    d_mixed = d_mixed + contract(d_logits, router_weight, 1, 1)
-    router_local = contract(mixed, d_logits, 0, 0)
+    sizes = (devices, capacity, slots_all)
+    weights = (router_weight, gate_weight, up_weight, down_weight)
+    if n_dp == 4 and n_owner == 8:
+        moe = experts_by_gather(
+            mixed, state, teacher, routes, cont_lengths, valid_slot, valid_count, *weights, *sizes, flat_rank
+        )
+    else:
+        moe = experts_by_all_to_all(
+            mixed, state, teacher, routes, valid_slot, valid_count, *weights, *sizes
+        )
+    layer_out, d_out, d_mixed, local_square, router_local, gate_grad, up_grad, down_grad = moe
     d_state_norm, d_post_gain = second_norm_back(d_mixed)
     d_state = d_out + d_state_norm
     d_branch = d_state.astype(BF16)

time: 1440 us -> 1060 us (0.74)
  Pallas kernels: 398 us -> 865 us
  blocking collectives: 371 us -> 76.7 us
  waiting for transfers between devices: 274 us -> 0.04 us
  local copies, waits for them, and re-layouts: 206 us -> 24 us
  matrix products: 84.3 us -> 37.9 us
  other arithmetic: 67.7 us -> 29.9 us
    pallas_call x0 -> x4, Pallas kernels: none -> 471 us  [the longest x2 229 us: sum_world(): pl.pallas_call(sum_world_kernel, out_shape=jax.ShapeDtypeStruct((rows, wi...]
    all_to_all x2 -> x0, blocking collectives: 333 us -> none  [the longest x1 168 us: body(): lax.all_to_all(d_send, ('dp', 'expert'), split_axis=0, concat_axis=0, til...]
    all_to_all x2 -> x0, waiting for transfers between devices: 274 us -> none  [the longest x1 144 us: body(): lax.all_to_all(produced, ('dp', 'expert'), split_axis=0, concat_axis=0, t...]
    gather x9 -> x0, local copies, waits for them, and re-layouts: 73 us -> none  [the longest x1 17.5 us: body(): d_send = d_copies_pad[row_of_slot].reshape(devices, capacity, model_width)]
    reshape x9 -> x0, local copies, waits for them, and re-layouts: 70.4 us -> none  [the longest x1 8.8 us: body(): flat_d = d_arrived.reshape(-1, model_width)]
    all_gather x0 -> x1, blocking collectives: none -> 38.2 us  [experts_by_gather(): routes_all = lax.all_gather(routes, ('dp', 'expert'), axis=0, tiled=False)]
    dot_general x4 -> x2, matrix products: 24.4 us -> 0.61 us  [the longest x1 0.42 us: experts_by_gather(): logits = jnp.dot(mixed, router_weight, preferred_element_type=F32)]
    dot_general x8 -> x5, matrix products: 59.9 us -> 37.3 us  [contract(): lax.dot_general(left_side, right_side, (((left_dim,), (right_dim,)), ((),...]
  transfers between devices with their start and end apart: 5 -> 3, of which waited for: 2 -> 0; matrix products, arithmetic and copies ran while one was open for 11% -> 5% of each run, Pallas kernels for 18% -> 18%
where the time goes in v2:
time: 1060 us; the launch traced here: 1050 us
  Pallas kernels  865 us (82%)
  blocking collectives  76.7 us (7%)
  matrix products  37.9 us (4%)
  other arithmetic  29.9 us (3%)
  local copies, waits for them, and re-layouts  24 us (2%)
  between operations  17.4 us (2%)
    pallas_call x2, Pallas kernels, sum_world(): pl.pallas_call(sum_world_kernel, out_shape=jax.ShapeDtypeStruct((rows, wi...  229 us
    pallas_call x1, Pallas kernels, experts_bwd(): pl.pallas_call(experts_bwd_kernel, out_shape=(jax.ShapeDtypeStruct((4, gr...  126 us
    pallas_call x1, Pallas kernels, experts_fwd(): pl.pallas_call(experts_fwd_kernel, out_shape=(jax.ShapeDtypeStruct((4, gr...  115 us
    pallas_call x1, Pallas kernels, owner_sums(): pl.pallas_call(functools.partial(owner_sum_kernel, n_owner, n), out_shape...  113 us
    pallas_call x1, Pallas kernels, project_qkv(): pl.pallas_call(functools.partial(qkv_kernel, tok), out_shape=(jax.ShapeDt...  89.2 us
    pallas_call x1, Pallas kernels, grad_qkv(): pl.pallas_call(dgrad_kernel, out_shape=(jax.ShapeDtypeStruct((tok, 4 * wi...  77.7 us
    psum x1, blocking collectives, body(): lax.psum((local_square, d_input_gain, d_post_gain, d_query_gain, d_key_ga...  38.5 us
    all_gather x1, blocking collectives, experts_by_gather(): routes_all = lax.all_gather(routes, ('dp', 'expert'), axis=0, tiled=False)  38.2 us
  transfers between devices with their start and end apart: 3, of which 0 were waited for; matrix products, arithmetic and copies ran while one was open for 5% of the time, Pallas kernels for 18%

profile of v2, /device:TPU:8, one launch (start us, length us, event | category | flops | bytes accessed | tf_op | source)
XLA Modules:
  0.0 1051.0 jit_solution(11943451218910194208)
XLA Ops:
  8.6 2.1 fusion.2.normed
  10.8 89.2 %qkv_exchange.1 = (f32[640,1280]{1,0:T(8,128)}, bf16[640,512]{1,0:T(8,128)(2,1)}) custom-call(bf16[160,2048]{1,0:T(8,128)(2,1)} %fusion.2.normed, bf16[512,4096]{1,0:T(8,128)(2,1)} %wq.3, bf16[512,512]{1,0:T(8,128)(2,1)} %wk.3, bf16[512,512]{1,0:T(8,128)(2,1)} %wv.3), custom_call_target="tpu_custom_call" | custom-call | tf_op jit(solution)/shard_map/qkv_exchange/pallas_call | solution.py:121
  108.7 38.2 %all-gather.1 = s32[32,160,8]{1,2,0:T(8,128)S(1)} all-gather(s32[1,160,8]{1,2,0:T(8,128)S(1)} %bitcast.105), channel_id=2, replica_groups=mesh['dp'=4,'expert'=8] {'dp','expert'}, dimensions={0}, use_global_device_ids=true | all-gather | bytes 168960 | tf_op jit(solution)/shard_map/all_gather | solution.py:1270
  150.7 15.8 %attention_fwd.1 = (bf16[640,1024]{1,0:T(8,128)(2,1)}, bf16[640,1024]{1,0:T(8,128)(2,1)}) custom-call(s32[5]{0:T(128)} %pad_add_fusion.lengths, f32[640,1280]{1,0:T(8,128)} %get-tuple-element.37.lin, f32[1,128]{1,0:T(1,128)} %bitcast.106, f32[4,160,128]{2,1,0:T(8,128)} %get-tuple-element.86.cos, f32[4,160,128]{2,1,0:T(8,128)} %get-tuple-element.78.sin, ...), custom_call_target="tpu_custom_call" | custom-call | tf_op jit(solution)/shard_map/attention_fwd/pallas_call | solution.py:475
  166.5 2.4 copy.66
  168.9 37.4 %out_exchange.1 = f32[160,2048]{1,0:T(8,128)} custom-call(bf16[640,1024]{1,0:T(8,128)(2,1)} %get-tuple-element.38.attn, bf16[1024,2048]{1,0:T(8,128)(2,1)} %wo.3), custom_call_target="tpu_custom_call" | custom-call | tf_op jit(solution)/shard_map/out_exchange/pallas_call | solution.py:177
  211.2 115.0 %experts_fwd.1 = (bf16[4,512,2048]{2,1,0:T(8,128)(2,1)}, bf16[4,512,2048]{2,1,0:T(8,128)(2,1)}, f32[4,512,128]{2,1,0:T(8,128)}) custom-call(bf16[160,2176]{1,0:T(8,128)(2,1)} %concatenate.67.mine, s32[32,1,160]{2,1,0:T(1,128)} %broadcast_in_dim.97.pos, bf16[2048,768]{1,0:T(8,128)(2,1)} %bitcast.70, bf16[2048,768]{1,0:T(8,128)(2,1)} %bitcast.72, ...), custom_call_target="tpu_custom_call" | custom-call | tf_op jit(solution)/shard_map/experts_fwd/pallas_call | solution.py:798
  326.2 105.3 %sum_world.2 = f32[160,2048]{1,0:T(8,128)} custom-call(bf16[4,8,64,2048]{3,2,1,0:T(8,128)(2,1)} %bitcast.77, s32[32,1,160]{2,1,0:T(1,128)} %broadcast_in_dim.97.pos), custom_call_target="tpu_custom_call" | custom-call | tf_op jit(solution)/shard_map/sum_world/pallas_call | solution.py:1121
  431.5 2.9 fusion.15
  434.5 126.5 %experts_bwd.1 = (bf16[4,512,2176]{2,1,0:T(8,128)(2,1)}, bf16[4,512,2048]{2,1,0:T(8,128)(2,1)}, bf16[4,512,768]{2,1,0:T(8,128)(2,1)}, bf16[4,512,768]{2,1,0:T(8,128)(2,1)}, bf16[4,512,768]{2,1,0:T(8,128)(2,1)}) custom-call(bf16[160,2048]{1,0:T(8,128)(2,1)} %get-tuple-element.73.mine, s32[32,1,160]{2,1,0:T(1,128)} %broadcast_in_dim.97.pos, ...), custom_call_target="tpu_custom_call" | custom-call | tf_op jit(solution)/shard_map/experts_bwd/pallas_call | solution.py:932
  561.0 124.0 %sum_world.3 = f32[160,2176]{1,0:T(8,128)} custom-call(bf16[4,8,64,2176]{3,2,1,0:T(8,128)(2,1)} %bitcast.76, s32[32,1,160]{2,1,0:T(1,128)} %broadcast_in_dim.97.pos), custom_call_target="tpu_custom_call" | custom-call | tf_op jit(solution)/shard_map/sum_world/pallas_call | solution.py:1121
  686.2 3.0 multiply_reduce_fusion
  689.2 2.1 fusion.35
  691.2 4.5 fusion.30
  695.7 35.1 %branch_exchange.1 = (bf16[640,1024]{1,0:T(8,128)(2,1)}, bf16[1024,2048]{1,0:T(8,128)(2,1)}) custom-call(bf16[160,2048]{1,0:T(8,128)(2,1)} %get-tuple-element.71.mine, bf16[1024,2048]{1,0:T(8,128)(2,1)} %wo.3, bf16[1024,640]{1,0:T(8,128)(2,1)} %bitcast.83), custom_call_target="tpu_custom_call" | custom-call | tf_op jit(solution)/shard_map/branch_exchange/pallas_call | solution.py:343
  730.9 26.4 %attention_bwd.1 = (bf16[640,1024]{1,0:T(8,128)(2,1)}, f32[4,384,128]{2,1,0:T(8,128)}, f32[4,384,128]{2,1,0:T(8,128)}, f32[4,8,128]{2,1,0:T(8,128)}) custom-call(s32[5]{0:T(128)} %pad_add_fusion.lengths, f32[640,1280]{1,0:T(8,128)} %get-tuple-element.37.lin, bf16[640,1024]{1,0:T(8,128)(2,1)} %get-tuple-element.43.queries, ...), custom_call_target="tpu_custom_call" | custom-call | tf_op jit(solution)/shard_map/attention_bwd/pallas_call | solution.py:545
  759.6 12.0 %convolution_bitcast_fusion.2 = f32[1,2048,768]{2,1,0:T(8,128)} fusion(bf16[4,512,2048]{2,1,0:T(8,128)(2,1)} %get-tuple-element.40.x_in, bf16[4,512,768]{2,1,0:T(8,128)(2,1)} %get-tuple-element.54), kind=kOutput, calls=%fused_computation.2 | convolution fusion | flops 6442450944 | bytes 17825792 | tf_op jit(solution)/shard_map/dot_general | solution.py:577
  771.7 11.4 %convolution_bitcast_fusion.1 = f32[1,2048,768]{2,1,0:T(8,128)} fusion(bf16[4,512,2048]{2,1,0:T(8,128)(2,1)} %get-tuple-element.40.x_in, bf16[4,512,768]{2,1,0:T(8,128)(2,1)S(1)} %copy-done.28), kind=kOutput, calls=%fused_computation.1 | convolution fusion | flops 6442450944 | bytes 17825792 | tf_op jit(solution)/shard_map/dot_general | solution.py:577
  783.1 8.8 convolution_bitcast_fusion
  797.3 77.7 %dqkv_exchange.1 = (f32[160,2048]{1,0:T(8,128)}, bf16[2048,1280]{1,0:T(8,128)(2,1)}) custom-call(bf16[640,1280]{1,0:T(8,128)(2,1)} %pad_maximum_fusion.mine, bf16[512,4096]{1,0:T(8,128)(2,1)} %wq.3, bf16[512,512]{1,0:T(8,128)(2,1)} %wk.3, bf16[512,512]{1,0:T(8,128)(2,1)} %wv.3, bf16[512,640]{1,0:T(8,128)(2,1)} %bitcast.85), custom_call_target="tpu_custom_call" | custom-call | tf_op jit(solution)/shard_map/dqkv_exchange/pallas_call | solution.py:265
  875.0 1.8 fusion.3
  876.9 5.4 copy.68
  882.3 112.6 %owner_sums.1 = (f32[256,1280]{1,0:T(8,128)}, f32[128,2048]{1,0:T(8,128)}) custom-call(bf16[8,256,1280]{2,1,0:T(8,128)(2,1)} %bitcast.69, bf16[8,128,2048]{2,1,0:T(8,128)(2,1)} %bitcast.84), custom_call_target="tpu_custom_call" | custom-call | tf_op jit(solution)/shard_map/owner_sums/pallas_call | solution.py:413
  999.5 38.5 %all-reduce.2 = (f32[]{:T(128)}, f32[2048]{0:T(1024)}, f32[2048]{0:T(1024)}, f32[128]{0:T(128)}, f32[128]{0:T(128)}) all-reduce(f32[]{:T(128)} %get-tuple-element.81, f32[2048]{0:T(1024)S(1)} %get-tuple-element.61, f32[2048]{0:T(1024)S(1)} %get-tuple-element.59, ...), channel_id=1, replica_groups=mesh['dp'=4,'expert'=8] {'dp','expert'}, use_global_device_ids=true, to_apply=%region_8.9 | all-reduce | flops 4353 | bytes 34824 | tf_op jit(solution)/shard_map/psum | solution.py:1466
  (144 shorter events, 35.5 us)
Async XLA Ops:
  7.2 200.9 %copy-start = (bf16[2048,32]{0,1:T(8,128)(2,1)S(1)}, bf16[2048,32]{0,1:T(8,128)(2,1)}, u32[]{:S(2)}) copy-start(bf16[2048,32]{0,1:T(8,128)(2,1)} %param.24) | copy-start | bytes 393220
  7.2 1033.8 %all-reduce.5.cloned.1.call-start = ((), (), s32[]{:S(2)}) async-start(), calls=%async_computation | async-start | bytes 524288 | tf_op jit(solution)/shard_map/psum | solution.py:1466
  8.6 91.4 %copy-start.17 = (f32[160]{0:T(256)}, f32[160]{0:T(256)S(1)}, u32[]{:S(2)}) copy-start(f32[160]{0:T(256)S(1)} %fusion.6) | copy-start | bytes 1924
  8.6 91.4 %copy-start.15 = (f32[160]{0:T(256)}, f32[160]{0:T(256)S(1)}, u32[]{:S(2)}) copy-start(f32[160]{0:T(256)S(1)} %fusion.26) | copy-start | bytes 1924
  10.8 91.5 %copy-start.23 = (f32[128]{0:T(128)S(1)}, f32[128]{0:T(128)}, u32[]{:S(2)}) copy-start(f32[128]{0:T(128)} %param.31) | copy-start | bytes 1540
  103.9 4.6 copy-start.13
  105.2 42.6 %copy-start.9 = (bf16[640,512]{1,0:T(8,128)(2,1)S(1)}, bf16[640,512]{1,0:T(8,128)(2,1)}, u32[]{:S(2)}) copy-start(bf16[640,512]{1,0:T(8,128)(2,1)} %get-tuple-element.48) | copy-start | bytes 1966084
  105.2 44.5 %collective-permute-start = (bf16[2,128,128]{2,1,0:T(8,128)(2,1)S(1)}, bf16[2,128,128]{2,1,0:T(8,128)(2,1)S(1)}, u32[]{:S(2)}, u32[]{:S(2)}) collective-permute-start(bf16[2,128,128]{2,1,0:T(8,128)(2,1)S(1)} %get-tuple-element.94), channel_id=1, source_target_pairs={{0,1},{1,0},{2,3},{3,2},{4,5},{5,4},{6,7},{7,6},{8,9},{9,8},{10,11... | collective-permute-start | bytes 196616 | tf_op jit(solution)/shard_map/ppermute | solution.py:565
  168.9 37.4 %copy-start.2 = (bf16[160,2048]{1,0:T(8,128)(2,1)S(1)}, bf16[160,2048]{1,0:T(8,128)(2,1)}, u32[]{:S(2)}) copy-start(bf16[160,2048]{1,0:T(8,128)(2,1)} %param.16) | copy-start | bytes 1966084
  326.2 105.3 %copy-start.6 = (bf16[160,2048]{1,0:T(8,128)(2,1)S(1)}, bf16[160,2048]{1,0:T(8,128)(2,1)}, u32[]{:S(2)}) copy-start(bf16[160,2048]{1,0:T(8,128)(2,1)} %param.17) | copy-start | bytes 1966084
  326.2 105.3 %copy-start.25 = (f32[160]{0:T(256)S(1)}, f32[160]{0:T(256)}, u32[]{:S(2)}) copy-start(f32[160]{0:T(256)} %or_convert_fusion) | copy-start | bytes 1924
  561.0 125.2 %copy-start.22 = (f32[160]{0:T(256)S(1)}, f32[160]{0:T(256)}, u32[]{:S(2)}) copy-start(f32[160]{0:T(256)} %copy-done.21) | copy-start | bytes 1924
  686.1 5.1 copy-start.20
  759.5 34.4 %collective-permute-start.1 = (f32[2,128,128]{2,1,0:T(8,128)S(1)}, f32[2,128,128]{2,1,0:T(8,128)S(1)}, u32[]{:S(2)}, u32[]{:S(2)}) collective-permute-start(f32[2,128,128]{2,1,0:T(8,128)S(1)} %broadcast_select_fusion), channel_id=1, source_target_pairs={{0,1},{1,0},{2,3},{3,2},{4,5},{5,4},{6,7},{7,6},{8,9},{9,8},{10,11... | collective-permute-start | bytes 393224 | tf_op jit(solution)/shard_map/ppermute | solution.py:565
  759.6 12.0 %copy-start.28 = (bf16[4,512,768]{2,1,0:T(8,128)(2,1)S(1)}, bf16[4,512,768]{2,1,0:T(8,128)(2,1)}, u32[]{:S(2)}) copy-start(bf16[4,512,768]{2,1,0:T(8,128)(2,1)} %get-tuple-element.55) | copy-start | bytes 9437188
  759.6 23.4 %slice-start = ((s8[8388608]{0:T(1024)(128)(4,1)}), s8[4194304]{0:T(1024)(128)(4,1)S(1)}, s32[]{:S(2)}) async-start(s8[8388608]{0:T(1024)(128)(4,1)} %bitcast.108), calls=%async_computation.1 | async-start | bytes 8388608
  771.6 11.4 %slice-start.1 = ((s8[8388608]{0:T(1024)(128)(4,1)}), s8[4194304]{0:T(1024)(128)(4,1)S(1)}, s32[]{:S(2)}) async-start(s8[8388608]{0:T(1024)(128)(4,1)} %bitcast.108), calls=%async_computation.2 | async-start | bytes 8388608
  771.7 11.4 %copy-start.27 = (bf16[4,512,768]{2,1,0:T(8,128)(2,1)S(1)}, bf16[4,512,768]{2,1,0:T(8,128)(2,1)}, u32[]{:S(2)}) copy-start(bf16[4,512,768]{2,1,0:T(8,128)(2,1)} %get-tuple-element.56) | copy-start | bytes 9437188
  783.0 10.8 %copy-start.14 = (f32[4,8,128]{2,1,0:T(8,128)S(1)}, f32[4,8,128]{2,1,0:T(8,128)}, u32[]{:S(2)}) copy-start(f32[4,8,128]{2,1,0:T(8,128)} %get-tuple-element.58) | copy-start | bytes 49156
  791.9 2.1 copy-start.5
  797.3 77.7 %copy-start.11 = (f32[2048]{0:T(1024)S(1)}, f32[2048]{0:T(1024)}, u32[]{:S(2)}) copy-start(f32[2048]{0:T(1024)} %param.28) | copy-start | bytes 24580
  797.3 77.7 %copy-start.16 = (f32[160]{0:T(256)S(1)}, f32[160]{0:T(256)}, u32[]{:S(2)}) copy-start(f32[160]{0:T(256)} %copy-done.15) | copy-start | bytes 1924
  994.9 2.5 copy-start.4
  999.5 41.5 %copy-start.8 = (f32[128,2048]{1,0:T(8,128)S(1)}, f32[128,2048]{1,0:T(8,128)}, u32[]{:S(2)}) copy-start(f32[128,2048]{1,0:T(8,128)} %get-tuple-element.124) | copy-start | bytes 3145732
  (10 other events, 12.6 us)
Sparse Core Ops, SparseCore 0:
  759.7 126.0 all-reduce.4

commit v3 on v2

--- a/solution.py
+++ b/solution.py
@@ -63,7 +63,65 @@
 PEER_MASKS = (3, 1, 2)
 
 
-def qkv_kernel(tok, normed, wq, wk, wv, lin, cols, send, recv, asend, arecv, ssem, rsem):
+def relay_sum(r, e, products, own, mine, send, half_in, full_in, hs, hr, fs, fr, step):
+    near, far, diag = r ^ 1, r ^ 2, r ^ 3
+    rows = mine.shape[0]
+    half = rows // 2
+    low, high = pl.ds(0, half), pl.ds(half, half)
+    products(diag, send.at[2])
+    relays = [
+        remote(send.at[2, low], half_in.at[0], hs.at[0], hr.at[0], (near, e)),
+        remote(send.at[2, high], half_in.at[1], hs.at[1], hr.at[1], (far, e)),
+    ]
+    for copy in relays:
+        copy.start()
+    parts = ((0, low, near), (1, high, far), (0, high, near), (1, low, far))
+    fulls = [
+        remote(send.at[i, part], full_in.at[i, part], fs.at[n], fr.at[n], (p, e))
+        for n, (i, part, p) in enumerate(parts)
+    ]
+    products(near, send.at[0])
+    fulls[0].start()
+    products(far, send.at[1])
+    fulls[1].start()
+    for i, start, slot, n in ((1, 0, 0, 3), (0, half, 1, 2)):
+        relays[slot].wait_recv()
+
+        def add(c, carry):
+            t = pl.ds(pl.multiple_of(start + c * step, step), step)
+            value = send[i, t, :].astype(F32) + half_in[slot, aligned(c, step), :].astype(F32)
+            send[i, t, :] = value.astype(BF16)
+            return carry
+
+        lax.fori_loop(0, half // step, add, 0)
+        fulls[n].start()
+    own()
+    for copy in fulls:
+        copy.wait_recv()
+
+    def total(c, carry):
+        t = aligned(c, step)
+        mine[t, :] = mine[t, :] + (full_in[0, t, :].astype(F32) + full_in[1, t, :].astype(F32))
+        return carry
+
+    lax.fori_loop(0, rows // step, total, 0)
+    for copy in relays + fulls:
+        copy.wait_send()
+
+
+def relay_scratch(rows, width):
+    return [
+        pltpu.VMEM((3, rows, width), BF16),
+        pltpu.VMEM((2, rows // 2, width), BF16),
+        pltpu.VMEM((2, rows, width), BF16),
+        pltpu.SemaphoreType.DMA((2,)),
+        pltpu.SemaphoreType.DMA((2,)),
+        pltpu.SemaphoreType.DMA((4,)),
+        pltpu.SemaphoreType.DMA((4,)),
+    ]
+
+
+def qkv_kernel(tok, normed, wq, wk, wv, lin, cols, asend, arecv, *relay):
     r, e = lax.axis_index("dp"), lax.axis_index("expert")
     peers = [r ^ m for m in PEER_MASKS]
     width = wq.shape[0]
@@ -94,24 +152,7 @@
 
         lax.fori_loop(0, rows // tok, chunk, 0)
 
-    second = []
-    for i, p in enumerate(peers):
-        products(p, send.at[i])
-        copy = remote(send.at[i], recv.at[i], ssem.at[i], rsem.at[i], (p, e))
-        copy.start()
-        second.append(copy)
-    products(r, lin)
-    for i in (1, 2, 0):
-        second[i].wait()
-
-    def total(c, carry):
-        t = aligned(c, 32)
-        lin[t, :] = lin[t, :] + (
-            recv[0, t, :].astype(F32) + recv[1, t, :].astype(F32) + recv[2, t, :].astype(F32)
-        )
-        return carry
-
-    lax.fori_loop(0, rows // 32, total, 0)
+    relay_sum(r, e, products, lambda: products(r, lin), lin, *relay, 32)
 
 
 def project_qkv(normed, wq, wk, wv):
@@ -126,23 +167,17 @@
         ),
         in_specs=[VMEM_SPEC] * 4,
         out_specs=(VMEM_SPEC, VMEM_SPEC),
-        scratch_shapes=[
-            pltpu.VMEM((3, rows, group), BF16),
-            pltpu.VMEM((3, rows, group), BF16),
-        ]
-        + [pltpu.SemaphoreType.DMA((3,))] * 4,
+        scratch_shapes=[pltpu.SemaphoreType.DMA((3,))] * 2 + relay_scratch(rows, group),
         compiler_params=params(1),
         name="qkv_exchange",
     )(normed, wq, wk, wv)
 
 
-def out_kernel(attn, wo, total, send, recv, ssem, rsem):
+def out_kernel(attn, wo, total, *relay):
     r, e = lax.axis_index("dp"), lax.axis_index("expert")
-    peers = [r ^ m for m in PEER_MASKS]
-    tok = total.shape[0]
-    width = total.shape[1]
+    tok, width = total.shape
     step = width // 4
-    greet([(p, e) for p in peers])
+    greet([(r ^ m, e) for m in PEER_MASKS])
 
     def products(p, dst):
         def chunk(c, carry):
@@ -152,24 +187,7 @@
 
         lax.fori_loop(0, width // step, chunk, 0)
 
-    copies = []
-    for i, p in enumerate(peers):
-        products(p, send.at[i])
-        copy = remote(send.at[i], recv.at[i], ssem.at[i], rsem.at[i], (p, e))
-        copy.start()
-        copies.append(copy)
-    products(r, total)
-    for i in (1, 2, 0):
-        copies[i].wait()
-
-    def add(c, carry):
-        t = aligned(c, 32)
-        total[t, :] = total[t, :] + (
-            recv[0, t, :].astype(F32) + recv[1, t, :].astype(F32) + recv[2, t, :].astype(F32)
-        )
-        return carry
-
-    lax.fori_loop(0, tok // 32, add, 0)
+    relay_sum(r, e, products, lambda: products(r, total), total, *relay, 16)
 
 
 def project_out(attn, wo):
@@ -179,17 +197,16 @@
         out_shape=jax.ShapeDtypeStruct((tok, wo.shape[1]), F32),
         in_specs=[VMEM_SPEC] * 2,
         out_specs=VMEM_SPEC,
-        scratch_shapes=[
-            pltpu.VMEM((3, tok, wo.shape[1]), BF16),
-            pltpu.VMEM((3, tok, wo.shape[1]), BF16),
-        ]
-        + [pltpu.SemaphoreType.DMA((3,))] * 2,
+        scratch_shapes=relay_scratch(tok, wo.shape[1]),
         compiler_params=params(2),
         name="out_exchange",
     )(attn, wo)
 
 
-def dgrad_kernel(mine, wq, wk, wv, cols_t, normal, grads, blocks, dsum, dsend, drecv, ssem, rsem, bsend, brecv):
+def dgrad_kernel(
+    mine, wq, wk, wv, cols_t, out_part, normal, grads, out_grad,
+    blocks, dsum, dsend, drecv, ssem, rsem, bsend, brecv, *scratch,
+):
     r, e = lax.axis_index("dp"), lax.axis_index("expert")
     rows = mine.shape[0]
     tok = rows // 4
@@ -199,7 +216,10 @@
     width = wq.shape[0]
     peers = [r ^ m for m in PEER_MASKS]
     near, far, diag = r ^ 1, r ^ 2, r ^ 3
-    greet([(p, e) for p in peers])
+    pair_in, send, recv, *sems = scratch
+    begin, middle, finish = owner_sum([out_part], [out_grad], [pair_in], [send], [recv], *sems)
+    greet([(p, e) for p in peers] + [(r, e ^ 1)] + owner_peers())
+    begin()
     low, high = pl.ds(0, half), pl.ds(half, half)
     first_near = remote(mine.at[low], blocks.at[0, low], ssem.at[0], rsem.at[0], (near, e))
     first_far = remote(mine.at[high], blocks.at[1, high], ssem.at[1], rsem.at[1], (far, e))
@@ -234,6 +254,7 @@
 
         lax.fori_loop(0, (qg + 2 * kg) // 128, outer, 0)
 
+    middle()
     products(r, mine, True)
     first_near.wait()
     pass_far.start()
@@ -256,9 +277,10 @@
     for i, p in enumerate(peers):
         back[i].wait()
         normal[:, aligned(p, width)] = drecv[i].astype(F32)
-
-
-def grad_qkv(mine, wq, wk, wv, cols_t):
+    finish()
+
+
+def grad_qkv(mine, wq, wk, wv, cols_t, out_part):
     rows, group = mine.shape
     tok = rows // 4
     width = wq.shape[0]
@@ -267,9 +289,10 @@
         out_shape=(
             jax.ShapeDtypeStruct((tok, 4 * width), F32),
             jax.ShapeDtypeStruct((4 * width, group), BF16),
+            jax.ShapeDtypeStruct(out_part.shape[1:], F32),
         ),
-        in_specs=[VMEM_SPEC] * 5,
-        out_specs=(VMEM_SPEC, VMEM_SPEC),
+        in_specs=[VMEM_SPEC] * 6,
+        out_specs=(VMEM_SPEC,) * 3,
         scratch_shapes=[
             pltpu.VMEM((3, rows, group), BF16),
             pltpu.VMEM((rows, width), F32),
@@ -279,10 +302,11 @@
             pltpu.SemaphoreType.DMA((6,)),
             pltpu.SemaphoreType.DMA((3,)),
             pltpu.SemaphoreType.DMA((3,)),
-        ],
+        ]
+        + owner_scratch([out_part]),
         compiler_params=params(4),
         name="dqkv_exchange",
-    )(mine, wq, wk, wv, cols_t)
+    )(mine, wq, wk, wv, cols_t, out_part)
 
 
 def branch_kernel(mine, wo, attn_t, d_attn, grads, full, ssem, rsem):
@@ -358,71 +382,154 @@
     )(mine, wo, attn_t)
 
 
-def owner_sum_kernel(n_owner, n_arrays, *refs):
-    arrays = refs[:n_arrays]
-    outs = refs[n_arrays : 2 * n_arrays]
-    scratch = refs[2 * n_arrays :]
-    pair_in = scratch[:n_arrays]
-    send = scratch[n_arrays : 2 * n_arrays]
-    recv = scratch[2 * n_arrays : 3 * n_arrays]
-    psend, precv, zsend, zrecv = scratch[3 * n_arrays :]
+def owner_order(n_z):
+    order = list(range(1, n_z)) + [0]
+    return order[1:2] + order[:1] + order[2:] if n_z > 2 else order
+
+
+def owner_sum(arrays, outs, pair_in, send, recv, psend, precv, zsend, zrecv):
     r, e = lax.axis_index("dp"), lax.axis_index("expert")
-    n_z = n_owner // 2
+    n_z = arrays[0].shape[0] // 2
     z, core = e // 2, e % 2
     targets = [lax.rem(z + j, n_z) for j in range(n_z)]
-    order = list(range(1, n_z)) + [0]
-    order = order[1:2] + order[:1] + order[2:] if n_z > 2 else order
-    greet([(r, e ^ 1)] + [(r, targets[j] * 2 + core) for j in range(1, n_z)])
-    pair = {}
-    for j in order:
-        for a in range(n_arrays):
-            copy = remote(
-                arrays[a].at[targets[j] * 2 + (1 - core)], pair_in[a].at[j],
-                psend.at[a, j], precv.at[a, j], (r, e ^ 1),
-            )
-            copy.start()
-            pair[a, j] = copy
-    moves = []
-    for j in order:
-        for a in range(n_arrays):
-            pair[a, j].wait()
-            own = arrays[a][targets[j] * 2 + core].astype(F32) + pair_in[a][j].astype(F32)
-            if j == 0:
-                outs[a][...] = own
-            else:
-                send[a][j - 1] = own.astype(BF16)
+    order = owner_order(n_z)
+    n_arrays = len(arrays)
+    pair, moves = {}, []
+
+    def begin():
+        for j in order:
+            for a in range(n_arrays):
                 copy = remote(
-                    send[a].at[j - 1], recv[a].at[j - 1],
-                    zsend.at[a, j - 1], zrecv.at[a, j - 1], (r, targets[j] * 2 + core),
+                    arrays[a].at[targets[j] * 2 + (1 - core)], pair_in[a].at[j],
+                    psend.at[a, j], precv.at[a, j], (r, e ^ 1),
                 )
                 copy.start()
-                moves.append(copy)
-    for copy in moves:
-        copy.wait()
-    for a in range(n_arrays):
-        value = outs[a][...]
-        for j in range(n_z - 1):
-            value = value + recv[a][j].astype(F32)
-        outs[a][...] = value
-
-
-def owner_sums(arrays, n_owner, collective_id):
+                pair[a, j] = copy
+
+    def middle():
+        for j in order:
+            for a in range(n_arrays):
+                pair[a, j].wait()
+                own = arrays[a][targets[j] * 2 + core].astype(F32) + pair_in[a][j].astype(F32)
+                if j == 0:
+                    outs[a][...] = own
+                else:
+                    send[a][j - 1] = own.astype(BF16)
+                    copy = remote(
+                        send[a].at[j - 1], recv[a].at[j - 1],
+                        zsend.at[a, j - 1], zrecv.at[a, j - 1], (r, targets[j] * 2 + core),
+                    )
+                    copy.start()
+                    moves.append(copy)
+
+    def finish():
+        for copy in moves:
+            copy.wait()
+        for a in range(n_arrays):
+            value = outs[a][...]
+            for j in range(n_z - 1):
+                value = value + recv[a][j].astype(F32)
+            outs[a][...] = value
+
+    return begin, middle, finish
+
+
+def owner_scratch(arrays):
+    n_z = arrays[0].shape[0] // 2
     n = len(arrays)
-    n_z = n_owner // 2
     shapes = [a.shape[1:] for a in arrays]
-    return pl.pallas_call(
-        functools.partial(owner_sum_kernel, n_owner, n),
-        out_shape=tuple(jax.ShapeDtypeStruct(s, F32) for s in shapes),
-        in_specs=[VMEM_SPEC] * n,
-        out_specs=(VMEM_SPEC,) * n,
-        scratch_shapes=[pltpu.VMEM((n_z, *s), BF16) for s in shapes]
+    return (
+        [pltpu.VMEM((n_z, *s), BF16) for s in shapes]
         + [pltpu.VMEM((n_z - 1, *s), BF16) for s in shapes]
         + [pltpu.VMEM((n_z - 1, *s), BF16) for s in shapes]
         + [pltpu.SemaphoreType.DMA((n, n_z))] * 2
-        + [pltpu.SemaphoreType.DMA((n, n_z - 1))] * 2,
-        compiler_params=params(collective_id),
-        name="owner_sums",
-    )(*arrays)
+        + [pltpu.SemaphoreType.DMA((n, n_z - 1))] * 2
+    )
+
+
+def owner_peers():
+    r, e = lax.axis_index("dp"), lax.axis_index("expert")
+    n_z = lax.axis_size("expert") // 2
+    return [(r, lax.rem(e // 2 + j, n_z) * 2 + e % 2) for j in range(1, n_z)]
+
+
+def last_sums_kernel(grads, small, grads_out, small_out, *scratch):
+    r, e = lax.axis_index("dp"), lax.axis_index("expert")
+    z, core = e // 2, e % 2
+    n_z = grads.shape[0] // 2
+    pair_in, send, recv, psend, precv, zsend, zrecv = scratch[:7]
+    first_in, piece, line_in, s1, r1, s2, r2, s3, r3 = scratch[7:]
+    begin, middle, finish = owner_sum(
+        [grads], [grads_out], [pair_in], [send], [recv], psend, precv, zsend, zrecv
+    )
+    others = [(m // 2, m % 2) for m in range(1, 8)]
+    plane = [(r ^ a, e ^ c) for a, c in others]
+    greet(plane + owner_peers())
+    begin()
+    firsts = []
+    for i, (a, c) in enumerate(others):
+        copy = remote(
+            small.at[(r ^ a) * 2 + (core ^ c)], first_in.at[i], s1.at[i], r1.at[i], plane[i]
+        )
+        copy.start()
+        firsts.append(copy)
+    middle()
+    for copy in firsts:
+        copy.wait()
+    mine = r * 2 + core
+    value = small[mine]
+    for i in range(7):
+        value = value + first_in[i]
+    piece[0] = value
+    seconds = []
+    for j in range(1, n_z):
+        copy = remote(
+            piece.at[0], line_in.at[j - 1], s2.at[j - 1], r2.at[j - 1], owner_peers()[j - 1]
+        )
+        copy.start()
+        seconds.append(copy)
+    for copy in seconds:
+        copy.wait()
+    value = piece[0]
+    for j in range(n_z - 1):
+        value = value + line_in[j]
+    small_out[mine] = value
+    thirds = []
+    for i, (a, c) in enumerate(others):
+        copy = remote(small_out.at[mine], small_out.at[mine], s3.at[i], r3.at[i], plane[i])
+        copy.start()
+        thirds.append(copy)
+    finish()
+    for copy in thirds:
+        copy.wait()
+
+
+def last_sums(grads, small):
+    n_z = grads.shape[0] // 2
+    piece = small.shape[1:]
+    return pl.pallas_call(
+        last_sums_kernel,
+        out_shape=(
+            jax.ShapeDtypeStruct(grads.shape[1:], F32),
+            jax.ShapeDtypeStruct(small.shape, F32),
+        ),
+        in_specs=[VMEM_SPEC] * 2,
+        out_specs=(VMEM_SPEC,) * 2,
+        scratch_shapes=owner_scratch([grads])
+        + [
+            pltpu.VMEM((7, *piece), F32),
+            pltpu.VMEM((1, *piece), F32),
+            pltpu.VMEM((n_z - 1, *piece), F32),
+            pltpu.SemaphoreType.DMA((7,)),
+            pltpu.SemaphoreType.DMA((7,)),
+            pltpu.SemaphoreType.DMA((n_z - 1,)),
+            pltpu.SemaphoreType.DMA((n_z - 1,)),
+            pltpu.SemaphoreType.DMA((7,)),
+            pltpu.SemaphoreType.DMA((7,)),
+        ],
+        compiler_params=params(5),
+        name="last_sums",
+    )(grads, small)
 
 
 def masks_of(block, own_length, slots, prompt_block, prompt_len, column, keys):
@@ -723,34 +830,64 @@
 
 def selector(pos, source, room):
     row = pos[source]
-    ids = lax.broadcasted_iota(jnp.int32, (room, row.shape[1]), 0)
+    ids = lax.broadcasted_iota(jnp.int32, (room, row.shape[1]), 0).astype(F32)
     return jnp.where(ids == row, 1.0, 0.0).astype(BF16)
 
 
+def start_all(copies):
+    for copy in copies:
+        copy.start()
+    return copies
+
+
+def wait_all(copies):
+    for copy in copies:
+        copy.wait()
+    copies.clear()
+
+
 def experts_fwd_kernel(
-    mine, pos, wg, wu, wd, x_out, y_out, gate_out,
-    buf, wg_v, wu_v, wd_v, x_v, y_v, hid_v, gate_v, local, zs, zr, ps, pr, ds, dr,
+    mine, wg, wu, wd, pos, x_out, y_out, g_out, u_out, o_out, hid_out, gate_out,
+    buf, wg_v, wu_v, wd_v, x_v, y_v, g_v, u_v, o_v, hid_v, gate_v, local, zs, zr, ps, pr, ds, dr,
 ):
     model = wg.shape[0]
+    rows_in = mine.shape[0]
     room = x_v.shape[0] // 8
     me = lax.axis_index("dp") * 8 + lax.axis_index("expert")
-    loads = [
-        pltpu.make_async_copy(a, b, local.at[i])
-        for i, (a, b) in enumerate(((wg, wg_v), (wu, wu_v), (wd, wd_v)))
-    ]
-    for copy in loads:
-        copy.start()
+    loads = start_all(
+        [
+            pltpu.make_async_copy(a, b, local.at[i])
+            for i, (a, b) in enumerate(((wg, wg_v), (wu, wu_v), (wd, wd_v)))
+        ]
+    )
+    leaving = []
+
+    def leave(b, pairs):
+        leaving.extend(
+            start_all([pltpu.make_async_copy(v, o.at[b], local.at[i]) for i, v, o in pairs])
+        )
 
     def before(k, b):
-        if k == 0:
-            for copy in loads:
-                copy.wait()
+        wait_all(loads)
 
     def group(k, b):
+        wait_all(leaving)
+        upto = jnp.where(
+            lax.broadcasted_iota(jnp.int32, (rows_in, rows_in), 0)
+            <= lax.broadcasted_iota(jnp.int32, (rows_in, rows_in), 1),
+            1.0,
+            0.0,
+        ).astype(BF16)
+        is_me = jnp.where(lax.broadcasted_iota(jnp.int32, (16, 128), 1) == me, 1.0, 0.0).astype(BF16)
+
         def pick(j, carry):
             s = j // 2 * 8 + b * 2 + j % 2
             rows = aligned(j, room)
-            sel = selector(pos, s, room)
+            named = jnp.where(dot_nt(is_me, buf[s, :, model:]) > 0.0, 1.0, 0.0)
+            place = dot_nn(named.astype(BF16), upto) * named - 1.0
+            pos[s] = place[:1]
+            ids = lax.broadcasted_iota(jnp.int32, (room, rows_in), 0).astype(F32)
+            sel = jnp.where(ids == place[:1], 1.0, 0.0).astype(BF16)
             for c in range(4):
                 n = slice(c * model // 4, (c + 1) * model // 4)
                 x_v[rows, n] = dot_nn(sel, buf[s, :, n]).astype(BF16)
@@ -762,48 +899,55 @@
             return carry
 
         lax.fori_loop(0, 8, pick, 0)
+        leave(b, ((0, x_v, x_out), (1, gate_v, gate_out)))
 
         def first(c, carry):
             n = aligned(c, 256)
             g = dot_nn(x_v[...], wg_v[:, n])
             u = dot_nn(x_v[...], wu_v[:, n])
+            g_v[:, n] = g.astype(BF16)
+            u_v[:, n] = u.astype(BF16)
             hid_v[:, n] = (g / (1.0 + jnp.exp(-g)) * u).astype(BF16)
             return carry
 
         lax.fori_loop(0, wg.shape[1] // 256, first, 0)
+        leave(b, ((2, g_v, g_out), (3, u_v, u_out), (4, hid_v, hid_out)))
 
         def second(c, carry):
             n = aligned(c, 256)
-            o = dot_nn(hid_v[...], wd_v[:, n]).astype(BF16).astype(F32)
-            y_v[:, n] = (o * gate_v[:, :1]).astype(BF16)
+            o = dot_nn(hid_v[...], wd_v[:, n]).astype(BF16)
+            o_v[:, n] = o
+            y_v[:, n] = (o.astype(F32) * gate_v[:, :1]).astype(BF16)
             return carry
 
         lax.fori_loop(0, model // 256, second, 0)
-        outs = [
-            pltpu.make_async_copy(a, o.at[b], local.at[i])
-            for i, (a, o) in enumerate(((x_v, x_out), (y_v, y_out), (gate_v, gate_out)))
-        ]
-        for copy in outs:
-            copy.start()
-        for copy in outs:
-            copy.wait()
+        leave(b, ((5, o_v, o_out), (6, y_v, y_out)))
+        if k == 3:
+            wait_all(leaving)
 
     gather_world(mine, buf, zs, zr, ps, pr, ds, dr, before, group)
 
 
-def experts_fwd(mine, pos, wg, wu, wd, room):
+def experts_fwd(mine, wg, wu, wd, room):
     rows, width = mine.shape
     model, ff = wg.shape
     group = 8 * room
-    return pl.pallas_call(
+    wide = jax.ShapeDtypeStruct((4, group, model), BF16)
+    thin = jax.ShapeDtypeStruct((4, group, ff), BF16)
+    pos, x, y, g, u, o, hidden, gates = pl.pallas_call(
         experts_fwd_kernel,
         out_shape=(
-            jax.ShapeDtypeStruct((4, group, model), BF16),
-            jax.ShapeDtypeStruct((4, group, model), BF16),
+            jax.ShapeDtypeStruct((32, 1, rows), F32),
+            wide,
+            wide,
+            thin,
+            thin,
+            wide,
+            thin,
             jax.ShapeDtypeStruct((4, group, 128), F32),
         ),
-        in_specs=[VMEM_SPEC, VMEM_SPEC, ANY_SPEC, ANY_SPEC, ANY_SPEC],
-        out_specs=(ANY_SPEC,) * 3,
+        in_specs=[VMEM_SPEC, ANY_SPEC, ANY_SPEC, ANY_SPEC],
+        out_specs=(VMEM_SPEC,) + (ANY_SPEC,) * 7,
         scratch_shapes=[
             pltpu.VMEM((32, rows, width), BF16),
             pltpu.VMEM((model, ff), BF16),
@@ -812,73 +956,78 @@
             pltpu.VMEM((group, model), BF16),
             pltpu.VMEM((group, model), BF16),
             pltpu.VMEM((group, ff), BF16),
+            pltpu.VMEM((group, ff), BF16),
+            pltpu.VMEM((group, model), BF16),
+            pltpu.VMEM((group, ff), BF16),
             pltpu.VMEM((group, 128), F32),
-            pltpu.SemaphoreType.DMA((3,)),
+            pltpu.SemaphoreType.DMA((7,)),
         ]
         + GATHER_SEMS,
         compiler_params=params(6),
         name="experts_fwd",
-    )(mine, pos, wg, wu, wd)
+    )(mine, wg, wu, wd)
+    return pos, x, y, (g, u, o, hidden, gates)
 
 
 def experts_bwd_kernel(
-    mine, pos, x_in, gate_in, wg, wu, wd, y_out, d_copy_out, hid_out, dg_out, du_out,
-    buf, wg_v, wu_v, wd_v, x_v, gate_v, g_v, u_v, o_v, y_v, d_copy_v, hid_v, dg_v, du_v,
-    local, zs, zr, ps, pr, ds, dr,
+    mine, pos, g_in, u_in, o_in, gate_in, wg, wu, wd, y_out, d_copy_out, dg_out, du_out,
+    buf, wg_v, wu_v, wd_v, g_v, u_v, o_v, gate_v, y_v, d_copy_v, dg_v, du_v,
+    local, ins, zs, zr, ps, pr, ds, dr,
 ):
     model, ff = wg.shape
-    room = x_v.shape[0] // 8
+    room = d_copy_v.shape[0] // 8
+    z = lax.axis_index("expert") // 2
     me = lax.axis_index("dp") * 8 + lax.axis_index("expert")
-    loads = [
-        pltpu.make_async_copy(a, b, local.at[i])
-        for i, (a, b) in enumerate(((wg, wg_v), (wu, wu_v), (wd, wd_v)))
-    ]
-    for copy in loads:
-        copy.start()
+    loads = start_all(
+        [
+            pltpu.make_async_copy(a, b, local.at[i])
+            for i, (a, b) in enumerate(((wg, wg_v), (wu, wu_v), (wd, wd_v)))
+        ]
+    )
+    leaving, coming = [], {}
+
+    def fetch(k):
+        b = plane_order(z)[k]
+        at = k % 2
+        coming[k] = start_all(
+            [
+                pltpu.make_async_copy(a.at[b], v.at[at], ins.at[at, i])
+                for i, (a, v) in enumerate(
+                    ((g_in, g_v), (u_in, u_v), (o_in, o_v), (gate_in, gate_v))
+                )
+            ]
+        )
+
+    fetch(0)
+
+    def leave(b, pairs):
+        leaving.extend(
+            start_all([pltpu.make_async_copy(v, o.at[b], local.at[i]) for i, v, o in pairs])
+        )
 
     def before(k, b):
-        if k == 0:
-            for copy in loads:
-                copy.wait()
-        ins = [
-            pltpu.make_async_copy(x_in.at[b], x_v, local.at[3]),
-            pltpu.make_async_copy(gate_in.at[b], gate_v, local.at[4]),
-        ]
-        for copy in ins:
-            copy.start()
-        for copy in ins:
-            copy.wait()
-
-        def first(c, carry):
-            n = aligned(c, 256)
-            g = dot_nn(x_v[...], wg_v[:, n])
-            u = dot_nn(x_v[...], wu_v[:, n])
-            g_v[:, n] = g
-            u_v[:, n] = u
-            hid_v[:, n] = (g / (1.0 + jnp.exp(-g)) * u).astype(BF16)
-            return carry
-
-        lax.fori_loop(0, ff // 256, first, 0)
-
-        def second(c, carry):
-            n = aligned(c, 256)
-            o_v[:, n] = dot_nn(hid_v[...], wd_v[:, n]).astype(BF16)
-            return carry
-
-        lax.fori_loop(0, model // 256, second, 0)
+        wait_all(loads)
+        wait_all(coming[k])
+        if k < 3:
+            fetch(k + 1)
 
     def group(k, b):
+        at = k % 2
+        wait_all(leaving)
+
         def pick(j, carry):
             s = j // 2 * 8 + b * 2 + j % 2
             rows = aligned(j, room)
             sel = selector(pos, s, room)
-            gate = gate_v[rows, :1]
+            gate = gate_v[at, rows, :1]
             inner = jnp.zeros((room, 1), F32)
             for c in range(4):
                 n = slice(c * model // 4, (c + 1) * model // 4)
                 picked = dot_nn(sel, buf[s, :, n])
                 d_copy_v[rows, n] = (gate * picked).astype(BF16)
-                inner = inner + jnp.sum(picked * o_v[rows, n].astype(F32), axis=-1, keepdims=True)
+                inner = inner + jnp.sum(
+                    picked * o_v[at, rows, n].astype(F32), axis=-1, keepdims=True
+                )
             top = inner.astype(BF16).astype(F32)
             rest = inner - top
             lane = lax.broadcasted_iota(jnp.int32, (room, 128), 1)
@@ -887,17 +1036,19 @@
             return carry
 
         lax.fori_loop(0, 8, pick, 0)
+        leave(b, ((0, d_copy_v, d_copy_out),))
 
         def third(c, carry):
             n = aligned(c, 256)
             d_hidden = dot_nt(d_copy_v[...], wd_v[n, :])
-            g, u = g_v[:, n], u_v[:, n]
+            g, u = g_v[at, :, n].astype(F32), u_v[at, :, n].astype(F32)
             s = 1.0 / (1.0 + jnp.exp(-g))
             dg_v[:, n] = (d_hidden * u * s * (1.0 + g * (1.0 - s))).astype(BF16)
             du_v[:, n] = (d_hidden * g * s).astype(BF16)
             return carry
 
         lax.fori_loop(0, ff // 256, third, 0)
+        leave(b, ((1, dg_v, dg_out), (2, du_v, du_out)))
 
         def fourth(c, carry):
             n = aligned(c, 256)
@@ -905,27 +1056,14 @@
             return carry
 
         lax.fori_loop(0, model // 256, fourth, 0)
-        outs = [
-            pltpu.make_async_copy(a, o.at[b], local.at[i])
-            for i, (a, o) in enumerate(
-                (
-                    (y_v, y_out),
-                    (d_copy_v, d_copy_out),
-                    (hid_v, hid_out),
-                    (dg_v, dg_out),
-                    (du_v, du_out),
-                )
-            )
-        ]
-        for copy in outs:
-            copy.start()
-        for copy in outs:
-            copy.wait()
+        leave(b, ((3, y_v, y_out),))
+        if k == 3:
+            wait_all(leaving)
 
     gather_world(mine, buf, zs, zr, ps, pr, ds, dr, before, group)
 
 
-def experts_bwd(mine, pos, x_in, gate_in, wg, wu, wd, room):
+def experts_bwd(mine, pos, kept, wg, wu, wd, room):
     rows, width = mine.shape
     model, ff = wg.shape
     group = 8 * room
@@ -936,31 +1074,29 @@
             jax.ShapeDtypeStruct((4, group, model), BF16),
             jax.ShapeDtypeStruct((4, group, ff), BF16),
             jax.ShapeDtypeStruct((4, group, ff), BF16),
-            jax.ShapeDtypeStruct((4, group, ff), BF16),
         ),
-        in_specs=[VMEM_SPEC, VMEM_SPEC] + [ANY_SPEC] * 5,
-        out_specs=(ANY_SPEC,) * 5,
+        in_specs=[VMEM_SPEC, VMEM_SPEC] + [ANY_SPEC] * 7,
+        out_specs=(ANY_SPEC,) * 4,
         scratch_shapes=[
             pltpu.VMEM((32, rows, width), BF16),
             pltpu.VMEM((model, ff), BF16),
             pltpu.VMEM((model, ff), BF16),
             pltpu.VMEM((ff, model), BF16),
-            pltpu.VMEM((group, model), BF16),
-            pltpu.VMEM((group, 128), F32),
-            pltpu.VMEM((group, ff), F32),
-            pltpu.VMEM((group, ff), F32),
-            pltpu.VMEM((group, model), BF16),
+            pltpu.VMEM((2, group, ff), BF16),
+            pltpu.VMEM((2, group, ff), BF16),
+            pltpu.VMEM((2, group, model), BF16),
+            pltpu.VMEM((2, group, 128), F32),
             pltpu.VMEM((group, model + 128), BF16),
             pltpu.VMEM((group, model), BF16),
             pltpu.VMEM((group, ff), BF16),
             pltpu.VMEM((group, ff), BF16),
-            pltpu.VMEM((group, ff), BF16),
-            pltpu.SemaphoreType.DMA((5,)),
+            pltpu.SemaphoreType.DMA((4,)),
+            pltpu.SemaphoreType.DMA((2, 4)),
         ]
         + GATHER_SEMS,
         compiler_params=params(7),
         name="experts_bwd",
-    )(mine, pos, x_in, gate_in, wg, wu, wd)
+    )(mine, pos, *kept, wg, wu, wd)
 
 
 def sum_world_kernel(
@@ -1259,38 +1395,31 @@
 
 
 def experts_by_gather(
-    mixed, state, teacher, routes, cont_lengths, valid_slot, valid_count, router_weight,
-    gate_weight, up_weight, down_weight, devices, capacity, slots_all, flat_rank,
+    mixed, state, teacher, routes, valid_slot, valid_count, router_weight,
+    gate_weight, up_weight, down_weight, devices, capacity, slots_all,
 ):
     tok_dev, model_width = mixed.shape
     room = -(-capacity // 16) * 16
     expert_range = jnp.arange(devices, dtype=jnp.int32)
-    slot_ids = jnp.arange(tok_dev, dtype=jnp.int32)
-    prompt_block = tok_dev - CMAX
-    routes_all = lax.all_gather(routes, ("dp", "expert"), axis=0, tiled=False)
-    valid_all = (slot_ids[None] < prompt_block) | (slot_ids[None] - prompt_block < cont_lengths[:, None])
-    named = jnp.any(routes_all == flat_rank, axis=-1) & valid_all
-    upto = (slot_ids[:, None] <= slot_ids[None]).astype(F32)
-    place = jnp.dot(named.astype(F32), upto, preferred_element_type=F32).astype(jnp.int32) - 1
-    pos = jnp.where(named, place, -1)[:, None, :]
-
     logits = jnp.dot(mixed, router_weight, preferred_element_type=F32)
     chosen = jnp.any(routes[:, :, None] == expert_range[None, None], axis=1)
     gates = jax.nn.softmax(jnp.where(chosen, logits, -jnp.inf), axis=-1)
-    gates_high = gates.astype(BF16)
-    gates_low = (gates - gates_high.astype(F32)).astype(BF16)
+    live_gates = jnp.where(valid_slot[:, None], gates, 0.0)
+    gates_high = live_gates.astype(BF16)
+    gates_low = (live_gates - gates_high.astype(F32)).astype(BF16)
     gap = jnp.zeros((tok_dev, 64 - devices), BF16)
     payload = jnp.concatenate([mixed, gates_high, gap, gates_low, gap], axis=1)
-    x_rows, y_rows, slot_gates = experts_fwd(
-        payload, pos, gate_weight[0], up_weight[0], down_weight[0], room
+    pos, x_rows, y_rows, kept = experts_fwd(
+        payload, gate_weight[0], up_weight[0], down_weight[0], room
     )
     layer_out = state + sum_world(y_rows.reshape(4, 8, room, model_width), pos, tok_dev, 8)
     live_tokens = valid_slot.astype(F32)[:, None]
     diff = (layer_out - teacher.astype(F32)) * live_tokens
     local_square = jnp.sum(diff * diff)
     d_out = 2.0 * slots_all * diff / valid_count
-    d_rows, d_copy, hidden, d_gate, d_up = experts_bwd(
-        d_out.astype(BF16), pos, x_rows, slot_gates, gate_weight[0], up_weight[0], down_weight[0], room
+    hidden = kept[3]
+    d_rows, d_copy, d_gate, d_up = experts_bwd(
+        d_out.astype(BF16), pos, kept[:3] + kept[4:], gate_weight[0], up_weight[0], down_weight[0], room
     )
     back = sum_world(d_rows.reshape(4, 8, room, model_width + 128), pos, tok_dev, 9)
 
@@ -1403,7 +1532,7 @@
     weights = (router_weight, gate_weight, up_weight, down_weight)
     if n_dp == 4 and n_owner == 8:
         moe = experts_by_gather(
-            mixed, state, teacher, routes, cont_lengths, valid_slot, valid_count, *weights, *sizes, flat_rank
+            mixed, state, teacher, routes, valid_slot, valid_count, *weights, *sizes
         )
     else:
         moe = experts_by_all_to_all(
@@ -1438,8 +1567,9 @@
         ],
         axis=1,
     )
-    d_normed, qkv_part = grad_qkv(
-        d_lin, query_weight, key_projection, value_projection, normed_cols.T
+    d_normed, qkv_part, output_grad = grad_qkv(
+        d_lin, query_weight, key_projection, value_projection, normed_cols.T,
+        out_part.reshape(n_owner, -1, model_width),
     )
     d_tokens_norm, d_input_gain = first_norm_back(d_normed)
     tokens_grad = d_state + d_tokens_norm
@@ -1451,9 +1581,21 @@
         .transpose(1, 0, 2, 3)
         .reshape(n_owner, n_dp * rows_here, group)
     )
-    qkv_rows, output_grad = owner_sums(
-        [by_owner, out_part.reshape(n_owner, -1, model_width)], n_owner, 5
-    )
+    small_parts = (
+        router_local, d_input_gain, d_post_gain, d_query_gain, d_key_gain, local_square[None]
+    )
+    small = jnp.concatenate([a.reshape(-1) for a in small_parts])
+    piece_rows = -(-small.shape[0] // (8 * 8 * 128)) * 8
+    small = jnp.pad(small, (0, 8 * piece_rows * 128 - small.shape[0]))
+    qkv_rows, small_sums = last_sums(by_owner, small.reshape(8, piece_rows, 128))
+    small_sums = small_sums.reshape(-1)
+    starts = [0]
+    for a in small_parts:
+        starts.append(starts[-1] + a.size)
+    router_grad, input_gain_grad, post_gain_grad, query_gain_grad, key_gain_grad, total_square = (
+        small_sums[i:j].reshape(a.shape) for a, i, j in zip(small_parts, starts, starts[1:])
+    )
+    loss = total_square[0] / (valid_count * model_width)
     qkv_rows = qkv_rows.reshape(n_dp, rows_here, group)
 
     def columns(start, size):
@@ -1462,13 +1604,6 @@
     query_grad = columns(0, query_group)
     key_grad = columns(query_group, head_dim)
     value_grad = columns(query_group + head_dim, head_dim)
-    total_square, input_gain_grad, post_gain_grad, query_gain_grad, key_gain_grad, router_grad = (
-        lax.psum(
-            (local_square, d_input_gain, d_post_gain, d_query_gain, d_key_gain, router_local),
-            ("dp", "expert"),
-        )
-    )
-    loss = total_square / (valid_count * model_width)
     return (
         layer_out,
         loss,

time: 1060 us -> 882 us (0.83)
  Pallas kernels: 865 us -> 765 us
  blocking collectives: 76.7 us -> 0 us
  between operations: 17.4 us -> 4.18 us
  local copies, waits for them, and re-layouts: 24 us -> 35.7 us
    psum x1 -> x0, blocking collectives: 38.5 us -> none  [body(): lax.psum((local_square, d_input_gain, d_post_gain, d_query_gain, d_key_ga...]
    all_gather x1 -> x0, blocking collectives: 38.2 us -> none  [experts_by_gather(): routes_all = lax.all_gather(routes, ('dp', 'expert'), axis=0, tiled=False)]
    pallas_call x2, Pallas kernels: 228 us -> 192 us  [the longest x1 118 us: experts_fwd(): pl.pallas_call(experts_fwd_kernel, out_shape=(jax.ShapeDtypeStruct((32, 1...]
    pallas_call x2, Pallas kernels: 229 us -> 208 us  [sum_world(): pl.pallas_call(sum_world_kernel, out_shape=jax.ShapeDtypeStruct((rows, wi...]
    pallas_call x1, Pallas kernels: 126 us -> 106 us  [experts_bwd(): pl.pallas_call(experts_bwd_kernel, out_shape=(jax.ShapeDtypeStruct((4, gr...]
    pallas_call x1, Pallas kernels: 89.2 us -> 72.5 us  [project_qkv(): pl.pallas_call(functools.partial(qkv_kernel, tok), out_shape=(jax.ShapeDt...]
  transfers between devices with their start and end apart: 3 -> 2, of which waited for: 0 -> 0; matrix products, arithmetic and copies ran while one was open for 5% -> 4% of each run, Pallas kernels for 18% -> 0%
where the time goes in v3:
time: 882 us; the launch traced here: 871 us
  Pallas kernels  765 us (87%)
  matrix products  37.8 us (4%)
  local copies, waits for them, and re-layouts  35.7 us (4%)
  other arithmetic  28.4 us (3%)
    pallas_call x2, Pallas kernels, sum_world(): pl.pallas_call(sum_world_kernel, out_shape=jax.ShapeDtypeStruct((rows, wi...  208 us
    pallas_call x1, Pallas kernels, experts_fwd(): pl.pallas_call(experts_fwd_kernel, out_shape=(jax.ShapeDtypeStruct((32, 1...  118 us
    pallas_call x1, Pallas kernels, experts_bwd(): pl.pallas_call(experts_bwd_kernel, out_shape=(jax.ShapeDtypeStruct((4, gr...  106 us
    pallas_call x1, Pallas kernels, grad_qkv(): pl.pallas_call(dgrad_kernel, out_shape=(jax.ShapeDtypeStruct((tok, 4 * wi...  78.7 us
    pallas_call x1, Pallas kernels, last_sums(): pl.pallas_call(last_sums_kernel, out_shape=(jax.ShapeDtypeStruct(grads.sh...  73.6 us
    pallas_call x1, Pallas kernels, project_qkv(): pl.pallas_call(functools.partial(qkv_kernel, tok), out_shape=(jax.ShapeDt...  72.5 us
    dot_general x5, matrix products, contract(): lax.dot_general(left_side, right_side, (((left_dim,), (right_dim,)), ((),...  37.4 us
    pallas_call x1, Pallas kernels, grad_branch(): pl.pallas_call(branch_kernel, out_shape=(jax.ShapeDtypeStruct((4 * tok, w...  35.6 us
  transfers between devices with their start and end apart: 2, of which 0 were waited for; matrix products, arithmetic and copies ran while one was open for 4% of the time, Pallas kernels for 0%

profile of v3, /device:TPU:8, one launch (start us, length us, event | category | flops | bytes accessed | tf_op | source)
XLA Modules:
  0.0 870.8 jit_solution(1688926012618391696)
XLA Ops:
  2.0 2.1 fusion.2.normed
  4.2 72.5 %qkv_exchange.1 = (f32[640,1280]{1,0:T(8,128)}, bf16[640,512]{1,0:T(8,128)(2,1)}) custom-call(bf16[160,2048]{1,0:T(8,128)(2,1)} %fusion.2.normed, bf16[512,4096]{1,0:T(8,128)(2,1)} %wq.3, bf16[512,512]{1,0:T(8,128)(2,1)} %wk.3, bf16[512,512]{1,0:T(8,128)(2,1)} %wv.3), custom_call_target="tpu_custom_call" | custom-call | tf_op jit(solution)/shard_map/qkv_exchange/pallas_call | solution.py:162
  87.9 15.6 %attention_fwd.1 = (bf16[640,1024]{1,0:T(8,128)(2,1)}, bf16[640,1024]{1,0:T(8,128)(2,1)}) custom-call(s32[5]{0:T(128)} %pad_add_fusion.lengths, f32[640,1280]{1,0:T(8,128)} %get-tuple-element.42.lin, f32[1,128]{1,0:T(1,128)} %bitcast.112, f32[4,160,128]{2,1,0:T(8,128)} %get-tuple-element.120.cos, f32[4,160,128]{2,1,0:T(8,128)} %get-tuple-element.113.sin, ...), custom_call_target="tpu_custom_call" | custom-call | tf_op jit(solution)/shard_map/attention_fwd/pallas_call | solution.py:582
  103.4 2.4 copy.58
  105.9 29.6 %out_exchange.1 = f32[160,2048]{1,0:T(8,128)} custom-call(bf16[640,1024]{1,0:T(8,128)(2,1)} %get-tuple-element.43.attn, bf16[1024,2048]{1,0:T(8,128)(2,1)} %wo.3), custom_call_target="tpu_custom_call" | custom-call | tf_op jit(solution)/shard_map/out_exchange/pallas_call | solution.py:195
  139.1 118.5 %experts_fwd.1 = (f32[32,1,160]{2,1,0:T(1,128)}, bf16[4,512,2048]{2,1,0:T(8,128)(2,1)}, bf16[4,512,2048]{2,1,0:T(8,128)(2,1)}, bf16[4,512,768]{2,1,0:T(8,128)(2,...) custom-call(bf16[160,2176]{1,0:T(8,128)(2,1)} %concatenate.70.mine, ...), custom_call_target="tpu_custom_call" | custom-call | tf_op jit(solution)/shard_map/experts_fwd/pallas_call | solution.py:937
  257.6 101.2 %sum_world.2 = f32[160,2048]{1,0:T(8,128)} custom-call(bf16[4,8,64,2048]{3,2,1,0:T(8,128)(2,1)} %bitcast.80, f32[32,1,160]{2,1,0:T(1,128)} %get-tuple-element.45.pos), custom_call_target="tpu_custom_call" | custom-call | tf_op jit(solution)/shard_map/sum_world/pallas_call | solution.py:1257
  358.8 2.4 multiply_reduce_fusion
  362.5 106.0 %experts_bwd.1 = (bf16[4,512,2176]{2,1,0:T(8,128)(2,1)}, bf16[4,512,2048]{2,1,0:T(8,128)(2,1)}, bf16[4,512,768]{2,1,0:T(8,128)(2,1)}, bf16[4,512,768]{2,1,0:T(8,128)(2,1)}) custom-call(bf16[160,2048]{1,0:T(8,128)(2,1)} %fusion.13.mine, f32[32,1,160]{2,1,0:T(1,128)} %get-tuple-element.45.pos, bf16[4,512,768]{2,1,0:T(8,128)(2,1)} %get-tuple-element.47.g_in, ...), custom_call_target="tpu_custom_call" | custom-call | tf_op jit(solution)/shard_map/experts_bwd/pallas_call | solution.py:1070
  468.5 107.0 %sum_world.3 = f32[160,2176]{1,0:T(8,128)} custom-call(bf16[4,8,64,2176]{3,2,1,0:T(8,128)(2,1)} %bitcast.79, f32[32,1,160]{2,1,0:T(1,128)} %get-tuple-element.45.pos), custom_call_target="tpu_custom_call" | custom-call | tf_op jit(solution)/shard_map/sum_world/pallas_call | solution.py:1257
  576.7 2.7 multiply_reduce_fusion.1
  579.5 2.5 fusion.29
  583.4 35.6 %branch_exchange.1 = (bf16[640,1024]{1,0:T(8,128)(2,1)}, bf16[1024,2048]{1,0:T(8,128)(2,1)}) custom-call(bf16[160,2048]{1,0:T(8,128)(2,1)} %get-tuple-element.108.mine, bf16[1024,2048]{1,0:T(8,128)(2,1)} %wo.3, bf16[1024,640]{1,0:T(8,128)(2,1)} %bitcast.86), custom_call_target="tpu_custom_call" | custom-call | tf_op jit(solution)/shard_map/branch_exchange/pallas_call | solution.py:367
  619.0 26.4 %attention_bwd.1 = (bf16[640,1024]{1,0:T(8,128)(2,1)}, f32[4,384,128]{2,1,0:T(8,128)}, f32[4,384,128]{2,1,0:T(8,128)}, f32[4,8,128]{2,1,0:T(8,128)}) custom-call(s32[5]{0:T(128)} %pad_add_fusion.lengths, f32[640,1280]{1,0:T(8,128)} %get-tuple-element.42.lin, bf16[640,1024]{1,0:T(8,128)(2,1)} %get-tuple-element.46.queries, ...), custom_call_target="tpu_custom_call" | custom-call | tf_op jit(solution)/shard_map/attention_bwd/pallas_call | solution.py:652
  648.7 12.0 %convolution_bitcast_fusion.2 = f32[1,2048,768]{2,1,0:T(8,128)} fusion(bf16[4,512,2048]{2,1,0:T(8,128)(2,1)} %get-tuple-element.64, bf16[4,512,768]{2,1,0:T(8,128)(2,1)} %get-tuple-element.65), kind=kOutput, calls=%fused_computation.2 | convolution fusion | flops 6442450944 | bytes 17825792 | tf_op jit(solution)/shard_map/dot_general | solution.py:684
  660.7 11.3 %convolution_bitcast_fusion.1 = f32[1,2048,768]{2,1,0:T(8,128)} fusion(bf16[4,512,2048]{2,1,0:T(8,128)(2,1)} %get-tuple-element.64, bf16[4,512,768]{2,1,0:T(8,128)(2,1)S(1)} %copy-done.29), kind=kOutput, calls=%fused_computation.1 | convolution fusion | flops 6442450944 | bytes 17825792 | tf_op jit(solution)/shard_map/dot_general | solution.py:684
  672.0 8.8 %convolution_bitcast_fusion = f32[1,768,2048]{2,1,0:T(8,128)} fusion(bf16[4,512,768]{2,1,0:T(8,128)(2,1)S(1)} %copy-done.28, bf16[4,512,2048]{2,1,0:T(8,128)(2,1)S(1)} %bitcast.115), kind=kOutput, calls=%fused_computation | convolution fusion | flops 6442450944 | bytes 17825792 | tf_op jit(solution)/shard_map/dot_general | solution.py:684
  688.3 78.7 %dqkv_exchange.1 = (f32[160,2048]{1,0:T(8,128)}, bf16[2048,1280]{1,0:T(8,128)(2,1)}, f32[128,2048]{1,0:T(8,128)}) custom-call(bf16[640,1280]{1,0:T(8,128)(2,1)} %pad_maximum_fusion.mine, bf16[512,4096]{1,0:T(8,128)(2,1)} %wq.3, bf16[512,512]{1,0:T(8,128)(2,1)} %wk.3, bf16[512,512]{1,0:T(8,128)(2,1)} %wv.3, bf16[512,640]{1,0:T(8,128)(2,1)} %bitcast.88, ...), custom_call_target="tpu_custom_call" | custom-call | tf_op jit(solution)/shard_map/dqkv_exchange/pallas_call | solution.py:287
  767.0 5.5 copy.60
  774.9 73.6 %last_sums.1 = (f32[256,1280]{1,0:T(8,128)}, f32[8,72,128]{2,1,0:T(8,128)}) custom-call(bf16[8,256,1280]{2,1,0:T(8,128)(2,1)} %bitcast.72, f32[8,72,128]{2,1,0:T(8,128)} %bitcast.95), custom_call_target="tpu_custom_call" | custom-call | tf_op jit(solution)/shard_map/last_sums/pallas_call | solution.py:510
  848.5 2.3 slice_bitcast_fusion
  851.8 2.3 slice.131
  859.1 2.4 copy.74
  863.9 2.2 copy.68
  (151 shorter events, 42.9 us)
Async XLA Ops:
  0.6 136.6 %copy-start = (bf16[2048,32]{0,1:T(8,128)(2,1)S(1)}, bf16[2048,32]{0,1:T(8,128)(2,1)}, u32[]{:S(2)}) copy-start(bf16[2048,32]{0,1:T(8,128)(2,1)} %param.24) | copy-start | bytes 393220
  4.2 74.8 %copy-start.24 = (f32[128]{0:T(128)S(1)}, f32[128]{0:T(128)}, u32[]{:S(2)}) copy-start(f32[128]{0:T(128)} %param.31) | copy-start | bytes 1540
  77.8 2.9 copy-start.6
  80.7 3.4 copy-start.22
  80.7 4.2 copy-start.18
  82.0 4.8 collective-permute-start
  105.9 29.6 %copy-start.2 = (bf16[160,2048]{1,0:T(8,128)(2,1)S(1)}, bf16[160,2048]{1,0:T(8,128)(2,1)}, u32[]{:S(2)}) copy-start(bf16[160,2048]{1,0:T(8,128)(2,1)} %param.16) | copy-start | bytes 1966084
  137.3 1.8 copy-start.4
  257.6 101.2 %copy-start.8 = (bf16[160,2048]{1,0:T(8,128)(2,1)S(1)}, bf16[160,2048]{1,0:T(8,128)(2,1)}, u32[]{:S(2)}) copy-start(bf16[160,2048]{1,0:T(8,128)(2,1)} %param.17) | copy-start | bytes 1966084
  361.2 220.8 %copy-start.3 = (f32[160,2048]{1,0:T(8,128)}, f32[160,2048]{1,0:T(8,128)S(1)}, u32[]{:S(2)}) copy-start(f32[160,2048]{1,0:T(8,128)S(1)} %get-tuple-element.158) | copy-start | bytes 3932164
  576.7 2.7 copy-start.5
  645.4 3.0 copy-start.12
  648.4 35.2 %collective-permute-start.1 = (f32[2,128,128]{2,1,0:T(8,128)}, f32[2,128,128]{2,1,0:T(8,128)}, u32[]{:S(2)}, u32[]{:S(2)}) collective-permute-start(f32[2,128,128]{2,1,0:T(8,128)} %broadcast_select_fusion), channel_id=1, source_target_pairs={{0,1},{1,0},{2,3},{3,2},{4,5},{5,4},{6,7},{7,6},{8,9},{9,8},{10,11... | collective-permute-start | bytes 393224 | tf_op jit(solution)/shard_map/ppermute | solution.py:672
  648.6 12.0 %copy-start.29 = (bf16[4,512,768]{2,1,0:T(8,128)(2,1)S(1)}, bf16[4,512,768]{2,1,0:T(8,128)(2,1)}, u32[]{:S(2)}) copy-start(bf16[4,512,768]{2,1,0:T(8,128)(2,1)} %get-tuple-element.66) | copy-start | bytes 9437188
  648.7 23.4 %slice-start = ((s8[8388608]{0:T(1024)(128)(4,1)}), s8[4194304]{0:T(1024)(128)(4,1)S(1)}, s32[]{:S(2)}) async-start(s8[8388608]{0:T(1024)(128)(4,1)} %bitcast.114), calls=%async_computation | async-start | bytes 8388608
  660.7 11.4 %slice-start.1 = ((s8[8388608]{0:T(1024)(128)(4,1)}), s8[4194304]{0:T(1024)(128)(4,1)S(1)}, s32[]{:S(2)}) async-start(s8[8388608]{0:T(1024)(128)(4,1)} %bitcast.114), calls=%async_computation.1 | async-start | bytes 8388608
  660.7 11.4 %copy-start.28 = (bf16[4,512,768]{2,1,0:T(8,128)(2,1)S(1)}, bf16[4,512,768]{2,1,0:T(8,128)(2,1)}, u32[]{:S(2)}) copy-start(bf16[4,512,768]{2,1,0:T(8,128)(2,1)} %get-tuple-element.67) | copy-start | bytes 9437188
  680.9 2.7 copy-start.21
  680.9 3.7 copy-start.10
  767.0 5.5 copy-start.9
  767.0 5.5 copy-start.19
  859.1 3.7 copy-start.11
  862.8 3.9 copy-start.26
  866.8 2.4 copy-start.1
  (10 other events, 12.1 us)

commit v4 on v3

--- a/solution.py
+++ b/solution.py
@@ -121,7 +121,7 @@
     ]
 
 
-def qkv_kernel(tok, normed, wq, wk, wv, lin, cols, asend, arecv, *relay):
+def qkv_kernel(tok, normed, wq, wk, wv, lin, cols_t, cols, asend, arecv, *relay):
     r, e = lax.axis_index("dp"), lax.axis_index("expert")
     peers = [r ^ m for m in PEER_MASKS]
     width = wq.shape[0]
@@ -152,7 +152,11 @@
 
         lax.fori_loop(0, rows // tok, chunk, 0)
 
-    relay_sum(r, e, products, lambda: products(r, lin), lin, *relay, 32)
+    def own():
+        products(r, lin)
+        cols_t[...] = cols[...].T
+
+    relay_sum(r, e, products, own, lin, *relay, 32)
 
 
 def project_qkv(normed, wq, wk, wv):
@@ -163,11 +167,13 @@
         functools.partial(qkv_kernel, tok),
         out_shape=(
             jax.ShapeDtypeStruct((rows, group), F32),
-            jax.ShapeDtypeStruct((rows, wq.shape[0]), BF16),
+            jax.ShapeDtypeStruct((wq.shape[0], rows), BF16),
         ),
         in_specs=[VMEM_SPEC] * 4,
         out_specs=(VMEM_SPEC, VMEM_SPEC),
-        scratch_shapes=[pltpu.SemaphoreType.DMA((3,))] * 2 + relay_scratch(rows, group),
+        scratch_shapes=[pltpu.VMEM((rows, wq.shape[0]), BF16)]
+        + [pltpu.SemaphoreType.DMA((3,))] * 2
+        + relay_scratch(rows, group),
         compiler_params=params(1),
         name="qkv_exchange",
     )(normed, wq, wk, wv)
@@ -309,7 +315,7 @@
     )(mine, wq, wk, wv, cols_t, out_part)
 
 
-def branch_kernel(mine, wo, attn_t, d_attn, grads, full, ssem, rsem):
+def branch_kernel(mine, wo, attn, d_attn, grads, full, attn_t, ssem, rsem):
     r, e = lax.axis_index("dp"), lax.axis_index("expert")
     tok = mine.shape[0]
     half = tok // 2
@@ -330,6 +336,7 @@
     for copy in (first_near, first_far, second_near, second_far):
         copy.start()
     full[aligned(r, tok), :] = mine[...]
+    attn_t[...] = attn[...].T
     heads = wo.shape[0]
     step = heads // 4
 
@@ -362,7 +369,7 @@
     lax.fori_loop(0, mine.shape[1] // 256, outer, 0)
 
 
-def grad_branch(mine, wo, attn_t):
+def grad_branch(mine, wo, attn):
     tok, width = mine.shape
     return pl.pallas_call(
         branch_kernel,
@@ -374,12 +381,13 @@
         out_specs=(VMEM_SPEC, VMEM_SPEC),
         scratch_shapes=[
             pltpu.VMEM((4 * tok, width), BF16),
+            pltpu.VMEM((wo.shape[0], 4 * tok), BF16),
             pltpu.SemaphoreType.DMA((6,)),
             pltpu.SemaphoreType.DMA((6,)),
         ],
         compiler_params=params(3),
         name="branch_exchange",
-    )(mine, wo, attn_t)
+    )(mine, wo, attn)
 
 
 def owner_order(n_z):
@@ -532,6 +540,304 @@
     )(grads, small)
 
 
+def line_sum(block, out, pair_in, work, lines, ps, pr, zs, zr):
+    r, e = lax.axis_index("dp"), lax.axis_index("expert")
+    z, core = e // 2, e % 2
+    order = plane_order(z)[::-1]
+    right = jnp.minimum(z + 1, 3) * 2 + core
+    left = jnp.maximum(z - 1, 0) * 2 + core
+    pairs, moves = [], []
+
+    def begin():
+        for k in range(4):
+            copy = remote(
+                block(order[k] * 2 + (1 - core)), pair_in.at[k], ps.at[k], pr.at[k], (r, e ^ 1)
+            )
+            copy.start()
+            pairs.append(copy)
+
+    def move(k, side, cond, to, add):
+        b = order[k]
+        copy = remote(work.at[k], lines.at[side, b], zs.at[side, k], zr.at[side, b], (r, to))
+        moves.append((cond, copy))
+
+        @pl.when(cond)
+        def _():
+            if add:
+                copy.wait_recv()
+                value = work[k].astype(F32) + lines[side, b].astype(F32)
+                work[k] = value.astype(BF16)
+            copy.start()
+
+    def first():
+        for k in range(4):
+            pairs[k].wait_recv()
+            value = block(order[k] * 2 + core)[...].astype(F32) + pair_in[k].astype(F32)
+            if k == 3:
+                out[...] = value
+            else:
+                work[k] = value.astype(BF16)
+        ends(0)
+
+    def ends(k):
+        move(k, 0, z == 0, right, False)
+        move(k, 1, z == 3, left, False)
+
+    def inner(k):
+        inside = (z > 0) & (z < 3)
+        move(k, 0, inside & (order[k] > z), right, True)
+        move(k, 1, inside & (order[k] < z), left, True)
+        if k < 2:
+            ends(k + 1)
+
+    def last():
+        for side, cond in ((0, z > 0), (1, z < 3)):
+
+            @pl.when(cond)
+            def _():
+                at = lines.at[side, z]
+                remote(at, at, zs.at[side, 3], zr.at[side, z], (r, e ^ 1)).wait_recv()
+                out[...] = out[...] + lines[side, z].astype(F32)
+
+        for copy in pairs:
+            copy.wait_send()
+        for cond, copy in moves:
+
+            @pl.when(cond)
+            def _():
+                copy.wait_send()
+
+    return begin, first, inner, last
+
+
+LINE_SEMS = [
+    pltpu.SemaphoreType.DMA((4,)),
+    pltpu.SemaphoreType.DMA((4,)),
+    pltpu.SemaphoreType.DMA((2, 4)),
+    pltpu.SemaphoreType.DMA((2, 4)),
+]
+
+
+def dgrad_line_kernel(
+    mine, wq, wk, wv, cols_t, out_part, small, unit_rows, normal, qkv_sum, out_sum, small_out,
+    grads, blocks, dsum, dsend, drecv, opair, owork, olines, qpair, qwork, qlines,
+    small_v, first_in, piece, line_in, ssem, rsem, bsend, brecv, s1, r1, s2, r2, s3, r3, *sems,
+):
+    r, e = lax.axis_index("dp"), lax.axis_index("expert")
+    z, core = e // 2, e % 2
+    rows = mine.shape[0]
+    tok = rows // 4
+    half = rows // 2
+    qg = wq.shape[1] // 4
+    kg = wk.shape[1] // 4
+    width = wq.shape[0]
+    share = width // 8
+    peers = [r ^ m for m in PEER_MASKS]
+    near, far, diag = r ^ 1, r ^ 2, r ^ 3
+    order = (r, near, far, diag)
+    out_begin, out_first, out_inner, out_last = line_sum(
+        lambda o: out_part.at[o], out_sum, opair, owork, olines, *sems[:4]
+    )
+    units = [
+        line_sum(
+            lambda o, p=p: grads.at[o, p], qkv_sum.at[p], qpair.at[i], qwork.at[i], qlines.at[i],
+            *(sem.at[i] for sem in sems[4:]),
+        )
+        for i, p in enumerate(order)
+    ]
+    line_peers = [(r, lax.rem(z + j, 4) * 2 + core) for j in (1, 2, 3)]
+    others = [(m // 2, m % 2) for m in (6, 7, 2, 3, 4, 5, 1)]
+    plane = [(r ^ a, e ^ c) for a, c in others]
+    greet(plane + line_peers)
+    low, high = pl.ds(0, half), pl.ds(half, half)
+    first_near = remote(mine.at[low], blocks.at[0, low], ssem.at[0], rsem.at[0], (near, e))
+    first_far = remote(mine.at[high], blocks.at[1, high], ssem.at[1], rsem.at[1], (far, e))
+    second_near = remote(mine.at[high], blocks.at[0, high], ssem.at[2], rsem.at[2], (near, e))
+    second_far = remote(mine.at[low], blocks.at[1, low], ssem.at[3], rsem.at[3], (far, e))
+    pass_far = remote(blocks.at[0, low], blocks.at[2, low], ssem.at[4], rsem.at[4], (far, e))
+    pass_near = remote(blocks.at[1, high], blocks.at[2, high], ssem.at[5], rsem.at[5], (near, e))
+    for copy in (first_near, first_far, second_near, second_far):
+        copy.start()
+    out_begin()
+
+    def outer(p, src):
+        def step(c, carry):
+            n = aligned(c, 256)
+            value = dot_nn(cols_t[...], src[:, n]).astype(BF16)
+            for o in range(8):
+                grads[o, p, :, n] = value[o * share : (o + 1) * share]
+            return carry
+
+        lax.fori_loop(0, (qg + 2 * kg) // 256, step, 0)
+
+    def inner(p, src, start):
+        def chunk(c, carry):
+            t = aligned(c, tok)
+            x = src[t, :]
+            value = (
+                dot_nt(x[:, :qg], wq[:, aligned(p, qg)])
+                + dot_nt(x[:, qg : qg + kg], wk[:, aligned(p, kg)])
+                + dot_nt(x[:, qg + kg :], wv[:, aligned(p, kg)])
+            )
+            if start:
+                dsum[t, :] = value
+            else:
+                dsum[t, :] = dsum[t, :] + value
+            return carry
+
+        lax.fori_loop(0, 4, chunk, 0)
+
+    def begin(i):
+        units[i][0]()
+
+    def first(i):
+        units[i][1]()
+
+    def onward(i, k):
+        units[i][2](k)
+
+    outer(r, mine)
+    begin(0)
+    out_first()
+    inner(r, mine, True)
+    first_near.wait()
+    pass_far.start()
+    first_far.wait()
+    pass_near.start()
+    out_inner(0)
+    first(0)
+    out_inner(1)
+    onward(0, 0)
+    second_near.wait()
+    outer(near, blocks.at[0])
+    begin(1)
+    second_far.wait()
+    outer(far, blocks.at[1])
+    begin(2)
+    out_inner(2)
+    onward(0, 1)
+    first(1)
+    inner(near, blocks.at[0], False)
+    onward(0, 2)
+    onward(1, 0)
+    first(2)
+    inner(far, blocks.at[1], False)
+    onward(1, 1)
+    pass_far.wait()
+    pass_near.wait()
+    outer(diag, blocks.at[2])
+    begin(3)
+    inner(diag, blocks.at[2], False)
+    back = []
+    for i, p in enumerate(peers):
+        dsend[i] = dsum[aligned(p, tok), :].astype(BF16)
+        copy = remote(dsend.at[i], drecv.at[i], bsend.at[i], brecv.at[i], (p, e))
+        copy.start()
+        back.append(copy)
+    onward(1, 2)
+    onward(2, 0)
+    first(3)
+    onward(2, 1)
+    onward(3, 0)
+    normal[:, aligned(r, width)] = dsum[aligned(r, tok), :]
+    for i, p in enumerate(peers):
+        back[i].wait()
+        normal[:, aligned(p, width)] = drecv[i].astype(F32)
+    at_small = small.shape[1]
+    small_v[:, :at_small] = small[...]
+    small_v[:, at_small:] = jnp.zeros((8, 8, 128), F32)
+    per = 4 * width // 8
+    for i in range(8):
+        n = slice(i * per, (i + 1) * per)
+        gain = jnp.sum(normal[:, n] * unit_rows[:, n], axis=0, keepdims=True)
+        for c in range(per // 128):
+            small_v[i, at_small + c : at_small + c + 1] = gain[:, c * 128 : (c + 1) * 128]
+    firsts = []
+    for i, (a, c) in enumerate(others):
+        copy = remote(
+            small_v.at[(r ^ a) * 2 + (core ^ c)], first_in.at[i], s1.at[i], r1.at[i], plane[i]
+        )
+        copy.start()
+        firsts.append(copy)
+    onward(2, 2)
+    onward(3, 1)
+    for copy in firsts:
+        copy.wait()
+    me = r * 2 + core
+    value = small_v[me]
+    for i in range(7):
+        value = value + first_in[i]
+    piece[0] = value
+    seconds = []
+    for j in range(3):
+        copy = remote(piece.at[0], line_in.at[j], s2.at[j], r2.at[j], line_peers[j])
+        copy.start()
+        seconds.append(copy)
+    onward(3, 2)
+    for copy in seconds:
+        copy.wait()
+    small_out[me] = piece[0] + line_in[0] + line_in[1] + line_in[2]
+    thirds = []
+    for i in range(7):
+        copy = remote(small_out.at[me], small_out.at[me], s3.at[i], r3.at[i], plane[i])
+        copy.start()
+        thirds.append(copy)
+    out_last()
+    for unit in units:
+        unit[3]()
+    for copy in thirds:
+        copy.wait()
+
+
+def grad_qkv_line(mine, wq, wk, wv, cols_t, out_part, small, unit_rows):
+    rows, group = mine.shape
+    tok = rows // 4
+    width = wq.shape[0]
+    piece = (width // 8, group)
+    out_piece = out_part.shape[1:]
+    small_shape = (8, small.shape[1] + 8, 128)
+    return pl.pallas_call(
+        dgrad_line_kernel,
+        out_shape=(
+            jax.ShapeDtypeStruct((tok, 4 * width), F32),
+            jax.ShapeDtypeStruct((4, *piece), F32),
+            jax.ShapeDtypeStruct(out_piece, F32),
+            jax.ShapeDtypeStruct(small_shape, F32),
+        ),
+        in_specs=[VMEM_SPEC] * 8,
+        out_specs=(VMEM_SPEC,) * 4,
+        scratch_shapes=[
+            pltpu.VMEM((8, 4, *piece), BF16),
+            pltpu.VMEM((3, rows, group), BF16),
+            pltpu.VMEM((rows, width), F32),
+            pltpu.VMEM((3, tok, width), BF16),
+            pltpu.VMEM((3, tok, width), BF16),
+            pltpu.VMEM((4, *out_piece), BF16),
+            pltpu.VMEM((3, *out_piece), BF16),
+            pltpu.VMEM((2, 4, *out_piece), BF16),
+            pltpu.VMEM((4, 4, *piece), BF16),
+            pltpu.VMEM((4, 3, *piece), BF16),
+            pltpu.VMEM((4, 2, 4, *piece), BF16),
+            pltpu.VMEM(small_shape, F32),
+            pltpu.VMEM((7, *small_shape[1:]), F32),
+            pltpu.VMEM((1, *small_shape[1:]), F32),
+            pltpu.VMEM((3, *small_shape[1:]), F32),
+            pltpu.SemaphoreType.DMA((6,)),
+            pltpu.SemaphoreType.DMA((6,)),
+        ]
+        + [pltpu.SemaphoreType.DMA((n,)) for n in (3, 3, 7, 7, 3, 3, 7, 7)]
+        + LINE_SEMS
+        + [
+            pltpu.SemaphoreType.DMA((4, 4)),
+            pltpu.SemaphoreType.DMA((4, 4)),
+            pltpu.SemaphoreType.DMA((4, 2, 4)),
+            pltpu.SemaphoreType.DMA((4, 2, 4)),
+        ],
+        compiler_params=params(10),
+        name="dqkv_line_exchange",
+    )(mine, wq, wk, wv, cols_t, out_part, small, unit_rows)
+
+
 def masks_of(block, own_length, slots, prompt_block, prompt_len, column, keys):
     slot = lax.broadcasted_iota(jnp.int32, (slots, keys), 0)
     key = lax.broadcasted_iota(jnp.int32, (slots, keys), 1)
@@ -703,7 +1009,7 @@
     return r, e, z, core, near, far, devices
 
 
-def gather_world(mine, buf, zs, zr, ps, pr, ds, dr, before, group):
+def gather_world(mine, buf, zs, zr, ps, pr, ds, dr, before, group, done):
     r, e, z, core, near, far, greeted = world(True)
     half = mine.shape[0] // 2
     low, high = pl.ds(0, half), pl.ds(half, half)
@@ -779,6 +1085,7 @@
         hand(k, 3, diag)
 
     def ready(k):
+        before(k)
         for i in range(4):
             pairs[k, i].wait_recv()
         group(k, order[k])
@@ -791,22 +1098,19 @@
     line_wait(2)
     corner(0)
     finish(1)
-    before(0, order[0])
     ready(0)
     passes(2)
     line_wait(3)
     corner(1)
     finish(2)
-    before(1, order[1])
     ready(1)
     passes(3)
     corner(2)
     finish(3)
-    before(2, order[2])
     ready(2)
-    before(3, order[3])
     corner(3)
     ready(3)
+    done()
     for copy in plane.values():
         copy.wait_send()
     for copy in pairs.values():
@@ -848,7 +1152,7 @@
 
 def experts_fwd_kernel(
     mine, wg, wu, wd, pos, x_out, y_out, g_out, u_out, o_out, hid_out, gate_out,
-    buf, wg_v, wu_v, wd_v, x_v, y_v, g_v, u_v, o_v, hid_v, gate_v, local, zs, zr, ps, pr, ds, dr,
+    buf, wg_v, wu_v, wd_v, x_v, y_v, g_v, u_v, o_v, hid_v, gate_v, local, *sems,
 ):
     model = wg.shape[0]
     rows_in = mine.shape[0]
@@ -867,38 +1171,43 @@
             start_all([pltpu.make_async_copy(v, o.at[b], local.at[i]) for i, v, o in pairs])
         )
 
-    def before(k, b):
+    def before(k):
         wait_all(loads)
+
+    upto = jnp.where(
+        lax.broadcasted_iota(jnp.int32, (rows_in, rows_in), 0)
+        <= lax.broadcasted_iota(jnp.int32, (rows_in, rows_in), 1),
+        1.0,
+        0.0,
+    ).astype(BF16)
+    is_me = jnp.where(lax.broadcasted_iota(jnp.int32, (16, 128), 1) == me, 1.0, 0.0).astype(BF16)
+
+    def pick_one(b, j):
+        s = j // 2 * 8 + b * 2 + j % 2
+        rows = aligned(j, room)
+        named = jnp.where(dot_nt(is_me, buf[s, :, model:]) > 0.0, 1.0, 0.0)
+        place = dot_nn(named.astype(BF16), upto) * named - 1.0
+        pos[s] = place[:1]
+        ids = lax.broadcasted_iota(jnp.int32, (room, rows_in), 0).astype(F32)
+        sel = jnp.where(ids == place[:1], 1.0, 0.0).astype(BF16)
+        for c in range(4):
+            n = slice(c * model // 4, (c + 1) * model // 4)
+            x_v[rows, n] = dot_nn(sel, buf[s, :, n]).astype(BF16)
+        extra = dot_nn(sel, buf[s, :, model:])
+        lane = lax.broadcasted_iota(jnp.int32, extra.shape, 1)
+        hit = (lane == me) | (lane == me + 64)
+        gate = jnp.sum(jnp.where(hit, extra, 0.0), axis=-1, keepdims=True)
+        gate_v[rows, :] = jnp.broadcast_to(gate, extra.shape)
 
     def group(k, b):
         wait_all(leaving)
-        upto = jnp.where(
-            lax.broadcasted_iota(jnp.int32, (rows_in, rows_in), 0)
-            <= lax.broadcasted_iota(jnp.int32, (rows_in, rows_in), 1),
-            1.0,
-            0.0,
-        ).astype(BF16)
-        is_me = jnp.where(lax.broadcasted_iota(jnp.int32, (16, 128), 1) == me, 1.0, 0.0).astype(BF16)
-
-        def pick(j, carry):
-            s = j // 2 * 8 + b * 2 + j % 2
-            rows = aligned(j, room)
-            named = jnp.where(dot_nt(is_me, buf[s, :, model:]) > 0.0, 1.0, 0.0)
-            place = dot_nn(named.astype(BF16), upto) * named - 1.0
-            pos[s] = place[:1]
-            ids = lax.broadcasted_iota(jnp.int32, (room, rows_in), 0).astype(F32)
-            sel = jnp.where(ids == place[:1], 1.0, 0.0).astype(BF16)
-            for c in range(4):
-                n = slice(c * model // 4, (c + 1) * model // 4)
-                x_v[rows, n] = dot_nn(sel, buf[s, :, n]).astype(BF16)
-            extra = dot_nn(sel, buf[s, :, model:])
-            lane = lax.broadcasted_iota(jnp.int32, extra.shape, 1)
-            hit = (lane == me) | (lane == me + 64)
-            gate = jnp.sum(jnp.where(hit, extra, 0.0), axis=-1, keepdims=True)
-            gate_v[rows, :] = jnp.broadcast_to(gate, extra.shape)
+
+        def four(j, carry):
+            for i in range(4):
+                pick_one(b, j * 4 + i)
             return carry
 
-        lax.fori_loop(0, 8, pick, 0)
+        lax.fori_loop(0, 2, four, 0)
         leave(b, ((0, x_v, x_out), (1, gate_v, gate_out)))
 
         def first(c, carry):
@@ -922,10 +1231,8 @@
 
         lax.fori_loop(0, model // 256, second, 0)
         leave(b, ((5, o_v, o_out), (6, y_v, y_out)))
-        if k == 3:
-            wait_all(leaving)
-
-    gather_world(mine, buf, zs, zr, ps, pr, ds, dr, before, group)
+
+    gather_world(mine, buf, *sems, before, group, lambda: wait_all(leaving))
 
 
 def experts_fwd(mine, wg, wu, wd, room):
@@ -972,7 +1279,7 @@
 def experts_bwd_kernel(
     mine, pos, g_in, u_in, o_in, gate_in, wg, wu, wd, y_out, d_copy_out, dg_out, du_out,
     buf, wg_v, wu_v, wd_v, g_v, u_v, o_v, gate_v, y_v, d_copy_v, dg_v, du_v,
-    local, ins, zs, zr, ps, pr, ds, dr,
+    local, ins, *sems,
 ):
     model, ff = wg.shape
     room = d_copy_v.shape[0] // 8
@@ -1005,37 +1312,39 @@
             start_all([pltpu.make_async_copy(v, o.at[b], local.at[i]) for i, v, o in pairs])
         )
 
-    def before(k, b):
+    def before(k):
         wait_all(loads)
         wait_all(coming[k])
         if k < 3:
             fetch(k + 1)
 
+    def pick_one(b, j, at):
+        s = j // 2 * 8 + b * 2 + j % 2
+        rows = aligned(j, room)
+        sel = selector(pos, s, room)
+        gate = gate_v[at, rows, :1]
+        inner = jnp.zeros((room, 1), F32)
+        for c in range(4):
+            n = slice(c * model // 4, (c + 1) * model // 4)
+            picked = dot_nn(sel, buf[s, :, n])
+            d_copy_v[rows, n] = (gate * picked).astype(BF16)
+            inner = inner + jnp.sum(picked * o_v[at, rows, n].astype(F32), axis=-1, keepdims=True)
+        top = inner.astype(BF16).astype(F32)
+        rest = inner - top
+        lane = lax.broadcasted_iota(jnp.int32, (room, 128), 1)
+        extra = jnp.where(lane == me, top, 0.0) + jnp.where(lane == me + 64, rest, 0.0)
+        y_v[rows, model:] = extra.astype(BF16)
+
     def group(k, b):
         at = k % 2
         wait_all(leaving)
 
-        def pick(j, carry):
-            s = j // 2 * 8 + b * 2 + j % 2
-            rows = aligned(j, room)
-            sel = selector(pos, s, room)
-            gate = gate_v[at, rows, :1]
-            inner = jnp.zeros((room, 1), F32)
-            for c in range(4):
-                n = slice(c * model // 4, (c + 1) * model // 4)
-                picked = dot_nn(sel, buf[s, :, n])
-                d_copy_v[rows, n] = (gate * picked).astype(BF16)
-                inner = inner + jnp.sum(
-                    picked * o_v[at, rows, n].astype(F32), axis=-1, keepdims=True
-                )
-            top = inner.astype(BF16).astype(F32)
-            rest = inner - top
-            lane = lax.broadcasted_iota(jnp.int32, (room, 128), 1)
-            extra = jnp.where(lane == me, top, 0.0) + jnp.where(lane == me + 64, rest, 0.0)
-            y_v[rows, model:] = extra.astype(BF16)
+        def four(j, carry):
+            for i in range(4):
+                pick_one(b, j * 4 + i, at)
             return carry
 
-        lax.fori_loop(0, 8, pick, 0)
+        lax.fori_loop(0, 2, four, 0)
         leave(b, ((0, d_copy_v, d_copy_out),))
 
         def third(c, carry):
@@ -1052,15 +1361,15 @@
 
         def fourth(c, carry):
             n = aligned(c, 256)
-            y_v[:, n] = (dot_nt(dg_v[...], wg_v[n, :]) + dot_nt(du_v[...], wu_v[n, :])).astype(BF16)
+            y_v[:, n] = (
+                dot_nt(dg_v[...], wg_v[n, :]) + dot_nt(du_v[...], wu_v[n, :])
+            ).astype(BF16)
             return carry
 
         lax.fori_loop(0, model // 256, fourth, 0)
         leave(b, ((3, y_v, y_out),))
-        if k == 3:
-            wait_all(leaving)
-
-    gather_world(mine, buf, zs, zr, ps, pr, ds, dr, before, group)
+
+    gather_world(mine, buf, *sems, before, group, lambda: wait_all(leaving))
 
 
 def experts_bwd(mine, pos, kept, wg, wu, wd, room):
@@ -1504,7 +1813,7 @@
         [lax.dynamic_index_in_dim(cont_lengths.reshape(n_dp, n_owner), rank_owner, 1, False), column[None]]
     ).astype(jnp.int32)
 
-    lin, normed_cols = project_qkv(normed, query_weight, key_projection, value_projection)
+    lin, normed_cols_t = project_qkv(normed, query_weight, key_projection, value_projection)
     key_lin = lin[:, query_group : query_group + head_dim].reshape(n_dp, tok_dev, head_dim)
     keys_float, key_back = jax.vjp(lambda a, b: head_rope(a, b, cos, sin), key_lin, key_gain)
     keys_own = keys_float.astype(BF16)
@@ -1542,7 +1851,7 @@
     d_state_norm, d_post_gain = second_norm_back(d_mixed)
     d_state = d_out + d_state_norm
     d_branch = d_state.astype(BF16)
-    d_attended, out_part = grad_branch(d_branch, output_weight, attended.T)
+    d_attended, out_part = grad_branch(d_branch, output_weight, attended)
     d_query_lin, d_keys, d_values, gain_parts = attention_bwd(
         lengths, lin, queries, d_attended, query_gain_row, cos, sin, all_keys, all_values, prompt_len
     )
@@ -1567,43 +1876,59 @@
         ],
         axis=1,
     )
-    d_normed, qkv_part, output_grad = grad_qkv(
-        d_lin, query_weight, key_projection, value_projection, normed_cols.T,
-        out_part.reshape(n_owner, -1, model_width),
-    )
-    d_tokens_norm, d_input_gain = first_norm_back(d_normed)
-    tokens_grad = d_state + d_tokens_norm
+    small_parts = [router_local, d_post_gain, d_query_gain, d_key_gain, local_square[None]]
     width = query_weight.shape[0]
     group = d_lin.shape[1]
     rows_here = width // n_owner
-    by_owner = (
-        qkv_part.reshape(n_dp, n_owner, rows_here, group)
-        .transpose(1, 0, 2, 3)
-        .reshape(n_owner, n_dp * rows_here, group)
-    )
-    small_parts = (
-        router_local, d_input_gain, d_post_gain, d_query_gain, d_key_gain, local_square[None]
-    )
-    small = jnp.concatenate([a.reshape(-1) for a in small_parts])
-    piece_rows = -(-small.shape[0] // (8 * 8 * 128)) * 8
-    small = jnp.pad(small, (0, 8 * piece_rows * 128 - small.shape[0]))
-    qkv_rows, small_sums = last_sums(by_owner, small.reshape(8, piece_rows, 128))
-    small_sums = small_sums.reshape(-1)
+    by_line = n_dp == 4 and n_owner == 8
+
+    def packed(parts):
+        small = jnp.concatenate([a.reshape(-1) for a in parts])
+        piece_rows = -(-small.shape[0] // (8 * 8 * 128)) * 8
+        small = jnp.pad(small, (0, 8 * piece_rows * 128 - small.shape[0]))
+        return small.reshape(8, piece_rows, 128)
+
+    dqkv_operands = (
+        d_lin, query_weight, key_projection, value_projection, normed_cols_t,
+        out_part.reshape(n_owner, -1, model_width),
+    )
+    if by_line:
+        small = packed(small_parts)
+        unit_rows = tokens_float * lax.rsqrt(
+            jnp.mean(tokens_float * tokens_float, axis=-1, keepdims=True) + norm_eps
+        )
+        d_normed, qkv_rows, output_grad, small_out = grad_qkv_line(*dqkv_operands, small, unit_rows)
+        input_gain_grad = small_out[:, small.shape[1] : small.shape[1] + model_width // 1024].reshape(-1)
+        small = small_out[:, : small.shape[1]]
+    else:
+        d_normed, qkv_part, output_grad = grad_qkv(*dqkv_operands)
+    d_tokens_norm, d_input_gain = first_norm_back(d_normed)
+    tokens_grad = d_state + d_tokens_norm
+    if not by_line:
+        small_parts.append(d_input_gain)
+        by_owner = (
+            qkv_part.reshape(n_dp, n_owner, rows_here, group)
+            .transpose(1, 0, 2, 3)
+            .reshape(n_owner, n_dp * rows_here, group)
+        )
+        qkv_rows, small = last_sums(by_owner, packed(small_parts))
+    qkv_rows = qkv_rows.reshape(n_dp, rows_here, group)
+
+    def columns(start, size):
+        return qkv_rows[:, :, start : start + size].transpose(1, 0, 2).reshape(rows_here, n_dp * size)
+
+    query_grad = columns(0, query_group)
+    key_grad = columns(query_group, head_dim)
+    value_grad = columns(query_group + head_dim, head_dim)
+    small = small.reshape(-1)
     starts = [0]
     for a in small_parts:
         starts.append(starts[-1] + a.size)
-    router_grad, input_gain_grad, post_gain_grad, query_gain_grad, key_gain_grad, total_square = (
-        small_sums[i:j].reshape(a.shape) for a, i, j in zip(small_parts, starts, starts[1:])
-    )
+    sums = [small[i:j].reshape(a.shape) for a, i, j in zip(small_parts, starts, starts[1:])]
+    router_grad, post_gain_grad, query_gain_grad, key_gain_grad, total_square = sums[:5]
+    if not by_line:
+        input_gain_grad = sums[5]
     loss = total_square[0] / (valid_count * model_width)
-    qkv_rows = qkv_rows.reshape(n_dp, rows_here, group)
-
-    def columns(start, size):
-        return qkv_rows[:, :, start : start + size].transpose(1, 0, 2).reshape(rows_here, n_dp * size)
-
-    query_grad = columns(0, query_group)
-    key_grad = columns(query_group, head_dim)
-    value_grad = columns(query_group + head_dim, head_dim)
     return (
         layer_out,
         loss,

time: 882 us -> 814 us (0.923)
  Pallas kernels: 765 us -> 707 us
  local copies, waits for them, and re-layouts: 35.7 us -> 25.9 us
    pallas_call x2 -> x1, Pallas kernels: 152 us -> 102 us  [grad_qkv_line(): pl.pallas_call(dgrad_line_kernel, out_shape=(jax.ShapeDtypeStruct((tok, 4...]
  transfers between devices with their start and end apart: 2 -> 2, of which waited for: 0 -> 0; matrix products, arithmetic and copies ran while one was open for 4% -> 5% of each run, Pallas kernels for 0% -> 0%
where the time goes in v4:
time: 814 us; the launch traced here: 802 us
  Pallas kernels  707 us (87%)
  matrix products  37.9 us (5%)
  other arithmetic  27.4 us (3%)
  local copies, waits for them, and re-layouts  25.9 us (3%)
    pallas_call x2, Pallas kernels, sum_world(): pl.pallas_call(sum_world_kernel, out_shape=jax.ShapeDtypeStruct((rows, wi...  207 us
    pallas_call x1, Pallas kernels, experts_fwd(): pl.pallas_call(experts_fwd_kernel, out_shape=(jax.ShapeDtypeStruct((32, 1...  116 us
    pallas_call x1, Pallas kernels, experts_bwd(): pl.pallas_call(experts_bwd_kernel, out_shape=(jax.ShapeDtypeStruct((4, gr...  104 us
    pallas_call x1, Pallas kernels, grad_qkv_line(): pl.pallas_call(dgrad_line_kernel, out_shape=(jax.ShapeDtypeStruct((tok, 4...  102 us
    pallas_call x1, Pallas kernels, project_qkv(): pl.pallas_call(functools.partial(qkv_kernel, tok), out_shape=(jax.ShapeDt...  72.5 us
    dot_general x5, matrix products, contract(): lax.dot_general(left_side, right_side, (((left_dim,), (right_dim,)), ((),...  37.4 us
    pallas_call x1, Pallas kernels, grad_branch(): pl.pallas_call(branch_kernel, out_shape=(jax.ShapeDtypeStruct((4 * tok, w...  34.2 us
    pallas_call x1, Pallas kernels, project_out(): pl.pallas_call(out_kernel, out_shape=jax.ShapeDtypeStruct((tok, wo.shape[...  29.6 us
  transfers between devices with their start and end apart: 2, of which 0 were waited for; matrix products, arithmetic and copies ran while one was open for 5% of the time, Pallas kernels for 0%

profile of v4, /device:TPU:8, one launch (start us, length us, event | category | flops | bytes accessed | tf_op | source)
XLA Modules:
  0.0 802.3 jit_solution(5161222729918134995)
XLA Ops:
  0.7 1.3 fusion.2
  2.0 2.6 convert_multiply_fusion.2
  4.6 72.5 %qkv_exchange.1 = (f32[640,1280]{1,0:T(8,128)}, bf16[512,640]{1,0:T(8,128)(2,1)}) custom-call(bf16[160,2048]{1,0:T(8,128)(2,1)} %get-tuple-element.115.normed, bf16[512,4096]{1,0:T(8,128)(2,1)} %wq.3, bf16[512,512]{1,0:T(8,128)(2,1)} %wk.3, bf16[512,512]{1,0:T(8,128)(2,1)} %wv.3), custom_call_target="tpu_custom_call" | custom-call | tf_op jit(solution)/shard_map/qkv_exchange/pallas_call | solution.py:166
  87.3 15.6 %attention_fwd.1 = (bf16[640,1024]{1,0:T(8,128)(2,1)}, bf16[640,1024]{1,0:T(8,128)(2,1)}) custom-call(s32[5]{0:T(128)} %pad_add_fusion.lengths, f32[640,1280]{1,0:T(8,128)} %get-tuple-element.41.lin, f32[1,128]{1,0:T(1,128)} %bitcast.101, f32[4,160,128]{2,1,0:T(8,128)} %get-tuple-element.118.cos, f32[4,160,128]{2,1,0:T(8,128)} %get-tuple-element.109.sin, ...), custom_call_target="tpu_custom_call" | custom-call | tf_op jit(solution)/shard_map/attention_fwd/pallas_call | solution.py:888
  102.9 29.6 %out_exchange.1 = f32[160,2048]{1,0:T(8,128)} custom-call(bf16[640,1024]{1,0:T(8,128)(2,1)} %get-tuple-element.42.attn, bf16[1024,2048]{1,0:T(8,128)(2,1)} %wo.3), custom_call_target="tpu_custom_call" | custom-call | tf_op jit(solution)/shard_map/out_exchange/pallas_call | solution.py:201
  132.5 1.6 multiply_reduce_fusion.3
  136.1 115.6 %experts_fwd.1 = (f32[32,1,160]{2,1,0:T(1,128)}, bf16[4,512,2048]{2,1,0:T(8,128)(2,1)}, bf16[4,512,2048]{2,1,0:T(8,128)(2,1)}, bf16[4,512,768]{2,1,0:T(8,128)(2,...) custom-call(bf16[160,2176]{1,0:T(8,128)(2,1)} %concatenate.70.mine, ...), custom_call_target="tpu_custom_call" | custom-call | tf_op jit(solution)/shard_map/experts_fwd/pallas_call | solution.py:1244
  251.7 100.0 %sum_world.2 = f32[160,2048]{1,0:T(8,128)} custom-call(bf16[4,8,64,2048]{3,2,1,0:T(8,128)(2,1)} %bitcast.73, f32[32,1,160]{2,1,0:T(1,128)} %get-tuple-element.44.pos), custom_call_target="tpu_custom_call" | custom-call | tf_op jit(solution)/shard_map/sum_world/pallas_call | solution.py:1566
  351.8 2.4 multiply_reduce_fusion
  355.5 103.6 %experts_bwd.1 = (bf16[4,512,2176]{2,1,0:T(8,128)(2,1)}, bf16[4,512,2048]{2,1,0:T(8,128)(2,1)}, bf16[4,512,768]{2,1,0:T(8,128)(2,1)}, bf16[4,512,768]{2,1,0:T(8,128)(2,1)}) custom-call(bf16[160,2048]{1,0:T(8,128)(2,1)} %fusion.9.mine, f32[32,1,160]{2,1,0:T(1,128)} %get-tuple-element.44.pos, bf16[4,512,768]{2,1,0:T(8,128)(2,1)} %get-tuple-element.46.g_in, ...), custom_call_target="tpu_custom_call" | custom-call | tf_op jit(solution)/shard_map/experts_bwd/pallas_call | solution.py:1379
  459.0 107.0 %sum_world.3 = f32[160,2176]{1,0:T(8,128)} custom-call(bf16[4,8,64,2176]{3,2,1,0:T(8,128)(2,1)} %bitcast.72, f32[32,1,160]{2,1,0:T(1,128)} %get-tuple-element.44.pos), custom_call_target="tpu_custom_call" | custom-call | tf_op jit(solution)/shard_map/sum_world/pallas_call | solution.py:1566
  567.3 2.7 multiply_reduce_fusion.1
  570.0 2.5 fusion.24
  572.6 1.4 fusion.18
  574.0 34.2 %branch_exchange.1 = (bf16[640,1024]{1,0:T(8,128)(2,1)}, bf16[1024,2048]{1,0:T(8,128)(2,1)}) custom-call(bf16[160,2048]{1,0:T(8,128)(2,1)} %get-tuple-element.104.mine, bf16[1024,2048]{1,0:T(8,128)(2,1)} %wo.3, bf16[640,1024]{1,0:T(8,128)(2,1)} %get-tuple-element.42.attn), custom_call_target="tpu_custom_call" | custom-call | tf_op jit(solution)/shard_map/branch_exchange/pallas_call | solution.py:374
  608.2 26.4 %attention_bwd.1 = (bf16[640,1024]{1,0:T(8,128)(2,1)}, f32[4,384,128]{2,1,0:T(8,128)}, f32[4,384,128]{2,1,0:T(8,128)}, f32[4,8,128]{2,1,0:T(8,128)}) custom-call(s32[5]{0:T(128)} %pad_add_fusion.lengths, f32[640,1280]{1,0:T(8,128)} %get-tuple-element.41.lin, bf16[640,1024]{1,0:T(8,128)(2,1)} %get-tuple-element.45.queries, ...), custom_call_target="tpu_custom_call" | custom-call | tf_op jit(solution)/shard_map/attention_bwd/pallas_call | solution.py:958
  637.9 12.0 %convolution_bitcast_fusion.2 = f32[1,2048,768]{2,1,0:T(8,128)} fusion(bf16[4,512,2048]{2,1,0:T(8,128)(2,1)} %get-tuple-element.62, bf16[4,512,768]{2,1,0:T(8,128)(2,1)} %get-tuple-element.63), kind=kOutput, calls=%fused_computation.2 | convolution fusion | flops 6442450944 | bytes 17825792 | tf_op jit(solution)/shard_map/dot_general | solution.py:990
  649.9 11.3 %convolution_bitcast_fusion.1 = f32[1,2048,768]{2,1,0:T(8,128)} fusion(bf16[4,512,2048]{2,1,0:T(8,128)(2,1)} %get-tuple-element.62, bf16[4,512,768]{2,1,0:T(8,128)(2,1)S(1)} %copy-done.29), kind=kOutput, calls=%fused_computation.1 | convolution fusion | flops 6442450944 | bytes 17825792 | tf_op jit(solution)/shard_map/dot_general | solution.py:990
  661.3 8.8 %convolution_bitcast_fusion = f32[1,768,2048]{2,1,0:T(8,128)} fusion(bf16[4,512,768]{2,1,0:T(8,128)(2,1)S(1)} %copy-done.28, bf16[4,512,2048]{2,1,0:T(8,128)(2,1)S(1)} %bitcast.104), kind=kOutput, calls=%fused_computation | convolution fusion | flops 6442450944 | bytes 17825792 | tf_op jit(solution)/shard_map/dot_general | solution.py:990
  677.8 102.3 %dqkv_line_exchange.1 = (f32[160,2048]{1,0:T(8,128)}, f32[4,64,1280]{2,1,0:T(8,128)}, f32[128,2048]{1,0:T(8,128)}, f32[8,80,128]{2,1,0:T(8,128)}) custom-call(bf16[640,1280]{1,0:T(8,128)(2,1)} %pad_maximum_fusion.mine, bf16[512,4096]{1,0:T(8,128)(2,1)} %wq.3, bf16[512,512]{1,0:T(8,128)(2,1)} %wk.3, bf16[512,512]{1,0:T(8,128)(2,1)} %wv.3, ...), custom_call_target="tpu_custom_call" | custom-call | tf_op jit(solution)/shard_map/dqkv_line_exchange/pallas_call | solution.py:799
  780.2 2.4 slice_bitcast_fusion
  785.0 2.3 slice.135
  795.4 2.2 copy.56
  798.3 1.4 fusion.1
  (148 shorter events, 36.2 us)
Async XLA Ops:
  0.6 133.6 %copy-start = (bf16[2048,32]{0,1:T(8,128)(2,1)S(1)}, bf16[2048,32]{0,1:T(8,128)(2,1)}, u32[]{:S(2)}) copy-start(bf16[2048,32]{0,1:T(8,128)(2,1)} %param.24) | copy-start | bytes 393220
  4.6 74.9 %copy-start.24 = (f32[128]{0:T(128)S(1)}, f32[128]{0:T(128)}, u32[]{:S(2)}) copy-start(f32[128]{0:T(128)} %param.31) | copy-start | bytes 1540
  78.3 2.9 copy-start.6
  81.2 3.4 copy-start.22
  82.5 3.7 collective-permute-start
  102.9 29.6 %copy-start.2 = (bf16[160,2048]{1,0:T(8,128)(2,1)S(1)}, bf16[160,2048]{1,0:T(8,128)(2,1)}, u32[]{:S(2)}) copy-start(bf16[160,2048]{1,0:T(8,128)(2,1)} %param.16) | copy-start | bytes 1966084
  251.7 100.0 %copy-start.8 = (bf16[160,2048]{1,0:T(8,128)(2,1)S(1)}, bf16[160,2048]{1,0:T(8,128)(2,1)}, u32[]{:S(2)}) copy-start(bf16[160,2048]{1,0:T(8,128)(2,1)} %param.17) | copy-start | bytes 1966084
  354.2 218.4 %copy-start.3 = (f32[160,2048]{1,0:T(8,128)}, f32[160,2048]{1,0:T(8,128)S(1)}, u32[]{:S(2)}) copy-start(f32[160,2048]{1,0:T(8,128)S(1)} %get-tuple-element.154) | copy-start | bytes 3932164
  567.3 2.8 copy-start.5
  634.6 3.0 copy-start.12
  637.6 34.6 %collective-permute-start.1 = (f32[2,128,128]{2,1,0:T(8,128)}, f32[2,128,128]{2,1,0:T(8,128)}, u32[]{:S(2)}, u32[]{:S(2)}) collective-permute-start(f32[2,128,128]{2,1,0:T(8,128)} %broadcast_select_fusion), channel_id=1, source_target_pairs={{0,1},{1,0},{2,3},{3,2},{4,5},{5,4},{6,7},{7,6},{8,9},{9,8},{10,11... | collective-permute-start | bytes 393224 | tf_op jit(solution)/shard_map/ppermute | solution.py:978
  637.9 12.0 %copy-start.29 = (bf16[4,512,768]{2,1,0:T(8,128)(2,1)S(1)}, bf16[4,512,768]{2,1,0:T(8,128)(2,1)}, u32[]{:S(2)}) copy-start(bf16[4,512,768]{2,1,0:T(8,128)(2,1)} %get-tuple-element.64) | copy-start | bytes 9437188
  637.9 23.4 %slice-start = ((s8[8388608]{0:T(1024)(128)(4,1)}), s8[4194304]{0:T(1024)(128)(4,1)S(1)}, s32[]{:S(2)}) async-start(s8[8388608]{0:T(1024)(128)(4,1)} %bitcast.103), calls=%async_computation | async-start | bytes 8388608
  649.9 11.4 %slice-start.1 = ((s8[8388608]{0:T(1024)(128)(4,1)}), s8[4194304]{0:T(1024)(128)(4,1)S(1)}, s32[]{:S(2)}) async-start(s8[8388608]{0:T(1024)(128)(4,1)} %bitcast.103), calls=%async_computation.1 | async-start | bytes 8388608
  649.9 11.4 %copy-start.28 = (bf16[4,512,768]{2,1,0:T(8,128)(2,1)S(1)}, bf16[4,512,768]{2,1,0:T(8,128)(2,1)}, u32[]{:S(2)}) copy-start(bf16[4,512,768]{2,1,0:T(8,128)(2,1)} %get-tuple-element.65) | copy-start | bytes 9437188
  661.3 8.9 %copy-start.23 = (f32[2048]{0:T(1024)S(1)}, f32[2048]{0:T(1024)}, u32[]{:S(2)}) copy-start(f32[2048]{0:T(1024)} %get-tuple-element.97) | copy-start | bytes 24580
  661.3 10.8 %copy-start.21 = (f32[4,8,128]{2,1,0:T(8,128)S(1)}, f32[4,8,128]{2,1,0:T(8,128)}, u32[]{:S(2)}) copy-start(f32[4,8,128]{2,1,0:T(8,128)} %get-tuple-element.57) | copy-start | bytes 49156
  670.1 3.1 copy-start.10
  780.2 3.5 copy-start.18
  782.5 8.6 %copy-start.9 = (f32[160,2048]{1,0:T(8,128)S(1)}, f32[160,2048]{1,0:T(8,128)}, u32[]{:S(2)}) copy-start(f32[160,2048]{1,0:T(8,128)} %get-tuple-element.59) | copy-start | bytes 3932164
  782.5 8.6 %copy-start.19 = (f32[2048]{0:T(1024)S(1)}, f32[2048]{0:T(1024)}, u32[]{:S(2)}) copy-start(f32[2048]{0:T(1024)} %param.28) | copy-start | bytes 24580
  787.2 4.7 copy-start.13
  794.3 3.9 copy-start.26
  798.3 2.4 copy-start.1
  (10 other events, 14.9 us)

commit v5 on v4

--- a/solution.py
+++ b/solution.py
@@ -143,14 +143,13 @@
 
     def products(p, dst):
         def chunk(c, carry):
-            t = aligned(c, tok)
-            x = cols[t, :]
-            dst[t, :qg] = dot_nn(x, wq[:, aligned(p, qg)]).astype(dst.dtype)
-            dst[t, qg : qg + kg] = dot_nn(x, wk[:, aligned(p, kg)]).astype(dst.dtype)
-            dst[t, qg + kg :] = dot_nn(x, wv[:, aligned(p, kg)]).astype(dst.dtype)
+            columns = pl.ds(pl.multiple_of(p * qg + c * 256, 256), 256)
+            dst[:, aligned(c, 256)] = dot_nn(cols[...], wq[:, columns]).astype(dst.dtype)
             return carry
 
-        lax.fori_loop(0, rows // tok, chunk, 0)
+        lax.fori_loop(0, qg // 256, chunk, 0)
+        dst[:, qg : qg + kg] = dot_nn(cols[...], wk[:, aligned(p, kg)]).astype(dst.dtype)
+        dst[:, qg + kg :] = dot_nn(cols[...], wv[:, aligned(p, kg)]).astype(dst.dtype)
 
     def own():
         products(r, lin)
@@ -168,11 +167,11 @@
         out_shape=(
             jax.ShapeDtypeStruct((rows, group), F32),
             jax.ShapeDtypeStruct((wq.shape[0], rows), BF16),
+            jax.ShapeDtypeStruct((rows, wq.shape[0]), BF16),
         ),
         in_specs=[VMEM_SPEC] * 4,
-        out_specs=(VMEM_SPEC, VMEM_SPEC),
-        scratch_shapes=[pltpu.VMEM((rows, wq.shape[0]), BF16)]
-        + [pltpu.SemaphoreType.DMA((3,))] * 2
+        out_specs=(VMEM_SPEC,) * 3,
+        scratch_shapes=[pltpu.SemaphoreType.DMA((3,))] * 2
         + relay_scratch(rows, group),
         compiler_params=params(1),
         name="qkv_exchange",
@@ -315,7 +314,7 @@
     )(mine, wq, wk, wv, cols_t, out_part)
 
 
-def branch_kernel(mine, wo, attn, d_attn, grads, full, attn_t, ssem, rsem):
+def branch_kernel(mine, wo, attn, d_attn, full, attn_t, ssem, rsem):
     r, e = lax.axis_index("dp"), lax.axis_index("expert")
     tok = mine.shape[0]
     half = tok // 2
@@ -361,13 +360,6 @@
     pass_near.wait()
     products(diag)
 
-    def outer(c, carry):
-        n = aligned(c, 256)
-        grads[:, n] = dot_nn(attn_t[...], full[:, n]).astype(BF16)
-        return carry
-
-    lax.fori_loop(0, mine.shape[1] // 256, outer, 0)
-
 
 def grad_branch(mine, wo, attn):
     tok, width = mine.shape
@@ -375,13 +367,12 @@
         branch_kernel,
         out_shape=(
             jax.ShapeDtypeStruct((4 * tok, wo.shape[0]), BF16),
-            jax.ShapeDtypeStruct((wo.shape[0], width), BF16),
+            jax.ShapeDtypeStruct((4 * tok, width), BF16),
+            jax.ShapeDtypeStruct((wo.shape[0], 4 * tok), BF16),
         ),
         in_specs=[VMEM_SPEC] * 3,
-        out_specs=(VMEM_SPEC, VMEM_SPEC),
+        out_specs=(VMEM_SPEC,) * 3,
         scratch_shapes=[
-            pltpu.VMEM((4 * tok, width), BF16),
-            pltpu.VMEM((wo.shape[0], 4 * tok), BF16),
             pltpu.SemaphoreType.DMA((6,)),
             pltpu.SemaphoreType.DMA((6,)),
         ],
@@ -619,9 +610,11 @@
 
 
 def dgrad_line_kernel(
-    mine, wq, wk, wv, cols_t, out_part, small, unit_rows, normal, qkv_sum, out_sum, small_out,
-    grads, blocks, dsum, dsend, drecv, opair, owork, olines, qpair, qwork, qlines,
-    small_v, first_in, piece, line_in, ssem, rsem, bsend, brecv, s1, r1, s2, r2, s3, r3, *sems,
+    mine, wq, wk, wv, cols_t, cols, out_part, small, gain,
+    normal, q_out, k_out, v_out, out_sum, small_out, gain_out,
+    qkv_sum, grads, blocks, dsum, dsend, drecv, opair, owork, olines, qpair, qwork, qlines,
+    first_in, piece, line_in, gain_v, gain_in,
+    ssem, rsem, bsend, brecv, s1, r1, s2, r2, s3, r3, s4, r4, s5, r5, *sems,
 ):
     r, e = lax.axis_index("dp"), lax.axis_index("expert")
     z, core = e // 2, e % 2
@@ -648,7 +641,8 @@
     line_peers = [(r, lax.rem(z + j, 4) * 2 + core) for j in (1, 2, 3)]
     others = [(m // 2, m % 2) for m in (6, 7, 2, 3, 4, 5, 1)]
     plane = [(r ^ a, e ^ c) for a, c in others]
-    greet(plane + line_peers)
+    owners = [(r, e ^ m) for m in range(1, 8)]
+    greet(plane + owners[1:])
     low, high = pl.ds(0, half), pl.ds(half, half)
     first_near = remote(mine.at[low], blocks.at[0, low], ssem.at[0], rsem.at[0], (near, e))
     first_far = remote(mine.at[high], blocks.at[1, high], ssem.at[1], rsem.at[1], (far, e))
@@ -656,9 +650,37 @@
     second_far = remote(mine.at[low], blocks.at[1, low], ssem.at[3], rsem.at[3], (far, e))
     pass_far = remote(blocks.at[0, low], blocks.at[2, low], ssem.at[4], rsem.at[4], (far, e))
     pass_near = remote(blocks.at[1, high], blocks.at[2, high], ssem.at[5], rsem.at[5], (near, e))
+    me = r * 2 + core
+    firsts = []
+    for i, (a, c) in enumerate(others):
+        copy = remote(small.at[(r ^ a) * 2 + (core ^ c)], first_in.at[i], s1.at[i], r1.at[i], plane[i])
+        copy.start()
+        firsts.append(copy)
     for copy in (first_near, first_far, second_near, second_far):
         copy.start()
     out_begin()
+    seconds, thirds = [], []
+
+    def small_second():
+        for copy in firsts:
+            copy.wait()
+        value = small[me]
+        for i in range(7):
+            value = value + first_in[i]
+        piece[0] = value
+        for j in range(3):
+            copy = remote(piece.at[0], line_in.at[j], s2.at[j], r2.at[j], line_peers[j])
+            copy.start()
+            seconds.append(copy)
+
+    def small_third():
+        for copy in seconds:
+            copy.wait()
+        small_out[me] = piece[0] + line_in[0] + line_in[1] + line_in[2]
+        for i in range(7):
+            copy = remote(small_out.at[me], small_out.at[me], s3.at[i], r3.at[i], plane[i])
+            copy.start()
+            thirds.append(copy)
 
     def outer(p, src):
         def step(c, carry):
@@ -672,20 +694,19 @@
 
     def inner(p, src, start):
         def chunk(c, carry):
-            t = aligned(c, tok)
-            x = src[t, :]
+            n = aligned(c, 128)
             value = (
-                dot_nt(x[:, :qg], wq[:, aligned(p, qg)])
-                + dot_nt(x[:, qg : qg + kg], wk[:, aligned(p, kg)])
-                + dot_nt(x[:, qg + kg :], wv[:, aligned(p, kg)])
+                dot_nt(src[:, :qg], wq[n, aligned(p, qg)])
+                + dot_nt(src[:, qg : qg + kg], wk[n, aligned(p, kg)])
+                + dot_nt(src[:, qg + kg :], wv[n, aligned(p, kg)])
             )
             if start:
-                dsum[t, :] = value
+                dsum[:, n] = value
             else:
-                dsum[t, :] = dsum[t, :] + value
+                dsum[:, n] = dsum[:, n] + value
             return carry
 
-        lax.fori_loop(0, 4, chunk, 0)
+        lax.fori_loop(0, width // 128, chunk, 0)
 
     def begin(i):
         units[i][0]()
@@ -699,6 +720,7 @@
     outer(r, mine)
     begin(0)
     out_first()
+    small_second()
     inner(r, mine, True)
     first_near.wait()
     pass_far.start()
@@ -707,6 +729,7 @@
     out_inner(0)
     first(0)
     out_inner(1)
+    small_third()
     onward(0, 0)
     second_near.wait()
     outer(near, blocks.at[0])
@@ -734,79 +757,77 @@
         copy = remote(dsend.at[i], drecv.at[i], bsend.at[i], brecv.at[i], (p, e))
         copy.start()
         back.append(copy)
+    scale = 1.0 / gain[:, aligned(r, width)]
+    gain_v[...] = jnp.broadcast_to(
+        jnp.sum(dsum[...] * cols[...].astype(F32), axis=0, keepdims=True) * scale, gain_v.shape
+    )
+    fourths = []
+    for i in range(7):
+        copy = remote(gain_v, gain_in.at[i], s4.at[i], r4.at[i], owners[i])
+        copy.start()
+        fourths.append(copy)
     onward(1, 2)
     onward(2, 0)
     first(3)
     onward(2, 1)
+    for copy in fourths:
+        copy.wait()
+    value = gain_v[...]
+    for i in range(7):
+        value = value + gain_in[i]
+    gain_out[r] = value
+    fifths = []
+    for i, p in enumerate(peers):
+        copy = remote(gain_out.at[r], gain_out.at[r], s5.at[i], r5.at[i], (p, e))
+        copy.start()
+        fifths.append(copy)
     onward(3, 0)
     normal[:, aligned(r, width)] = dsum[aligned(r, tok), :]
     for i, p in enumerate(peers):
         back[i].wait()
         normal[:, aligned(p, width)] = drecv[i].astype(F32)
-    at_small = small.shape[1]
-    small_v[:, :at_small] = small[...]
-    small_v[:, at_small:] = jnp.zeros((8, 8, 128), F32)
-    per = 4 * width // 8
-    for i in range(8):
-        n = slice(i * per, (i + 1) * per)
-        gain = jnp.sum(normal[:, n] * unit_rows[:, n], axis=0, keepdims=True)
-        for c in range(per // 128):
-            small_v[i, at_small + c : at_small + c + 1] = gain[:, c * 128 : (c + 1) * 128]
-    firsts = []
-    for i, (a, c) in enumerate(others):
-        copy = remote(
-            small_v.at[(r ^ a) * 2 + (core ^ c)], first_in.at[i], s1.at[i], r1.at[i], plane[i]
-        )
-        copy.start()
-        firsts.append(copy)
     onward(2, 2)
     onward(3, 1)
-    for copy in firsts:
+    out_last()
+
+    def close(i):
+        p = order[i]
+        units[i][3]()
+        q_out[:, aligned(p, qg)] = qkv_sum[p, :, :qg]
+        k_out[:, aligned(p, kg)] = qkv_sum[p, :, qg : qg + kg]
+        v_out[:, aligned(p, kg)] = qkv_sum[p, :, qg + kg :]
+
+    close(0)
+    close(1)
+    onward(3, 2)
+    close(2)
+    close(3)
+    for copy in fifths + thirds:
         copy.wait()
-    me = r * 2 + core
-    value = small_v[me]
-    for i in range(7):
-        value = value + first_in[i]
-    piece[0] = value
-    seconds = []
-    for j in range(3):
-        copy = remote(piece.at[0], line_in.at[j], s2.at[j], r2.at[j], line_peers[j])
-        copy.start()
-        seconds.append(copy)
-    onward(3, 2)
-    for copy in seconds:
-        copy.wait()
-    small_out[me] = piece[0] + line_in[0] + line_in[1] + line_in[2]
-    thirds = []
-    for i in range(7):
-        copy = remote(small_out.at[me], small_out.at[me], s3.at[i], r3.at[i], plane[i])
-        copy.start()
-        thirds.append(copy)
-    out_last()
-    for unit in units:
-        unit[3]()
-    for copy in thirds:
-        copy.wait()
-
-
-def grad_qkv_line(mine, wq, wk, wv, cols_t, out_part, small, unit_rows):
+
+
+def grad_qkv_line(mine, wq, wk, wv, cols_t, cols, out_part, small, gain):
     rows, group = mine.shape
     tok = rows // 4
     width = wq.shape[0]
     piece = (width // 8, group)
     out_piece = out_part.shape[1:]
-    small_shape = (8, small.shape[1] + 8, 128)
+    small_piece = small.shape[1:]
     return pl.pallas_call(
         dgrad_line_kernel,
         out_shape=(
             jax.ShapeDtypeStruct((tok, 4 * width), F32),
-            jax.ShapeDtypeStruct((4, *piece), F32),
+            jax.ShapeDtypeStruct((width // 8, wq.shape[1]), F32),
+            jax.ShapeDtypeStruct((width // 8, wk.shape[1]), F32),
+            jax.ShapeDtypeStruct((width // 8, wv.shape[1]), F32),
             jax.ShapeDtypeStruct(out_piece, F32),
-            jax.ShapeDtypeStruct(small_shape, F32),
+            jax.ShapeDtypeStruct(small.shape, F32),
+            jax.ShapeDtypeStruct((4, 8, width), F32),
         ),
-        in_specs=[VMEM_SPEC] * 8,
-        out_specs=(VMEM_SPEC,) * 4,
+        in_specs=[VMEM_SPEC] * 9,
+        out_specs=(VMEM_SPEC,) * 7,
         scratch_shapes=[
+            pltpu.VMEM((4, *piece), F32),
             pltpu.VMEM((8, 4, *piece), BF16),
             pltpu.VMEM((3, rows, group), BF16),
             pltpu.VMEM((rows, width), F32),
@@ -818,14 +839,15 @@
             pltpu.VMEM((4, 4, *piece), BF16),
             pltpu.VMEM((4, 3, *piece), BF16),
             pltpu.VMEM((4, 2, 4, *piece), BF16),
-            pltpu.VMEM(small_shape, F32),
-            pltpu.VMEM((7, *small_shape[1:]), F32),
-            pltpu.VMEM((1, *small_shape[1:]), F32),
-            pltpu.VMEM((3, *small_shape[1:]), F32),
+            pltpu.VMEM((7, *small_piece), F32),
+            pltpu.VMEM((1, *small_piece), F32),
+            pltpu.VMEM((3, *small_piece), F32),
+            pltpu.VMEM((8, width), F32),
+            pltpu.VMEM((7, 8, width), F32),
             pltpu.SemaphoreType.DMA((6,)),
             pltpu.SemaphoreType.DMA((6,)),
         ]
-        + [pltpu.SemaphoreType.DMA((n,)) for n in (3, 3, 7, 7, 3, 3, 7, 7)]
+        + [pltpu.SemaphoreType.DMA((n,)) for n in (3, 3, 7, 7, 3, 3, 7, 7, 7, 7, 3, 3)]
         + LINE_SEMS
         + [
             pltpu.SemaphoreType.DMA((4, 4)),
@@ -835,7 +857,7 @@
         ],
         compiler_params=params(10),
         name="dqkv_line_exchange",
-    )(mine, wq, wk, wv, cols_t, out_part, small, unit_rows)
+    )(mine, wq, wk, wv, cols_t, cols, out_part, small, gain)
 
 
 def masks_of(block, own_length, slots, prompt_block, prompt_len, column, keys):
@@ -903,7 +925,8 @@
 
 
 def attention_bwd_kernel(
-    prompt_len, lengths, lin, queries, d_attn, gain, cos, sin, keys, values, d_lin, d_keys, d_values, d_gain
+    prompt_len, lengths, lin, queries, d_attn, gain, cos, sin, keys, values, attn_t, d_branch,
+    d_lin, d_keys, d_values, d_gain, out_part,
 ):
     block = pl.program_id(0)
     slots = lin.shape[0]
@@ -942,36 +965,53 @@
         d_lin[:, part] = (
             inverse * (weighted - unit * jnp.mean(weighted * unit, axis=-1, keepdims=True))
         ).astype(BF16)
+        if h % 4 == 3:
+            n = slice(h // 4 * 256, h // 4 * 256 + 256)
+            out_part[:, n] = dot_nn(attn_t[...], d_branch[:, n]).astype(BF16)
     d_keys[0] = key_total * scale
     d_values[0] = value_total
     d_gain[0] = gain_total
 
 
-def attention_bwd(lengths, lin, queries, d_attn, gain, cos, sin, keys, values, prompt_len):
+def attention_bwd(
+    lengths, lin, queries, d_attn, gain, cos, sin, keys, values, attn_t, d_branch, prompt_len
+):
     blocks, total_keys, head = keys.shape
     slots = lin.shape[0] // blocks
     width = lin.shape[1] - 2 * head
     row = pl.BlockSpec((slots, width), lambda i, *_: (i, 0))
     table = pl.BlockSpec((1, slots, head), lambda i, *_: (i, 0, 0))
     kv = pl.BlockSpec((1, total_keys, head), lambda i, *_: (i, 0, 0))
+    step = d_branch.shape[1] // blocks
     one = pl.BlockSpec((1, head), lambda i, *_: (0, 0))
     return pl.pallas_call(
         functools.partial(attention_bwd_kernel, prompt_len),
         grid_spec=pltpu.PrefetchScalarGridSpec(
             num_scalar_prefetch=1,
             grid=(blocks,),
-            in_specs=[row, row, row, one, table, table, kv, kv],
-            out_specs=[row, kv, kv, pl.BlockSpec((1, 8, head), lambda i, *_: (i, 0, 0))],
+            in_specs=[row, row, row, one, table, table, kv, kv]
+            + [
+                pl.BlockSpec(attn_t.shape, lambda i, *_: (0, 0)),
+                pl.BlockSpec((d_branch.shape[0], step), lambda i, *_: (0, i)),
+            ],
+            out_specs=[
+                row,
+                kv,
+                kv,
+                pl.BlockSpec((1, 8, head), lambda i, *_: (i, 0, 0)),
+                pl.BlockSpec((attn_t.shape[0], step), lambda i, *_: (0, i)),
+            ],
         ),
         out_shape=(
             jax.ShapeDtypeStruct((lin.shape[0], width), BF16),
             jax.ShapeDtypeStruct(keys.shape, F32),
             jax.ShapeDtypeStruct(values.shape, F32),
             jax.ShapeDtypeStruct((blocks, 8, head), F32),
+            jax.ShapeDtypeStruct((attn_t.shape[0], d_branch.shape[1]), BF16),
         ),
         compiler_params=params(),
         name="attention_bwd",
-    )(lengths, lin, queries, d_attn, gain, cos, sin, keys, values)
+    )(lengths, lin, queries, d_attn, gain, cos, sin, keys, values, attn_t, d_branch)
 
 
 def partner(shard, axis, bit):
@@ -1084,11 +1124,13 @@
         plane[k, 5].wait_recv()
         hand(k, 3, diag)
 
+    who = (r, near, far, diag)
+
     def ready(k):
         before(k)
         for i in range(4):
             pairs[k, i].wait_recv()
-        group(k, order[k])
+        group(k, [(k * 4 + i, who[i] * 8 + order[k] * 2) for i in range(4)])
 
     issue(0)
     passes(0)
@@ -1122,6 +1164,10 @@
             copy.wait_send()
 
 
+def group_rows(k, room):
+    return pl.ds(k * 4 * room, 4 * room)
+
+
 GATHER_SEMS = [
     pltpu.SemaphoreType.DMA((4, 2)),
     pltpu.SemaphoreType.DMA((4,)),
@@ -1132,8 +1178,7 @@
 ]
 
 
-def selector(pos, source, room):
-    row = pos[source]
+def selector(row, room):
     ids = lax.broadcasted_iota(jnp.int32, (room, row.shape[1]), 0).astype(F32)
     return jnp.where(ids == row, 1.0, 0.0).astype(BF16)
 
@@ -1151,28 +1196,36 @@
 
 
 def experts_fwd_kernel(
-    mine, wg, wu, wd, pos, x_out, y_out, g_out, u_out, o_out, hid_out, gate_out,
+    capacity, mine, wg, wu, wd, pos, x_out, y_out, g_out, u_out, o_out, hid_out, gate_out,
     buf, wg_v, wu_v, wd_v, x_v, y_v, g_v, u_v, o_v, hid_v, gate_v, local, *sems,
 ):
     model = wg.shape[0]
     rows_in = mine.shape[0]
-    room = x_v.shape[0] // 8
+    room = x_v.shape[0] // 4
     me = lax.axis_index("dp") * 8 + lax.axis_index("expert")
     loads = start_all(
         [
-            pltpu.make_async_copy(a, b, local.at[i])
+            pltpu.make_async_copy(a, b, local.at[0, i])
             for i, (a, b) in enumerate(((wg, wg_v), (wu, wu_v), (wd, wd_v)))
         ]
     )
-    leaving = []
-
-    def leave(b, pairs):
-        leaving.extend(
-            start_all([pltpu.make_async_copy(v, o.at[b], local.at[i]) for i, v, o in pairs])
+    leaving = {g: [] for g in range(4)}
+
+    def leave(g, pairs):
+        kept = group_rows(g, room)
+        leaving[g].extend(
+            start_all(
+                [
+                    pltpu.make_async_copy(v, o.at[kept], local.at[g % 2, i])
+                    for i, v, o in pairs
+                ]
+            )
         )
 
-    def before(k):
+    def before(g):
         wait_all(loads)
+        if g > 0:
+            wait_all(leaving[g - 1])
 
     upto = jnp.where(
         lax.broadcasted_iota(jnp.int32, (rows_in, rows_in), 0)
@@ -1182,45 +1235,40 @@
     ).astype(BF16)
     is_me = jnp.where(lax.broadcasted_iota(jnp.int32, (16, 128), 1) == me, 1.0, 0.0).astype(BF16)
 
-    def pick_one(b, j):
-        s = j // 2 * 8 + b * 2 + j % 2
-        rows = aligned(j, room)
-        named = jnp.where(dot_nt(is_me, buf[s, :, model:]) > 0.0, 1.0, 0.0)
-        place = dot_nn(named.astype(BF16), upto) * named - 1.0
-        pos[s] = place[:1]
-        ids = lax.broadcasted_iota(jnp.int32, (room, rows_in), 0).astype(F32)
-        sel = jnp.where(ids == place[:1], 1.0, 0.0).astype(BF16)
+    def pick(at, s, start):
+        rows = pl.ds(start, room)
+        sels = []
+        for c in range(2):
+            named = jnp.where(dot_nt(is_me, buf[s + c, :, model:]) > 0.0, 1.0, 0.0)
+            place = (dot_nn(named.astype(BF16), upto) + (c * capacity)) * named - 1.0
+            pos[at * 2 + c] = place[:1]
+            sels.append(selector(place[:1], room))
         for c in range(4):
             n = slice(c * model // 4, (c + 1) * model // 4)
-            x_v[rows, n] = dot_nn(sel, buf[s, :, n]).astype(BF16)
-        extra = dot_nn(sel, buf[s, :, model:])
+            x_v[rows, n] = (dot_nn(sels[0], buf[s, :, n]) + dot_nn(sels[1], buf[s + 1, :, n])).astype(BF16)
+        extra = dot_nn(sels[0], buf[s, :, model:]) + dot_nn(sels[1], buf[s + 1, :, model:])
         lane = lax.broadcasted_iota(jnp.int32, extra.shape, 1)
         hit = (lane == me) | (lane == me + 64)
         gate = jnp.sum(jnp.where(hit, extra, 0.0), axis=-1, keepdims=True)
         gate_v[rows, :] = jnp.broadcast_to(gate, extra.shape)
 
-    def group(k, b):
-        wait_all(leaving)
-
-        def four(j, carry):
-            for i in range(4):
-                pick_one(b, j * 4 + i)
-            return carry
-
-        lax.fori_loop(0, 2, four, 0)
-        leave(b, ((0, x_v, x_out), (1, gate_v, gate_out)))
+    def group(g, blocks):
+        for j, (at, s) in enumerate(blocks):
+            pick(at, s, j * room)
+        leave(g, ((0, x_v, x_out), (1, gate_v, gate_out)))
 
         def first(c, carry):
             n = aligned(c, 256)
-            g = dot_nn(x_v[...], wg_v[:, n])
-            u = dot_nn(x_v[...], wu_v[:, n])
-            g_v[:, n] = g.astype(BF16)
+            x = x_v[...]
+            gates = dot_nn(x, wg_v[:, n])
+            u = dot_nn(x, wu_v[:, n])
+            g_v[:, n] = gates.astype(BF16)
             u_v[:, n] = u.astype(BF16)
-            hid_v[:, n] = (g / (1.0 + jnp.exp(-g)) * u).astype(BF16)
+            hid_v[:, n] = (gates / (1.0 + jnp.exp(-gates)) * u).astype(BF16)
             return carry
 
         lax.fori_loop(0, wg.shape[1] // 256, first, 0)
-        leave(b, ((2, g_v, g_out), (3, u_v, u_out), (4, hid_v, hid_out)))
+        leave(g, ((2, g_v, g_out), (3, u_v, u_out), (4, hid_v, hid_out)))
 
         def second(c, carry):
             n = aligned(c, 256)
@@ -1230,19 +1278,23 @@
             return carry
 
         lax.fori_loop(0, model // 256, second, 0)
-        leave(b, ((5, o_v, o_out), (6, y_v, y_out)))
-
-    gather_world(mine, buf, *sems, before, group, lambda: wait_all(leaving))
-
-
-def experts_fwd(mine, wg, wu, wd, room):
+        leave(g, ((5, o_v, o_out), (6, y_v, y_out)))
+
+    def done():
+        for copies in leaving.values():
+            wait_all(copies)
+
+    gather_world(mine, buf, *sems, before, group, done)
+
+
+def experts_fwd(mine, wg, wu, wd, capacity, room):
     rows, width = mine.shape
     model, ff = wg.shape
-    group = 8 * room
-    wide = jax.ShapeDtypeStruct((4, group, model), BF16)
-    thin = jax.ShapeDtypeStruct((4, group, ff), BF16)
+    group = 4 * room
+    wide = jax.ShapeDtypeStruct((16 * room, model), BF16)
+    thin = jax.ShapeDtypeStruct((16 * room, ff), BF16)
     pos, x, y, g, u, o, hidden, gates = pl.pallas_call(
-        experts_fwd_kernel,
+        functools.partial(experts_fwd_kernel, capacity),
         out_shape=(
             jax.ShapeDtypeStruct((32, 1, rows), F32),
             wide,
@@ -1251,7 +1303,7 @@
             thin,
             wide,
             thin,
-            jax.ShapeDtypeStruct((4, group, 128), F32),
+            jax.ShapeDtypeStruct((16 * room, 128), F32),
         ),
         in_specs=[VMEM_SPEC, ANY_SPEC, ANY_SPEC, ANY_SPEC],
         out_specs=(VMEM_SPEC,) + (ANY_SPEC,) * 7,
@@ -1267,7 +1319,7 @@
             pltpu.VMEM((group, model), BF16),
             pltpu.VMEM((group, ff), BF16),
             pltpu.VMEM((group, 128), F32),
-            pltpu.SemaphoreType.DMA((7,)),
+            pltpu.SemaphoreType.DMA((2, 7)),
         ]
         + GATHER_SEMS,
         compiler_params=params(6),
@@ -1282,23 +1334,21 @@
     local, ins, *sems,
 ):
     model, ff = wg.shape
-    room = d_copy_v.shape[0] // 8
-    z = lax.axis_index("expert") // 2
+    room = d_copy_v.shape[0] // 4
     me = lax.axis_index("dp") * 8 + lax.axis_index("expert")
     loads = start_all(
         [
-            pltpu.make_async_copy(a, b, local.at[i])
+            pltpu.make_async_copy(a, b, local.at[0, i])
             for i, (a, b) in enumerate(((wg, wg_v), (wu, wu_v), (wd, wd_v)))
         ]
     )
-    leaving, coming = [], {}
-
-    def fetch(k):
-        b = plane_order(z)[k]
-        at = k % 2
-        coming[k] = start_all(
+    leaving, coming = {g: [] for g in range(4)}, {}
+
+    def fetch(g):
+        kept = group_rows(g, room)
+        coming[g] = start_all(
             [
-                pltpu.make_async_copy(a.at[b], v.at[at], ins.at[at, i])
+                pltpu.make_async_copy(a.at[kept], v.at[g % 2], ins.at[g % 2, i])
                 for i, (a, v) in enumerate(
                     ((g_in, g_v), (u_in, u_v), (o_in, o_v), (gate_in, gate_v))
                 )
@@ -1307,57 +1357,58 @@
 
     fetch(0)
 
-    def leave(b, pairs):
-        leaving.extend(
-            start_all([pltpu.make_async_copy(v, o.at[b], local.at[i]) for i, v, o in pairs])
+    def leave(g, pairs):
+        kept = group_rows(g, room)
+        leaving[g].extend(
+            start_all(
+                [
+                    pltpu.make_async_copy(v, o.at[kept], local.at[g % 2, i])
+                    for i, v, o in pairs
+                ]
+            )
         )
 
-    def before(k):
+    def before(g):
         wait_all(loads)
-        wait_all(coming[k])
-        if k < 3:
-            fetch(k + 1)
-
-    def pick_one(b, j, at):
-        s = j // 2 * 8 + b * 2 + j % 2
-        rows = aligned(j, room)
-        sel = selector(pos, s, room)
-        gate = gate_v[at, rows, :1]
+        wait_all(coming[g])
+        if g + 1 < 4:
+            fetch(g + 1)
+        if g > 0:
+            wait_all(leaving[g - 1])
+
+    def pick(slot, at, s, start):
+        rows = pl.ds(start, room)
+        sels = [selector(pos[at * 2 + c], room) for c in range(2)]
+        gate = gate_v[slot, rows, :1]
         inner = jnp.zeros((room, 1), F32)
         for c in range(4):
             n = slice(c * model // 4, (c + 1) * model // 4)
-            picked = dot_nn(sel, buf[s, :, n])
+            picked = dot_nn(sels[0], buf[s, :, n]) + dot_nn(sels[1], buf[s + 1, :, n])
             d_copy_v[rows, n] = (gate * picked).astype(BF16)
-            inner = inner + jnp.sum(picked * o_v[at, rows, n].astype(F32), axis=-1, keepdims=True)
+            inner = inner + jnp.sum(picked * o_v[slot, rows, n].astype(F32), axis=-1, keepdims=True)
         top = inner.astype(BF16).astype(F32)
         rest = inner - top
         lane = lax.broadcasted_iota(jnp.int32, (room, 128), 1)
         extra = jnp.where(lane == me, top, 0.0) + jnp.where(lane == me + 64, rest, 0.0)
         y_v[rows, model:] = extra.astype(BF16)
 
-    def group(k, b):
-        at = k % 2
-        wait_all(leaving)
-
-        def four(j, carry):
-            for i in range(4):
-                pick_one(b, j * 4 + i, at)
-            return carry
-
-        lax.fori_loop(0, 2, four, 0)
-        leave(b, ((0, d_copy_v, d_copy_out),))
+    def group(g, blocks):
+        slot = g % 2
+        for j, (at, s) in enumerate(blocks):
+            pick(slot, at, s, j * room)
+        leave(g, ((0, d_copy_v, d_copy_out),))
 
         def third(c, carry):
             n = aligned(c, 256)
             d_hidden = dot_nt(d_copy_v[...], wd_v[n, :])
-            g, u = g_v[at, :, n].astype(F32), u_v[at, :, n].astype(F32)
-            s = 1.0 / (1.0 + jnp.exp(-g))
-            dg_v[:, n] = (d_hidden * u * s * (1.0 + g * (1.0 - s))).astype(BF16)
-            du_v[:, n] = (d_hidden * g * s).astype(BF16)
+            gates, u = g_v[slot, :, n].astype(F32), u_v[slot, :, n].astype(F32)
+            s = 1.0 / (1.0 + jnp.exp(-gates))
+            dg_v[:, n] = (d_hidden * u * s * (1.0 + gates * (1.0 - s))).astype(BF16)
+            du_v[:, n] = (d_hidden * gates * s).astype(BF16)
             return carry
 
         lax.fori_loop(0, ff // 256, third, 0)
-        leave(b, ((1, dg_v, dg_out), (2, du_v, du_out)))
+        leave(g, ((1, dg_v, dg_out), (2, du_v, du_out)))
 
         def fourth(c, carry):
             n = aligned(c, 256)
@@ -1367,22 +1418,26 @@
             return carry
 
         lax.fori_loop(0, model // 256, fourth, 0)
-        leave(b, ((3, y_v, y_out),))
-
-    gather_world(mine, buf, *sems, before, group, lambda: wait_all(leaving))
+        leave(g, ((3, y_v, y_out),))
+
+    def done():
+        for copies in leaving.values():
+            wait_all(copies)
+
+    gather_world(mine, buf, *sems, before, group, done)
 
 
 def experts_bwd(mine, pos, kept, wg, wu, wd, room):
     rows, width = mine.shape
     model, ff = wg.shape
-    group = 8 * room
+    group = 4 * room
     return pl.pallas_call(
         experts_bwd_kernel,
         out_shape=(
-            jax.ShapeDtypeStruct((4, group, model + 128), BF16),
-            jax.ShapeDtypeStruct((4, group, model), BF16),
-            jax.ShapeDtypeStruct((4, group, ff), BF16),
-            jax.ShapeDtypeStruct((4, group, ff), BF16),
+            jax.ShapeDtypeStruct((16 * room, model + 128), BF16),
+            jax.ShapeDtypeStruct((16 * room, model), BF16),
+            jax.ShapeDtypeStruct((16 * room, ff), BF16),
+            jax.ShapeDtypeStruct((16 * room, ff), BF16),
         ),
         in_specs=[VMEM_SPEC, VMEM_SPEC] + [ANY_SPEC] * 7,
         out_specs=(ANY_SPEC,) * 4,
@@ -1399,7 +1454,7 @@
             pltpu.VMEM((group, model), BF16),
             pltpu.VMEM((group, ff), BF16),
             pltpu.VMEM((group, ff), BF16),
-            pltpu.SemaphoreType.DMA((4,)),
+            pltpu.SemaphoreType.DMA((2, 4)),
             pltpu.SemaphoreType.DMA((2, 4)),
         ]
         + GATHER_SEMS,
@@ -1414,12 +1469,10 @@
 ):
     r, e, z, core, near, far, greeted = world(True)
     rows, width = out.shape
-    room = y.shape[2]
+    room = y.shape[1]
     half = rows // 2
     low, high = pl.ds(0, half), pl.ds(half, half)
     order = plane_order(z)[::-1]
-    diag = r ^ 3
-    who = [r, near, far, diag]
     body_width = width // 512 * 512
     greet(greeted)
 
@@ -1432,19 +1485,21 @@
         if width > body_width:
             fn(pl.ds(body_width, width - body_width))
 
-    def scattered(sel, q, b, c, n):
-        return dot_tn(sel, y[b, q * 2 + c, :, n])
+    def scattered(sel, k, i, n):
+        return dot_tn(sel, y[(3 - k) * 4 + i, :, n])
+
+    def select(k, i, c):
+        return selector(pos[((3 - k) * 4 + i) * 2 + c], room)
 
     pairs, halves, fulls, moves = {}, {}, {}, []
 
     def stage_a(k):
-        b = order[k]
         for i in (3, 1, 2, 0):
             at = k * 4 + i
-            sel = selector(pos, who[i] * 8 + b * 2 + (1 - core), room)
+            sel = select(k, i, 1 - core)
 
             def fill(n):
-                psend[at, :, n] = scattered(sel, who[i], b, 1 - core, n).astype(BF16)
+                psend[at, :, n] = scattered(sel, k, i, n).astype(BF16)
 
             for_columns(fill)
             copy = remote(psend.at[at], pair.at[at], ds.at[at], dr.at[at], (r, e ^ 1))
@@ -1452,11 +1507,11 @@
             pairs[at] = copy
         for i in (3, 1, 2, 0):
             at = k * 4 + i
-            sel = selector(pos, who[i] * 8 + b * 2 + core, room)
+            sel = select(k, i, core)
             pairs[at].wait_recv()
 
             def add(n):
-                value = scattered(sel, who[i], b, core, n) + pair[at, :, n].astype(F32)
+                value = scattered(sel, k, i, n) + pair[at, :, n].astype(F32)
                 pair[at, :, n] = value.astype(BF16)
 
             for_columns(add)
@@ -1558,7 +1613,7 @@
 
 
 def sum_world(y, pos, rows, collective_id):
-    groups, per, room, width = y.shape
+    width = y.shape[-1]
 
     def blocks(n, size):
         return pltpu.VMEM((n, size, width), BF16)
@@ -1590,6 +1645,43 @@
     )(y, pos)
 
 
+def expert_grads_kernel(x, d_gate, d_up, hidden, d_copy, gate_grad, up_grad, down_grad, hidden_t):
+    @pl.when(pl.program_id(0) == 0)
+    def _():
+        hidden_t[...] = hidden[...].T
+
+    rows = x[...].T
+    gate_grad[...] = dot_nn(rows, d_gate[...])
+    up_grad[...] = dot_nn(rows, d_up[...])
+    down_grad[...] = dot_nn(hidden_t[...], d_copy[...])
+
+
+def expert_grads(x, d_gate, d_up, hidden, d_copy):
+    slots, model = x.shape
+    ff = hidden.shape[1]
+    step = 256
+    whole = pl.BlockSpec((slots, ff), lambda i: (0, 0))
+    columns = pl.BlockSpec((slots, step), lambda i: (0, i))
+    return pl.pallas_call(
+        expert_grads_kernel,
+        grid=(model // step,),
+        in_specs=[columns, whole, whole, whole, columns],
+        out_specs=[
+            pl.BlockSpec((step, ff), lambda i: (i, 0)),
+            pl.BlockSpec((step, ff), lambda i: (i, 0)),
+            pl.BlockSpec((ff, step), lambda i: (0, i)),
+        ],
+        out_shape=(
+            jax.ShapeDtypeStruct((model, ff), F32),
+            jax.ShapeDtypeStruct((model, ff), F32),
+            jax.ShapeDtypeStruct((ff, model), F32),
+        ),
+        scratch_shapes=[pltpu.VMEM((ff, slots), BF16)],
+        compiler_params=params(),
+        name="expert_grads",
+    )(x, d_gate, d_up, hidden, d_copy)
+
+
 def experts_by_all_to_all(
     mixed, state, teacher, routes, valid_slot, valid_count, router_weight, gate_weight, up_weight, down_weight,
     devices, capacity, slots_all,
@@ -1699,7 +1791,7 @@
         dtype=jnp.float32,
     )
     d_mixed = d_mixed + contract(d_logits, router_weight, 1, 1)
-    router_local = contract(mixed, d_logits, 0, 0)
+    router_local = contract(d_logits, mixed, 0, 0)
     return layer_out, d_out, d_mixed, local_square, router_local, gate_grad, up_grad, down_grad
 
 
@@ -1708,7 +1800,7 @@
     gate_weight, up_weight, down_weight, devices, capacity, slots_all,
 ):
     tok_dev, model_width = mixed.shape
-    room = -(-capacity // 16) * 16
+    room = -(-2 * capacity // 16) * 16
     expert_range = jnp.arange(devices, dtype=jnp.int32)
     logits = jnp.dot(mixed, router_weight, preferred_element_type=F32)
     chosen = jnp.any(routes[:, :, None] == expert_range[None, None], axis=1)
@@ -1719,9 +1811,9 @@
     gap = jnp.zeros((tok_dev, 64 - devices), BF16)
     payload = jnp.concatenate([mixed, gates_high, gap, gates_low, gap], axis=1)
     pos, x_rows, y_rows, kept = experts_fwd(
-        payload, gate_weight[0], up_weight[0], down_weight[0], room
-    )
-    layer_out = state + sum_world(y_rows.reshape(4, 8, room, model_width), pos, tok_dev, 8)
+        payload, gate_weight[0], up_weight[0], down_weight[0], capacity, room
+    )
+    layer_out = state + sum_world(y_rows.reshape(16, room, model_width), pos, tok_dev, 8)
     live_tokens = valid_slot.astype(F32)[:, None]
     diff = (layer_out - teacher.astype(F32)) * live_tokens
     local_square = jnp.sum(diff * diff)
@@ -1730,18 +1822,15 @@
     d_rows, d_copy, d_gate, d_up = experts_bwd(
         d_out.astype(BF16), pos, kept[:3] + kept[4:], gate_weight[0], up_weight[0], down_weight[0], room
     )
-    back = sum_world(d_rows.reshape(4, 8, room, model_width + 128), pos, tok_dev, 9)
-
-    def flat(a):
-        return a.reshape(4 * 8 * room, a.shape[-1])
-
-    down_grad = contract(flat(hidden), flat(d_copy), 0, 0)[None]
-    gate_grad = contract(flat(x_rows), flat(d_gate), 0, 0)[None]
-    up_grad = contract(flat(x_rows), flat(d_up), 0, 0)[None]
+    back = sum_world(d_rows.reshape(16, room, model_width + 128), pos, tok_dev, 9)
+
+    gate_grad, up_grad, down_grad = (
+        grad[None] for grad in expert_grads(x_rows, d_gate, d_up, hidden, d_copy)
+    )
     d_gates = back[:, model_width : model_width + devices] + back[:, model_width + 64 : model_width + 64 + devices]
     d_logits = (gates * (d_gates - jnp.sum(gates * d_gates, axis=-1, keepdims=True))).astype(BF16)
     d_mixed = back[:, :model_width] + contract(d_logits, router_weight, 1, 1)
-    router_local = contract(mixed, d_logits, 0, 0)
+    router_local = contract(d_logits, mixed, 0, 0)
     return layer_out, d_out, d_mixed, local_square, router_local, gate_grad, up_grad, down_grad
 
 
@@ -1813,7 +1902,7 @@
         [lax.dynamic_index_in_dim(cont_lengths.reshape(n_dp, n_owner), rank_owner, 1, False), column[None]]
     ).astype(jnp.int32)
 
-    lin, normed_cols_t = project_qkv(normed, query_weight, key_projection, value_projection)
+    lin, normed_cols_t, normed_cols = project_qkv(normed, query_weight, key_projection, value_projection)
     key_lin = lin[:, query_group : query_group + head_dim].reshape(n_dp, tok_dev, head_dim)
     keys_float, key_back = jax.vjp(lambda a, b: head_rope(a, b, cos, sin), key_lin, key_gain)
     keys_own = keys_float.astype(BF16)
@@ -1851,9 +1940,10 @@
     d_state_norm, d_post_gain = second_norm_back(d_mixed)
     d_state = d_out + d_state_norm
     d_branch = d_state.astype(BF16)
-    d_attended, out_part = grad_branch(d_branch, output_weight, attended)
-    d_query_lin, d_keys, d_values, gain_parts = attention_bwd(
-        lengths, lin, queries, d_attended, query_gain_row, cos, sin, all_keys, all_values, prompt_len
+    d_attended, d_branch_all, attended_t = grad_branch(d_branch, output_weight, attended)
+    d_query_lin, d_keys, d_values, gain_parts, out_part = attention_bwd(
+        lengths, lin, queries, d_attended, query_gain_row, cos, sin, all_keys, all_values,
+        attended_t, d_branch_all, prompt_len,
     )
     d_query_gain = jnp.sum(gain_parts, axis=(0, 1))
     prompt_grads = jnp.stack(
@@ -1888,23 +1978,33 @@
         small = jnp.pad(small, (0, 8 * piece_rows * 128 - small.shape[0]))
         return small.reshape(8, piece_rows, 128)
 
-    dqkv_operands = (
-        d_lin, query_weight, key_projection, value_projection, normed_cols_t,
-        out_part.reshape(n_owner, -1, model_width),
-    )
+    out_part = out_part.reshape(n_owner, -1, model_width)
+    weights = (query_weight, key_projection, value_projection)
     if by_line:
-        small = packed(small_parts)
-        unit_rows = tokens_float * lax.rsqrt(
-            jnp.mean(tokens_float * tokens_float, axis=-1, keepdims=True) + norm_eps
+
+        def line(parts):
+            flat = jnp.concatenate(parts)
+            return jnp.pad(flat, (0, model_width - flat.shape[0]))[None]
+
+        small = jnp.concatenate(
+            [router_local, d_post_gain[None], line([d_query_gain, d_key_gain]), line([local_square[None]])]
         )
-        d_normed, qkv_rows, output_grad, small_out = grad_qkv_line(*dqkv_operands, small, unit_rows)
-        input_gain_grad = small_out[:, small.shape[1] : small.shape[1] + model_width // 1024].reshape(-1)
-        small = small_out[:, : small.shape[1]]
+        small_rows = -(-small.shape[0] // 8) * 8
+        small = jnp.pad(small, ((0, small_rows - small.shape[0]), (0, 0)))
+        small = small.reshape(small_rows, 8, -1).transpose(1, 0, 2)
+        d_normed, query_grad, key_grad, value_grad, output_grad, small, input_gain_grad = grad_qkv_line(
+            d_lin, *weights, normed_cols_t, normed_cols, out_part, small, input_gain[None]
+        )
+        input_gain_grad = input_gain_grad[:, 0].reshape(-1)
+        sums = small.transpose(1, 0, 2).reshape(small_rows, model_width)
+        at = router_local.shape[0]
+        router_grad, post_gain_grad = sums[:at].T, sums[at]
+        query_gain_grad, key_gain_grad = sums[at + 1, :head_dim], sums[at + 1, head_dim : 2 * head_dim]
+        total_square = sums[at + 2, :1]
+        d_tokens_norm = first_norm_back(d_normed)[0]
     else:
-        d_normed, qkv_part, output_grad = grad_qkv(*dqkv_operands)
-    d_tokens_norm, d_input_gain = first_norm_back(d_normed)
-    tokens_grad = d_state + d_tokens_norm
-    if not by_line:
+        d_normed, qkv_part, output_grad = grad_qkv(d_lin, *weights, normed_cols_t, out_part)
+        d_tokens_norm, d_input_gain = first_norm_back(d_normed)
         small_parts.append(d_input_gain)
         by_owner = (
             qkv_part.reshape(n_dp, n_owner, rows_here, group)
@@ -1912,22 +2012,23 @@
             .reshape(n_owner, n_dp * rows_here, group)
         )
         qkv_rows, small = last_sums(by_owner, packed(small_parts))
-    qkv_rows = qkv_rows.reshape(n_dp, rows_here, group)
-
-    def columns(start, size):
-        return qkv_rows[:, :, start : start + size].transpose(1, 0, 2).reshape(rows_here, n_dp * size)
-
-    query_grad = columns(0, query_group)
-    key_grad = columns(query_group, head_dim)
-    value_grad = columns(query_group + head_dim, head_dim)
-    small = small.reshape(-1)
-    starts = [0]
-    for a in small_parts:
-        starts.append(starts[-1] + a.size)
-    sums = [small[i:j].reshape(a.shape) for a, i, j in zip(small_parts, starts, starts[1:])]
-    router_grad, post_gain_grad, query_gain_grad, key_gain_grad, total_square = sums[:5]
-    if not by_line:
-        input_gain_grad = sums[5]
+        qkv_rows = qkv_rows.reshape(n_dp, rows_here, group)
+
+        def columns(start, size):
+            part = qkv_rows[:, :, start : start + size]
+            return part.transpose(1, 0, 2).reshape(rows_here, n_dp * size)
+
+        query_grad = columns(0, query_group)
+        key_grad = columns(query_group, head_dim)
+        value_grad = columns(query_group + head_dim, head_dim)
+        small = small.reshape(-1)
+        starts = [0]
+        for a in small_parts:
+            starts.append(starts[-1] + a.size)
+        sums = [small[i:j].reshape(a.shape) for a, i, j in zip(small_parts, starts, starts[1:])]
+        router_grad, post_gain_grad, query_gain_grad, key_gain_grad, total_square, input_gain_grad = sums
+        router_grad = router_grad.T
+    tokens_grad = d_state + d_tokens_norm
     loss = total_square[0] / (valid_count * model_width)
     return (
         layer_out,

time: 814 us -> 790 us (0.971)
  matrix products: 37.9 us -> 3.84 us
  Pallas kernels: 707 us -> 728 us
    dot_general x5 -> x2, matrix products: 37.4 us -> 3.43 us  [contract(): lax.dot_general(left_side, right_side, (((left_dim,), (right_dim,)), ((),...]
    pallas_call x2 -> x3, Pallas kernels: 219 us -> 238 us  [the longest x1 112 us: experts_fwd(): pl.pallas_call(functools.partial(experts_fwd_kernel, capacity), out_shape...]
  transfers between devices with their start and end apart: 2 -> 2, of which waited for: 0 -> 0; matrix products, arithmetic and copies ran while one was open for 5% -> 1% of each run, Pallas kernels for 0% -> 3%
where the time goes in v5:
time: 790 us; the launch traced here: 781 us
  Pallas kernels  728 us (92%)
  other arithmetic  26.2 us (3%)
  local copies, waits for them, and re-layouts  18.1 us (2%)
    pallas_call x2, Pallas kernels, sum_world(): pl.pallas_call(sum_world_kernel, out_shape=jax.ShapeDtypeStruct((rows, wi...  210 us
    pallas_call x1, Pallas kernels, experts_fwd(): pl.pallas_call(functools.partial(experts_fwd_kernel, capacity), out_shape...  112 us
    pallas_call x1, Pallas kernels, grad_qkv_line(): pl.pallas_call(dgrad_line_kernel, out_shape=(jax.ShapeDtypeStruct((tok, 4...  104 us
    pallas_call x1, Pallas kernels, experts_bwd(): pl.pallas_call(experts_bwd_kernel, out_shape=(jax.ShapeDtypeStruct((16 *...  102 us
    pallas_call x1, Pallas kernels, project_qkv(): pl.pallas_call(functools.partial(qkv_kernel, tok), out_shape=(jax.ShapeDt...  72.7 us
    pallas_call x1, Pallas kernels, project_out(): pl.pallas_call(out_kernel, out_shape=jax.ShapeDtypeStruct((tok, wo.shape[...  29.6 us
    pallas_call x1, Pallas kernels, grad_branch(): pl.pallas_call(branch_kernel, out_shape=(jax.ShapeDtypeStruct((4 * tok, w...  29.6 us
    pallas_call x1, Pallas kernels, attention_bwd(): pl.pallas_call(functools.partial(attention_bwd_kernel, prompt_len), grid_...  28.5 us
  transfers between devices with their start and end apart: 2, of which 0 were waited for; matrix products, arithmetic and copies ran while one was open for 1% of the time, Pallas kernels for 3%

profile of v5, /device:TPU:8, one launch (start us, length us, event | category | flops | bytes accessed | tf_op | source)
XLA Modules:
  0.0 780.6 jit_solution(12145733689309127003)
XLA Ops:
  0.7 1.3 fusion.2
  2.0 2.1 fusion.4.normed
  4.2 72.7 %qkv_exchange.1 = (f32[640,1280]{1,0:T(8,128)}, bf16[512,640]{1,0:T(8,128)(2,1)}, bf16[640,512]{1,0:T(8,128)(2,1)}) custom-call(bf16[160,2048]{1,0:T(8,128)(2,1)} %fusion.4.normed, bf16[512,4096]{1,0:T(8,128)(2,1)} %wq.3, bf16[512,512]{1,0:T(8,128)(2,1)} %wk.3, bf16[512,512]{1,0:T(8,128)(2,1)} %wv.3), custom_call_target="tpu_custom_call" | custom-call | tf_op jit(solution)/shard_map/qkv_exchange/pallas_call | solution.py:165
  81.0 1.3 fusion.8
  87.1 15.6 %attention_fwd.1 = (bf16[640,1024]{1,0:T(8,128)(2,1)}, bf16[640,1024]{1,0:T(8,128)(2,1)}) custom-call(s32[5]{0:T(128)} %pad_add_fusion.lengths, f32[640,1280]{1,0:T(8,128)} %get-tuple-element.50.lin, f32[1,128]{1,0:T(1,128)} %bitcast.101, f32[4,160,128]{2,1,0:T(8,128)} %get-tuple-element.104.cos, f32[4,160,128]{2,1,0:T(8,128)} %get-tuple-element.97.sin, ...), custom_call_target="tpu_custom_call" | custom-call | tf_op jit(solution)/shard_map/attention_fwd/pallas_call | solution.py:910
  102.6 29.6 %out_exchange.1 = f32[160,2048]{1,0:T(8,128)} custom-call(bf16[640,1024]{1,0:T(8,128)(2,1)} %get-tuple-element.51.attn, bf16[1024,2048]{1,0:T(8,128)(2,1)} %wo.3), custom_call_target="tpu_custom_call" | custom-call | tf_op jit(solution)/shard_map/out_exchange/pallas_call | solution.py:200
  132.2 1.6 multiply_reduce_fusion.3
  135.9 112.1 %experts_fwd.1 = (f32[32,1,160]{2,1,0:T(1,128)}, bf16[1792,2048]{1,0:T(8,128)(2,1)}, bf16[1792,2048]{1,0:T(8,128)(2,1)}, bf16[1792,768]{1,0:T(8,128)(2,1)}, bf16...) custom-call(bf16[160,2176]{1,0:T(8,128)(2,1)} %concatenate.73.mine, ...), custom_call_target="tpu_custom_call" | custom-call | tf_op jit(solution)/shard_map/experts_fwd/pallas_call | solution.py:1296
  248.0 100.2 %sum_world.2 = f32[160,2048]{1,0:T(8,128)} custom-call(bf16[16,112,2048]{2,1,0:T(8,128)(2,1)} %bitcast.71, f32[32,1,160]{2,1,0:T(1,128)} %get-tuple-element.53.pos), custom_call_target="tpu_custom_call" | custom-call | tf_op jit(solution)/shard_map/sum_world/pallas_call | solution.py:1621
  348.2 2.4 multiply_reduce_fusion
  351.9 101.6 %experts_bwd.1 = (bf16[1792,2176]{1,0:T(8,128)(2,1)}, bf16[1792,2048]{1,0:T(8,128)(2,1)}, bf16[1792,768]{1,0:T(8,128)(2,1)}, bf16[1792,768]{1,0:T(8,128)(2,1)}) custom-call(bf16[160,2048]{1,0:T(8,128)(2,1)} %fusion.11.mine, f32[32,1,160]{2,1,0:T(1,128)} %get-tuple-element.53.pos, bf16[1792,768]{1,0:T(8,128)(2,1)} %get-tuple-element.55.g_in, ...), custom_call_target="tpu_custom_call" | custom-call | tf_op jit(solution)/shard_map/experts_bwd/pallas_call | solution.py:1434
  453.4 109.5 %sum_world.3 = f32[160,2176]{1,0:T(8,128)} custom-call(bf16[16,112,2176]{2,1,0:T(8,128)(2,1)} %bitcast.70, f32[32,1,160]{2,1,0:T(1,128)} %get-tuple-element.53.pos), custom_call_target="tpu_custom_call" | custom-call | tf_op jit(solution)/shard_map/sum_world/pallas_call | solution.py:1621
  564.1 2.1 multiply_reduce_fusion.1
  566.2 1.4 fusion.20
  567.6 29.6 %branch_exchange.1 = (bf16[640,1024]{1,0:T(8,128)(2,1)}, bf16[640,2048]{1,0:T(8,128)(2,1)}, bf16[1024,640]{1,0:T(8,128)(2,1)}) custom-call(bf16[160,2048]{1,0:T(8,128)(2,1)} %get-tuple-element.92.mine, bf16[1024,2048]{1,0:T(8,128)(2,1)} %wo.3, bf16[640,1024]{1,0:T(8,128)(2,1)} %get-tuple-element.51.attn), custom_call_target="tpu_custom_call" | custom-call | tf_op jit(solution)/shard_map/branch_exchange/pallas_call | solution.py:366
  597.2 28.5 %attention_bwd.1 = (bf16[640,1024]{1,0:T(8,128)(2,1)}, f32[4,384,128]{2,1,0:T(8,128)}, f32[4,384,128]{2,1,0:T(8,128)}, f32[4,8,128]{2,1,0:T(8,128)}, bf16[1024,2048]{1,0:T(8,128)(2,1)}) custom-call(s32[5]{0:T(128)} %pad_add_fusion.lengths, f32[640,1280]{1,0:T(8,128)} %get-tuple-element.50.lin, bf16[640,1024]{1,0:T(8,128)(2,1)} %get-tuple-element.54.queries, ...), custom_call_target="tpu_custom_call" | custom-call | tf_op jit(solution)/shard_map/attention_bwd/pallas_call | solution.py:987
  630.6 24.7 %expert_grads.1 = (f32[2048,768]{1,0:T(8,128)}, f32[2048,768]{1,0:T(8,128)}, f32[768,2048]{1,0:T(8,128)}) custom-call(bf16[1792,2048]{1,0:T(8,128)(2,1)} %get-tuple-element.76.x, bf16[1792,768]{1,0:T(8,128)(2,1)} %get-tuple-element.77.d_gate, bf16[1792,768]{1,0:T(8,128)(2,1)} %get-tuple-element.78.d_up, bf16[1792,768]{1,0:T(8,128)(2,1)} %get-tuple-element.79.hidden, ...), custom_call_target="tpu_custom_call" | custom-call | tf_op jit(solution)/shard_map/expert_grads/pallas_call | solution.py:1665
  655.3 1.4 fusion.25
  659.8 1.3 pad_maximum_fusion.mine
  661.1 104.3 %dqkv_line_exchange.1 = (f32[160,2048]{1,0:T(8,128)}, f32[64,4096]{1,0:T(8,128)}, f32[64,512]{1,0:T(8,128)}, f32[64,512]{1,0:T(8,128)}, f32[128,2048]{1,0:T(8,12...) custom-call(bf16[640,1280]{1,0:T(8,128)(2,1)} %pad_maximum_fusion.mine, bf16[512,4096]{1,0:T(8,128)(2,1)} %wq.3, ...), custom_call_target="tpu_custom_call" | custom-call | tf_op jit(solution)/shard_map/dqkv_line_exchange/pallas_call | solution.py:816
  766.4 1.4 slice.142
  769.9 1.6 fusion.5
  772.2 1.4 slice.122
  774.3 1.4 fusion.1
  (123 shorter events, 27.5 us)
Async XLA Ops:
  0.6 133.4 %copy-start = (bf16[2048,32]{0,1:T(8,128)(2,1)S(1)}, bf16[2048,32]{0,1:T(8,128)(2,1)}, u32[]{:S(2)}) copy-start(bf16[2048,32]{0,1:T(8,128)(2,1)} %param.24) | copy-start | bytes 393220
  4.2 75.1 %copy-start.22 = (f32[128]{0:T(128)S(1)}, f32[128]{0:T(128)}, u32[]{:S(2)}) copy-start(f32[128]{0:T(128)} %param.31) | copy-start | bytes 1540
  78.1 2.9 copy-start.6
  81.0 1.3 copy-start.11
  81.0 1.4 copy-start.23
  81.0 3.4 copy-start.21
  82.3 3.7 collective-permute-start
  102.6 29.6 %copy-start.2 = (bf16[160,2048]{1,0:T(8,128)(2,1)S(1)}, bf16[160,2048]{1,0:T(8,128)(2,1)}, u32[]{:S(2)}) copy-start(bf16[160,2048]{1,0:T(8,128)(2,1)} %param.16) | copy-start | bytes 1966084
  132.2 1.6 copy-start.19
  134.0 1.8 copy-start.4
  248.0 100.2 %copy-start.8 = (bf16[160,2048]{1,0:T(8,128)(2,1)S(1)}, bf16[160,2048]{1,0:T(8,128)(2,1)}, u32[]{:S(2)}) copy-start(bf16[160,2048]{1,0:T(8,128)(2,1)} %param.17) | copy-start | bytes 1966084
  350.6 215.6 %copy-start.3 = (f32[160,2048]{1,0:T(8,128)}, f32[160,2048]{1,0:T(8,128)S(1)}, u32[]{:S(2)}) copy-start(f32[160,2048]{1,0:T(8,128)S(1)} %get-tuple-element.138) | copy-start | bytes 3932164
  625.7 4.9 copy-start.20
  629.9 26.8 %collective-permute-start.1 = (f32[2,128,128]{2,1,0:T(8,128)S(1)}, f32[2,128,128]{2,1,0:T(8,128)S(1)}, u32[]{:S(2)}, u32[]{:S(2)}) collective-permute-start(f32[2,128,128]{2,1,0:T(8,128)S(1)} %broadcast_select_fusion), channel_id=1, source_target_pairs={{0,1},{1,0},{2,3},{3,2},{4,5},{5,4},{6,7},{7,6},{8,9},{9,8},{10,11... | collective-permute-start | bytes 393224 | tf_op jit(solution)/shard_map/ppermute | solution.py:1018
  630.6 24.7 %copy-start.5 = (bf16[160,2048]{1,0:T(8,128)(2,1)S(1)}, bf16[160,2048]{1,0:T(8,128)(2,1)}, u32[]{:S(2)}) copy-start(bf16[160,2048]{1,0:T(8,128)(2,1)} %copy-done.4) | copy-start | bytes 1966084
  655.3 1.5 copy-start.9
  656.7 1.1 copy-start.12
  658.3 1.4 copy-start.13
  661.1 108.8 %copy-start.18 = (f32[2048]{0:T(1024)S(1)}, f32[2048]{0:T(1024)}, u32[]{:S(2)}) copy-start(f32[2048]{0:T(1024)} %param.28) | copy-start | bytes 24580
  768.8 5.5 copy-start.10
  774.3 1.4 copy-start.15
  775.7 1.7 copy-start.16
  775.7 2.3 copy-start.14
  775.7 3.3 copy-start.1
  (2 other events, 2.0 us)

commit v6 on v5

--- a/solution.py
+++ b/solution.py
@@ -42,6 +42,22 @@
         device_id=device,
         device_id_type=MESH,
     )
+
+
+def start_all(copies):
+    for copy in copies:
+        copy.start()
+    return copies
+
+
+def wait_all(copies):
+    for copy in copies:
+        copy.wait()
+    copies.clear()
+
+
+def loading(pairs, sems):
+    return [start_all([pltpu.make_async_copy(a, b, sems.at[i])]) for i, (a, b) in enumerate(pairs)]
 
 
 def aligned(index, size):
@@ -121,14 +137,18 @@
     ]
 
 
-def qkv_kernel(tok, normed, wq, wk, wv, lin, cols_t, cols, asend, arecv, *relay):
+def qkv_kernel(
+    tok, normed, wq_in, wk_in, wv_in, gain, cos, sin, lin, cols_t, cols, key_lin, keys, values,
+    wq, wk, wv, own_kv, other_kv, local, asend, arecv, ksend, krecv, *relay,
+):
     r, e = lax.axis_index("dp"), lax.axis_index("expert")
     peers = [r ^ m for m in PEER_MASKS]
     width = wq.shape[0]
     qg = wq.shape[1] // 4
     kg = wk.shape[1] // 4
     rows = cols.shape[0]
-    greet([(p, e) for p in peers])
+    loads = loading(((wq_in, wq), (wk_in, wk), (wv_in, wv)), local)
+    greet([(p, e) for p in peers] + [(r, e ^ 1)])
     first = []
     for i, p in enumerate(peers):
         copy = remote(
@@ -140,6 +160,8 @@
     cols[aligned(r, tok), :] = normed[:, aligned(r, width)]
     for copy in first:
         copy.wait()
+    for copies in loads:
+        wait_all(copies)
 
     def products(p, dst):
         def chunk(c, carry):
@@ -156,33 +178,67 @@
         cols_t[...] = cols[...].T
 
     relay_sum(r, e, products, own, lin, *relay, 32)
-
-
-def project_qkv(normed, wq, wk, wv):
+    core = e % 2
+    head = gain.shape[1]
+    prompt = tok - CMAX
+    column = 4 * prompt
+    for i in range(4):
+        rows_i = slice(i * tok, (i + 1) * tok)
+        x = lin[rows_i, qg : qg + kg]
+        key_lin[rows_i, :] = x
+        x = x * lax.rsqrt(jnp.mean(x * x, axis=-1, keepdims=True) + norm_eps) * gain[...]
+        k = (x * cos[i] + pltpu.roll(x, head // 2, 1) * sin[i]).astype(BF16)
+        v = lin[rows_i, qg + kg :].astype(BF16)
+        for n, (part, out) in enumerate(((k, keys), (v, values))):
+            own_kv[n, i * prompt : (i + 1) * prompt] = part[:prompt]
+            out[i, 2 * column :] = part[prompt:]
+    copy = remote(own_kv, other_kv, ksend.at[0], krecv.at[0], (r, e ^ 1))
+    copy.start()
+    for n, out in enumerate((keys, values)):
+        for i in range(4):
+            out[i, aligned(core, column)] = own_kv[n]
+    copy.wait()
+    for n, out in enumerate((keys, values)):
+        for i in range(4):
+            out[i, aligned(1 - core, column)] = other_kv[n]
+
+
+def project_qkv(normed, wq, wk, wv, gain, cos, sin):
     tok = normed.shape[0]
     rows = 4 * tok
     group = (wq.shape[1] + wk.shape[1] + wv.shape[1]) // 4
+    head = gain.shape[1]
+    total_keys = 8 * (tok - CMAX) + CMAX
     return pl.pallas_call(
         functools.partial(qkv_kernel, tok),
         out_shape=(
             jax.ShapeDtypeStruct((rows, group), F32),
             jax.ShapeDtypeStruct((wq.shape[0], rows), BF16),
             jax.ShapeDtypeStruct((rows, wq.shape[0]), BF16),
+            jax.ShapeDtypeStruct((rows, head), F32),
+            jax.ShapeDtypeStruct((4, total_keys, head), BF16),
+            jax.ShapeDtypeStruct((4, total_keys, head), BF16),
         ),
-        in_specs=[VMEM_SPEC] * 4,
-        out_specs=(VMEM_SPEC,) * 3,
-        scratch_shapes=[pltpu.SemaphoreType.DMA((3,))] * 2
+        in_specs=[VMEM_SPEC] + [ANY_SPEC] * 3 + [VMEM_SPEC] * 3,
+        out_specs=(VMEM_SPEC,) * 6,
+        scratch_shapes=[pltpu.VMEM(w.shape, BF16) for w in (wq, wk, wv)]
+        + [pltpu.VMEM((2, 4 * (tok - CMAX), head), BF16)] * 2
+        + [pltpu.SemaphoreType.DMA((3,))] * 3
+        + [pltpu.SemaphoreType.DMA((1,))] * 2
         + relay_scratch(rows, group),
         compiler_params=params(1),
         name="qkv_exchange",
-    )(normed, wq, wk, wv)
-
-
-def out_kernel(attn, wo, total, *relay):
+    )(normed, wq, wk, wv, gain, cos, sin)
+
+
+def out_kernel(attn_in, wo_in, total, attn, wo, local, *relay):
     r, e = lax.axis_index("dp"), lax.axis_index("expert")
     tok, width = total.shape
     step = width // 4
+    loads = loading(((attn_in, attn), (wo_in, wo)), local)
     greet([(r ^ m, e) for m in PEER_MASKS])
+    for copies in loads:
+        wait_all(copies)
 
     def products(p, dst):
         def chunk(c, carry):
@@ -200,9 +256,14 @@
     return pl.pallas_call(
         out_kernel,
         out_shape=jax.ShapeDtypeStruct((tok, wo.shape[1]), F32),
-        in_specs=[VMEM_SPEC] * 2,
+        in_specs=[ANY_SPEC] * 2,
         out_specs=VMEM_SPEC,
-        scratch_shapes=relay_scratch(tok, wo.shape[1]),
+        scratch_shapes=[
+            pltpu.VMEM(attn.shape, BF16),
+            pltpu.VMEM(wo.shape, BF16),
+            pltpu.SemaphoreType.DMA((2,)),
+        ]
+        + relay_scratch(tok, wo.shape[1]),
         compiler_params=params(2),
         name="out_exchange",
     )(attn, wo)
@@ -314,12 +375,15 @@
     )(mine, wq, wk, wv, cols_t, out_part)
 
 
-def branch_kernel(mine, wo, attn, d_attn, full, attn_t, ssem, rsem):
+def branch_kernel(
+    mine, wo_in, attn_in, d_attn, full_out, attn_t_out, wo, attn, full, attn_t, local, ssem, rsem
+):
     r, e = lax.axis_index("dp"), lax.axis_index("expert")
     tok = mine.shape[0]
     half = tok // 2
     peers = [r ^ m for m in PEER_MASKS]
     near, far, diag = r ^ 1, r ^ 2, r ^ 3
+    loads = loading(((attn_in, attn), (wo_in, wo)), local)
     greet([(p, e) for p in peers])
 
     def part(q, which):
@@ -335,7 +399,10 @@
     for copy in (first_near, first_far, second_near, second_far):
         copy.start()
     full[aligned(r, tok), :] = mine[...]
+    wait_all(loads[0])
     attn_t[...] = attn[...].T
+    leaving = start_all([pltpu.make_async_copy(attn_t, attn_t_out, local.at[0])])
+    wait_all(loads[1])
     heads = wo.shape[0]
     step = heads // 4
 
@@ -358,7 +425,9 @@
     products(far)
     pass_far.wait()
     pass_near.wait()
+    leaving += start_all([pltpu.make_async_copy(full, full_out, local.at[1])])
     products(diag)
+    wait_all(leaving)
 
 
 def grad_branch(mine, wo, attn):
@@ -370,9 +439,14 @@
             jax.ShapeDtypeStruct((4 * tok, width), BF16),
             jax.ShapeDtypeStruct((wo.shape[0], 4 * tok), BF16),
         ),
-        in_specs=[VMEM_SPEC] * 3,
-        out_specs=(VMEM_SPEC,) * 3,
+        in_specs=[VMEM_SPEC, ANY_SPEC, ANY_SPEC],
+        out_specs=(VMEM_SPEC, ANY_SPEC, ANY_SPEC),
         scratch_shapes=[
+            pltpu.VMEM(wo.shape, BF16),
+            pltpu.VMEM(attn.shape, BF16),
+            pltpu.VMEM((4 * tok, width), BF16),
+            pltpu.VMEM((wo.shape[0], 4 * tok), BF16),
+            pltpu.SemaphoreType.DMA((2,)),
             pltpu.SemaphoreType.DMA((6,)),
             pltpu.SemaphoreType.DMA((6,)),
         ],
@@ -610,9 +684,10 @@
 
 
 def dgrad_line_kernel(
-    mine, wq, wk, wv, cols_t, cols, out_part, small, gain,
+    d_q, d_keys, d_values, key_lin, cos, sin, key_gain,
+    wq_in, wk_in, wv_in, cols_t_in, cols_in, out_part_in, small, gain,
     normal, q_out, k_out, v_out, out_sum, small_out, gain_out,
-    qkv_sum, grads, blocks, dsum, dsend, drecv, opair, owork, olines, qpair, qwork, qlines,
+    mine, prompt_sum, prompt_in, ksend, krecv, wq, wk, wv, cols_t, cols, out_part, local, qkv_sum, grads, blocks, dsum, dsend, drecv, opair, owork, olines, qpair, qwork, qlines,
     first_in, piece, line_in, gain_v, gain_in,
     ssem, rsem, bsend, brecv, s1, r1, s2, r2, s3, r3, s4, r4, s5, r5, *sems,
 ):
@@ -642,7 +717,44 @@
     others = [(m // 2, m % 2) for m in (6, 7, 2, 3, 4, 5, 1)]
     plane = [(r ^ a, e ^ c) for a, c in others]
     owners = [(r, e ^ m) for m in range(1, 8)]
+    loads = loading(
+        (
+            (out_part_in, out_part), (cols_t_in, cols_t), (wq_in, wq), (wk_in, wk), (wv_in, wv),
+            (cols_in, cols),
+        ),
+        local,
+    )
+    mine[:, :qg] = d_q[...]
+    prompt = tok - CMAX
+    column = 4 * prompt
+    for n, d in enumerate((d_keys, d_values)):
+        for c in range(2):
+            part = slice(c * column, (c + 1) * column)
+            prompt_sum[c, n] = d[0, part] + d[1, part] + d[2, part] + d[3, part]
     greet(plane + owners[1:])
+    swap = remote(prompt_sum.at[1 - core], prompt_in, ksend.at[0], krecv.at[0], (r, e ^ 1))
+    swap.start()
+    swap.wait()
+    prompt_in[...] = prompt_in[...] + prompt_sum[core]
+    head = key_gain.shape[1]
+    key_gain_sum = jnp.zeros((1, head), F32)
+    for i in range(4):
+        for at, size, dk, dv in (
+            (0, prompt, prompt_in[0, i * prompt : (i + 1) * prompt], prompt_in[1, i * prompt : (i + 1) * prompt]),
+            (prompt, CMAX, d_keys[i, 2 * column :], d_values[i, 2 * column :]),
+        ):
+            t = slice(at, at + size)
+            rows_i = slice(i * tok + at, i * tok + at + size)
+            turned = dk * cos[i, t] + pltpu.roll(dk * sin[i, t], head // 2, 1)
+            x = key_lin[rows_i, :]
+            inverse = lax.rsqrt(jnp.mean(x * x, axis=-1, keepdims=True) + norm_eps)
+            unit = x * inverse
+            key_gain_sum = key_gain_sum + jnp.sum(turned * unit, axis=0, keepdims=True)
+            weighted = turned * key_gain[...]
+            mine[rows_i, qg : qg + kg] = (
+                inverse * (weighted - unit * jnp.mean(weighted * unit, axis=-1, keepdims=True))
+            ).astype(BF16)
+            mine[rows_i, qg + kg :] = dv.astype(BF16)
     low, high = pl.ds(0, half), pl.ds(half, half)
     first_near = remote(mine.at[low], blocks.at[0, low], ssem.at[0], rsem.at[0], (near, e))
     first_far = remote(mine.at[high], blocks.at[1, high], ssem.at[1], rsem.at[1], (far, e))
@@ -658,6 +770,7 @@
         firsts.append(copy)
     for copy in (first_near, first_far, second_near, second_far):
         copy.start()
+    wait_all(loads[0])
     out_begin()
     seconds, thirds = [], []
 
@@ -717,10 +830,13 @@
     def onward(i, k):
         units[i][2](k)
 
+    wait_all(loads[1])
     outer(r, mine)
     begin(0)
     out_first()
     small_second()
+    for copies in loads[2:5]:
+        wait_all(copies)
     inner(r, mine, True)
     first_near.wait()
     pass_far.start()
@@ -757,10 +873,12 @@
         copy = remote(dsend.at[i], drecv.at[i], bsend.at[i], brecv.at[i], (p, e))
         copy.start()
         back.append(copy)
+    wait_all(loads[5])
     scale = 1.0 / gain[:, aligned(r, width)]
     gain_v[...] = jnp.broadcast_to(
         jnp.sum(dsum[...] * cols[...].astype(F32), axis=0, keepdims=True) * scale, gain_v.shape
     )
+    gain_v[1:2, :head] = key_gain_sum
     fourths = []
     for i in range(7):
         copy = remote(gain_v, gain_in.at[i], s4.at[i], r4.at[i], owners[i])
@@ -806,8 +924,11 @@
         copy.wait()
 
 
-def grad_qkv_line(mine, wq, wk, wv, cols_t, cols, out_part, small, gain):
-    rows, group = mine.shape
+def grad_qkv_line(
+    d_q, d_keys, d_values, key_lin, cos, sin, key_gain, wq, wk, wv, cols_t, cols, out_part, small, gain
+):
+    rows, head = key_lin.shape
+    group = d_q.shape[1] + 2 * head
     tok = rows // 4
     width = wq.shape[0]
     piece = (width // 8, group)
@@ -824,9 +945,18 @@
             jax.ShapeDtypeStruct(small.shape, F32),
             jax.ShapeDtypeStruct((4, 8, width), F32),
         ),
-        in_specs=[VMEM_SPEC] * 9,
+        in_specs=[VMEM_SPEC] * 7 + [ANY_SPEC] * 6 + [VMEM_SPEC] * 2,
         out_specs=(VMEM_SPEC,) * 7,
         scratch_shapes=[
+            pltpu.VMEM((rows, group), BF16),
+            pltpu.VMEM((2, 2, 4 * (tok - CMAX), head), F32),
+            pltpu.VMEM((2, 4 * (tok - CMAX), head), F32),
+            pltpu.SemaphoreType.DMA((1,)),
+            pltpu.SemaphoreType.DMA((1,)),
+        ]
+        + [pltpu.VMEM(a.shape, BF16) for a in (wq, wk, wv, cols_t, cols, out_part)]
+        + [
+            pltpu.SemaphoreType.DMA((6,)),
             pltpu.VMEM((4, *piece), F32),
             pltpu.VMEM((8, 4, *piece), BF16),
             pltpu.VMEM((3, rows, group), BF16),
@@ -857,7 +987,9 @@
         ],
         compiler_params=params(10),
         name="dqkv_line_exchange",
-    )(mine, wq, wk, wv, cols_t, cols, out_part, small, gain)
+    )(
+        d_q, d_keys, d_values, key_lin, cos, sin, key_gain, wq, wk, wv, cols_t, cols, out_part, small, gain
+    )
 
 
 def masks_of(block, own_length, slots, prompt_block, prompt_len, column, keys):
@@ -1183,18 +1315,6 @@
     return jnp.where(ids == row, 1.0, 0.0).astype(BF16)
 
 
-def start_all(copies):
-    for copy in copies:
-        copy.start()
-    return copies
-
-
-def wait_all(copies):
-    for copy in copies:
-        copy.wait()
-    copies.clear()
-
-
 def experts_fwd_kernel(
     capacity, mine, wg, wu, wd, pos, x_out, y_out, g_out, u_out, o_out, hid_out, gate_out,
     buf, wg_v, wu_v, wd_v, x_v, y_v, g_v, u_v, o_v, hid_v, gate_v, local, *sems,
@@ -1464,7 +1584,7 @@
 
 
 def sum_world_kernel(
-    y, pos, out, psend, pair, half_near, half_far, full_near, full_far, lines,
+    y_in, pos, out, y, local, psend, pair, half_near, half_far, full_near, full_far, lines,
     ds, dr, hs, hr, fs, fr, zs, zr,
 ):
     r, e, z, core, near, far, greeted = world(True)
@@ -1474,6 +1594,9 @@
     low, high = pl.ds(0, half), pl.ds(half, half)
     order = plane_order(z)[::-1]
     body_width = width // 512 * 512
+    loads = loading(
+        [(y_in.at[pl.ds(12 - 4 * k, 4)], y.at[pl.ds(12 - 4 * k, 4)]) for k in range(4)], local
+    )
     greet(greeted)
 
     def for_columns(fn):
@@ -1494,6 +1617,7 @@
     pairs, halves, fulls, moves = {}, {}, {}, []
 
     def stage_a(k):
+        wait_all(loads[k])
         for i in (3, 1, 2, 0):
             at = k * 4 + i
             sel = select(k, i, 1 - core)
@@ -1621,9 +1745,11 @@
     return pl.pallas_call(
         sum_world_kernel,
         out_shape=jax.ShapeDtypeStruct((rows, width), F32),
-        in_specs=[VMEM_SPEC, VMEM_SPEC],
+        in_specs=[ANY_SPEC, VMEM_SPEC],
         out_specs=VMEM_SPEC,
         scratch_shapes=[
+            pltpu.VMEM(y.shape, BF16),
+            pltpu.SemaphoreType.DMA((4,)),
             blocks(16, rows),
             blocks(16, rows),
             blocks(4, rows // 2),
@@ -1902,23 +2028,9 @@
         [lax.dynamic_index_in_dim(cont_lengths.reshape(n_dp, n_owner), rank_owner, 1, False), column[None]]
     ).astype(jnp.int32)
 
-    lin, normed_cols_t, normed_cols = project_qkv(normed, query_weight, key_projection, value_projection)
-    key_lin = lin[:, query_group : query_group + head_dim].reshape(n_dp, tok_dev, head_dim)
-    keys_float, key_back = jax.vjp(lambda a, b: head_rope(a, b, cos, sin), key_lin, key_gain)
-    keys_own = keys_float.astype(BF16)
-    values_own = lin[:, query_group + head_dim :].reshape(n_dp, tok_dev, head_dim).astype(BF16)
-    column_kv = jnp.stack([keys_own[:, :prompt_block], values_own[:, :prompt_block]]).reshape(
-        2, half_prompt, head_dim
-    )
-    other_kv = partner(column_kv, "expert", 0)
-    full_kv = jnp.where(
-        first_column,
-        jnp.concatenate([column_kv, other_kv], axis=1),
-        jnp.concatenate([other_kv, column_kv], axis=1),
-    )
-    spread = jnp.broadcast_to(full_kv[:, None], (2, n_dp, prompt_len, head_dim))
-    all_keys = jnp.concatenate([spread[0], keys_own[:, prompt_block:]], axis=1)
-    all_values = jnp.concatenate([spread[1], values_own[:, prompt_block:]], axis=1)
+    lin, normed_cols_t, normed_cols, key_lin, all_keys, all_values = project_qkv(
+        normed, query_weight, key_projection, value_projection, key_gain[None], cos, sin
+    )
     query_gain_row = query_gain[None]
     queries, attended = attention_fwd(
         lengths, lin, query_gain_row, cos, sin, all_keys, all_values, prompt_len
@@ -1946,29 +2058,8 @@
         attended_t, d_branch_all, prompt_len,
     )
     d_query_gain = jnp.sum(gain_parts, axis=(0, 1))
-    prompt_grads = jnp.stack(
-        [jnp.sum(d_keys[:, :prompt_len], axis=0), jnp.sum(d_values[:, :prompt_len], axis=0)]
-    )
-    mine_part = jnp.where(first_column, prompt_grads[:, :half_prompt], prompt_grads[:, half_prompt:])
-    their_part = jnp.where(first_column, prompt_grads[:, half_prompt:], prompt_grads[:, :half_prompt])
-    own_prompt = (mine_part + partner(their_part, "expert", 0)).reshape(
-        2, n_dp, prompt_block, head_dim
-    )
-    d_key_post = jnp.concatenate([own_prompt[0], d_keys[:, prompt_len:]], axis=1)
-    d_value_lin = jnp.concatenate([own_prompt[1], d_values[:, prompt_len:]], axis=1)
-    d_key_float, d_key_gain = key_back(d_key_post)
-    rows = n_dp * tok_dev
-    d_lin = jnp.concatenate(
-        [
-            d_query_lin,
-            d_key_float.astype(BF16).reshape(rows, head_dim),
-            d_value_lin.astype(BF16).reshape(rows, head_dim),
-        ],
-        axis=1,
-    )
-    small_parts = [router_local, d_post_gain, d_query_gain, d_key_gain, local_square[None]]
     width = query_weight.shape[0]
-    group = d_lin.shape[1]
+    group = query_group + 2 * head_dim
     rows_here = width // n_owner
     by_line = n_dp == 4 and n_owner == 8
 
@@ -1987,22 +2078,48 @@
             return jnp.pad(flat, (0, model_width - flat.shape[0]))[None]
 
         small = jnp.concatenate(
-            [router_local, d_post_gain[None], line([d_query_gain, d_key_gain]), line([local_square[None]])]
+            [router_local, d_post_gain[None], line([d_query_gain]), line([local_square[None]])]
         )
         small_rows = -(-small.shape[0] // 8) * 8
         small = jnp.pad(small, ((0, small_rows - small.shape[0]), (0, 0)))
         small = small.reshape(small_rows, 8, -1).transpose(1, 0, 2)
         d_normed, query_grad, key_grad, value_grad, output_grad, small, input_gain_grad = grad_qkv_line(
-            d_lin, *weights, normed_cols_t, normed_cols, out_part, small, input_gain[None]
+            d_query_lin, d_keys, d_values, key_lin, cos, sin, key_gain[None],
+            *weights, normed_cols_t, normed_cols, out_part, small, input_gain[None],
         )
+        key_gain_grad = jnp.sum(input_gain_grad[:, 1, :head_dim], axis=0)
         input_gain_grad = input_gain_grad[:, 0].reshape(-1)
         sums = small.transpose(1, 0, 2).reshape(small_rows, model_width)
         at = router_local.shape[0]
         router_grad, post_gain_grad = sums[:at].T, sums[at]
-        query_gain_grad, key_gain_grad = sums[at + 1, :head_dim], sums[at + 1, head_dim : 2 * head_dim]
+        query_gain_grad = sums[at + 1, :head_dim]
         total_square = sums[at + 2, :1]
         d_tokens_norm = first_norm_back(d_normed)[0]
     else:
+        _, key_back = jax.vjp(
+            lambda a, b: head_rope(a, b, cos, sin), key_lin.reshape(n_dp, tok_dev, head_dim), key_gain
+        )
+        prompt_grads = jnp.stack(
+            [jnp.sum(d_keys[:, :prompt_len], axis=0), jnp.sum(d_values[:, :prompt_len], axis=0)]
+        )
+        mine_part = jnp.where(first_column, prompt_grads[:, :half_prompt], prompt_grads[:, half_prompt:])
+        their_part = jnp.where(first_column, prompt_grads[:, half_prompt:], prompt_grads[:, :half_prompt])
+        own_prompt = (mine_part + partner(their_part, "expert", 0)).reshape(
+            2, n_dp, prompt_block, head_dim
+        )
+        d_key_post = jnp.concatenate([own_prompt[0], d_keys[:, prompt_len:]], axis=1)
+        d_value_lin = jnp.concatenate([own_prompt[1], d_values[:, prompt_len:]], axis=1)
+        d_key_float, d_key_gain = key_back(d_key_post)
+        rows = n_dp * tok_dev
+        d_lin = jnp.concatenate(
+            [
+                d_query_lin,
+                d_key_float.astype(BF16).reshape(rows, head_dim),
+                d_value_lin.astype(BF16).reshape(rows, head_dim),
+            ],
+            axis=1,
+        )
+        small_parts = [router_local, d_post_gain, d_query_gain, d_key_gain, local_square[None]]
         d_normed, qkv_part, output_grad = grad_qkv(d_lin, *weights, normed_cols_t, out_part)
         d_tokens_norm, d_input_gain = first_norm_back(d_normed)
         small_parts.append(d_input_gain)

time: 790 us -> 774 us (0.980)
  Pallas kernels: 728 us -> 718 us
  transfers between devices with their start and end apart: 2 -> 0, of which waited for: 0 -> 0; matrix products, arithmetic and copies ran while one was open for 1% -> 0% of each run, Pallas kernels for 3% -> 0%
where the time goes in v6:
time: 774 us; the launch traced here: 764 us
  Pallas kernels  718 us (93%)
  other arithmetic  22.8 us (3%)
  local copies, waits for them, and re-layouts  15 us (2%)
    pallas_call x2, Pallas kernels, sum_world(): pl.pallas_call(sum_world_kernel, out_shape=jax.ShapeDtypeStruct((rows, wi...  205 us
    pallas_call x1, Pallas kernels, experts_fwd(): pl.pallas_call(functools.partial(experts_fwd_kernel, capacity), out_shape...  112 us
    pallas_call x1, Pallas kernels, grad_qkv_line(): pl.pallas_call(dgrad_line_kernel, out_shape=(jax.ShapeDtypeStruct((tok, 4...  103 us
    pallas_call x1, Pallas kernels, experts_bwd(): pl.pallas_call(experts_bwd_kernel, out_shape=(jax.ShapeDtypeStruct((16 *...  101 us
    pallas_call x1, Pallas kernels, project_qkv(): pl.pallas_call(functools.partial(qkv_kernel, tok), out_shape=(jax.ShapeDt...  73.1 us
    pallas_call x1, Pallas kernels, attention_bwd(): pl.pallas_call(functools.partial(attention_bwd_kernel, prompt_len), grid_...  28.6 us
    pallas_call x1, Pallas kernels, project_out(): pl.pallas_call(out_kernel, out_shape=jax.ShapeDtypeStruct((tok, wo.shape[...  27.9 us
    pallas_call x1, Pallas kernels, grad_branch(): pl.pallas_call(branch_kernel, out_shape=(jax.ShapeDtypeStruct((4 * tok, w...  26.5 us

profile of v6, /device:TPU:8, one launch (start us, length us, event | category | flops | bytes accessed | tf_op | source)
XLA Modules:
  0.0 763.8 jit_solution(9113162802683701931)
XLA Ops:
  0.7 1.3 dynamic_slice.8
  4.1 1.3 fusion.2
  5.4 2.1 fusion.4.normed
  10.0 73.1 %qkv_exchange.1 = (f32[640,1280]{1,0:T(8,128)}, bf16[512,640]{1,0:T(8,128)(2,1)}, bf16[640,512]{1,0:T(8,128)(2,1)}, f32[640,128]{1,0:T(8,128)}, bf16[4,384,128]{...) custom-call(bf16[160,2048]{1,0:T(8,128)(2,1)} %fusion.4.normed, bf16[512,4096]{1,0:T(8,128)(2,1)} %wq_in.3, ...), custom_call_target="tpu_custom_call" | custom-call | tf_op jit(solution)/shard_map/qkv_exchange/pallas_call | solution.py:212
  83.1 15.6 %attention_fwd.1 = (bf16[640,1024]{1,0:T(8,128)(2,1)}, bf16[640,1024]{1,0:T(8,128)(2,1)}) custom-call(s32[5]{0:T(128)} %pad_add_fusion.lengths, f32[640,1280]{1,0:T(8,128)} %get-tuple-element.53.lin, f32[1,128]{1,0:T(1,128)} %bitcast.65, f32[4,160,128]{2,1,0:T(8,128)} %get-tuple-element.109.cos, f32[4,160,128]{2,1,0:T(8,128)} %get-tuple-element.110.sin, ...), custom_call_target="tpu_custom_call" | custom-call | tf_op jit(solution)/shard_map/attention_fwd/pallas_call | solution.py:1042
  98.7 27.9 %out_exchange.1 = f32[160,2048]{1,0:T(8,128)} custom-call(bf16[640,1024]{1,0:T(8,128)(2,1)} %get-tuple-element.56.attn_in, bf16[1024,2048]{1,0:T(8,128)(2,1)} %wo_in.3), custom_call_target="tpu_custom_call" | custom-call | tf_op jit(solution)/shard_map/out_exchange/pallas_call | solution.py:256
  126.6 1.6 multiply_reduce_fusion.3
  130.8 112.5 %experts_fwd.1 = (f32[32,1,160]{2,1,0:T(1,128)}, bf16[1792,2048]{1,0:T(8,128)(2,1)}, bf16[1792,2048]{1,0:T(8,128)(2,1)}, bf16[1792,768]{1,0:T(8,128)(2,1)}, bf16...) custom-call(bf16[160,2176]{1,0:T(8,128)(2,1)} %concatenate.18.mine, ...), custom_call_target="tpu_custom_call" | custom-call | tf_op jit(solution)/shard_map/experts_fwd/pallas_call | solution.py:1416
  243.4 98.0 %sum_world.2 = f32[160,2048]{1,0:T(8,128)} custom-call(bf16[16,112,2048]{2,1,0:T(8,128)(2,1)} %bitcast.49, f32[32,1,160]{2,1,0:T(1,128)} %get-tuple-element.58.pos), custom_call_target="tpu_custom_call" | custom-call | tf_op jit(solution)/shard_map/sum_world/pallas_call | solution.py:1745
  341.4 2.5 multiply_reduce_fusion
  345.2 2.2 fusion.7.mine
  347.4 101.5 %experts_bwd.1 = (bf16[1792,2176]{1,0:T(8,128)(2,1)}, bf16[1792,2048]{1,0:T(8,128)(2,1)}, bf16[1792,768]{1,0:T(8,128)(2,1)}, bf16[1792,768]{1,0:T(8,128)(2,1)}) custom-call(bf16[160,2048]{1,0:T(8,128)(2,1)} %fusion.7.mine, f32[32,1,160]{2,1,0:T(1,128)} %get-tuple-element.58.pos, bf16[1792,768]{1,0:T(8,128)(2,1)} %get-tuple-element.60.g_in, ...), custom_call_target="tpu_custom_call" | custom-call | tf_op jit(solution)/shard_map/experts_bwd/pallas_call | solution.py:1554
  448.9 106.7 %sum_world.3 = f32[160,2176]{1,0:T(8,128)} custom-call(bf16[16,112,2176]{2,1,0:T(8,128)(2,1)} %bitcast.48, f32[32,1,160]{2,1,0:T(1,128)} %get-tuple-element.58.pos), custom_call_target="tpu_custom_call" | custom-call | tf_op jit(solution)/shard_map/sum_world/pallas_call | solution.py:1745
  556.8 2.1 multiply_reduce_fusion.1
  559.0 1.9 fusion.14
  560.8 26.5 %branch_exchange.1 = (bf16[640,1024]{1,0:T(8,128)(2,1)}, bf16[640,2048]{1,0:T(8,128)(2,1)}, bf16[1024,640]{1,0:T(8,128)(2,1)}) custom-call(bf16[160,2048]{1,0:T(8,128)(2,1)} %get-tuple-element.95.mine, bf16[1024,2048]{1,0:T(8,128)(2,1)} %wo_in.3, bf16[640,1024]{1,0:T(8,128)(2,1)} %get-tuple-element.56.attn_in), custom_call_target="tpu_custom_call" | custom-call | tf_op jit(solution)/shard_map/branch_exchange/pallas_call | solution.py:435
  587.3 28.6 %attention_bwd.1 = (bf16[640,1024]{1,0:T(8,128)(2,1)}, f32[4,384,128]{2,1,0:T(8,128)}, f32[4,384,128]{2,1,0:T(8,128)}, f32[4,8,128]{2,1,0:T(8,128)}, bf16[1024,2048]{1,0:T(8,128)(2,1)}) custom-call(s32[5]{0:T(128)} %pad_add_fusion.lengths, f32[640,1280]{1,0:T(8,128)} %get-tuple-element.53.lin, bf16[640,1024]{1,0:T(8,128)(2,1)} %get-tuple-element.59.queries, ...), custom_call_target="tpu_custom_call" | custom-call | tf_op jit(solution)/shard_map/attention_bwd/pallas_call | solution.py:1119
  617.3 1.3 fusion.17
  619.5 103.4 %dqkv_line_exchange.1 = (f32[160,2048]{1,0:T(8,128)}, f32[64,4096]{1,0:T(8,128)}, f32[64,512]{1,0:T(8,128)}, f32[64,512]{1,0:T(8,128)}, f32[128,2048]{1,0:T(8,12...) custom-call(bf16[640,1024]{1,0:T(8,128)(2,1)} %get-tuple-element.68.d_q, f32[4,384,128]{2,1,0:T(8,128)} %get-tuple-element.69.d_keys, ...), custom_call_target="tpu_custom_call" | custom-call | tf_op jit(solution)/shard_map/dqkv_line_exchange/pallas_call | solution.py:937
  726.0 1.6 fusion.5
  727.6 1.4 fusion.1
  729.8 24.6 %expert_grads.1 = (f32[2048,768]{1,0:T(8,128)}, f32[2048,768]{1,0:T(8,128)}, f32[768,2048]{1,0:T(8,128)}) custom-call(bf16[1792,2048]{1,0:T(8,128)(2,1)} %get-tuple-element.82.x, bf16[1792,768]{1,0:T(8,128)(2,1)} %get-tuple-element.83.d_gate, bf16[1792,768]{1,0:T(8,128)(2,1)} %get-tuple-element.84.d_up, bf16[1792,768]{1,0:T(8,128)(2,1)} %get-tuple-element.85.hidden, ...), custom_call_target="tpu_custom_call" | custom-call | tf_op jit(solution)/shard_map/expert_grads/pallas_call | solution.py:1791
  754.4 1.5 slice.37
  757.7 1.2 slice_reduce_fusion
  (80 shorter events, 19.6 us)
Async XLA Ops:
  0.6 128.4 %copy-start = (bf16[2048,32]{0,1:T(8,128)(2,1)S(1)}, bf16[2048,32]{0,1:T(8,128)(2,1)}, u32[]{:S(2)}) copy-start(bf16[2048,32]{0,1:T(8,128)(2,1)} %param.24) | copy-start | bytes 393220
  98.7 27.9 %copy-start.2 = (bf16[160,2048]{1,0:T(8,128)(2,1)S(1)}, bf16[160,2048]{1,0:T(8,128)(2,1)}, u32[]{:S(2)}) copy-start(bf16[160,2048]{1,0:T(8,128)(2,1)} %param.16) | copy-start | bytes 1966084
  126.6 1.6 copy-start.17
  128.2 0.7 copy-start.18
  128.4 2.5 copy-start.4
  243.3 98.0 %copy-start.6 = (bf16[160,2048]{1,0:T(8,128)(2,1)S(1)}, bf16[160,2048]{1,0:T(8,128)(2,1)}, u32[]{:S(2)}) copy-start(bf16[160,2048]{1,0:T(8,128)(2,1)} %param.17) | copy-start | bytes 1966084
  341.3 2.5 copy-start.19
  343.8 215.1 %copy-start.3 = (f32[160,2048]{1,0:T(8,128)}, f32[160,2048]{1,0:T(8,128)S(1)}, u32[]{:S(2)}) copy-start(f32[160,2048]{1,0:T(8,128)S(1)} %get-tuple-element.126) | copy-start | bytes 3932164
  556.8 2.2 copy-start.7
  587.3 30.0 %copy-start.5 = (bf16[160,2048]{1,0:T(8,128)(2,1)S(1)}, bf16[160,2048]{1,0:T(8,128)(2,1)}, u32[]{:S(2)}) copy-start(bf16[160,2048]{1,0:T(8,128)(2,1)} %copy-done.4) | copy-start | bytes 1966084
  619.5 106.5 %copy-start.14 = (f32[2048]{0:T(1024)S(1)}, f32[2048]{0:T(1024)}, u32[]{:S(2)}) copy-start(f32[2048]{0:T(1024)} %param.28) | copy-start | bytes 24580
  722.9 4.7 copy-start.8
  722.9 4.7 copy-start.9
  724.1 0.7 copy-start.13
  727.6 1.4 copy-start.10
  729.8 29.2 %copy-start.12 = (f32[64,4096]{1,0:T(8,128)S(1)}, f32[64,4096]{1,0:T(8,128)}, u32[]{:S(2)}) copy-start(f32[64,4096]{1,0:T(8,128)} %get-tuple-element.129) | copy-start | bytes 3145732
  754.4 5.5 copy-start.16
  754.4 6.2 copy-start.15
  758.9 2.3 copy-start.11
  758.9 3.3 copy-start.1

commit v7 on v6

--- a/solution.py
+++ b/solution.py
@@ -1012,9 +1012,9 @@
     block = pl.program_id(0)
     slots = lin.shape[0]
     head = gain.shape[1]
-    allowed = masks_of(
-        block, lengths[block], slots, slots - CMAX, prompt_len, lengths[4], keys.shape[1]
-    )
+    e = lax.axis_index("expert")
+    own_length = lengths[block * lax.axis_size("expert") + e]
+    allowed = masks_of(block, own_length, slots, slots - CMAX, prompt_len, e % 2, keys.shape[1])
     scale = head ** (-0.5)
     k, v = keys[0], values[0]
     c, s, g = cos[0], sin[0], gain[...]
@@ -1063,9 +1063,9 @@
     block = pl.program_id(0)
     slots = lin.shape[0]
     head = gain.shape[1]
-    allowed = masks_of(
-        block, lengths[block], slots, slots - CMAX, prompt_len, lengths[4], keys.shape[1]
-    )
+    e = lax.axis_index("expert")
+    own_length = lengths[block * lax.axis_size("expert") + e]
+    allowed = masks_of(block, own_length, slots, slots - CMAX, prompt_len, e % 2, keys.shape[1])
     scale = head ** (-0.5)
     k, v = keys[0], values[0]
     c, s, g = cos[0], sin[0], gain[...]
@@ -1181,12 +1181,39 @@
     return r, e, z, core, near, far, devices
 
 
-def gather_world(mine, buf, zs, zr, ps, pr, ds, dr, before, group, done):
+def everyone():
+    me = lax.axis_index("dp") * 8 + lax.axis_index("expert")
+    return me, [lax.rem(me + j, 32) for j in range(1, 32)]
+
+
+def scatter_rows(rows, rows_in, ss, rs):
+    me, others = everyone()
+    copies = start_all(
+        [
+            remote(rows.at[d], rows_in.at[me], ss.at[j], rs.at[j], (d // 8, lax.rem(d, 8)))
+            for j, d in enumerate(others)
+        ]
+    )
+    rows_in[me] = rows[me]
+    return copies
+
+
+def greet_everyone():
+    greet([(d // 8, lax.rem(d, 8)) for d in everyone()[1]])
+
+
+ROW_SEMS = [pltpu.SemaphoreType.DMA((31,)), pltpu.SemaphoreType.DMA((31,))]
+
+
+def gather_world(mine, buf, zs, zr, ps, pr, ds, dr, before, group, done, greeting=None):
     r, e, z, core, near, far, greeted = world(True)
     half = mine.shape[0] // 2
     low, high = pl.ds(0, half), pl.ds(half, half)
     order = plane_order(z)
-    greet(greeted)
+    if greeting is None:
+        greet(greeted)
+    else:
+        greeting()
 
     def slot(q, b, c):
         return q * 8 + b * 2 + c
@@ -1316,13 +1343,12 @@
 
 
 def experts_fwd_kernel(
-    capacity, mine, wg, wu, wd, pos, x_out, y_out, g_out, u_out, o_out, hid_out, gate_out,
-    buf, wg_v, wu_v, wd_v, x_v, y_v, g_v, u_v, o_v, hid_v, gate_v, local, *sems,
+    capacity, mine, gate_rows, wg, wu, wd, pos, x_out, y_out, g_out, u_out, o_out, hid_out, gate_out,
+    buf, wg_v, wu_v, wd_v, x_v, y_v, g_v, u_v, o_v, hid_v, gate_v, gate_in, local, rs, rr, *sems,
 ):
     model = wg.shape[0]
     rows_in = mine.shape[0]
     room = x_v.shape[0] // 4
-    me = lax.axis_index("dp") * 8 + lax.axis_index("expert")
     loads = start_all(
         [
             pltpu.make_async_copy(a, b, local.at[0, i])
@@ -1330,6 +1356,11 @@
         ]
     )
     leaving = {g: [] for g in range(4)}
+    scattered = []
+
+    def greeting():
+        greet_everyone()
+        scattered.extend(scatter_rows(gate_rows, gate_in, rs, rr))
 
     def leave(g, pairs):
         kept = group_rows(g, room)
@@ -1344,6 +1375,7 @@
 
     def before(g):
         wait_all(loads)
+        wait_all(scattered)
         if g > 0:
             wait_all(leaving[g - 1])
 
@@ -1353,24 +1385,25 @@
         1.0,
         0.0,
     ).astype(BF16)
-    is_me = jnp.where(lax.broadcasted_iota(jnp.int32, (16, 128), 1) == me, 1.0, 0.0).astype(BF16)
+    line = lax.broadcasted_iota(jnp.int32, (16, rows_in), 0)
 
     def pick(at, s, start):
         rows = pl.ds(start, room)
         sels = []
+        gate = jnp.zeros((room, 1), F32)
         for c in range(2):
-            named = jnp.where(dot_nt(is_me, buf[s + c, :, model:]) > 0.0, 1.0, 0.0)
+            row = jnp.broadcast_to(gate_in[s + c], (16, rows_in))
+            named = jnp.where(row > 0.0, 1.0, 0.0)
             place = (dot_nn(named.astype(BF16), upto) + (c * capacity)) * named - 1.0
             pos[at * 2 + c] = place[:1]
             sels.append(selector(place[:1], room))
+            top = row.astype(BF16).astype(F32)
+            parts = jnp.where(line == 0, top, jnp.where(line == 1, row - top, 0.0)).astype(BF16)
+            gate = gate + jnp.sum(dot_nt(sels[c], parts), axis=-1, keepdims=True)
         for c in range(4):
             n = slice(c * model // 4, (c + 1) * model // 4)
             x_v[rows, n] = (dot_nn(sels[0], buf[s, :, n]) + dot_nn(sels[1], buf[s + 1, :, n])).astype(BF16)
-        extra = dot_nn(sels[0], buf[s, :, model:]) + dot_nn(sels[1], buf[s + 1, :, model:])
-        lane = lax.broadcasted_iota(jnp.int32, extra.shape, 1)
-        hit = (lane == me) | (lane == me + 64)
-        gate = jnp.sum(jnp.where(hit, extra, 0.0), axis=-1, keepdims=True)
-        gate_v[rows, :] = jnp.broadcast_to(gate, extra.shape)
+        gate_v[rows, :] = jnp.broadcast_to(gate, (room, 128))
 
     def group(g, blocks):
         for j, (at, s) in enumerate(blocks):
@@ -1404,10 +1437,10 @@
         for copies in leaving.values():
             wait_all(copies)
 
-    gather_world(mine, buf, *sems, before, group, done)
-
-
-def experts_fwd(mine, wg, wu, wd, capacity, room):
+    gather_world(mine, buf, *sems, before, group, done, greeting)
+
+
+def experts_fwd(mine, gate_rows, wg, wu, wd, capacity, room):
     rows, width = mine.shape
     model, ff = wg.shape
     group = 4 * room
@@ -1425,7 +1458,7 @@
             thin,
             jax.ShapeDtypeStruct((16 * room, 128), F32),
         ),
-        in_specs=[VMEM_SPEC, ANY_SPEC, ANY_SPEC, ANY_SPEC],
+        in_specs=[VMEM_SPEC, VMEM_SPEC, ANY_SPEC, ANY_SPEC, ANY_SPEC],
         out_specs=(VMEM_SPEC,) + (ANY_SPEC,) * 7,
         scratch_shapes=[
             pltpu.VMEM((32, rows, width), BF16),
@@ -1439,23 +1472,24 @@
             pltpu.VMEM((group, model), BF16),
             pltpu.VMEM((group, ff), BF16),
             pltpu.VMEM((group, 128), F32),
+            pltpu.VMEM((32, 1, rows), F32),
             pltpu.SemaphoreType.DMA((2, 7)),
         ]
+        + ROW_SEMS
         + GATHER_SEMS,
         compiler_params=params(6),
         name="experts_fwd",
-    )(mine, wg, wu, wd)
+    )(mine, gate_rows, wg, wu, wd)
     return pos, x, y, (g, u, o, hidden, gates)
 
 
 def experts_bwd_kernel(
-    mine, pos, g_in, u_in, o_in, gate_in, wg, wu, wd, y_out, d_copy_out, dg_out, du_out,
+    mine, pos, g_in, u_in, o_in, gate_in, wg, wu, wd, d_gates, y_out, d_copy_out, dg_out, du_out,
     buf, wg_v, wu_v, wd_v, g_v, u_v, o_v, gate_v, y_v, d_copy_v, dg_v, du_v,
     local, ins, *sems,
 ):
     model, ff = wg.shape
     room = d_copy_v.shape[0] // 4
-    me = lax.axis_index("dp") * 8 + lax.axis_index("expert")
     loads = start_all(
         [
             pltpu.make_async_copy(a, b, local.at[0, i])
@@ -1509,8 +1543,10 @@
         top = inner.astype(BF16).astype(F32)
         rest = inner - top
         lane = lax.broadcasted_iota(jnp.int32, (room, 128), 1)
-        extra = jnp.where(lane == me, top, 0.0) + jnp.where(lane == me + 64, rest, 0.0)
-        y_v[rows, model:] = extra.astype(BF16)
+        parts = jnp.where(lane == 0, top, jnp.where(lane == 1, rest, 0.0)).astype(BF16)
+        for c in range(2):
+            both = dot_tn(parts, sels[c])
+            d_gates[s + c] = both[:1] + both[1:2]
 
     def group(g, blocks):
         slot = g % 2
@@ -1554,13 +1590,14 @@
     return pl.pallas_call(
         experts_bwd_kernel,
         out_shape=(
-            jax.ShapeDtypeStruct((16 * room, model + 128), BF16),
+            jax.ShapeDtypeStruct((32, 1, rows), F32),
+            jax.ShapeDtypeStruct((16 * room, model), BF16),
             jax.ShapeDtypeStruct((16 * room, model), BF16),
             jax.ShapeDtypeStruct((16 * room, ff), BF16),
             jax.ShapeDtypeStruct((16 * room, ff), BF16),
         ),
         in_specs=[VMEM_SPEC, VMEM_SPEC] + [ANY_SPEC] * 7,
-        out_specs=(ANY_SPEC,) * 4,
+        out_specs=(VMEM_SPEC,) + (ANY_SPEC,) * 4,
         scratch_shapes=[
             pltpu.VMEM((32, rows, width), BF16),
             pltpu.VMEM((model, ff), BF16),
@@ -1570,7 +1607,7 @@
             pltpu.VMEM((2, group, ff), BF16),
             pltpu.VMEM((2, group, model), BF16),
             pltpu.VMEM((2, group, 128), F32),
-            pltpu.VMEM((group, model + 128), BF16),
+            pltpu.VMEM((group, model), BF16),
             pltpu.VMEM((group, model), BF16),
             pltpu.VMEM((group, ff), BF16),
             pltpu.VMEM((group, ff), BF16),
@@ -1583,10 +1620,15 @@
     )(mine, pos, *kept, wg, wu, wd)
 
 
-def sum_world_kernel(
-    y_in, pos, out, y, local, psend, pair, half_near, half_far, full_near, full_far, lines,
-    ds, dr, hs, hr, fs, fr, zs, zr,
-):
+def sum_world_kernel(with_rows, *refs):
+    if with_rows:
+        y_in, pos, rows_given, out, rows_out, *refs, rs, rr = refs
+    else:
+        y_in, pos, out, *refs = refs
+    (
+        y, local, psend, pair, half_near, half_far, full_near, full_far, lines,
+        ds, dr, hs, hr, fs, fr, zs, zr,
+    ) = refs
     r, e, z, core, near, far, greeted = world(True)
     rows, width = out.shape
     room = y.shape[1]
@@ -1597,7 +1639,11 @@
     loads = loading(
         [(y_in.at[pl.ds(12 - 4 * k, 4)], y.at[pl.ds(12 - 4 * k, 4)]) for k in range(4)], local
     )
-    greet(greeted)
+    if with_rows:
+        greet_everyone()
+        scattering = scatter_rows(rows_given, rows_out, rs, rr)
+    else:
+        greet(greeted)
 
     def for_columns(fn):
         def step(c, carry):
@@ -1735,18 +1781,23 @@
         def _():
             copy.wait_send()
 
-
-def sum_world(y, pos, rows, collective_id):
+    if with_rows:
+        wait_all(scattering)
+
+
+def sum_world(y, pos, rows, collective_id, given=None):
     width = y.shape[-1]
 
     def blocks(n, size):
         return pltpu.VMEM((n, size, width), BF16)
 
+    extra = () if given is None else (given,)
     return pl.pallas_call(
-        sum_world_kernel,
-        out_shape=jax.ShapeDtypeStruct((rows, width), F32),
-        in_specs=[ANY_SPEC, VMEM_SPEC],
-        out_specs=VMEM_SPEC,
+        functools.partial(sum_world_kernel, len(extra) > 0),
+        out_shape=(jax.ShapeDtypeStruct((rows, width), F32),)
+        + tuple(jax.ShapeDtypeStruct(a.shape, F32) for a in extra),
+        in_specs=[ANY_SPEC, VMEM_SPEC] + [VMEM_SPEC] * len(extra),
+        out_specs=(VMEM_SPEC,) * (1 + len(extra)),
         scratch_shapes=[
             pltpu.VMEM(y.shape, BF16),
             pltpu.SemaphoreType.DMA((4,)),
@@ -1765,10 +1816,11 @@
             pltpu.SemaphoreType.DMA((4, 2)),
             pltpu.SemaphoreType.DMA((2, 4)),
             pltpu.SemaphoreType.DMA((2, 4)),
-        ],
+        ]
+        + (ROW_SEMS if extra else []),
         compiler_params=params(collective_id),
         name="sum_world",
-    )(y, pos)
+    )(y, pos, *extra)
 
 
 def expert_grads_kernel(x, d_gate, d_up, hidden, d_copy, gate_grad, up_grad, down_grad, hidden_t):
@@ -1932,30 +1984,27 @@
     chosen = jnp.any(routes[:, :, None] == expert_range[None, None], axis=1)
     gates = jax.nn.softmax(jnp.where(chosen, logits, -jnp.inf), axis=-1)
     live_gates = jnp.where(valid_slot[:, None], gates, 0.0)
-    gates_high = live_gates.astype(BF16)
-    gates_low = (live_gates - gates_high.astype(F32)).astype(BF16)
-    gap = jnp.zeros((tok_dev, 64 - devices), BF16)
-    payload = jnp.concatenate([mixed, gates_high, gap, gates_low, gap], axis=1)
+    gate_rows = live_gates.T[:, None]
     pos, x_rows, y_rows, kept = experts_fwd(
-        payload, gate_weight[0], up_weight[0], down_weight[0], capacity, room
-    )
-    layer_out = state + sum_world(y_rows.reshape(16, room, model_width), pos, tok_dev, 8)
+        mixed, gate_rows, gate_weight[0], up_weight[0], down_weight[0], capacity, room
+    )
+    layer_out = state + sum_world(y_rows.reshape(16, room, model_width), pos, tok_dev, 8)[0]
     live_tokens = valid_slot.astype(F32)[:, None]
     diff = (layer_out - teacher.astype(F32)) * live_tokens
     local_square = jnp.sum(diff * diff)
     d_out = 2.0 * slots_all * diff / valid_count
     hidden = kept[3]
-    d_rows, d_copy, d_gate, d_up = experts_bwd(
+    d_gates, d_rows, d_copy, d_gate, d_up = experts_bwd(
         d_out.astype(BF16), pos, kept[:3] + kept[4:], gate_weight[0], up_weight[0], down_weight[0], room
     )
-    back = sum_world(d_rows.reshape(16, room, model_width + 128), pos, tok_dev, 9)
+    back, d_gates = sum_world(d_rows.reshape(16, room, model_width), pos, tok_dev, 9, d_gates)
+    d_gates = d_gates[:, 0].T
 
     gate_grad, up_grad, down_grad = (
         grad[None] for grad in expert_grads(x_rows, d_gate, d_up, hidden, d_copy)
     )
-    d_gates = back[:, model_width : model_width + devices] + back[:, model_width + 64 : model_width + 64 + devices]
     d_logits = (gates * (d_gates - jnp.sum(gates * d_gates, axis=-1, keepdims=True))).astype(BF16)
-    d_mixed = back[:, :model_width] + contract(d_logits, router_weight, 1, 1)
+    d_mixed = back + contract(d_logits, router_weight, 1, 1)
     router_local = contract(d_logits, mixed, 0, 0)
     return layer_out, d_out, d_mixed, local_square, router_local, gate_grad, up_grad, down_grad
 
@@ -2024,16 +2073,12 @@
     cos_half, sin_half = jnp.cos(angles), jnp.sin(angles)
     cos = jnp.concatenate([cos_half, cos_half], axis=-1)
     sin = jnp.concatenate([-sin_half, sin_half], axis=-1)
-    lengths = jnp.concatenate(
-        [lax.dynamic_index_in_dim(cont_lengths.reshape(n_dp, n_owner), rank_owner, 1, False), column[None]]
-    ).astype(jnp.int32)
-
     lin, normed_cols_t, normed_cols, key_lin, all_keys, all_values = project_qkv(
         normed, query_weight, key_projection, value_projection, key_gain[None], cos, sin
     )
     query_gain_row = query_gain[None]
     queries, attended = attention_fwd(
-        lengths, lin, query_gain_row, cos, sin, all_keys, all_values, prompt_len
+        cont_lengths, lin, query_gain_row, cos, sin, all_keys, all_values, prompt_len
     )
     state = tokens_float + project_out(attended, output_weight)
     mixed_float, second_norm_back = jax.vjp(root_mean_scale, state, post_gain)
@@ -2054,7 +2099,7 @@
     d_branch = d_state.astype(BF16)
     d_attended, d_branch_all, attended_t = grad_branch(d_branch, output_weight, attended)
     d_query_lin, d_keys, d_values, gain_parts, out_part = attention_bwd(
-        lengths, lin, queries, d_attended, query_gain_row, cos, sin, all_keys, all_values,
+        cont_lengths, lin, queries, d_attended, query_gain_row, cos, sin, all_keys, all_values,
         attended_t, d_branch_all, prompt_len,
     )
     d_query_gain = jnp.sum(gain_parts, axis=(0, 1))

time: 774 us -> 765 us (0.988)
  no operation moved by 1% of the time
where the time goes in v7:
time: 765 us; the launch traced here: 754 us
  Pallas kernels  713 us (93%)
  other arithmetic  21.5 us (3%)
  local copies, waits for them, and re-layouts  13.6 us (2%)
    pallas_call x2, Pallas kernels, sum_world(): pl.pallas_call(functools.partial(sum_world_kernel, len(extra) > 0), out_s...  201 us
    pallas_call x1, Pallas kernels, experts_fwd(): pl.pallas_call(functools.partial(experts_fwd_kernel, capacity), out_shape...  108 us
    pallas_call x1, Pallas kernels, experts_bwd(): pl.pallas_call(experts_bwd_kernel, out_shape=(jax.ShapeDtypeStruct((32, 1...  104 us
    pallas_call x1, Pallas kernels, grad_qkv_line(): pl.pallas_call(dgrad_line_kernel, out_shape=(jax.ShapeDtypeStruct((tok, 4...  103 us
    pallas_call x1, Pallas kernels, project_qkv(): pl.pallas_call(functools.partial(qkv_kernel, tok), out_shape=(jax.ShapeDt...  73.2 us
    pallas_call x1, Pallas kernels, attention_bwd(): pl.pallas_call(functools.partial(attention_bwd_kernel, prompt_len), grid_...  28.6 us
    pallas_call x1, Pallas kernels, project_out(): pl.pallas_call(out_kernel, out_shape=jax.ShapeDtypeStruct((tok, wo.shape[...  27.9 us
    pallas_call x1, Pallas kernels, grad_branch(): pl.pallas_call(branch_kernel, out_shape=(jax.ShapeDtypeStruct((4 * tok, w...  26.6 us

profile of v7, /device:TPU:8, one launch (start us, length us, event | category | flops | bytes accessed | tf_op | source)
XLA Modules:
  0.0 754.3 jit_solution(8833299584950663080)
XLA Ops:
  0.7 1.3 dynamic_slice.3
  2.6 1.3 fusion.2
  3.9 2.1 fusion.4.normed
  6.2 1.2 fusion.8
  8.5 73.2 %qkv_exchange.1 = (f32[640,1280]{1,0:T(8,128)}, bf16[512,640]{1,0:T(8,128)(2,1)}, bf16[640,512]{1,0:T(8,128)(2,1)}, f32[640,128]{1,0:T(8,128)}, bf16[4,384,128]{...) custom-call(bf16[160,2048]{1,0:T(8,128)(2,1)} %fusion.4.normed, bf16[512,4096]{1,0:T(8,128)(2,1)} %wq_in.3, ...), custom_call_target="tpu_custom_call" | custom-call | tf_op jit(solution)/shard_map/qkv_exchange/pallas_call | solution.py:212
  81.7 15.6 %attention_fwd.1 = (bf16[640,1024]{1,0:T(8,128)(2,1)}, bf16[640,1024]{1,0:T(8,128)(2,1)}) custom-call(s32[32]{0:T(128)} %lengths.3, f32[640,1280]{1,0:T(8,128)} %get-tuple-element.56.lin, f32[1,128]{1,0:T(1,128)} %bitcast.81, f32[4,160,128]{2,1,0:T(8,128)} %get-tuple-element.113.cos, f32[4,160,128]{2,1,0:T(8,128)} %get-tuple-element.114.sin, ...), custom_call_target="tpu_custom_call" | custom-call | tf_op jit(solution)/shard_map/attention_fwd/pallas_call | solution.py:1042
  97.2 27.9 %out_exchange.1 = f32[160,2048]{1,0:T(8,128)} custom-call(bf16[640,1024]{1,0:T(8,128)(2,1)} %get-tuple-element.59.attn_in, bf16[1024,2048]{1,0:T(8,128)(2,1)} %wo_in.3), custom_call_target="tpu_custom_call" | custom-call | tf_op jit(solution)/shard_map/out_exchange/pallas_call | solution.py:256
  125.1 1.6 multiply_reduce_fusion.3
  128.5 108.2 %experts_fwd.1 = (f32[32,1,160]{2,1,0:T(1,128)}, bf16[1792,2048]{1,0:T(8,128)(2,1)}, bf16[1792,2048]{1,0:T(8,128)(2,1)}, bf16[1792,768]{1,0:T(8,128)(2,1)}, bf16...) custom-call(bf16[160,2048]{1,0:T(8,128)(2,1)} %copy-done.4, ...), custom_call_target="tpu_custom_call" | custom-call | tf_op jit(solution)/shard_map/experts_fwd/pallas_call | solution.py:1449
  236.7 100.9 %sum_world.2 = f32[160,2048]{1,0:T(8,128)} custom-call(bf16[16,112,2048]{2,1,0:T(8,128)(2,1)} %bitcast.65, f32[32,1,160]{2,1,0:T(1,128)} %get-tuple-element.61.refs_1_.pos), custom_call_target="tpu_custom_call" | custom-call | tf_op jit(solution)/shard_map/sum_world/pallas_call | solution.py:1795
  337.7 2.5 multiply_reduce_fusion
  341.6 2.2 fusion.7.mine
  343.7 104.2 %experts_bwd.1 = (f32[32,1,160]{2,1,0:T(1,128)}, bf16[1792,2048]{1,0:T(8,128)(2,1)}, bf16[1792,2048]{1,0:T(8,128)(2,1)}, bf16[1792,768]{1,0:T(8,128)(2,1)}, bf16[1792,768]{1,0:T(8,128)(2,1)}) custom-call(bf16[160,2048]{1,0:T(8,128)(2,1)} %fusion.7.mine, f32[32,1,160]{2,1,0:T(1,128)} %get-tuple-element.61.refs_1_.pos, ...), custom_call_target="tpu_custom_call" | custom-call | tf_op jit(solution)/shard_map/experts_bwd/pallas_call | solution.py:1590
  448.0 99.8 %sum_world.3 = (f32[160,2048]{1,0:T(8,128)}, f32[32,1,160]{2,1,0:T(1,128)}) custom-call(bf16[16,112,2048]{2,1,0:T(8,128)(2,1)} %bitcast.64, f32[32,1,160]{2,1,0:T(1,128)} %get-tuple-element.61.refs_1_.pos, f32[32,1,160]{2,1,0:T(1,128)} %get-tuple-element.68.refs_2_), custom_call_target="tpu_custom_call" | custom-call | tf_op jit(solution)/shard_map/sum_world/pallas_call | solution.py:1795
  548.6 2.0 multiply_reduce_fusion.1
  550.6 1.9 fusion.17
  552.5 26.6 %branch_exchange.1 = (bf16[640,1024]{1,0:T(8,128)(2,1)}, bf16[640,2048]{1,0:T(8,128)(2,1)}, bf16[1024,640]{1,0:T(8,128)(2,1)}) custom-call(bf16[160,2048]{1,0:T(8,128)(2,1)} %get-tuple-element.101.mine, bf16[1024,2048]{1,0:T(8,128)(2,1)} %wo_in.3, bf16[640,1024]{1,0:T(8,128)(2,1)} %get-tuple-element.59.attn_in), custom_call_target="tpu_custom_call" | custom-call | tf_op jit(solution)/shard_map/branch_exchange/pallas_call | solution.py:435
  579.1 28.6 %attention_bwd.1 = (bf16[640,1024]{1,0:T(8,128)(2,1)}, f32[4,384,128]{2,1,0:T(8,128)}, f32[4,384,128]{2,1,0:T(8,128)}, f32[4,8,128]{2,1,0:T(8,128)}, bf16[1024,2048]{1,0:T(8,128)(2,1)}) custom-call(s32[32]{0:T(128)} %lengths.3, f32[640,1280]{1,0:T(8,128)} %get-tuple-element.56.lin, bf16[640,1024]{1,0:T(8,128)(2,1)} %get-tuple-element.62.queries, ...), custom_call_target="tpu_custom_call" | custom-call | tf_op jit(solution)/shard_map/attention_bwd/pallas_call | solution.py:1119
  610.2 103.3 %dqkv_line_exchange.1 = (f32[160,2048]{1,0:T(8,128)}, f32[64,4096]{1,0:T(8,128)}, f32[64,512]{1,0:T(8,128)}, f32[64,512]{1,0:T(8,128)}, f32[128,2048]{1,0:T(8,12...) custom-call(bf16[640,1024]{1,0:T(8,128)(2,1)} %get-tuple-element.74.d_q, f32[4,384,128]{2,1,0:T(8,128)} %get-tuple-element.75.d_keys, ...), custom_call_target="tpu_custom_call" | custom-call | tf_op jit(solution)/shard_map/dqkv_line_exchange/pallas_call | solution.py:937
  716.5 1.6 fusion.5
  718.1 1.4 fusion.1
  720.3 24.6 %expert_grads.1 = (f32[2048,768]{1,0:T(8,128)}, f32[2048,768]{1,0:T(8,128)}, f32[768,2048]{1,0:T(8,128)}) custom-call(bf16[1792,2048]{1,0:T(8,128)(2,1)} %get-tuple-element.88.x, bf16[1792,768]{1,0:T(8,128)(2,1)} %get-tuple-element.89.d_gate, bf16[1792,768]{1,0:T(8,128)(2,1)} %get-tuple-element.90.d_up, bf16[1792,768]{1,0:T(8,128)(2,1)} %get-tuple-element.91.hidden, ...), custom_call_target="tpu_custom_call" | custom-call | tf_op jit(solution)/shard_map/expert_grads/pallas_call | solution.py:1843
  744.9 1.5 slice.25
  748.2 1.2 slice_reduce_fusion
  (77 shorter events, 15.8 us)
Async XLA Ops:
  0.6 126.8 %copy-start = (bf16[2048,32]{0,1:T(8,128)(2,1)S(1)}, bf16[2048,32]{0,1:T(8,128)(2,1)}, u32[]{:S(2)}) copy-start(bf16[2048,32]{0,1:T(8,128)(2,1)} %param.24) | copy-start | bytes 393220
  97.2 27.9 %copy-start.2 = (bf16[160,2048]{1,0:T(8,128)(2,1)S(1)}, bf16[160,2048]{1,0:T(8,128)(2,1)}, u32[]{:S(2)}) copy-start(bf16[160,2048]{1,0:T(8,128)(2,1)} %param.16) | copy-start | bytes 1966084
  125.1 1.6 copy-start.18
  126.7 0.7 copy-start.19
  126.9 1.6 copy-start.4
  236.7 101.0 %copy-start.6 = (bf16[160,2048]{1,0:T(8,128)(2,1)S(1)}, bf16[160,2048]{1,0:T(8,128)(2,1)}, u32[]{:S(2)}) copy-start(bf16[160,2048]{1,0:T(8,128)(2,1)} %param.17) | copy-start | bytes 1966084
  337.7 2.5 copy-start.20
  340.2 210.5 %copy-start.3 = (f32[160,2048]{1,0:T(8,128)}, f32[160,2048]{1,0:T(8,128)S(1)}, u32[]{:S(2)}) copy-start(f32[160,2048]{1,0:T(8,128)S(1)} %get-tuple-element.130) | copy-start | bytes 3932164
  548.6 2.1 copy-start.7
  579.1 30.0 %copy-start.5 = (bf16[160,2048]{1,0:T(8,128)(2,1)S(1)}, bf16[160,2048]{1,0:T(8,128)(2,1)}, u32[]{:S(2)}) copy-start(bf16[160,2048]{1,0:T(8,128)(2,1)} %copy-done.4) | copy-start | bytes 1966084
  579.1 30.0 %copy-start.14 = (f32[32,1,160]{2,1,0:T(1,128)S(1)}, f32[32,1,160]{2,1,0:T(1,128)}, u32[]{:S(2)}) copy-start(f32[32,1,160]{2,1,0:T(1,128)} %get-tuple-element.70) | copy-start | bytes 61444
  610.2 106.3 %copy-start.15 = (f32[2048]{0:T(1024)S(1)}, f32[2048]{0:T(1024)}, u32[]{:S(2)}) copy-start(f32[2048]{0:T(1024)} %param.28) | copy-start | bytes 24580
  713.4 4.7 copy-start.8
  713.4 4.7 copy-start.9
  714.6 0.7 copy-start.13
  718.1 1.4 copy-start.10
  720.3 29.2 %copy-start.12 = (f32[64,4096]{1,0:T(8,128)S(1)}, f32[64,4096]{1,0:T(8,128)}, u32[]{:S(2)}) copy-start(f32[64,4096]{1,0:T(8,128)} %get-tuple-element.133) | copy-start | bytes 3145732
  744.9 5.5 copy-start.17
  744.9 6.2 copy-start.16
  749.4 2.3 copy-start.11
  749.4 3.3 copy-start.1

commit v8 on v7

--- a/solution.py
+++ b/solution.py
@@ -1008,7 +1008,9 @@
     return sees_prompt | sees_cont
 
 
-def attention_fwd_kernel(prompt_len, lengths, lin, gain, cos, sin, keys, values, queries, attn):
+def attention_fwd_kernel(
+    prompt_len, lengths, lin, gain, cos, sin, keys, values, queries, attn, q_all, score_all, low_all
+):
     block = pl.program_id(0)
     slots = lin.shape[0]
     head = gain.shape[1]
@@ -1018,17 +1020,24 @@
     scale = head ** (-0.5)
     k, v = keys[0], values[0]
     c, s, g = cos[0], sin[0], gain[...]
-    for h in range(lin.shape[1] // head):
-        part = slice(h * head, (h + 1) * head)
-        x = lin[:, part]
+    heads = lin.shape[1] // head
+    parts = [slice(h * head, (h + 1) * head) for h in range(heads)]
+    rows = [slice(h * slots, (h + 1) * slots) for h in range(heads)]
+    for h in range(heads):
+        x = lin[:, parts[h]]
         x = x * lax.rsqrt(jnp.mean(x * x, axis=-1, keepdims=True) + norm_eps) * g
         q = (x * c + pltpu.roll(x, head // 2, 1) * s).astype(BF16)
-        queries[:, part] = q
-        score = jnp.where(allowed, dot_nt(q, k) * scale, -jnp.inf)
+        queries[:, parts[h]] = q
+        q_all[rows[h]] = q
+    score_all[...] = dot_nt(q_all[...], k)
+    for h in range(heads):
+        score = jnp.where(allowed, score_all[rows[h]] * scale, -jnp.inf)
         peak = jnp.max(score, axis=-1, keepdims=True)
         exponent = jnp.exp(score - peak)
-        low = (exponent * (1.0 / jnp.sum(exponent, axis=-1, keepdims=True))).astype(BF16)
-        attn[:, part] = dot_nn(low, v).astype(BF16)
+        low_all[rows[h]] = (exponent * (1.0 / jnp.sum(exponent, axis=-1, keepdims=True))).astype(BF16)
+    out = dot_nn(low_all[...], v)
+    for h in range(heads):
+        attn[:, parts[h]] = out[rows[h]].astype(BF16)
 
 
 def attention_fwd(lengths, lin, gain, cos, sin, keys, values, prompt_len):
@@ -1046,6 +1055,11 @@
             grid=(blocks,),
             in_specs=[row, one, table, table, kv, kv],
             out_specs=[row, row],
+            scratch_shapes=[
+                pltpu.VMEM((slots * width // head, head), BF16),
+                pltpu.VMEM((slots * width // head, total_keys), F32),
+                pltpu.VMEM((slots * width // head, total_keys), BF16),
+            ],
         ),
         out_shape=(
             jax.ShapeDtypeStruct((lin.shape[0], width), BF16),
@@ -1059,6 +1073,7 @@
 def attention_bwd_kernel(
     prompt_len, lengths, lin, queries, d_attn, gain, cos, sin, keys, values, attn_t, d_branch,
     d_lin, d_keys, d_values, d_gain, out_part,
+    q_all, d_all, score_all, d_probs_all, low_all, d_score_all, d_q_all,
 ):
     block = pl.program_id(0)
     slots = lin.shape[0]
@@ -1069,39 +1084,43 @@
     scale = head ** (-0.5)
     k, v = keys[0], values[0]
     c, s, g = cos[0], sin[0], gain[...]
-    key_total = jnp.zeros(k.shape, F32)
-    value_total = jnp.zeros(v.shape, F32)
-    gain_total = jnp.zeros((8, head), F32)
-    for h in range(lin.shape[1] // head):
-        part = slice(h * head, (h + 1) * head)
-        q = queries[:, part]
-        score = jnp.where(allowed, dot_nt(q, k) * scale, -jnp.inf)
+    heads = lin.shape[1] // head
+    parts = [slice(h * head, (h + 1) * head) for h in range(heads)]
+    rows = [slice(h * slots, (h + 1) * slots) for h in range(heads)]
+    for h in range(heads):
+        q_all[rows[h]] = queries[:, parts[h]]
+        d_all[rows[h]] = d_attn[:, parts[h]]
+    score_all[...] = dot_nt(q_all[...], k)
+    d_probs_all[...] = dot_nt(d_all[...], v)
+    for h in range(heads):
+        score = jnp.where(allowed, score_all[rows[h]] * scale, -jnp.inf)
         peak = jnp.max(score, axis=-1, keepdims=True)
         exponent = jnp.exp(score - peak)
         probs = exponent * (1.0 / jnp.sum(exponent, axis=-1, keepdims=True))
-        d_out = d_attn[:, part]
-        d_probs = dot_nt(d_out, v)
+        d_probs = d_probs_all[rows[h]]
         inner = jnp.sum(probs * d_probs, axis=-1, keepdims=True)
-        d_score = (probs * (d_probs - inner)).astype(BF16)
-        key_total = key_total + dot_tn(d_score, q)
-        value_total = value_total + dot_tn(probs.astype(BF16), d_out)
-        d_q = dot_nn(d_score, k) * scale
+        low_all[rows[h]] = probs.astype(BF16)
+        d_score_all[rows[h]] = (probs * (d_probs - inner)).astype(BF16)
+    d_q_all[...] = dot_nn(d_score_all[...], k)
+    d_keys[0] = dot_tn(d_score_all[...], q_all[...]) * scale
+    d_values[0] = dot_tn(low_all[...], d_all[...])
+    for n in range(2):
+        half = slice(n * out_part.shape[1] // 2, (n + 1) * out_part.shape[1] // 2)
+        out_part[:, half] = dot_nn(attn_t[...], d_branch[:, half]).astype(BF16)
+    gain_total = jnp.zeros((8, head), F32)
+    for h in range(heads):
+        d_q = d_q_all[rows[h]] * scale
         turned = d_q * c + pltpu.roll(d_q * s, head // 2, 1)
-        x = lin[:, part]
+        x = lin[:, parts[h]]
         inverse = lax.rsqrt(jnp.mean(x * x, axis=-1, keepdims=True) + norm_eps)
         unit = x * inverse
         pairs = turned * unit
         for j in range(slots // 8):
             gain_total = gain_total + pairs[j * 8 : (j + 1) * 8]
         weighted = turned * g
-        d_lin[:, part] = (
+        d_lin[:, parts[h]] = (
             inverse * (weighted - unit * jnp.mean(weighted * unit, axis=-1, keepdims=True))
         ).astype(BF16)
-        if h % 4 == 3:
-            n = slice(h // 4 * 256, h // 4 * 256 + 256)
-            out_part[:, n] = dot_nn(attn_t[...], d_branch[:, n]).astype(BF16)
-    d_keys[0] = key_total * scale
-    d_values[0] = value_total
     d_gain[0] = gain_total
 
 
@@ -1132,6 +1151,15 @@
                 kv,
                 pl.BlockSpec((1, 8, head), lambda i, *_: (i, 0, 0)),
                 pl.BlockSpec((attn_t.shape[0], step), lambda i, *_: (0, i)),
+            ],
+            scratch_shapes=[
+                pltpu.VMEM((slots * width // head, head), BF16),
+                pltpu.VMEM((slots * width // head, head), BF16),
+                pltpu.VMEM((slots * width // head, total_keys), F32),
+                pltpu.VMEM((slots * width // head, total_keys), F32),
+                pltpu.VMEM((slots * width // head, total_keys), BF16),
+                pltpu.VMEM((slots * width // head, total_keys), BF16),
+                pltpu.VMEM((slots * width // head, head), F32),
             ],
         ),
         out_shape=(

time: 765 us -> 750 us (0.980)
  Pallas kernels: 713 us -> 698 us
    pallas_call x1, Pallas kernels: 28.6 us -> 17.3 us  [attention_bwd(): pl.pallas_call(functools.partial(attention_bwd_kernel, prompt_len), grid_...]
where the time goes in v8:
time: 750 us; the launch traced here: 739 us
  Pallas kernels  698 us (93%)
  other arithmetic  21.5 us (3%)
  local copies, waits for them, and re-layouts  13.6 us (2%)
    pallas_call x2, Pallas kernels, sum_world(): pl.pallas_call(functools.partial(sum_world_kernel, len(extra) > 0), out_s...  201 us
    pallas_call x1, Pallas kernels, experts_fwd(): pl.pallas_call(functools.partial(experts_fwd_kernel, capacity), out_shape...  108 us
    pallas_call x1, Pallas kernels, experts_bwd(): pl.pallas_call(experts_bwd_kernel, out_shape=(jax.ShapeDtypeStruct((32, 1...  104 us
    pallas_call x1, Pallas kernels, grad_qkv_line(): pl.pallas_call(dgrad_line_kernel, out_shape=(jax.ShapeDtypeStruct((tok, 4...  103 us
    pallas_call x1, Pallas kernels, project_qkv(): pl.pallas_call(functools.partial(qkv_kernel, tok), out_shape=(jax.ShapeDt...  73.2 us
    pallas_call x1, Pallas kernels, project_out(): pl.pallas_call(out_kernel, out_shape=jax.ShapeDtypeStruct((tok, wo.shape[...  27.9 us
    pallas_call x1, Pallas kernels, grad_branch(): pl.pallas_call(branch_kernel, out_shape=(jax.ShapeDtypeStruct((4 * tok, w...  26.6 us
    pallas_call x1, Pallas kernels, expert_grads(): pl.pallas_call(expert_grads_kernel, grid=(model // step,), in_specs=[colu...  24.6 us

profile of v8, /device:TPU:8, one launch (start us, length us, event | category | flops | bytes accessed | tf_op | source)
XLA Modules:
  0.0 739.2 jit_solution(1923137958542949122)
XLA Ops:
  0.7 1.3 dynamic_slice.3
  2.6 1.3 fusion.2
  3.9 2.1 fusion.4.normed
  6.2 1.2 fusion.8
  8.5 73.2 %qkv_exchange.1 = (f32[640,1280]{1,0:T(8,128)}, bf16[512,640]{1,0:T(8,128)(2,1)}, bf16[640,512]{1,0:T(8,128)(2,1)}, f32[640,128]{1,0:T(8,128)}, bf16[4,384,128]{...) custom-call(bf16[160,2048]{1,0:T(8,128)(2,1)} %fusion.4.normed, bf16[512,4096]{1,0:T(8,128)(2,1)} %wq_in.3, ...), custom_call_target="tpu_custom_call" | custom-call | tf_op jit(solution)/shard_map/qkv_exchange/pallas_call | solution.py:212
  81.7 11.8 %attention_fwd.1 = (bf16[640,1024]{1,0:T(8,128)(2,1)}, bf16[640,1024]{1,0:T(8,128)(2,1)}) custom-call(s32[32]{0:T(128)} %lengths.3, f32[640,1280]{1,0:T(8,128)} %get-tuple-element.56.lin, f32[1,128]{1,0:T(1,128)} %bitcast.81, f32[4,160,128]{2,1,0:T(8,128)} %get-tuple-element.113.cos, f32[4,160,128]{2,1,0:T(8,128)} %get-tuple-element.114.sin, ...), custom_call_target="tpu_custom_call" | custom-call | tf_op jit(solution)/shard_map/attention_fwd/pallas_call | solution.py:1051
  93.4 27.9 %out_exchange.1 = f32[160,2048]{1,0:T(8,128)} custom-call(bf16[640,1024]{1,0:T(8,128)(2,1)} %get-tuple-element.59.attn_in, bf16[1024,2048]{1,0:T(8,128)(2,1)} %wo_in.3), custom_call_target="tpu_custom_call" | custom-call | tf_op jit(solution)/shard_map/out_exchange/pallas_call | solution.py:256
  121.3 1.6 multiply_reduce_fusion.3
  124.7 108.2 %experts_fwd.1 = (f32[32,1,160]{2,1,0:T(1,128)}, bf16[1792,2048]{1,0:T(8,128)(2,1)}, bf16[1792,2048]{1,0:T(8,128)(2,1)}, bf16[1792,768]{1,0:T(8,128)(2,1)}, bf16...) custom-call(bf16[160,2048]{1,0:T(8,128)(2,1)} %copy-done.4, ...), custom_call_target="tpu_custom_call" | custom-call | tf_op jit(solution)/shard_map/experts_fwd/pallas_call | solution.py:1477
  232.9 101.0 %sum_world.2 = f32[160,2048]{1,0:T(8,128)} custom-call(bf16[16,112,2048]{2,1,0:T(8,128)(2,1)} %bitcast.65, f32[32,1,160]{2,1,0:T(1,128)} %get-tuple-element.61.refs_1_.pos), custom_call_target="tpu_custom_call" | custom-call | tf_op jit(solution)/shard_map/sum_world/pallas_call | solution.py:1823
  333.9 2.5 multiply_reduce_fusion
  337.8 2.2 fusion.7.mine
  339.9 104.2 %experts_bwd.1 = (f32[32,1,160]{2,1,0:T(1,128)}, bf16[1792,2048]{1,0:T(8,128)(2,1)}, bf16[1792,2048]{1,0:T(8,128)(2,1)}, bf16[1792,768]{1,0:T(8,128)(2,1)}, bf16[1792,768]{1,0:T(8,128)(2,1)}) custom-call(bf16[160,2048]{1,0:T(8,128)(2,1)} %fusion.7.mine, f32[32,1,160]{2,1,0:T(1,128)} %get-tuple-element.61.refs_1_.pos, ...), custom_call_target="tpu_custom_call" | custom-call | tf_op jit(solution)/shard_map/experts_bwd/pallas_call | solution.py:1618
  444.2 99.8 %sum_world.3 = (f32[160,2048]{1,0:T(8,128)}, f32[32,1,160]{2,1,0:T(1,128)}) custom-call(bf16[16,112,2048]{2,1,0:T(8,128)(2,1)} %bitcast.64, f32[32,1,160]{2,1,0:T(1,128)} %get-tuple-element.61.refs_1_.pos, f32[32,1,160]{2,1,0:T(1,128)} %get-tuple-element.68.refs_2_), custom_call_target="tpu_custom_call" | custom-call | tf_op jit(solution)/shard_map/sum_world/pallas_call | solution.py:1823
  544.8 2.0 multiply_reduce_fusion.1
  546.8 1.9 fusion.17
  548.7 26.6 %branch_exchange.1 = (bf16[640,1024]{1,0:T(8,128)(2,1)}, bf16[640,2048]{1,0:T(8,128)(2,1)}, bf16[1024,640]{1,0:T(8,128)(2,1)}) custom-call(bf16[160,2048]{1,0:T(8,128)(2,1)} %get-tuple-element.101.mine, bf16[1024,2048]{1,0:T(8,128)(2,1)} %wo_in.3, bf16[640,1024]{1,0:T(8,128)(2,1)} %get-tuple-element.59.attn_in), custom_call_target="tpu_custom_call" | custom-call | tf_op jit(solution)/shard_map/branch_exchange/pallas_call | solution.py:435
  575.3 17.3 %attention_bwd.1 = (bf16[640,1024]{1,0:T(8,128)(2,1)}, f32[4,384,128]{2,1,0:T(8,128)}, f32[4,384,128]{2,1,0:T(8,128)}, f32[4,8,128]{2,1,0:T(8,128)}, bf16[1024,2048]{1,0:T(8,128)(2,1)}) custom-call(s32[32]{0:T(128)} %lengths.3, f32[640,1280]{1,0:T(8,128)} %get-tuple-element.56.lin, bf16[640,1024]{1,0:T(8,128)(2,1)} %get-tuple-element.62.queries, ...), custom_call_target="tpu_custom_call" | custom-call | tf_op jit(solution)/shard_map/attention_bwd/pallas_call | solution.py:1138
  595.1 103.3 %dqkv_line_exchange.1 = (f32[160,2048]{1,0:T(8,128)}, f32[64,4096]{1,0:T(8,128)}, f32[64,512]{1,0:T(8,128)}, f32[64,512]{1,0:T(8,128)}, f32[128,2048]{1,0:T(8,12...) custom-call(bf16[640,1024]{1,0:T(8,128)(2,1)} %get-tuple-element.74.d_q, f32[4,384,128]{2,1,0:T(8,128)} %get-tuple-element.75.d_keys, ...), custom_call_target="tpu_custom_call" | custom-call | tf_op jit(solution)/shard_map/dqkv_line_exchange/pallas_call | solution.py:937
  701.4 1.6 fusion.5
  703.0 1.4 fusion.1
  705.2 24.6 %expert_grads.1 = (f32[2048,768]{1,0:T(8,128)}, f32[2048,768]{1,0:T(8,128)}, f32[768,2048]{1,0:T(8,128)}) custom-call(bf16[1792,2048]{1,0:T(8,128)(2,1)} %get-tuple-element.88.x, bf16[1792,768]{1,0:T(8,128)(2,1)} %get-tuple-element.89.d_gate, bf16[1792,768]{1,0:T(8,128)(2,1)} %get-tuple-element.90.d_up, bf16[1792,768]{1,0:T(8,128)(2,1)} %get-tuple-element.91.hidden, ...), custom_call_target="tpu_custom_call" | custom-call | tf_op jit(solution)/shard_map/expert_grads/pallas_call | solution.py:1871
  729.8 1.5 slice.25
  733.1 1.2 slice_reduce_fusion
  (77 shorter events, 15.8 us)
Async XLA Ops:
  0.6 123.0 %copy-start = (bf16[2048,32]{0,1:T(8,128)(2,1)S(1)}, bf16[2048,32]{0,1:T(8,128)(2,1)}, u32[]{:S(2)}) copy-start(bf16[2048,32]{0,1:T(8,128)(2,1)} %param.24) | copy-start | bytes 393220
  93.4 27.9 %copy-start.2 = (bf16[160,2048]{1,0:T(8,128)(2,1)S(1)}, bf16[160,2048]{1,0:T(8,128)(2,1)}, u32[]{:S(2)}) copy-start(bf16[160,2048]{1,0:T(8,128)(2,1)} %param.16) | copy-start | bytes 1966084
  121.3 1.6 copy-start.18
  122.9 0.7 copy-start.19
  123.1 1.6 copy-start.4
  232.9 101.0 %copy-start.6 = (bf16[160,2048]{1,0:T(8,128)(2,1)S(1)}, bf16[160,2048]{1,0:T(8,128)(2,1)}, u32[]{:S(2)}) copy-start(bf16[160,2048]{1,0:T(8,128)(2,1)} %param.17) | copy-start | bytes 1966084
  333.9 2.5 copy-start.20
  336.3 210.5 %copy-start.3 = (f32[160,2048]{1,0:T(8,128)}, f32[160,2048]{1,0:T(8,128)S(1)}, u32[]{:S(2)}) copy-start(f32[160,2048]{1,0:T(8,128)S(1)} %get-tuple-element.130) | copy-start | bytes 3932164
  544.8 2.1 copy-start.7
  575.3 18.7 %copy-start.5 = (bf16[160,2048]{1,0:T(8,128)(2,1)S(1)}, bf16[160,2048]{1,0:T(8,128)(2,1)}, u32[]{:S(2)}) copy-start(bf16[160,2048]{1,0:T(8,128)(2,1)} %copy-done.4) | copy-start | bytes 1966084
  575.3 18.7 %copy-start.14 = (f32[32,1,160]{2,1,0:T(1,128)S(1)}, f32[32,1,160]{2,1,0:T(1,128)}, u32[]{:S(2)}) copy-start(f32[32,1,160]{2,1,0:T(1,128)} %get-tuple-element.70) | copy-start | bytes 61444
  595.1 106.3 %copy-start.15 = (f32[2048]{0:T(1024)S(1)}, f32[2048]{0:T(1024)}, u32[]{:S(2)}) copy-start(f32[2048]{0:T(1024)} %param.28) | copy-start | bytes 24580
  698.4 4.7 copy-start.8
  698.4 4.7 copy-start.9
  699.5 0.7 copy-start.13
  703.0 1.4 copy-start.10
  705.2 29.2 %copy-start.12 = (f32[64,4096]{1,0:T(8,128)S(1)}, f32[64,4096]{1,0:T(8,128)}, u32[]{:S(2)}) copy-start(f32[64,4096]{1,0:T(8,128)} %get-tuple-element.133) | copy-start | bytes 3145732
  729.8 5.5 copy-start.17
  729.8 6.2 copy-start.16
  734.4 2.3 copy-start.11
  734.4 3.3 copy-start.1

commit v9 on v8

--- a/solution.py
+++ b/solution.py
@@ -138,8 +138,9 @@
 
 
 def qkv_kernel(
-    tok, normed, wq_in, wk_in, wv_in, gain, cos, sin, lin, cols_t, cols, key_lin, keys, values,
-    wq, wk, wv, own_kv, other_kv, local, asend, arecv, ksend, krecv, *relay,
+    tok, tokens, in_gain, wq_in, wk_in, wv_in, gain, cos, sin,
+    lin, cols_t, cols, key_lin, keys, values, inverse_out,
+    normed, wq, wk, wv, own_kv, other_kv, local, asend, arecv, ksend, krecv, *relay,
 ):
     r, e = lax.axis_index("dp"), lax.axis_index("expert")
     peers = [r ^ m for m in PEER_MASKS]
@@ -148,6 +149,10 @@
     kg = wk.shape[1] // 4
     rows = cols.shape[0]
     loads = loading(((wq_in, wq), (wk_in, wk), (wv_in, wv)), local)
+    value = tokens[...].astype(F32)
+    inverse = lax.rsqrt(jnp.mean(value * value, axis=-1, keepdims=True) + norm_eps)
+    normed[...] = (value * inverse * in_gain[...]).astype(BF16)
+    inverse_out[...] = jnp.broadcast_to(inverse, inverse_out.shape)
     greet([(p, e) for p in peers] + [(r, e ^ 1)])
     first = []
     for i, p in enumerate(peers):
@@ -203,8 +208,8 @@
             out[i, aligned(1 - core, column)] = other_kv[n]
 
 
-def project_qkv(normed, wq, wk, wv, gain, cos, sin):
-    tok = normed.shape[0]
+def project_qkv(tokens, in_gain, wq, wk, wv, gain, cos, sin):
+    tok = tokens.shape[0]
     rows = 4 * tok
     group = (wq.shape[1] + wk.shape[1] + wv.shape[1]) // 4
     head = gain.shape[1]
@@ -218,17 +223,18 @@
             jax.ShapeDtypeStruct((rows, head), F32),
             jax.ShapeDtypeStruct((4, total_keys, head), BF16),
             jax.ShapeDtypeStruct((4, total_keys, head), BF16),
+            jax.ShapeDtypeStruct((tok, 128), F32),
         ),
-        in_specs=[VMEM_SPEC] + [ANY_SPEC] * 3 + [VMEM_SPEC] * 3,
-        out_specs=(VMEM_SPEC,) * 6,
-        scratch_shapes=[pltpu.VMEM(w.shape, BF16) for w in (wq, wk, wv)]
+        in_specs=[VMEM_SPEC] * 2 + [ANY_SPEC] * 3 + [VMEM_SPEC] * 3,
+        out_specs=(VMEM_SPEC,) * 7,
+        scratch_shapes=[pltpu.VMEM(w.shape, BF16) for w in (tokens, wq, wk, wv)]
         + [pltpu.VMEM((2, 4 * (tok - CMAX), head), BF16)] * 2
         + [pltpu.SemaphoreType.DMA((3,))] * 3
         + [pltpu.SemaphoreType.DMA((1,))] * 2
         + relay_scratch(rows, group),
         compiler_params=params(1),
         name="qkv_exchange",
-    )(normed, wq, wk, wv, gain, cos, sin)
+    )(tokens, in_gain, wq, wk, wv, gain, cos, sin)
 
 
 def out_kernel(attn_in, wo_in, total, attn, wo, local, *relay):
@@ -1998,7 +2004,7 @@
     )
     d_mixed = d_mixed + contract(d_logits, router_weight, 1, 1)
     router_local = contract(d_logits, mixed, 0, 0)
-    return layer_out, d_out, d_mixed, local_square, router_local, gate_grad, up_grad, down_grad
+    return layer_out, d_out, d_mixed, local_square, router_local, (gate_grad, up_grad, down_grad)
 
 
 def experts_by_gather(
@@ -2028,13 +2034,11 @@
     back, d_gates = sum_world(d_rows.reshape(16, room, model_width), pos, tok_dev, 9, d_gates)
     d_gates = d_gates[:, 0].T
 
-    gate_grad, up_grad, down_grad = (
-        grad[None] for grad in expert_grads(x_rows, d_gate, d_up, hidden, d_copy)
-    )
+    grad_rows = (x_rows, d_gate, d_up, hidden, d_copy)
     d_logits = (gates * (d_gates - jnp.sum(gates * d_gates, axis=-1, keepdims=True))).astype(BF16)
     d_mixed = back + contract(d_logits, router_weight, 1, 1)
     router_local = contract(d_logits, mixed, 0, 0)
-    return layer_out, d_out, d_mixed, local_square, router_local, gate_grad, up_grad, down_grad
+    return layer_out, d_out, d_mixed, local_square, router_local, grad_rows
 
 
 def head_rope(linear, gain_vec, cos, sin):
@@ -2082,12 +2086,11 @@
     capacity = max(2, tok_dev * top_count * 5 // (4 * devices))
     slots_all = devices * tok_dev
     slot_ids = jnp.arange(tok_dev, dtype=jnp.int32)
-    own_length = cont_lengths[flat_rank]
+    is_own = jnp.arange(devices, dtype=jnp.int32) == flat_rank
+    own_length = jnp.sum(jnp.where(is_own, cont_lengths, 0))
     valid_slot = (slot_ids < prompt_block) | (slot_ids - prompt_block < own_length)
     valid_count = (devices * prompt_block + jnp.sum(cont_lengths)).astype(F32)
     tokens_float = tokens.astype(F32)
-    normed_float, first_norm_back = jax.vjp(root_mean_scale, tokens_float, input_gain)
-    normed = normed_float.astype(BF16)
 
     block_ids = jnp.arange(n_dp, dtype=jnp.int32)[:, None]
     positions = jnp.where(
@@ -2101,8 +2104,8 @@
     cos_half, sin_half = jnp.cos(angles), jnp.sin(angles)
     cos = jnp.concatenate([cos_half, cos_half], axis=-1)
     sin = jnp.concatenate([-sin_half, sin_half], axis=-1)
-    lin, normed_cols_t, normed_cols, key_lin, all_keys, all_values = project_qkv(
-        normed, query_weight, key_projection, value_projection, key_gain[None], cos, sin
+    lin, normed_cols_t, normed_cols, key_lin, all_keys, all_values, inverse = project_qkv(
+        tokens, input_gain[None], query_weight, key_projection, value_projection, key_gain[None], cos, sin
     )
     query_gain_row = query_gain[None]
     queries, attended = attention_fwd(
@@ -2121,7 +2124,7 @@
         moe = experts_by_all_to_all(
             mixed, state, teacher, routes, valid_slot, valid_count, *weights, *sizes
         )
-    layer_out, d_out, d_mixed, local_square, router_local, gate_grad, up_grad, down_grad = moe
+    layer_out, d_out, d_mixed, local_square, router_local, grad_rows = moe
     d_state_norm, d_post_gain = second_norm_back(d_mixed)
     d_state = d_out + d_state_norm
     d_branch = d_state.astype(BF16)
@@ -2167,7 +2170,6 @@
         router_grad, post_gain_grad = sums[:at].T, sums[at]
         query_gain_grad = sums[at + 1, :head_dim]
         total_square = sums[at + 2, :1]
-        d_tokens_norm = first_norm_back(d_normed)[0]
     else:
         _, key_back = jax.vjp(
             lambda a, b: head_rope(a, b, cos, sin), key_lin.reshape(n_dp, tok_dev, head_dim), key_gain
@@ -2194,8 +2196,7 @@
         )
         small_parts = [router_local, d_post_gain, d_query_gain, d_key_gain, local_square[None]]
         d_normed, qkv_part, output_grad = grad_qkv(d_lin, *weights, normed_cols_t, out_part)
-        d_tokens_norm, d_input_gain = first_norm_back(d_normed)
-        small_parts.append(d_input_gain)
+        small_parts.append(jnp.sum(d_normed * tokens_float * inverse[:, :1], axis=0))
         by_owner = (
             qkv_part.reshape(n_dp, n_owner, rows_here, group)
             .transpose(1, 0, 2, 3)
@@ -2218,7 +2219,15 @@
         sums = [small[i:j].reshape(a.shape) for a, i, j in zip(small_parts, starts, starts[1:])]
         router_grad, post_gain_grad, query_gain_grad, key_gain_grad, total_square, input_gain_grad = sums
         router_grad = router_grad.T
-    tokens_grad = d_state + d_tokens_norm
+    inverse = inverse[:, :1]
+    weighted = d_normed * input_gain
+    along = jnp.mean(weighted * tokens_float, axis=-1, keepdims=True) * inverse * inverse
+    tokens_grad = d_state + inverse * (weighted - tokens_float * along)
+    if by_line:
+        gate_grad, up_grad, down_grad = expert_grads(*grad_rows)
+        gate_grad, up_grad, down_grad = gate_grad[None], up_grad[None], down_grad[None]
+    else:
+        gate_grad, up_grad, down_grad = grad_rows
     loss = total_square[0] / (valid_count * model_width)
     return (
         layer_out,

time: 750 us -> 745 us (level)
  no operation moved by 1% of the time
where the time goes in v9:
time: 745 us; the launch traced here: 735 us
  Pallas kernels  698 us (94%)
  other arithmetic  17.7 us (2%)
  local copies, waits for them, and re-layouts  12.4 us (2%)
    pallas_call x2, Pallas kernels, sum_world(): pl.pallas_call(functools.partial(sum_world_kernel, len(extra) > 0), out_s...  201 us
    pallas_call x1, Pallas kernels, experts_fwd(): pl.pallas_call(functools.partial(experts_fwd_kernel, capacity), out_shape...  108 us
    pallas_call x1, Pallas kernels, experts_bwd(): pl.pallas_call(experts_bwd_kernel, out_shape=(jax.ShapeDtypeStruct((32, 1...  104 us
    pallas_call x1, Pallas kernels, grad_qkv_line(): pl.pallas_call(dgrad_line_kernel, out_shape=(jax.ShapeDtypeStruct((tok, 4...  103 us
    pallas_call x1, Pallas kernels, project_qkv(): pl.pallas_call(functools.partial(qkv_kernel, tok), out_shape=(jax.ShapeDt...  73.5 us
    pallas_call x1, Pallas kernels, project_out(): pl.pallas_call(out_kernel, out_shape=jax.ShapeDtypeStruct((tok, wo.shape[...  27.9 us
    pallas_call x1, Pallas kernels, grad_branch(): pl.pallas_call(branch_kernel, out_shape=(jax.ShapeDtypeStruct((4 * tok, w...  26.6 us
    pallas_call x1, Pallas kernels, expert_grads(): pl.pallas_call(expert_grads_kernel, grid=(model // step,), in_specs=[colu...  24.6 us

profile of v9, /device:TPU:8, one launch (start us, length us, event | category | flops | bytes accessed | tf_op | source)
XLA Modules:
  0.0 734.6 jit_solution(8128960311160172494)
XLA Ops:
  0.7 1.3 fusion.17
  2.8 1.2 fusion.7
  5.1 73.5 %qkv_exchange.1 = (f32[640,1280]{1,0:T(8,128)}, bf16[512,640]{1,0:T(8,128)(2,1)}, bf16[640,512]{1,0:T(8,128)(2,1)}, f32[640,128]{1,0:T(8,128)}, bf16[4,384,128]{...) custom-call(bf16[160,2048]{1,0:T(8,128)(2,1)} %tokens.1, f32[1,2048]{1,0:T(1,128)} %bitcast.75, ...), custom_call_target="tpu_custom_call" | custom-call | tf_op jit(solution)/shard_map/qkv_exchange/pallas_call | solution.py:217
  78.6 11.8 %attention_fwd.1 = (bf16[640,1024]{1,0:T(8,128)(2,1)}, bf16[640,1024]{1,0:T(8,128)(2,1)}) custom-call(s32[32]{0:T(128)} %lengths.3, f32[640,1280]{1,0:T(8,128)} %get-tuple-element.57.lin, f32[1,128]{1,0:T(1,128)} %bitcast.83, f32[4,160,128]{2,1,0:T(8,128)} %get-tuple-element.119.cos, f32[4,160,128]{2,1,0:T(8,128)} %get-tuple-element.120.sin, ...), custom_call_target="tpu_custom_call" | custom-call | tf_op jit(solution)/shard_map/attention_fwd/pallas_call | solution.py:1057
  90.3 27.9 %out_exchange.1 = f32[160,2048]{1,0:T(8,128)} custom-call(bf16[640,1024]{1,0:T(8,128)(2,1)} %get-tuple-element.60.attn_in, bf16[1024,2048]{1,0:T(8,128)(2,1)} %wo_in.3), custom_call_target="tpu_custom_call" | custom-call | tf_op jit(solution)/shard_map/out_exchange/pallas_call | solution.py:262
  118.2 1.6 multiply_reduce_fusion.3
  121.6 108.2 %experts_fwd.1 = (f32[32,1,160]{2,1,0:T(1,128)}, bf16[1792,2048]{1,0:T(8,128)(2,1)}, bf16[1792,2048]{1,0:T(8,128)(2,1)}, bf16[1792,768]{1,0:T(8,128)(2,1)}, bf16...) custom-call(bf16[160,2048]{1,0:T(8,128)(2,1)} %copy-done.3, ...), custom_call_target="tpu_custom_call" | custom-call | tf_op jit(solution)/shard_map/experts_fwd/pallas_call | solution.py:1483
  229.8 100.9 %sum_world.2 = f32[160,2048]{1,0:T(8,128)} custom-call(bf16[16,112,2048]{2,1,0:T(8,128)(2,1)} %bitcast.65, f32[32,1,160]{2,1,0:T(1,128)} %get-tuple-element.62.refs_1_.pos), custom_call_target="tpu_custom_call" | custom-call | tf_op jit(solution)/shard_map/sum_world/pallas_call | solution.py:1829
  330.8 2.4 multiply_reduce_fusion
  333.9 1.1 fusion.6.mine
  335.0 104.2 %experts_bwd.1 = (f32[32,1,160]{2,1,0:T(1,128)}, bf16[1792,2048]{1,0:T(8,128)(2,1)}, bf16[1792,2048]{1,0:T(8,128)(2,1)}, bf16[1792,768]{1,0:T(8,128)(2,1)}, bf16[1792,768]{1,0:T(8,128)(2,1)}) custom-call(bf16[160,2048]{1,0:T(8,128)(2,1)} %fusion.6.mine, f32[32,1,160]{2,1,0:T(1,128)} %get-tuple-element.62.refs_1_.pos, ...), custom_call_target="tpu_custom_call" | custom-call | tf_op jit(solution)/shard_map/experts_bwd/pallas_call | solution.py:1624
  439.2 99.8 %sum_world.3 = (f32[160,2048]{1,0:T(8,128)}, f32[32,1,160]{2,1,0:T(1,128)}) custom-call(bf16[16,112,2048]{2,1,0:T(8,128)(2,1)} %bitcast.64, f32[32,1,160]{2,1,0:T(1,128)} %get-tuple-element.62.refs_1_.pos, f32[32,1,160]{2,1,0:T(1,128)} %get-tuple-element.69.refs_2_), custom_call_target="tpu_custom_call" | custom-call | tf_op jit(solution)/shard_map/sum_world/pallas_call | solution.py:1829
  539.8 2.0 multiply_reduce_fusion.1
  541.8 1.8 fusion.18
  543.6 26.6 %branch_exchange.1 = (bf16[640,1024]{1,0:T(8,128)(2,1)}, bf16[640,2048]{1,0:T(8,128)(2,1)}, bf16[1024,640]{1,0:T(8,128)(2,1)}) custom-call(bf16[160,2048]{1,0:T(8,128)(2,1)} %get-tuple-element.107.mine, bf16[1024,2048]{1,0:T(8,128)(2,1)} %wo_in.3, bf16[640,1024]{1,0:T(8,128)(2,1)} %get-tuple-element.60.attn_in), custom_call_target="tpu_custom_call" | custom-call | tf_op jit(solution)/shard_map/branch_exchange/pallas_call | solution.py:441
  570.3 17.3 %attention_bwd.1 = (bf16[640,1024]{1,0:T(8,128)(2,1)}, f32[4,384,128]{2,1,0:T(8,128)}, f32[4,384,128]{2,1,0:T(8,128)}, f32[4,8,128]{2,1,0:T(8,128)}, bf16[1024,2048]{1,0:T(8,128)(2,1)}) custom-call(s32[32]{0:T(128)} %lengths.3, f32[640,1280]{1,0:T(8,128)} %get-tuple-element.57.lin, bf16[640,1024]{1,0:T(8,128)(2,1)} %get-tuple-element.63.queries, ...), custom_call_target="tpu_custom_call" | custom-call | tf_op jit(solution)/shard_map/attention_bwd/pallas_call | solution.py:1144
  590.0 103.3 %dqkv_line_exchange.1 = (f32[160,2048]{1,0:T(8,128)}, f32[64,4096]{1,0:T(8,128)}, f32[64,512]{1,0:T(8,128)}, f32[64,512]{1,0:T(8,128)}, f32[128,2048]{1,0:T(8,12...) custom-call(bf16[640,1024]{1,0:T(8,128)(2,1)} %get-tuple-element.75.d_q, f32[4,384,128]{2,1,0:T(8,128)} %get-tuple-element.76.d_keys, ...), custom_call_target="tpu_custom_call" | custom-call | tf_op jit(solution)/shard_map/dqkv_line_exchange/pallas_call | solution.py:943
  693.4 1.1 copy.46
  696.4 1.6 fusion
  698.3 1.5 fusion.3
  700.6 24.6 %expert_grads.1 = (f32[2048,768]{1,0:T(8,128)}, f32[2048,768]{1,0:T(8,128)}, f32[768,2048]{1,0:T(8,128)}) custom-call(bf16[1792,2048]{1,0:T(8,128)(2,1)} %get-tuple-element.90.x, bf16[1792,768]{1,0:T(8,128)(2,1)} %get-tuple-element.91.d_gate, bf16[1792,768]{1,0:T(8,128)(2,1)} %get-tuple-element.92.d_up, bf16[1792,768]{1,0:T(8,128)(2,1)} %get-tuple-element.93.hidden, ...), custom_call_target="tpu_custom_call" | custom-call | tf_op jit(solution)/shard_map/expert_grads/pallas_call | solution.py:1877
  725.2 1.5 slice.29
  727.3 1.2 slice_bitcast_fusion.1
  728.5 1.2 slice_reduce_fusion.1
  (75 shorter events, 13.0 us)
Async XLA Ops:
  0.6 119.9 %copy-start = (bf16[2048,32]{0,1:T(8,128)(2,1)S(1)}, bf16[2048,32]{0,1:T(8,128)(2,1)}, u32[]{:S(2)}) copy-start(bf16[2048,32]{0,1:T(8,128)(2,1)} %param.24) | copy-start | bytes 393220
  90.3 27.9 %copy-start.5 = (bf16[160,2048]{1,0:T(8,128)(2,1)S(1)}, bf16[160,2048]{1,0:T(8,128)(2,1)}, u32[]{:S(2)}) copy-start(bf16[160,2048]{1,0:T(8,128)(2,1)} %tokens.1) | copy-start | bytes 1966084
  118.2 1.6 copy-start.19
  119.8 0.7 copy-start.20
  120.0 1.6 copy-start.3
  229.8 101.0 %copy-start.7 = (bf16[160,2048]{1,0:T(8,128)(2,1)S(1)}, bf16[160,2048]{1,0:T(8,128)(2,1)}, u32[]{:S(2)}) copy-start(bf16[160,2048]{1,0:T(8,128)(2,1)} %param.17) | copy-start | bytes 1966084
  333.2 208.6 %copy-start.2 = (f32[160,2048]{1,0:T(8,128)}, f32[160,2048]{1,0:T(8,128)S(1)}, u32[]{:S(2)}) copy-start(f32[160,2048]{1,0:T(8,128)S(1)} %get-tuple-element.136) | copy-start | bytes 3932164
  570.3 18.7 %copy-start.4 = (bf16[160,2048]{1,0:T(8,128)(2,1)S(1)}, bf16[160,2048]{1,0:T(8,128)(2,1)}, u32[]{:S(2)}) copy-start(bf16[160,2048]{1,0:T(8,128)(2,1)} %copy-done.3) | copy-start | bytes 1966084
  570.3 18.7 %copy-start.14 = (f32[32,1,160]{2,1,0:T(1,128)S(1)}, f32[32,1,160]{2,1,0:T(1,128)}, u32[]{:S(2)}) copy-start(f32[32,1,160]{2,1,0:T(1,128)} %get-tuple-element.71) | copy-start | bytes 61444
  590.0 106.4 %copy-start.6 = (bf16[160,2048]{1,0:T(8,128)(2,1)S(1)}, bf16[160,2048]{1,0:T(8,128)(2,1)}, u32[]{:S(2)}) copy-start(bf16[160,2048]{1,0:T(8,128)(2,1)} %tokens.1) | copy-start | bytes 1966084
  590.0 106.4 %copy-start.15 = (f32[2048]{0:T(1024)S(1)}, f32[2048]{0:T(1024)}, u32[]{:S(2)}) copy-start(f32[2048]{0:T(1024)} %param.28) | copy-start | bytes 24580
  693.3 4.8 copy-start.18
  693.4 5.0 copy-start.8
  693.4 5.0 copy-start.9
  694.5 0.7 copy-start.13
  698.3 1.5 copy-start.10
  700.6 29.2 %copy-start.12 = (f32[64,4096]{1,0:T(8,128)S(1)}, f32[64,4096]{1,0:T(8,128)}, u32[]{:S(2)}) copy-start(f32[64,4096]{1,0:T(8,128)} %get-tuple-element.139) | copy-start | bytes 3145732
  725.2 5.5 copy-start.17
  725.2 6.2 copy-start.16
  729.8 2.3 copy-start.11
  729.8 3.3 copy-start.1

commit v10 on v9

--- a/solution.py
+++ b/solution.py
@@ -112,15 +112,15 @@
         lax.fori_loop(0, half // step, add, 0)
         fulls[n].start()
     own()
-    for copy in fulls:
-        copy.wait_recv()
-
-    def total(c, carry):
-        t = aligned(c, step)
-        mine[t, :] = mine[t, :] + (full_in[0, t, :].astype(F32) + full_in[1, t, :].astype(F32))
-        return carry
-
-    lax.fori_loop(0, rows // step, total, 0)
+    for n, (i, start) in enumerate(((0, 0), (1, half), (0, half), (1, 0))):
+        fulls[n].wait_recv()
+
+        def total(c, carry):
+            t = pl.ds(pl.multiple_of(start + c * step, step), step)
+            mine[t, :] = mine[t, :] + full_in[i, t, :].astype(F32)
+            return carry
+
+        lax.fori_loop(0, half // step, total, 0)
     for copy in relays + fulls:
         copy.wait_send()
 

time: 745 us -> 745 us (level)
  no operation moved by 1% of the time
where the time goes in v10:
time: 745 us; the launch traced here: 734 us
  Pallas kernels  698 us (94%)
  other arithmetic  17.7 us (2%)
  local copies, waits for them, and re-layouts  12.4 us (2%)
    pallas_call x2, Pallas kernels, sum_world(): pl.pallas_call(functools.partial(sum_world_kernel, len(extra) > 0), out_s...  201 us
    pallas_call x1, Pallas kernels, experts_fwd(): pl.pallas_call(functools.partial(experts_fwd_kernel, capacity), out_shape...  108 us
    pallas_call x1, Pallas kernels, experts_bwd(): pl.pallas_call(experts_bwd_kernel, out_shape=(jax.ShapeDtypeStruct((32, 1...  104 us
    pallas_call x1, Pallas kernels, grad_qkv_line(): pl.pallas_call(dgrad_line_kernel, out_shape=(jax.ShapeDtypeStruct((tok, 4...  103 us
    pallas_call x1, Pallas kernels, project_qkv(): pl.pallas_call(functools.partial(qkv_kernel, tok), out_shape=(jax.ShapeDt...  73.1 us
    pallas_call x1, Pallas kernels, project_out(): pl.pallas_call(out_kernel, out_shape=jax.ShapeDtypeStruct((tok, wo.shape[...  28 us
    pallas_call x1, Pallas kernels, grad_branch(): pl.pallas_call(branch_kernel, out_shape=(jax.ShapeDtypeStruct((4 * tok, w...  26.6 us
    pallas_call x1, Pallas kernels, expert_grads(): pl.pallas_call(expert_grads_kernel, grid=(model // step,), in_specs=[colu...  24.6 us

profile of v10, /device:TPU:8, one launch (start us, length us, event | category | flops | bytes accessed | tf_op | source)
XLA Modules:
  0.0 734.4 jit_solution(13824180221574041215)
XLA Ops:
  0.7 1.3 fusion.17
  2.8 1.2 fusion.7
  5.1 73.1 %qkv_exchange.1 = (f32[640,1280]{1,0:T(8,128)}, bf16[512,640]{1,0:T(8,128)(2,1)}, bf16[640,512]{1,0:T(8,128)(2,1)}, f32[640,128]{1,0:T(8,128)}, bf16[4,384,128]{...) custom-call(bf16[160,2048]{1,0:T(8,128)(2,1)} %tokens.1, f32[1,2048]{1,0:T(1,128)} %bitcast.75, ...), custom_call_target="tpu_custom_call" | custom-call | tf_op jit(solution)/shard_map/qkv_exchange/pallas_call | solution.py:217
  78.2 11.8 %attention_fwd.1 = (bf16[640,1024]{1,0:T(8,128)(2,1)}, bf16[640,1024]{1,0:T(8,128)(2,1)}) custom-call(s32[32]{0:T(128)} %lengths.3, f32[640,1280]{1,0:T(8,128)} %get-tuple-element.57.lin, f32[1,128]{1,0:T(1,128)} %bitcast.83, f32[4,160,128]{2,1,0:T(8,128)} %get-tuple-element.119.cos, f32[4,160,128]{2,1,0:T(8,128)} %get-tuple-element.120.sin, ...), custom_call_target="tpu_custom_call" | custom-call | tf_op jit(solution)/shard_map/attention_fwd/pallas_call | solution.py:1057
  89.9 28.0 %out_exchange.1 = f32[160,2048]{1,0:T(8,128)} custom-call(bf16[640,1024]{1,0:T(8,128)(2,1)} %get-tuple-element.60.attn_in, bf16[1024,2048]{1,0:T(8,128)(2,1)} %wo_in.3), custom_call_target="tpu_custom_call" | custom-call | tf_op jit(solution)/shard_map/out_exchange/pallas_call | solution.py:262
  118.0 1.6 multiply_reduce_fusion.3
  121.4 108.2 %experts_fwd.1 = (f32[32,1,160]{2,1,0:T(1,128)}, bf16[1792,2048]{1,0:T(8,128)(2,1)}, bf16[1792,2048]{1,0:T(8,128)(2,1)}, bf16[1792,768]{1,0:T(8,128)(2,1)}, bf16...) custom-call(bf16[160,2048]{1,0:T(8,128)(2,1)} %copy-done.3, ...), custom_call_target="tpu_custom_call" | custom-call | tf_op jit(solution)/shard_map/experts_fwd/pallas_call | solution.py:1483
  229.6 100.9 %sum_world.2 = f32[160,2048]{1,0:T(8,128)} custom-call(bf16[16,112,2048]{2,1,0:T(8,128)(2,1)} %bitcast.65, f32[32,1,160]{2,1,0:T(1,128)} %get-tuple-element.62.refs_1_.pos), custom_call_target="tpu_custom_call" | custom-call | tf_op jit(solution)/shard_map/sum_world/pallas_call | solution.py:1829
  330.6 2.4 multiply_reduce_fusion
  333.6 1.1 fusion.6.mine
  334.8 104.2 %experts_bwd.1 = (f32[32,1,160]{2,1,0:T(1,128)}, bf16[1792,2048]{1,0:T(8,128)(2,1)}, bf16[1792,2048]{1,0:T(8,128)(2,1)}, bf16[1792,768]{1,0:T(8,128)(2,1)}, bf16[1792,768]{1,0:T(8,128)(2,1)}) custom-call(bf16[160,2048]{1,0:T(8,128)(2,1)} %fusion.6.mine, f32[32,1,160]{2,1,0:T(1,128)} %get-tuple-element.62.refs_1_.pos, ...), custom_call_target="tpu_custom_call" | custom-call | tf_op jit(solution)/shard_map/experts_bwd/pallas_call | solution.py:1624
  439.0 99.8 %sum_world.3 = (f32[160,2048]{1,0:T(8,128)}, f32[32,1,160]{2,1,0:T(1,128)}) custom-call(bf16[16,112,2048]{2,1,0:T(8,128)(2,1)} %bitcast.64, f32[32,1,160]{2,1,0:T(1,128)} %get-tuple-element.62.refs_1_.pos, f32[32,1,160]{2,1,0:T(1,128)} %get-tuple-element.69.refs_2_), custom_call_target="tpu_custom_call" | custom-call | tf_op jit(solution)/shard_map/sum_world/pallas_call | solution.py:1829
  539.6 2.0 multiply_reduce_fusion.1
  541.6 1.8 fusion.18
  543.4 26.6 %branch_exchange.1 = (bf16[640,1024]{1,0:T(8,128)(2,1)}, bf16[640,2048]{1,0:T(8,128)(2,1)}, bf16[1024,640]{1,0:T(8,128)(2,1)}) custom-call(bf16[160,2048]{1,0:T(8,128)(2,1)} %get-tuple-element.107.mine, bf16[1024,2048]{1,0:T(8,128)(2,1)} %wo_in.3, bf16[640,1024]{1,0:T(8,128)(2,1)} %get-tuple-element.60.attn_in), custom_call_target="tpu_custom_call" | custom-call | tf_op jit(solution)/shard_map/branch_exchange/pallas_call | solution.py:441
  570.1 17.3 %attention_bwd.1 = (bf16[640,1024]{1,0:T(8,128)(2,1)}, f32[4,384,128]{2,1,0:T(8,128)}, f32[4,384,128]{2,1,0:T(8,128)}, f32[4,8,128]{2,1,0:T(8,128)}, bf16[1024,2048]{1,0:T(8,128)(2,1)}) custom-call(s32[32]{0:T(128)} %lengths.3, f32[640,1280]{1,0:T(8,128)} %get-tuple-element.57.lin, bf16[640,1024]{1,0:T(8,128)(2,1)} %get-tuple-element.63.queries, ...), custom_call_target="tpu_custom_call" | custom-call | tf_op jit(solution)/shard_map/attention_bwd/pallas_call | solution.py:1144
  589.8 103.3 %dqkv_line_exchange.1 = (f32[160,2048]{1,0:T(8,128)}, f32[64,4096]{1,0:T(8,128)}, f32[64,512]{1,0:T(8,128)}, f32[64,512]{1,0:T(8,128)}, f32[128,2048]{1,0:T(8,12...) custom-call(bf16[640,1024]{1,0:T(8,128)(2,1)} %get-tuple-element.75.d_q, f32[4,384,128]{2,1,0:T(8,128)} %get-tuple-element.76.d_keys, ...), custom_call_target="tpu_custom_call" | custom-call | tf_op jit(solution)/shard_map/dqkv_line_exchange/pallas_call | solution.py:943
  693.2 1.1 copy.46
  696.2 1.6 fusion
  698.1 1.5 fusion.3
  700.4 24.6 %expert_grads.1 = (f32[2048,768]{1,0:T(8,128)}, f32[2048,768]{1,0:T(8,128)}, f32[768,2048]{1,0:T(8,128)}) custom-call(bf16[1792,2048]{1,0:T(8,128)(2,1)} %get-tuple-element.90.x, bf16[1792,768]{1,0:T(8,128)(2,1)} %get-tuple-element.91.d_gate, bf16[1792,768]{1,0:T(8,128)(2,1)} %get-tuple-element.92.d_up, bf16[1792,768]{1,0:T(8,128)(2,1)} %get-tuple-element.93.hidden, ...), custom_call_target="tpu_custom_call" | custom-call | tf_op jit(solution)/shard_map/expert_grads/pallas_call | solution.py:1877
  725.0 1.5 slice.29
  727.1 1.2 slice_bitcast_fusion.1
  728.3 1.2 slice_reduce_fusion.1
  (75 shorter events, 13.0 us)
Async XLA Ops:
  0.6 119.7 %copy-start = (bf16[2048,32]{0,1:T(8,128)(2,1)S(1)}, bf16[2048,32]{0,1:T(8,128)(2,1)}, u32[]{:S(2)}) copy-start(bf16[2048,32]{0,1:T(8,128)(2,1)} %param.24) | copy-start | bytes 393220
  89.9 28.0 %copy-start.5 = (bf16[160,2048]{1,0:T(8,128)(2,1)S(1)}, bf16[160,2048]{1,0:T(8,128)(2,1)}, u32[]{:S(2)}) copy-start(bf16[160,2048]{1,0:T(8,128)(2,1)} %tokens.1) | copy-start | bytes 1966084
  118.0 1.6 copy-start.19
  119.6 0.7 copy-start.20
  119.8 1.6 copy-start.3
  229.6 101.0 %copy-start.7 = (bf16[160,2048]{1,0:T(8,128)(2,1)S(1)}, bf16[160,2048]{1,0:T(8,128)(2,1)}, u32[]{:S(2)}) copy-start(bf16[160,2048]{1,0:T(8,128)(2,1)} %param.17) | copy-start | bytes 1966084
  333.0 208.6 %copy-start.2 = (f32[160,2048]{1,0:T(8,128)}, f32[160,2048]{1,0:T(8,128)S(1)}, u32[]{:S(2)}) copy-start(f32[160,2048]{1,0:T(8,128)S(1)} %get-tuple-element.136) | copy-start | bytes 3932164
  570.0 18.7 %copy-start.4 = (bf16[160,2048]{1,0:T(8,128)(2,1)S(1)}, bf16[160,2048]{1,0:T(8,128)(2,1)}, u32[]{:S(2)}) copy-start(bf16[160,2048]{1,0:T(8,128)(2,1)} %copy-done.3) | copy-start | bytes 1966084
  570.1 18.7 %copy-start.14 = (f32[32,1,160]{2,1,0:T(1,128)S(1)}, f32[32,1,160]{2,1,0:T(1,128)}, u32[]{:S(2)}) copy-start(f32[32,1,160]{2,1,0:T(1,128)} %get-tuple-element.71) | copy-start | bytes 61444
  589.8 106.4 %copy-start.6 = (bf16[160,2048]{1,0:T(8,128)(2,1)S(1)}, bf16[160,2048]{1,0:T(8,128)(2,1)}, u32[]{:S(2)}) copy-start(bf16[160,2048]{1,0:T(8,128)(2,1)} %tokens.1) | copy-start | bytes 1966084
  589.8 106.4 %copy-start.15 = (f32[2048]{0:T(1024)S(1)}, f32[2048]{0:T(1024)}, u32[]{:S(2)}) copy-start(f32[2048]{0:T(1024)} %param.28) | copy-start | bytes 24580
  693.1 4.8 copy-start.18
  693.1 5.0 copy-start.8
  693.2 5.0 copy-start.9
  694.3 0.7 copy-start.13
  698.1 1.5 copy-start.10
  700.4 29.2 %copy-start.12 = (f32[64,4096]{1,0:T(8,128)S(1)}, f32[64,4096]{1,0:T(8,128)}, u32[]{:S(2)}) copy-start(f32[64,4096]{1,0:T(8,128)} %get-tuple-element.139) | copy-start | bytes 3145732
  725.0 5.5 copy-start.17
  725.0 6.2 copy-start.16
  729.6 2.3 copy-start.11
  729.6 3.3 copy-start.1
